TPU v7x, 32 devices: a whole 2x2x4 slice. The times are simulated.
32 devices in a mesh: dp: 32 (over z, y, x, core).
Axes of the slice: x: 2, y: 2, z: 4, core: 2. Of those that a mesh axis runs over, the one named last changes fastest.
Arguments:
- frames: bfloat16 [32, 1024, 768], P('dp'), may hold values from -6 to 6
- cotangent: bfloat16 [32, 1024, 768], P('dp'), may hold values from -6 to 6
- lengths: int32 [32], P('dp'), may hold values from 128 to 1024, as said below
- w_qkv: float32 [768, 2304], P('dp'), may hold values from -4 to 4
- w_attn: float32 [768, 768], P('dp'), may hold values from -4 to 4
- w_in: float32 [768, 3072], P('dp'), may hold values from -4 to 4
- w_out: float32 [3072, 768], P('dp'), may hold values from -4 to 4
- vectors: float32 [9216], P('dp'), may hold values from -4 to 4
- moment_qkv: float32 [768, 2304], P('dp'), may hold values from -43.44464 to 43.44464
- moment_attn: float32 [768, 768], P('dp'), may hold values from -43.44464 to 43.44464
- moment_in: float32 [768, 3072], P('dp'), may hold values from -43.44464 to 43.44464
- moment_out: float32 [3072, 768], P('dp'), may hold values from -43.44464 to 43.44464
- moment_vec: float32 [9216], P('dp'), may hold values from -43.44464 to 43.44464
- square_qkv: float32 [768, 2304], P('dp'), may hold values from 4.9152 to 19.6608
- square_attn: float32 [768, 768], P('dp'), may hold values from 4.9152 to 19.6608
- square_in: float32 [768, 3072], P('dp'), may hold values from 4.9152 to 19.6608
- square_out: float32 [3072, 768], P('dp'), may hold values from 4.9152 to 19.6608
- square_vec: float32 [9216], P('dp'), may hold values from 4.9152 to 19.6608
Outputs:
- mixed: bfloat16 [32, 1024, 768], P('dp')
- input_grad: float32 [32, 1024, 768], P('dp')
- new_qkv: float32 [768, 2304], P('dp')
- new_attn: float32 [768, 768], P('dp')
- new_in: float32 [768, 3072], P('dp')
- new_out: float32 [3072, 768], P('dp')
- new_vectors: float32 [9216], P('dp')
- next_moment_qkv: float32 [768, 2304], P('dp')
- next_moment_attn: float32 [768, 768], P('dp')
- next_moment_in: float32 [768, 3072], P('dp')
- next_moment_out: float32 [3072, 768], P('dp')
- next_moment_vec: float32 [9216], P('dp')
- next_square_qkv: float32 [768, 2304], P('dp')
- next_square_attn: float32 [768, 768], P('dp')
- next_square_in: float32 [768, 3072], P('dp')
- next_square_out: float32 [3072, 768], P('dp')
- next_square_vec: float32 [9216], P('dp')
- norms: float32 [8], replicated
Inputs may be any that keep to these rules, and one draw needn't show every extreme that they name: `lengths`: some clip has all 1024 frames.
All inputs are finite; a program needn't handle non-finite values.
Results may differ from a plain program's by a relative error of at most 0.014.
The roundings to bfloat16 on the way count: a program that leaves them out, or rounds other values in their place, can miss the bound.
Values may be sent and summed in bfloat16 or wider, within the bound.
No kernel may reach another device: no remote copies, remote signals or barrier semaphores. Data moves between devices by JAX's collectives and lax.ppermute only.
A program may use at most 192 MiB of HBM per device.

v0:
```python
from functools import partial

import jax
import jax.numpy as jnp
from jax import lax
from jax.sharding import PartitionSpec as P

D = 768
FF = 3072
HEADS = 12
HEAD_DIM = 64
STEP = 10


def layer_norm(resid):
    center = resid - jnp.mean(resid, axis=-1, keepdims=True)
    spread = jnp.mean(center * center, axis=-1, keepdims=True)
    return center * lax.rsqrt(spread + 1e-05)


def normalize(resid, gain, shift):
    return layer_norm(resid) * gain + shift


def split_vector(vec):
    widths = [D, D, D, D, D, FF, D, D, D]
    pieces = []
    offset = 0
    for width in widths:
        pieces.append(vec[offset : offset + width])
        offset = offset + width
    return pieces


def adapt(weight, grad, moment, square, decay):
    new_moment = 0.9 * moment + 0.1 * grad
    new_square = 0.999 * square + 0.001 * grad * grad
    update = new_moment / (1.0 - 0.9**STEP) / (jnp.sqrt(new_square / (1.0 - 0.999**STEP)) + 1e-06)
    return (new_moment, new_square, update + decay * weight)


def body(
    frames,
    cotangent,
    lengths,
    w_qkv,
    w_attn,
    w_in,
    w_out,
    vectors,
    moment_qkv,
    moment_attn,
    moment_in,
    moment_out,
    moment_vec,
    square_qkv,
    square_attn,
    square_in,
    square_out,
    square_vec,
):
    low_all = (
        w_qkv.astype(jnp.bfloat16),
        w_attn.astype(jnp.bfloat16),
        w_in.astype(jnp.bfloat16),
        w_out.astype(jnp.bfloat16),
        vectors.astype(jnp.bfloat16),
    )
    full_qkv, full_attn, full_in, full_out, full_vec = (
        lax.all_gather(low_all[0], "dp", axis=0, tiled=True),
        lax.all_gather(low_all[1], "dp", axis=0, tiled=True),
        lax.all_gather(low_all[2], "dp", axis=0, tiled=True),
        lax.all_gather(low_all[3], "dp", axis=0, tiled=True),
        lax.all_gather(low_all[4], "dp", axis=0, tiled=True),
    )
    bias_q, bias_v, bias_o, gain1, shift1, bias1, bias2, gain2, shift2 = split_vector(
        full_vec.astype(jnp.float32)
    )
    bias_qkv = jnp.concatenate([bias_q, jnp.zeros((D,), jnp.float32), bias_v])
    seq = frames.shape[1]
    block = min(512, seq)
    count = seq // block
    grad_out = jnp.zeros((FF, D), jnp.float32)
    grad_vec = jnp.zeros((8 * D + FF,), jnp.float32)
    clip_in = frames[0]
    keep = jnp.arange(seq) < lengths[0]
    keepf = keep.astype(jnp.float32)
    packed = (jnp.dot(clip_in, full_qkv, preferred_element_type=jnp.float32) + bias_qkv).astype(
        jnp.bfloat16
    )
    queries = packed[:, :D].reshape(seq, HEADS, HEAD_DIM)
    keys_all = packed[:, D : 2 * D].reshape(seq, HEADS, HEAD_DIM)
    values_all = packed[:, 2 * D :].reshape(seq, HEADS, HEAD_DIM)
    query_blocks = queries.reshape(count, block, HEADS, HEAD_DIM)

    def masked_scores(query_block):
        scores = (
            jnp.einsum("qhd,khd->hqk", query_block, keys_all, preferred_element_type=jnp.float32)
            * 0.125
        )
        return jnp.where(keep[None, None, :], scores, -1000000000.0)

    def attend(query_block):
        scores = masked_scores(query_block)
        peak = jnp.max(scores, axis=-1, keepdims=True)
        expo = jnp.exp(scores - peak)
        total = jnp.sum(expo, axis=-1, keepdims=True)
        probb = (expo / total).astype(jnp.bfloat16)
        context = jnp.einsum("hqk,khd->qhd", probb, values_all, preferred_element_type=jnp.float32)
        return (context, (peak + jnp.log(total))[..., 0])

    context, logsum = lax.map(attend, query_blocks)
    context_b = context.reshape(seq, D).astype(jnp.bfloat16)
    attended = jnp.dot(context_b, full_attn, preferred_element_type=jnp.float32) + bias_o
    first, first_pull = jax.vjp(normalize, clip_in.astype(jnp.float32) + attended, gain1, shift1)
    first_b = first.astype(jnp.bfloat16)
    hidden = jnp.dot(first_b, full_in, preferred_element_type=jnp.float32) + bias1
    active, gelu_pull = jax.vjp(partial(jax.nn.gelu, approximate=False), hidden)
    active_b = active.astype(jnp.bfloat16)
    branch = jnp.dot(active_b, full_out, preferred_element_type=jnp.float32) + bias2
    result, second_pull = jax.vjp(normalize, first + branch, gain2, shift2)
    mixed_rows = [(result * keepf[:, None]).astype(jnp.bfloat16)]
    dresult = cotangent[0].astype(jnp.float32) * keepf[:, None]
    dres2, dgain2, dshift2 = second_pull(dresult)
    dbranch = dres2.astype(jnp.bfloat16)
    grad_out = grad_out + jnp.einsum(
        "tf,td->fd", active_b, dbranch, preferred_element_type=jnp.float32
    )
    dbias2 = jnp.sum(dbranch.astype(jnp.float32), axis=0)
    dactive = jnp.einsum("td,fd->tf", dbranch, full_out, preferred_element_type=jnp.float32)
    dhidden = gelu_pull(dactive)[0].astype(jnp.bfloat16)
    grad_in = jnp.einsum("td,tf->df", first_b, dhidden, preferred_element_type=jnp.float32)
    dbias1 = jnp.sum(dhidden.astype(jnp.float32), axis=0)
    dfirst = dres2 + jnp.einsum("tf,df->td", dhidden, full_in, preferred_element_type=jnp.float32)
    dres1, dgain1, dshift1 = first_pull(dfirst)
    dattend = dres1.astype(jnp.bfloat16)
    grad_attn = jnp.einsum("tj,td->jd", context_b, dattend, preferred_element_type=jnp.float32)
    dbias_o = jnp.sum(dattend.astype(jnp.float32), axis=0)
    dcontext = jnp.einsum(
        "td,jd->tj", dattend, full_attn, preferred_element_type=jnp.float32
    ).astype(jnp.bfloat16)
    dcontext_blocks = dcontext.reshape(count, block, HEADS, HEAD_DIM)

    def attend_back(carry, item):
        dkeys, dvalues = carry
        query_block, dcontext_block, logsum_block = item
        probs = jnp.exp(masked_scores(query_block) - logsum_block[..., None])
        probb = probs.astype(jnp.bfloat16)
        dvalues = dvalues + jnp.einsum(
            "hqk,qhd->khd", probb, dcontext_block, preferred_element_type=jnp.float32
        )
        dprob = jnp.einsum(
            "qhd,khd->hqk", dcontext_block, values_all, preferred_element_type=jnp.float32
        )
        inner = jnp.sum(dprob * probs, axis=-1, keepdims=True)
        dscore = (probs * (dprob - inner)).astype(jnp.bfloat16)
        dquery = (
            jnp.einsum("hqk,khd->qhd", dscore, keys_all, preferred_element_type=jnp.float32) * 0.125
        )
        dkeys = (
            dkeys
            + jnp.einsum("hqk,qhd->khd", dscore, query_block, preferred_element_type=jnp.float32)
            * 0.125
        )
        return ((dkeys, dvalues), dquery)

    empty = jnp.zeros((seq, HEADS, HEAD_DIM), jnp.float32)
    (dkeys, dvalues), dqueries = lax.scan(
        attend_back, (empty, empty), (query_blocks, dcontext_blocks, logsum)
    )
    dpacked = jnp.concatenate(
        [dqueries.reshape(seq, D), dkeys.reshape(seq, D), dvalues.reshape(seq, D)], axis=1
    ).astype(jnp.bfloat16)
    grad_qkv = jnp.einsum("td,tj->dj", clip_in, dpacked, preferred_element_type=jnp.float32)
    dbias_qkv = jnp.sum(dpacked.astype(jnp.float32), axis=0)
    input_rows = [
        dres1 + jnp.einsum("tj,dj->td", dpacked, full_qkv, preferred_element_type=jnp.float32)
    ]
    grad_vec = grad_vec + jnp.concatenate(
        [
            dbias_qkv[:D],
            dbias_qkv[2 * D :],
            dbias_o,
            dgain1,
            dshift1,
            dbias1,
            dbias2,
            dgain2,
            dshift2,
        ]
    )
    locals_all = (grad_qkv, grad_attn, grad_in, grad_out, grad_vec)
    owned = (w_qkv, w_attn, w_in, w_out, vectors)
    totals = lax.psum(
        (locals_all[0], locals_all[1], locals_all[2], locals_all[3], locals_all[4]), "dp"
    )
    index = lax.axis_index("dp")
    shares = tuple(
        (
            lax.dynamic_slice_in_dim(total, index * local.shape[0], local.shape[0], 0)
            for total, local in zip(totals, owned)
        )
    )
    matrices = [w_qkv, w_attn, w_in, w_out]
    moments = [moment_qkv, moment_attn, moment_in, moment_out]
    squares = [square_qkv, square_attn, square_in, square_out]
    new_moments = []
    new_squares = []
    updates = []
    for weight, grad, moment, square in zip(matrices, shares[:4], moments, squares):
        new_moment, new_square, update = adapt(weight, grad, moment, square, 0.01)
        new_moments.append(new_moment)
        new_squares.append(new_square)
        updates.append(update)
    partial_sums = jnp.stack(
        [jnp.sum(weight * weight) for weight in matrices]
        + [jnp.sum(update * update) for update in updates]
    )
    norms = jnp.sqrt(lax.psum(partial_sums, "dp"))
    new_weights = [
        weight - 0.25 * (norms[place] / norms[4 + place]) * update
        for place, (weight, update) in enumerate(zip(matrices, updates))
    ]
    vec_moment, vec_square, vec_update = adapt(vectors, shares[4], moment_vec, square_vec, 0.0)
    new_vec = vectors - 0.4 * vec_update
    return (
        jnp.stack(mixed_rows),
        jnp.stack(input_rows),
        new_weights[0],
        new_weights[1],
        new_weights[2],
        new_weights[3],
        new_vec,
        new_moments[0],
        new_moments[1],
        new_moments[2],
        new_moments[3],
        vec_moment,
        new_squares[0],
        new_squares[1],
        new_squares[2],
        new_squares[3],
        vec_square,
        norms,
    )


def solution(mesh):
    placed = (
        P("dp", None, None),
        P("dp", None, None),
        P("dp"),
        P("dp", None),
        P("dp", None),
        P("dp", None),
        P("dp", None),
        P("dp"),
        P("dp", None),
        P("dp", None),
        P("dp", None),
        P("dp", None),
        P("dp"),
        P("dp", None),
        P("dp", None),
        P("dp", None),
        P("dp", None),
        P("dp"),
    )
    return jax.shard_map(
        body,
        mesh=mesh,
        in_specs=placed,
        out_specs=(
            P("dp", None, None),
            P("dp", None, None),
            P("dp", None),
            P("dp", None),
            P("dp", None),
            P("dp", None),
            P("dp"),
            P("dp", None),
            P("dp", None),
            P("dp", None),
            P("dp", None),
            P("dp"),
            P("dp", None),
            P("dp", None),
            P("dp", None),
            P("dp", None),
            P("dp"),
            P(),
        ),
        check_vma=False,
    )
```

profile of v0, /device:TPU:0, one launch (start us, length us, event | category | flops | bytes accessed | tf_op | source)
XLA Modules:
  0.0 1031.9 jit_solution(17739972291747860445)
XLA Ops:
  14.9 42.4 %all-reduce = bf16[9216]{0:T(1024)(128)(2,1)S(1)} all-reduce(bf16[9216]{0:T(1024)(128)(2,1)S(1)} %dynamic-update-slice), channel_id=1, replica_groups=mesh['dp'=32] {'dp'}, use_global_device_ids=true, to_apply=%add | all-reduce | flops 9216 | bytes 36864
  59.8 2.7 copy.84
  64.1 10.5 %all-gather.5.cloned.1.call-done = bf16[768,2304]{1,0:T(8,128)(2,1)} async-done(((bf16[24,2304]{1,0:T(8,128)(2,1)}), bf16[768,2304]{1,0:T(8,128)(2,1)}) %all-gather.5.cloned.1.call-update) | async-done | bytes 3538960 | tf_op jit(solution)/shard_map/all_gather | solution.py:70
  74.6 6.0 add_convert_fusion.1
  87.1 3.8 reshape_reshape.3
  94.0 80.1 %while.28 = (s32[]{:T(128)}, bf16[2,512,12,64]{1,3,2,0:T(8,128)(2,1)}, f32[2,12,512]{2,1,0:T(8,128)S(1)}, bf16[2,512,12,64]{1,3,2,0:T(8,128)(2,1)S(1)}, bf16[102...) while((s32[]{:T(128)}, ...), condition=%wide.region_3.4_spmd.clone, body=%wide.region_0.3_spmd.clone.sunk | while | flops 1686105088 | bytes 100118728 | solution.py:112
  94.7 10.2 fusion.120
  104.8 11.4 %fusion.121 = f32[12,512]{1,0:T(8,128)S(1)} fusion(f32[12,512,1024]{2,1,0:T(8,128)} %get-tuple-element.480, f32[12,512]{1,0:T(8,128)S(1)} %get-tuple-element.481, pred[1024]{0:T(1024)(128)(4,1)S(1)} %iota_compare_fusion.5), kind=kLoop, calls=%fused_computation.6.clone.1 | loop fusion | flops 25159680 | bytes 25216000 | tf_op jit(solution)/shard_map/while/body/eval_jaxpr/reduce_sum | solution.py:107
  116.2 11.3 %bitcast_dynamic-update-slice_fusion.6 = bf16[2,512,12,64]{1,3,2,0:T(8,128)(2,1)S(1)} fusion(bf16[2,512,12,64]{1,3,2,0:T(8,128)(2,1)S(1)} %copy-done.12, s32[]{:T(128)S(6)} %copy.106, bf16[1024,12,64]{0,2,1:T(8,128)(2,1)S(1)} %copy-done.5, f32[12,512,1024]{2,1,0:T(8,128)} %get-tuple-element.480, f32[12,512]{1,0:T(8,128)S(1)} %fusion.121, ...), kind=kOutput, calls=%fused_computation.8.clone.1 | convolution fusion | flops 836763648 | bytes 28378116 | tf_op jit(solution)/shard_map/while/body/eval_jaxpr/hqk,khd->qhd/dot_general | solution.py:109
  129.4 10.1 fusion.120
  139.5 11.5 %fusion.121 = f32[12,512]{1,0:T(8,128)S(1)} fusion(f32[12,512,1024]{2,1,0:T(8,128)} %get-tuple-element.480, f32[12,512]{1,0:T(8,128)S(1)} %get-tuple-element.481, pred[1024]{0:T(1024)(128)(4,1)S(1)} %iota_compare_fusion.5), kind=kLoop, calls=%fused_computation.6.clone.1 | loop fusion | flops 25159680 | bytes 25216000 | tf_op jit(solution)/shard_map/while/body/eval_jaxpr/reduce_sum | solution.py:107
  151.1 11.3 %bitcast_dynamic-update-slice_fusion.6 = bf16[2,512,12,64]{1,3,2,0:T(8,128)(2,1)S(1)} fusion(bf16[2,512,12,64]{1,3,2,0:T(8,128)(2,1)S(1)} %copy-done.12, s32[]{:T(128)S(6)} %copy.106, bf16[1024,12,64]{0,2,1:T(8,128)(2,1)S(1)} %copy-done.5, f32[12,512,1024]{2,1,0:T(8,128)} %get-tuple-element.480, f32[12,512]{1,0:T(8,128)S(1)} %fusion.121, ...), kind=kOutput, calls=%fused_computation.8.clone.1 | convolution fusion | flops 836763648 | bytes 28378116 | tf_op jit(solution)/shard_map/while/body/eval_jaxpr/hqk,khd->qhd/dot_general | solution.py:109
  174.2 4.2 copy.83
  179.9 3.8 fusion.75
  185.1 11.9 %all-gather.9.cloned.1.call-done = bf16[768,3072]{1,0:T(8,128)(2,1)} async-done(((bf16[24,3072]{1,0:T(8,128)(2,1)}), bf16[768,3072]{1,0:T(8,128)(2,1)}) %all-gather.9.cloned.1.call-update) | async-done | bytes 4718608 | tf_op jit(solution)/shard_map/all_gather | solution.py:72
  197.0 37.7 %multiply_convert_fusion.1 = (bf16[1024,3072]{1,0:T(8,128)(2,1)}, f32[1024,3072]{1,0:T(8,128)}, f32[1024,3072]{1,0:T(8,128)}) fusion(f32[3072]{0:T(1024)S(1)} %copy-done.38, bf16[768,3072]{1,0:T(8,128)(2,1)} %all-gather.9.cloned.1.call-done, f32[1024,768]{0,1:T(8,128)S(1)} %get-tuple-element.375, f32[768]{0:T(1024)S(1)} %copy-done.40, ...), kind=kOutput, calls=%fused_computation.48 | convolution fusion | flops 5043388416 | bytes 39348224 | tf_op jit(solution)/shard_map/dot_general | solution.py:117
  234.7 28.1 %all-gather.11.cloned.1.call-done = bf16[3072,768]{1,0:T(8,128)(2,1)} async-done(((bf16[96,768]{1,0:T(8,128)(2,1)}), bf16[3072,768]{1,0:T(8,128)(2,1)}) %all-gather.11.cloned.1.call-update) | async-done | bytes 4718608 | tf_op jit(solution)/shard_map/all_gather | solution.py:73
  262.8 9.9 fusion.76
  276.0 3.6 convert_reduce_fusion.2
  279.6 7.6 fusion.78
  287.2 17.7 %convert_reduce_fusion = (f32[3072]{0:T(1024)}, bf16[1024,3072]{1,0:T(8,128)(2,1)}) fusion(f32[1024,3072]{1,0:T(8,128)} %get-tuple-element.347, bf16[1024,768]{0,1:T(8,128)(2,1)S(1)} %get-tuple-element.333, bf16[3072,768]{1,0:T(8,128)(2,1)} %all-gather.11.cloned.1.call-done, f32[1024,3072]{1,0:T(8,128)} %get-tuple-element.376, f32[3072]{0:T(1024)S(1)} %copy-done.38), kind=kOutput, calls=%fused_computation.46 | convolution fusion | flops 4885312512 | bytes 37773312 | tf_op jit(solution)/shard_map/td,fd->tf/dot_general | solution.py:130
  304.9 11.3 %fusion.60 = f32[768,3072]{1,0:T(8,128)} fusion(bf16[1024,3072]{1,0:T(8,128)(2,1)} %get-tuple-element.381, f32[1024,768]{0,1:T(8,128)} %copy-done.10, f32[768]{0:T(1024)S(1)} %copy-done.40, f32[768]{0:T(1024)S(1)} %copy-done.29, f32[1024]{0:T(1024)S(1)} %fusion.57, f32[1024]{0:T(1024)S(1)} %broadcast_multiply_fusion.1), kind=kOutput, calls=%fused_computation.149 | convolution fusion | flops 4835770368 | bytes 18888704 | tf_op jit(solution)/shard_map/td,tf->df/dot_general | solution.py:132
  316.2 9.8 multiply_reduce_fusion.1
  329.4 2.9 fusion.77
  336.9 3.1 copy.88
  341.2 163.1 %while.29 = (s32[]{:T(128)}, f32[1024,12,64]{0,2,1:T(8,128)}, f32[1024,12,64]{0,2,1:T(8,128)}, bf16[2,512,12,64]{1,3,2,0:T(8,128)(2,1)}, bf16[2,512,12,64]{1,3,2...) while((s32[]{:T(128)}, f32[1024,12,64]{0,2,1:T(8,128)}, ...), condition=%wide.region_14.15_spmd.clone, body=%wide.region_12.14_spmd.clone.sunk | while | flops 4125223936 | bytes 217239728 | solution.py:168
  342.3 10.1 fusion.131
  352.4 12.9 %bitcast_add_fusion.5 = f32[1024,12,64]{0,2,1:T(8,128)} fusion(f32[1024,12,64]{0,2,1:T(8,128)} %get-tuple-element.532, f32[12,512,1024]{2,1,0:T(8,128)} %fusion.131, f32[12,512]{1,0:T(8,128)S(1)} %dynamic-slice_bitcast_fusion.2, pred[1024]{0:T(1024)(128)(4,1)S(1)} %iota_compare_fusion.6, pred[]{:T(512)S(6)} %compare.3, ...), kind=kOutput, calls=%fused_computation.23.clone.1 | convolution fusion | flops 832045056 | bytes 32277508 | tf_op jit(solution)/shard_map/while/body/eval_jaxpr/hqk,qhd->khd/dot_general | solution.py:149
  365.3 17.4 %multiply_reduce_fusion.14 = (f32[12,512]{1,0:T(8,128)S(1)}, f32[12,512,1024]{2,1,0:T(8,128)}) fusion(f32[12,512,1024]{2,1,0:T(8,128)} %fusion.131, f32[12,512]{1,0:T(8,128)S(1)} %dynamic-slice_bitcast_fusion.2, pred[1024]{0:T(1024)(128)(4,1)S(1)} %iota_compare_fusion.6, bf16[1024,12,64]{0,2,1:T(8,128)(2,1)} %get-tuple-element.550, ...), kind=kOutput, calls=%fused_computation.18.clone.1 | convolution fusion | flops 836757504 | bytes 52741124 | tf_op jit(solution)/shard_map/while/body/eval_jaxpr/qhd,khd->hqk/dot_general | solution.py:152
  382.7 21.4 %multiply_convert_fusion.4 = bf16[12,512,1024]{2,1,0:T(8,128)(2,1)} fusion(f32[12,512,1024]{2,1,0:T(8,128)} %get-tuple-element.492, f32[12,512,1024]{2,1,0:T(8,128)} %fusion.131, f32[12,512]{1,0:T(8,128)S(1)} %get-tuple-element.493, f32[12,512]{1,0:T(8,128)S(1)} %dynamic-slice_bitcast_fusion.2, pred[1024]{0:T(1024)(128)(4,1)S(1)} %iota_compare_fusion.6), kind=kLoop, calls=%fused_computation.17.clone.1 | loop fusion | flops 37748736 | bytes 62964736 | tf_op jit(solution)/shard_map/while/body/eval_jaxpr/convert_element_type | solution.py:156
  404.1 9.4 bitcast_dynamic-update-slice_fusion.8
  413.5 8.5 bitcast_add_fusion.4
  422.7 10.1 fusion.131
  432.8 13.8 %bitcast_add_fusion.5 = f32[1024,12,64]{0,2,1:T(8,128)} fusion(f32[1024,12,64]{0,2,1:T(8,128)} %get-tuple-element.532, f32[12,512,1024]{2,1,0:T(8,128)} %fusion.131, f32[12,512]{1,0:T(8,128)S(1)} %dynamic-slice_bitcast_fusion.2, pred[1024]{0:T(1024)(128)(4,1)S(1)} %iota_compare_fusion.6, pred[]{:T(512)S(6)} %compare.3, ...), kind=kOutput, calls=%fused_computation.23.clone.1 | convolution fusion | flops 832045056 | bytes 32277508 | tf_op jit(solution)/shard_map/while/body/eval_jaxpr/hqk,qhd->khd/dot_general | solution.py:149
  446.6 17.4 %multiply_reduce_fusion.14 = (f32[12,512]{1,0:T(8,128)S(1)}, f32[12,512,1024]{2,1,0:T(8,128)}) fusion(f32[12,512,1024]{2,1,0:T(8,128)} %fusion.131, f32[12,512]{1,0:T(8,128)S(1)} %dynamic-slice_bitcast_fusion.2, pred[1024]{0:T(1024)(128)(4,1)S(1)} %iota_compare_fusion.6, bf16[1024,12,64]{0,2,1:T(8,128)(2,1)} %get-tuple-element.550, ...), kind=kOutput, calls=%fused_computation.18.clone.1 | convolution fusion | flops 836757504 | bytes 52741124 | tf_op jit(solution)/shard_map/while/body/eval_jaxpr/qhd,khd->hqk/dot_general | solution.py:152
  464.0 21.4 %multiply_convert_fusion.4 = bf16[12,512,1024]{2,1,0:T(8,128)(2,1)} fusion(f32[12,512,1024]{2,1,0:T(8,128)} %get-tuple-element.492, f32[12,512,1024]{2,1,0:T(8,128)} %fusion.131, f32[12,512]{1,0:T(8,128)S(1)} %get-tuple-element.493, f32[12,512]{1,0:T(8,128)S(1)} %dynamic-slice_bitcast_fusion.2, pred[1024]{0:T(1024)(128)(4,1)S(1)} %iota_compare_fusion.6), kind=kLoop, calls=%fused_computation.17.clone.1 | loop fusion | flops 37748736 | bytes 62964736 | tf_op jit(solution)/shard_map/while/body/eval_jaxpr/convert_element_type | solution.py:156
  485.4 9.4 bitcast_dynamic-update-slice_fusion.8
  494.8 9.4 bitcast_add_fusion.4
  504.4 3.2 copy.89
  511.7 9.3 convolution_bitcast_fusion
  521.0 2.6 copy.92
  527.6 7.6 add_bitcast_fusion
  535.1 417.0 %all-reduce.5.cloned.1.call-done = (f32[768,2304]{1,0:T(8,128)}, f32[768,768]{1,0:T(8,128)}, f32[768,3072]{1,0:T(8,128)}, f32[3072,768]{1,0:T(8,128)}) async-done(((f32[768,2304]{1,0:T(8,128)}, f32[768,768]{1,0:T(8,128)}, f32[768,3072]{1,0:T(8,128)}, f32[3072,768]{1,0:T(8,128)}), (f32[768,2304]{1,0:T(8,128)}, f32[768,768]{1,0:T(8,128)}, f32[768,3072]{1,0:T(8,128)}, ...) | async-done | bytes 28311568 | tf_op jit(solution)/shard_map/psum | solution.py:194
  952.1 2.8 multiply_reduce_fusion.9
  954.9 2.9 multiply_reduce_fusion.6
  960.1 2.8 multiply_reduce_fusion.5
  962.9 5.3 stack.43
  970.5 40.6 %all-reduce.1 = (f32[8]{0:T(128)S(1)}, f32[9216]{0:T(1024)S(1)}) all-reduce(f32[8]{0:T(128)S(1)} %stack.43, f32[9216]{0:T(1024)S(1)} %constant_dynamic-update-slice_fusion), channel_id=1, replica_groups=mesh['dp'=32] {'dp'}, use_global_device_ids=true, to_apply=%region_27.28 | all-reduce | flops 9224 | bytes 73792 | tf_op jit(solution)/shard_map/psum | solution.py:219
  (192 shorter events, 62.3 us)
Async XLA Ops:
  7.2 55.3 %copy-start.18 = (bf16[1,1024,768]{2,1,0:T(8,128)(2,1)S(1)}, bf16[1,1024,768]{2,1,0:T(8,128)(2,1)}, u32[]{:S(2)}) copy-start(bf16[1,1024,768]{2,1,0:T(8,128)(2,1)} %param.22) | copy-start | bytes 4718596
  7.2 67.4 %all-gather.5.cloned.1.call-start = ((), (), s32[]{:S(2)}) async-start(), calls=%async_computation | async-start | bytes 3649536 | tf_op jit(solution)/shard_map/all_gather | solution.py:70
  9.0 171.0 %all-gather.7.cloned.1.call-start = ((), (), s32[]{:S(2)}) async-start(), calls=%async_computation.1 | async-start | bytes 1216512 | tf_op jit(solution)/shard_map/all_gather | solution.py:71
  10.6 186.4 %all-gather.9.cloned.1.call-start = ((), (), s32[]{:S(2)}) async-start(), calls=%async_computation.2 | async-start | bytes 4866048 | tf_op jit(solution)/shard_map/all_gather | solution.py:72
  12.3 250.5 %all-gather.11.cloned.1.call-start = ((), (), s32[]{:S(2)}) async-start(), calls=%async_computation.3 | async-start | bytes 4866048 | tf_op jit(solution)/shard_map/all_gather | solution.py:73
  14.0 938.2 %all-reduce.5.cloned.1.call-start = ((), (), s32[]{:S(2)}) async-start(), calls=%async_computation.4 | async-start | bytes 56623104 | tf_op jit(solution)/shard_map/psum | solution.py:194
  104.8 11.4 %copy-start.5 = (bf16[1024,12,64]{0,2,1:T(8,128)(2,1)S(1)}, bf16[1024,12,64]{0,2,1:T(8,128)(2,1)}, u32[]{:S(2)}) copy-start(bf16[1024,12,64]{0,2,1:T(8,128)(2,1)} %get-tuple-element.515) | copy-start | bytes 4718596 | tf_op jit(solution)/shard_map/while
  104.8 11.4 %copy-start.12 = (bf16[2,512,12,64]{1,3,2,0:T(8,128)(2,1)S(1)}, bf16[2,512,12,64]{1,3,2,0:T(8,128)(2,1)}, u32[]{:S(2)}) copy-start(bf16[2,512,12,64]{1,3,2,0:T(8,128)(2,1)} %get-tuple-element.503) | copy-start | bytes 4718596 | tf_op jit(solution)/shard_map/while
  139.5 11.6 %copy-start.5 = (bf16[1024,12,64]{0,2,1:T(8,128)(2,1)S(1)}, bf16[1024,12,64]{0,2,1:T(8,128)(2,1)}, u32[]{:S(2)}) copy-start(bf16[1024,12,64]{0,2,1:T(8,128)(2,1)} %get-tuple-element.515) | copy-start | bytes 4718596 | tf_op jit(solution)/shard_map/while
  139.5 11.6 %copy-start.12 = (bf16[2,512,12,64]{1,3,2,0:T(8,128)(2,1)S(1)}, bf16[2,512,12,64]{1,3,2,0:T(8,128)(2,1)}, u32[]{:S(2)}) copy-start(bf16[2,512,12,64]{1,3,2,0:T(8,128)(2,1)} %get-tuple-element.503) | copy-start | bytes 4718596 | tf_op jit(solution)/shard_map/while
  174.1 5.8 copy-start
  174.1 5.8 copy-start.3
  174.1 5.8 copy-start.22
  174.1 5.8 copy-start.42
  183.8 50.9 %copy-start.10 = (f32[1024,768]{0,1:T(8,128)}, f32[1024,768]{0,1:T(8,128)S(1)}, u32[]{:S(2)}) copy-start(f32[1024,768]{0,1:T(8,128)S(1)} %get-tuple-element.375) | copy-start | bytes 9437188
  183.8 13.2 %copy-start.29 = (f32[768]{0:T(1024)S(1)}, f32[768]{0:T(1024)}, u32[]{:S(2)}) copy-start(f32[768]{0:T(1024)} %get-tuple-element.359) | copy-start | bytes 9220
  183.8 13.2 %copy-start.38 = (f32[3072]{0:T(1024)S(1)}, f32[3072]{0:T(1024)}, u32[]{:S(2)}) copy-start(f32[3072]{0:T(1024)} %slice.96) | copy-start | bytes 36868
  183.8 13.2 %copy-start.40 = (f32[768]{0:T(1024)S(1)}, f32[768]{0:T(1024)}, u32[]{:S(2)}) copy-start(f32[768]{0:T(1024)} %get-tuple-element.360) | copy-start | bytes 9220
  197.0 65.8 %copy-start.41 = (f32[768]{0:T(1024)S(1)}, f32[768]{0:T(1024)}, u32[]{:S(2)}) copy-start(f32[768]{0:T(1024)} %get-tuple-element.358) | copy-start | bytes 9220
  262.8 9.9 copy-start.6
  262.8 9.9 copy-start.24
  262.8 9.9 copy-start.25
  273.6 5.9 slice-start
  276.0 3.6 slice-start.1
  304.9 11.3 %copy-start.11 = (f32[1024,768]{0,1:T(8,128)S(1)}, f32[1024,768]{0,1:T(8,128)}, u32[]{:S(2)}) copy-start(f32[1024,768]{0,1:T(8,128)} %copy-done.10) | copy-start | bytes 9437188
  304.9 11.3 %copy-start.48 = (bf16[1024,3072]{1,0:T(8,128)(2,1)S(1)}, bf16[1024,3072]{1,0:T(8,128)(2,1)}, u32[]{:S(2)}) copy-start(bf16[1024,3072]{1,0:T(8,128)(2,1)} %get-tuple-element.381) | copy-start | bytes 18874372
  316.2 9.8 copy-start.27
  326.8 5.4 copy-start.8
  326.8 5.4 copy-start.34
  329.4 2.9 copy-start.47
  336.8 4.4 copy-start.1
  336.9 4.4 copy-start.4
  336.9 4.4 copy-start.23
  342.3 10.1 copy-start.7
  422.7 10.1 copy-start.7
  504.4 3.6 copy-start.2
  508.2 3.4 copy-start.19
  521.0 4.8 copy-start.44
  523.6 3.0 copy-start.9
  523.6 3.9 copy-start.15
  523.6 3.9 copy-start.35
  527.6 430.3 %copy-start.21 = (f32[24,768]{1,0:T(8,128)S(1)}, f32[24,768]{1,0:T(8,128)}, u32[]{:S(2)}) copy-start(f32[24,768]{1,0:T(8,128)} %param.26) | copy-start | bytes 221188
  535.1 425.0 %copy-start.17 = (f32[96,768]{1,0:T(8,128)S(1)}, f32[96,768]{1,0:T(8,128)}, u32[]{:S(2)}) copy-start(f32[96,768]{1,0:T(8,128)} %param.28) | copy-start | bytes 884740
  535.1 433.0 %copy-start.16 = (f32[1,1024,768]{1,2,0:T(8,128)S(1)}, f32[1,1024,768]{1,2,0:T(8,128)}, u32[]{:S(2)}) copy-start(f32[1,1024,768]{1,2,0:T(8,128)} %add_bitcast_fusion) | copy-start | bytes 9437188
  970.5 54.1 %copy-start.39 = (f32[288]{0:T(512)S(1)}, f32[288]{0:T(512)}, u32[]{:S(2)}) copy-start(f32[288]{0:T(512)} %param.29) | copy-start | bytes 3460
  970.5 54.1 %copy-start.45 = (f32[288]{0:T(512)S(1)}, f32[288]{0:T(512)}, u32[]{:S(2)}) copy-start(f32[288]{0:T(512)} %param.34) | copy-start | bytes 3460
  970.5 54.1 %copy-start.46 = (f32[288]{0:T(512)S(1)}, f32[288]{0:T(512)}, u32[]{:S(2)}) copy-start(f32[288]{0:T(512)} %param.39) | copy-start | bytes 3460
  1011.1 14.1 %copy-start.28 = (f32[8]{0:T(128)}, f32[8]{0:T(128)S(1)}, u32[]{:S(2)}) copy-start(f32[8]{0:T(128)S(1)} %sqrt.22) | copy-start | bytes 100
  (12 other events, 22.7 us)
Sparse Core Ops, SparseCore 0:
  11.5 63.0 all-gather.4
  78.1 52.8 all-gather.6
  134.4 62.5 all-gather.8
  200.3 62.4 all-gather.10
  521.1 431.0 all-reduce.4
where the time goes:
time: 1040 us; the launch traced here: 1030 us
  waiting for transfers between devices  468 us (45%)
  matrix products  286 us (28%)
  other arithmetic  109 us (10%)
  blocking collectives  83 us (8%)
  local copies, waits for them, and re-layouts  54.5 us (5%)
  between operations  20.6 us (2%)
  loops' own time  11.3 us (1%)
    psum x1, waiting for transfers between devices, body(): lax.psum((locals_all[0], locals_all[1], locals_all[2], locals_all[3], loc...  417 us
    convert_element_type x2, other arithmetic, attend_back(): dscore = (probs * (dprob - inner)).astype(jnp.bfloat16)  42.8 us
    unnamed x1, blocking collectives  42.4 us
    psum x1, blocking collectives, body(): norms = jnp.sqrt(lax.psum(partial_sums, 'dp'))  40.6 us
    dot_general x4, matrix products, masked_scores(): jnp.einsum('qhd,khd->hqk', query_block, keys_all, preferred_element_type=...  40.4 us
    dot_general x1, matrix products, body(): jnp.dot(first_b, full_in, preferred_element_type=jnp.float32) + bias1  37.7 us
    dot_general x2, matrix products, attend_back(): jnp.einsum('qhd,khd->hqk', dcontext_block, values_all, preferred_element_...  34.8 us
    all_gather x1, waiting for transfers between devices, body(): lax.all_gather(low_all[3], 'dp', axis=0, tiled=True)  28.1 us
  transfers between devices with their start and end apart: 5, of which 4 were waited for; matrix products, arithmetic and copies ran while one was open for 15% of the time, Pallas kernels for 0%

commit v1 on v0

--- a/solution.py
+++ b/solution.py
@@ -39,7 +39,18 @@
     return (new_moment, new_square, update + decay * weight)
 
 
+def swap(value, bit, n):
+    return lax.ppermute(value, "dp", [(i, i ^ (1 << bit)) for i in range(n)])
+
+
+def sum_all(value, n):
+    for bit in range(n.bit_length() - 1):
+        value = value + swap(value, bit, n)
+    return value
+
+
 def body(
+    n,
     frames,
     cotangent,
     lengths,
@@ -59,20 +70,32 @@
     square_out,
     square_vec,
 ):
-    low_all = (
-        w_qkv.astype(jnp.bfloat16),
-        w_attn.astype(jnp.bfloat16),
-        w_in.astype(jnp.bfloat16),
-        w_out.astype(jnp.bfloat16),
-        vectors.astype(jnp.bfloat16),
-    )
-    full_qkv, full_attn, full_in, full_out, full_vec = (
-        lax.all_gather(low_all[0], "dp", axis=0, tiled=True),
-        lax.all_gather(low_all[1], "dp", axis=0, tiled=True),
-        lax.all_gather(low_all[2], "dp", axis=0, tiled=True),
-        lax.all_gather(low_all[3], "dp", axis=0, tiled=True),
-        lax.all_gather(low_all[4], "dp", axis=0, tiled=True),
-    )
+    def gather(shard):
+        return lax.all_gather(shard.astype(jnp.bfloat16), "dp", axis=0, tiled=True)
+
+    def blocks(matrix, rows):
+        return matrix.reshape(rows, -1, D).transpose(1, 0, 2).reshape(-1, D)
+
+    rows_d, rows_f = w_qkv.shape[0], w_out.shape[0]
+    width = vectors.shape[0]
+    vec_rows = jnp.zeros((8, D), jnp.float32).at[0, :width].set(vectors)
+    pack = jnp.concatenate(
+        [blocks(w_qkv, rows_d), w_attn, blocks(w_in, rows_d), w_out, vec_rows], axis=0
+    )
+    whole = gather(pack[None])
+    full_vec = whole[:, 8 * rows_d + rows_f, :width].reshape(-1)
+
+    def columns(first, count):
+        parts = [
+            whole[:, first + i * rows_d : first + (i + 1) * rows_d].reshape(D, D)
+            for i in range(count)
+        ]
+        return parts[0] if count == 1 else jnp.concatenate(parts, axis=1)
+
+    full_qkv = columns(0, 3)
+    full_attn = columns(3 * rows_d, 1)
+    full_in = columns(4 * rows_d, FF // D)
+    full_out = whole[:, 8 * rows_d : 8 * rows_d + rows_f].reshape(FF, D)
     bias_q, bias_v, bias_o, gain1, shift1, bias1, bias2, gain2, shift2 = split_vector(
         full_vec.astype(jnp.float32)
     )
@@ -191,15 +214,29 @@
     )
     locals_all = (grad_qkv, grad_attn, grad_in, grad_out, grad_vec)
     owned = (w_qkv, w_attn, w_in, w_out, vectors)
-    totals = lax.psum(
-        (locals_all[0], locals_all[1], locals_all[2], locals_all[3], locals_all[4]), "dp"
-    )
+    def spread(matrix):
+        return matrix.reshape(n, rows_d, -1, D).transpose(0, 2, 1, 3).reshape(n, -1, D)
+
+    packed_grads = jnp.concatenate(
+        [spread(grad_qkv), spread(grad_attn), spread(grad_in), grad_out.reshape(n, rows_f, D)],
+        axis=1,
+    ).astype(jnp.bfloat16)
+    share = lax.psum_scatter(packed_grads, "dp", scatter_dimension=0, tiled=True)[0].astype(
+        jnp.float32
+    )
+
+    def unblock(first, count):
+        parts = [share[first + i * rows_d : first + (i + 1) * rows_d] for i in range(count)]
+        return parts[0] if count == 1 else jnp.concatenate(parts, axis=1)
+
+    total_vec = sum_all(grad_vec.reshape(-1, 128), n).reshape(-1)
     index = lax.axis_index("dp")
-    shares = tuple(
-        (
-            lax.dynamic_slice_in_dim(total, index * local.shape[0], local.shape[0], 0)
-            for total, local in zip(totals, owned)
-        )
+    shares = (
+        unblock(0, 3),
+        unblock(3 * rows_d, 1),
+        unblock(4 * rows_d, FF // D),
+        share[8 * rows_d :],
+        lax.dynamic_slice_in_dim(total_vec, index * width, width, 0),
     )
     matrices = [w_qkv, w_attn, w_in, w_out]
     moments = [moment_qkv, moment_attn, moment_in, moment_out]
@@ -216,7 +253,7 @@
         [jnp.sum(weight * weight) for weight in matrices]
         + [jnp.sum(update * update) for update in updates]
     )
-    norms = jnp.sqrt(lax.psum(partial_sums, "dp"))
+    norms = jnp.sqrt(sum_all(partial_sums, n))
     new_weights = [
         weight - 0.25 * (norms[place] / norms[4 + place]) * update
         for place, (weight, update) in enumerate(zip(matrices, updates))
@@ -267,7 +304,7 @@
         P("dp"),
     )
     return jax.shard_map(
-        body,
+        partial(body, mesh.shape["dp"]),
         mesh=mesh,
         in_specs=placed,
         out_specs=(

time: 1040 us -> 773 us (0.74)
  waiting for transfers between devices: 468 us -> 250 us
  blocking collectives: 83 us -> 0 us
  local copies, waits for them, and re-layouts: 54.5 us -> 88.6 us
  loops' own time: 11.3 us -> 0.85 us
    psum x1 -> x0, waiting for transfers between devices: 417 us -> none  [body(): lax.psum((locals_all[0], locals_all[1], locals_all[2], locals_all[3], loc...]
    reduce_scatter x0 -> x1, waiting for transfers between devices: none -> 126 us  [body(): lax.psum_scatter(packed_grads, 'dp', scatter_dimension=0, tiled=True)[0]]
    all_gather x4 -> x1, waiting for transfers between devices: 50.4 us -> 103 us  [gather(): return lax.all_gather(shard.astype(jnp.bfloat16), 'dp', axis=0, tiled=True)]
    unnamed x1 -> x0, blocking collectives: 42.4 us -> none
    psum x1 -> x0, blocking collectives: 40.6 us -> none  [body(): norms = jnp.sqrt(lax.psum(partial_sums, 'dp'))]
    ppermute x0 -> x10, waiting for transfers between devices: none -> 21.1 us  [swap(): return lax.ppermute(value, 'dp', [(i, i ^ 1 << bit) for i in range(n)])]
    reshape x0 -> x4, local copies, waits for them, and re-layouts: none -> 19 us  [the longest x2 19 us: spread(): matrix.reshape(n, rows_d, -1, D).transpose(0, 2, 1, 3).reshape(n, -1, D)]
    unnamed x112 -> x168, local copies, waits for them, and re-layouts: 21.7 us -> 20.7 us
  transfers between devices with their start and end apart: 5 -> 12, of which waited for: 4 -> 11; matrix products, arithmetic and copies ran while one was open for 15% -> 3% of each run, Pallas kernels for 0% -> 0%
where the time goes in v1:
time: 773 us; the launch traced here: 764 us
  matrix products  281 us (36%)
  waiting for transfers between devices  250 us (32%)
  other arithmetic  112 us (14%)
  local copies, waits for them, and re-layouts  88.6 us (11%)
  between operations  21.5 us (3%)
  starting transfers between devices  10 us (1%)
    reduce_scatter x1, waiting for transfers between devices, body(): lax.psum_scatter(packed_grads, 'dp', scatter_dimension=0, tiled=True)[0]  126 us
    all_gather x1, waiting for transfers between devices, gather(): return lax.all_gather(shard.astype(jnp.bfloat16), 'dp', axis=0, tiled=True)  103 us
    convert_element_type x2, other arithmetic, attend_back(): dscore = (probs * (dprob - inner)).astype(jnp.bfloat16)  42.9 us
    dot_general x4, matrix products, masked_scores(): jnp.einsum('qhd,khd->hqk', query_block, keys_all, preferred_element_type=...  40.7 us
    dot_general x1, matrix products, body(): jnp.dot(first_b, full_in, preferred_element_type=jnp.float32) + bias1  39.2 us
    dot_general x2, matrix products, attend_back(): jnp.einsum('qhd,khd->hqk', dcontext_block, values_all, preferred_element_...  34.9 us
    dot_general x2, matrix products, attend_back(): jnp.einsum('hqk,qhd->khd', probb, dcontext_block, preferred_element_type=...  26.7 us
    reduce_sum x2, other arithmetic, attend(): total = jnp.sum(expo, axis=-1, keepdims=True)  22.8 us
  transfers between devices with their start and end apart: 12, of which 11 were waited for; matrix products, arithmetic and copies ran while one was open for 3% of the time, Pallas kernels for 0%

profile of v1, /device:TPU:0, one launch (start us, length us, event | category | flops | bytes accessed | tf_op | source)
XLA Modules:
  0.0 764.0 jit_solution(5498451821777207660)
XLA Ops:
  20.0 103.1 %all-gather.2.cloned.1.call-done = bf16[32,296,768]{2,1,0:T(8,128)(2,1)} async-done(((bf16[1,296,768]{2,1,0:T(8,128)(2,1)}), bf16[32,296,768]{2,1,0:T(8,128)(2,1)}) %all-gather.2.cloned.1.call-update) | async-done | bytes 14549008 | tf_op jit(solution)/shard_map/all_gather | solution.py:74
  125.5 6.4 fusion.83
  131.9 5.0 fusion.41
  143.9 69.5 %while.29 = (s32[]{:T(128)}, bf16[2,512,12,64]{1,3,2,0:T(8,128)(2,1)}, f32[2,12,512]{2,1,0:T(8,128)S(1)}, bf16[2,512,12,64]{1,3,2,0:T(8,128)(2,1)S(1)}, bf16[102...) while((s32[]{:T(128)}, ...), condition=%wide.region_3.4_spmd.clone, body=%wide.region_0.3_spmd.clone.sunk | while | flops 1686105088 | bytes 100118728 | solution.py:135
  144.6 10.2 %fusion.126 = (f32[12,512]{1,0:T(8,128)S(1)}, f32[12,512,1024]{2,1,0:T(8,128)}) fusion(pred[1024]{0:T(1024)(128)(4,1)S(1)} %iota_compare_fusion.5, bf16[1024,12,64]{0,2,1:T(8,128)(2,1)S(1)} %get-tuple-element.570, bf16[2,512,12,64]{1,3,2,0:T(8,128)(2,1)S(1)} %get-tuple-element.569, s32[]{:T(128)S(6)} %copy.121), kind=kOutput, calls=%fused_computation.5.clone.1 | convolution fusion | flops 824174592 | bytes 27550724 | tf_op jit(solution)/shard_map/while/body/eval_jaxpr/qhd,khd->hqk/dot_general | solution.py:121
  154.8 11.4 %fusion.127 = f32[12,512]{1,0:T(8,128)S(1)} fusion(f32[12,512,1024]{2,1,0:T(8,128)} %get-tuple-element.536, f32[12,512]{1,0:T(8,128)S(1)} %get-tuple-element.537, pred[1024]{0:T(1024)(128)(4,1)S(1)} %iota_compare_fusion.5), kind=kLoop, calls=%fused_computation.6.clone.1 | loop fusion | flops 25159680 | bytes 25216000 | tf_op jit(solution)/shard_map/while/body/eval_jaxpr/reduce_sum | solution.py:130
  166.2 11.2 %bitcast_dynamic-update-slice_fusion.9 = bf16[2,512,12,64]{1,3,2,0:T(8,128)(2,1)S(1)} fusion(bf16[2,512,12,64]{1,3,2,0:T(8,128)(2,1)S(1)} %copy-done.12, s32[]{:T(128)S(6)} %copy.121, bf16[1024,12,64]{0,2,1:T(8,128)(2,1)S(1)} %copy-done.5, f32[12,512,1024]{2,1,0:T(8,128)} %get-tuple-element.536, f32[12,512]{1,0:T(8,128)S(1)} %fusion.127, ...), kind=kOutput, calls=%fused_computation.8.clone.1 | convolution fusion | flops 836763648 | bytes 28378116 | tf_op jit(solution)/shard_map/while/body/eval_jaxpr/hqk,khd->qhd/dot_general | solution.py:132
  179.2 10.2 %fusion.126 = (f32[12,512]{1,0:T(8,128)S(1)}, f32[12,512,1024]{2,1,0:T(8,128)}) fusion(pred[1024]{0:T(1024)(128)(4,1)S(1)} %iota_compare_fusion.5, bf16[1024,12,64]{0,2,1:T(8,128)(2,1)S(1)} %get-tuple-element.570, bf16[2,512,12,64]{1,3,2,0:T(8,128)(2,1)S(1)} %get-tuple-element.569, s32[]{:T(128)S(6)} %copy.121), kind=kOutput, calls=%fused_computation.5.clone.1 | convolution fusion | flops 824174592 | bytes 27550724 | tf_op jit(solution)/shard_map/while/body/eval_jaxpr/qhd,khd->hqk/dot_general | solution.py:121
  189.4 11.4 %fusion.127 = f32[12,512]{1,0:T(8,128)S(1)} fusion(f32[12,512,1024]{2,1,0:T(8,128)} %get-tuple-element.536, f32[12,512]{1,0:T(8,128)S(1)} %get-tuple-element.537, pred[1024]{0:T(1024)(128)(4,1)S(1)} %iota_compare_fusion.5), kind=kLoop, calls=%fused_computation.6.clone.1 | loop fusion | flops 25159680 | bytes 25216000 | tf_op jit(solution)/shard_map/while/body/eval_jaxpr/reduce_sum | solution.py:130
  200.8 11.2 %bitcast_dynamic-update-slice_fusion.9 = bf16[2,512,12,64]{1,3,2,0:T(8,128)(2,1)S(1)} fusion(bf16[2,512,12,64]{1,3,2,0:T(8,128)(2,1)S(1)} %copy-done.12, s32[]{:T(128)S(6)} %copy.121, bf16[1024,12,64]{0,2,1:T(8,128)(2,1)S(1)} %copy-done.5, f32[12,512,1024]{2,1,0:T(8,128)} %get-tuple-element.536, f32[12,512]{1,0:T(8,128)S(1)} %fusion.127, ...), kind=kOutput, calls=%fused_computation.8.clone.1 | convolution fusion | flops 836763648 | bytes 28378116 | tf_op jit(solution)/shard_map/while/body/eval_jaxpr/hqk,khd->qhd/dot_general | solution.py:132
  213.5 4.2 copy.88
  222.8 39.2 %multiply_convert_fusion.1 = (bf16[1024,3072]{1,0:T(8,128)(2,1)}, f32[1024,3072]{1,0:T(8,128)}, f32[1024,3072]{1,0:T(8,128)}) fusion(f32[3072]{0:T(1024)S(1)} %copy-done.67, bf16[768,768]{1,0:T(8,128)(2,1)S(1)} %bitcast.259, bf16[768,768]{1,0:T(8,128)(2,1)S(1)} %bitcast.261, bf16[768,768]{1,0:T(8,128)(2,1)S(1)} %bitcast.263, ...), kind=kOutput, calls=%fused_computation.49 | convolution fusion | flops 5062262784 | bytes 39348224 | tf_op jit(solution)/shard_map/dot_general | solution.py:140
  264.7 9.4 %fusion.88 = (f32[1024]{0:T(1024)S(1)}, f32[1024,768]{0,1:T(8,128)S(1)}) fusion(f32[768]{0:T(1024)S(1)} %copy-done.70, bf16[1024,3072]{1,0:T(8,128)(2,1)} %get-tuple-element.387, bf16[3072,768]{1,0:T(8,128)(2,1)S(1)} %bitcast.244, f32[768]{0:T(1024)S(1)} %copy-done.69, f32[768]{0:T(1024)S(1)} %copy-done.58, f32[1024]{0:T(1024)S(1)} %fusion.66, ...), kind=kOutput, calls=%fused_computation.193 | convolution fusion | flops 4837342208 | bytes 17323008 | tf_op jit(solution)/shard_map/dot_general | solution.py:143
  277.4 3.7 convert_reduce_fusion.2
  281.1 6.9 convolution_convert_fusion
  288.0 17.9 %convert_reduce_fusion = (f32[3072]{0:T(1024)}, bf16[1024,3072]{1,0:T(8,128)(2,1)}) fusion(f32[1024,3072]{1,0:T(8,128)} %get-tuple-element.388, bf16[1024,768]{0,1:T(8,128)(2,1)S(1)} %get-tuple-element.374, bf16[3072,768]{1,0:T(8,128)(2,1)} %bitcast.245, f32[1024,3072]{1,0:T(8,128)} %get-tuple-element.432, f32[3072]{0:T(1024)S(1)} %copy-done.67), kind=kOutput, calls=%fused_computation.47 | convolution fusion | flops 4885312512 | bytes 37773312 | tf_op jit(solution)/shard_map/td,fd->tf/dot_general | solution.py:153
  305.9 11.8 %multiply_reduce_fusion.1 = (f32[768]{0:T(1024)}, f32[1024]{0:T(1024)S(1)}, f32[768]{0:T(1024)}, f32[1024,768]{0,1:T(8,128)S(1)}) fusion(f32[1024,768]{0,1:T(8,128)} %copy-done.10, f32[1024]{0:T(1024)S(1)} %fusion.66, f32[1024]{0:T(1024)S(1)} %broadcast_multiply_fusion.1, f32[768]{0:T(1024)S(1)} %copy-done.58, bf16[1024,3072]{1,0:T(8,128)(2,1)} %get-tuple-element.437, ...), kind=kOutput, calls=%fused_computation.84 | convolution fusion | flops 4864865280 | bytes 22065152 | tf_op jit(solution)/shard_map/tf,df->td/dot_general | solution.py:157
  317.7 7.2 convolution_convert_fusion.1
  325.8 10.2 %reshape.374 = bf16[32,24,4,768]{3,2,1,0:T(4,128)(2,1)} reshape(bf16[768,3072]{1,0:T(8,128)(2,1)} %convolution_convert_fusion.1) | data formatting | bytes 9437184 | tf_op jit(solution)/shard_map/reshape | solution.py:218
  335.9 5.4 copy.99
  349.7 3.0 copy.93
  354.1 163.2 %while.30 = (s32[]{:T(128)}, f32[1024,12,64]{0,2,1:T(8,128)}, f32[1024,12,64]{0,2,1:T(8,128)}, bf16[2,512,12,64]{1,3,2,0:T(8,128)(2,1)}, bf16[2,512,12,64]{1,3,2...) while((s32[]{:T(128)}, f32[1024,12,64]{0,2,1:T(8,128)}, ...), condition=%wide.region_14.15_spmd.clone, body=%wide.region_12.14_spmd.clone.sunk | while | flops 4125223936 | bytes 217239728 | solution.py:191
  355.0 10.1 %fusion.137 = f32[12,512,1024]{2,1,0:T(8,128)} fusion(bf16[1024,12,64]{0,2,1:T(8,128)(2,1)S(1)} %get-tuple-element.603, bf16[2,512,12,64]{1,3,2,0:T(8,128)(2,1)S(1)} %get-tuple-element.602, s32[]{:T(128)S(6)} %copy.131), kind=kOutput, calls=%fused_computation.30.clone.1 | convolution fusion | flops 805306368 | bytes 27525124 | tf_op jit(solution)/shard_map/while/body/eval_jaxpr/qhd,khd->hqk/dot_general | solution.py:121
  365.1 12.9 %bitcast_add_fusion.6 = f32[1024,12,64]{0,2,1:T(8,128)} fusion(f32[1024,12,64]{0,2,1:T(8,128)} %get-tuple-element.588, f32[12,512,1024]{2,1,0:T(8,128)} %fusion.137, f32[12,512]{1,0:T(8,128)S(1)} %dynamic-slice_bitcast_fusion.2, pred[1024]{0:T(1024)(128)(4,1)S(1)} %iota_compare_fusion.6, pred[]{:T(512)S(6)} %compare.9, ...), kind=kOutput, calls=%fused_computation.23.clone.1 | convolution fusion | flops 832045056 | bytes 32277508 | tf_op jit(solution)/shard_map/while/body/eval_jaxpr/hqk,qhd->khd/dot_general | solution.py:172
  378.0 17.4 %multiply_reduce_fusion.14 = (f32[12,512]{1,0:T(8,128)S(1)}, f32[12,512,1024]{2,1,0:T(8,128)}) fusion(f32[12,512,1024]{2,1,0:T(8,128)} %fusion.137, f32[12,512]{1,0:T(8,128)S(1)} %dynamic-slice_bitcast_fusion.2, pred[1024]{0:T(1024)(128)(4,1)S(1)} %iota_compare_fusion.6, bf16[1024,12,64]{0,2,1:T(8,128)(2,1)} %get-tuple-element.606, ...), kind=kOutput, calls=%fused_computation.18.clone.1 | convolution fusion | flops 836757504 | bytes 52741124 | tf_op jit(solution)/shard_map/while/body/eval_jaxpr/qhd,khd->hqk/dot_general | solution.py:175
  395.4 21.4 %multiply_convert_fusion.4 = bf16[12,512,1024]{2,1,0:T(8,128)(2,1)} fusion(f32[12,512,1024]{2,1,0:T(8,128)} %get-tuple-element.548, f32[12,512,1024]{2,1,0:T(8,128)} %fusion.137, f32[12,512]{1,0:T(8,128)S(1)} %get-tuple-element.549, f32[12,512]{1,0:T(8,128)S(1)} %dynamic-slice_bitcast_fusion.2, pred[1024]{0:T(1024)(128)(4,1)S(1)} %iota_compare_fusion.6), kind=kLoop, calls=%fused_computation.17.clone.1 | loop fusion | flops 37748736 | bytes 62964736 | tf_op jit(solution)/shard_map/while/body/eval_jaxpr/convert_element_type | solution.py:179
  416.8 9.4 %bitcast_dynamic-update-slice_fusion.11 = bf16[2,512,12,64]{1,3,2,0:T(8,128)(2,1)} fusion(bf16[2,512,12,64]{1,3,2,0:T(8,128)(2,1)} %get-tuple-element.589, s32[]{:T(128)S(6)} %copy.131, bf16[12,512,1024]{2,1,0:T(8,128)(2,1)} %multiply_convert_fusion.4, bf16[1024,12,64]{0,2,1:T(8,128)(2,1)S(1)} %get-tuple-element.603), kind=kOutput, calls=%fused_computation.25.clone.1 | convolution fusion | flops 805699584 | bytes 15728644 | tf_op jit(solution)/shard_map/while/body/eval_jaxpr/hqk,khd->qhd/dot_general | solution.py:181
  426.2 8.5 %bitcast_add_fusion.5 = f32[1024,12,64]{0,2,1:T(8,128)} fusion(f32[1024,12,64]{0,2,1:T(8,128)} %get-tuple-element.587, bf16[12,512,1024]{2,1,0:T(8,128)(2,1)} %multiply_convert_fusion.4, pred[]{:T(512)S(6)} %compare.9, bf16[2,512,12,64]{1,3,2,0:T(8,128)(2,1)S(1)} %get-tuple-element.602, s32[]{:T(128)S(6)} %copy.131), kind=kOutput, calls=%fused_computation.24.clone.1 | convolution fusion | flops 807665664 | bytes 19660804 | tf_op jit(solution)/shard_map/while/body/eval_jaxpr/hqk,qhd->khd/dot_general | solution.py:185
  435.5 10.1 %fusion.137 = f32[12,512,1024]{2,1,0:T(8,128)} fusion(bf16[1024,12,64]{0,2,1:T(8,128)(2,1)S(1)} %get-tuple-element.603, bf16[2,512,12,64]{1,3,2,0:T(8,128)(2,1)S(1)} %get-tuple-element.602, s32[]{:T(128)S(6)} %copy.131), kind=kOutput, calls=%fused_computation.30.clone.1 | convolution fusion | flops 805306368 | bytes 27525124 | tf_op jit(solution)/shard_map/while/body/eval_jaxpr/qhd,khd->hqk/dot_general | solution.py:121
  445.6 13.8 %bitcast_add_fusion.6 = f32[1024,12,64]{0,2,1:T(8,128)} fusion(f32[1024,12,64]{0,2,1:T(8,128)} %get-tuple-element.588, f32[12,512,1024]{2,1,0:T(8,128)} %fusion.137, f32[12,512]{1,0:T(8,128)S(1)} %dynamic-slice_bitcast_fusion.2, pred[1024]{0:T(1024)(128)(4,1)S(1)} %iota_compare_fusion.6, pred[]{:T(512)S(6)} %compare.9, ...), kind=kOutput, calls=%fused_computation.23.clone.1 | convolution fusion | flops 832045056 | bytes 32277508 | tf_op jit(solution)/shard_map/while/body/eval_jaxpr/hqk,qhd->khd/dot_general | solution.py:172
  459.4 17.4 %multiply_reduce_fusion.14 = (f32[12,512]{1,0:T(8,128)S(1)}, f32[12,512,1024]{2,1,0:T(8,128)}) fusion(f32[12,512,1024]{2,1,0:T(8,128)} %fusion.137, f32[12,512]{1,0:T(8,128)S(1)} %dynamic-slice_bitcast_fusion.2, pred[1024]{0:T(1024)(128)(4,1)S(1)} %iota_compare_fusion.6, bf16[1024,12,64]{0,2,1:T(8,128)(2,1)} %get-tuple-element.606, ...), kind=kOutput, calls=%fused_computation.18.clone.1 | convolution fusion | flops 836757504 | bytes 52741124 | tf_op jit(solution)/shard_map/while/body/eval_jaxpr/qhd,khd->hqk/dot_general | solution.py:175
  476.8 21.4 %multiply_convert_fusion.4 = bf16[12,512,1024]{2,1,0:T(8,128)(2,1)} fusion(f32[12,512,1024]{2,1,0:T(8,128)} %get-tuple-element.548, f32[12,512,1024]{2,1,0:T(8,128)} %fusion.137, f32[12,512]{1,0:T(8,128)S(1)} %get-tuple-element.549, f32[12,512]{1,0:T(8,128)S(1)} %dynamic-slice_bitcast_fusion.2, pred[1024]{0:T(1024)(128)(4,1)S(1)} %iota_compare_fusion.6), kind=kLoop, calls=%fused_computation.17.clone.1 | loop fusion | flops 37748736 | bytes 62964736 | tf_op jit(solution)/shard_map/while/body/eval_jaxpr/convert_element_type | solution.py:179
  498.3 9.4 %bitcast_dynamic-update-slice_fusion.11 = bf16[2,512,12,64]{1,3,2,0:T(8,128)(2,1)} fusion(bf16[2,512,12,64]{1,3,2,0:T(8,128)(2,1)} %get-tuple-element.589, s32[]{:T(128)S(6)} %copy.131, bf16[12,512,1024]{2,1,0:T(8,128)(2,1)} %multiply_convert_fusion.4, bf16[1024,12,64]{0,2,1:T(8,128)(2,1)S(1)} %get-tuple-element.603), kind=kOutput, calls=%fused_computation.25.clone.1 | convolution fusion | flops 805699584 | bytes 15728644 | tf_op jit(solution)/shard_map/while/body/eval_jaxpr/hqk,khd->qhd/dot_general | solution.py:181
  507.6 9.4 %bitcast_add_fusion.5 = f32[1024,12,64]{0,2,1:T(8,128)} fusion(f32[1024,12,64]{0,2,1:T(8,128)} %get-tuple-element.587, bf16[12,512,1024]{2,1,0:T(8,128)(2,1)} %multiply_convert_fusion.4, pred[]{:T(512)S(6)} %compare.9, bf16[2,512,12,64]{1,3,2,0:T(8,128)(2,1)S(1)} %get-tuple-element.602, s32[]{:T(128)S(6)} %copy.131), kind=kOutput, calls=%fused_computation.24.clone.1 | convolution fusion | flops 807665664 | bytes 19660804 | tf_op jit(solution)/shard_map/while/body/eval_jaxpr/hqk,qhd->khd/dot_general | solution.py:185
  517.3 3.2 copy.94
  521.2 3.0 convert.67
  525.3 7.3 fusion.42
  532.7 4.0 copy.96
  536.7 8.8 %reshape.372 = bf16[32,24,3,768]{3,2,1,0:T(4,128)(2,1)} reshape(bf16[768,2304]{1,0:T(8,128)(2,1)} %copy.96) | data formatting | bytes 7077888 | tf_op jit(solution)/shard_map/reshape | solution.py:218
  545.5 3.1 copy.97
  549.5 8.7 %pad_maximum_fusion = bf16[32,288,768]{2,1,0:T(8,128)(2,1)} fusion(bf16[32,96,768]{2,1,0:T(8,128)(2,1)} %bitcast.243, bf16[32,96,768]{2,1,0:T(8,128)(2,1)S(1)} %bitcast.228, bf16[32,24,768]{2,1,0:T(8,128)(2,1)S(1)} %copy-done.37, bf16[32,72,768]{2,1,0:T(8,128)(2,1)S(1)} %bitcast.231), kind=kLoop, calls=%fused_computation.45 | loop fusion | flops 56623104 | bytes 28311552 | tf_op jit(solution)/shard_map/concatenate | solution.py:220
  558.3 2.9 convert_reduce_fusion.1
  571.3 3.4 collective-permute-done.8
  576.3 9.4 %add_bitcast_fusion = f32[1,1024,768]{1,2,0:T(8,128)} fusion(f32[1024,768]{0,1:T(8,128)S(1)} %copy-done.9, f32[1024]{0:T(1024)S(1)} %copy-done.61, bf16[768,768]{1,0:T(8,128)(2,1)} %bitcast.249, bf16[768,768]{1,0:T(8,128)(2,1)} %bitcast.251, bf16[768,768]{1,0:T(8,128)(2,1)} %bitcast.253, bf16[1024,768]{0,1:T(8,128)(2,1)} %bitcast.242, ...), kind=kOutput, calls=%fused_computation.86 | convolution fusion | flops 3650224128 | bytes 14553088 | tf_op jit(solution)/shard_map/tj,dj->td/dot_general | solution.py:200
  593.6 125.8 %reduce-scatter.2.cloned.1.call-done = bf16[1,288,768]{2,1,0:T(8,128)(2,1)} async-done(((bf16[32,288,768]{2,1,0:T(8,128)(2,1)}), bf16[1,288,768]{2,1,0:T(8,128)(2,1)}) %reduce-scatter.2.cloned.1.call-update) | async-done | bytes 442384 | tf_op jit(solution)/shard_map/reduce_scatter | solution.py:224
  726.1 5.2 stack.43
  740.2 2.8 collective-permute-done.3
  744.2 3.3 collective-permute-done.4
  (281 shorter events, 90.4 us)
Async XLA Ops:
  7.2 115.9 %all-gather.2.cloned.1.call-start = ((), (), s32[]{:S(2)}) async-start(), calls=%async_computation.1 | async-start | bytes 15003648 | tf_op jit(solution)/shard_map/all_gather | solution.py:74
  8.0 9.7 %copy-start.23 = (bf16[1,1024,768]{2,1,0:T(8,128)(2,1)S(1)}, bf16[1,1024,768]{2,1,0:T(8,128)(2,1)}, u32[]{:S(2)}) copy-start(bf16[1,1024,768]{2,1,0:T(8,128)(2,1)} %param.24) | copy-start | bytes 4718596
  15.3 704.1 %reduce-scatter.2.cloned.1.call-start = ((), (), s32[]{:S(2)}) async-start(), calls=%async_computation.2 | async-start | bytes 14598144 | tf_op jit(solution)/shard_map/reduce_scatter | solution.py:224
  154.8 11.4 %copy-start.5 = (bf16[1024,12,64]{0,2,1:T(8,128)(2,1)S(1)}, bf16[1024,12,64]{0,2,1:T(8,128)(2,1)}, u32[]{:S(2)}) copy-start(bf16[1024,12,64]{0,2,1:T(8,128)(2,1)} %get-tuple-element.571) | copy-start | bytes 4718596 | tf_op jit(solution)/shard_map/while
  154.8 11.4 %copy-start.12 = (bf16[2,512,12,64]{1,3,2,0:T(8,128)(2,1)S(1)}, bf16[2,512,12,64]{1,3,2,0:T(8,128)(2,1)}, u32[]{:S(2)}) copy-start(bf16[2,512,12,64]{1,3,2,0:T(8,128)(2,1)} %get-tuple-element.559) | copy-start | bytes 4718596 | tf_op jit(solution)/shard_map/while
  189.4 11.4 %copy-start.5 = (bf16[1024,12,64]{0,2,1:T(8,128)(2,1)S(1)}, bf16[1024,12,64]{0,2,1:T(8,128)(2,1)}, u32[]{:S(2)}) copy-start(bf16[1024,12,64]{0,2,1:T(8,128)(2,1)} %get-tuple-element.571) | copy-start | bytes 4718596 | tf_op jit(solution)/shard_map/while
  189.4 11.4 %copy-start.12 = (bf16[2,512,12,64]{1,3,2,0:T(8,128)(2,1)S(1)}, bf16[2,512,12,64]{1,3,2,0:T(8,128)(2,1)}, u32[]{:S(2)}) copy-start(bf16[2,512,12,64]{1,3,2,0:T(8,128)(2,1)} %get-tuple-element.559) | copy-start | bytes 4718596 | tf_op jit(solution)/shard_map/while
  219.9 44.8 %copy-start.10 = (f32[1024,768]{0,1:T(8,128)}, f32[1024,768]{0,1:T(8,128)S(1)}, u32[]{:S(2)}) copy-start(f32[1024,768]{0,1:T(8,128)S(1)} %get-tuple-element.431) | copy-start | bytes 9437188
  220.4 41.6 %copy-start.55 = (f32[1024]{0:T(1024)}, f32[1024]{0:T(1024)S(1)}, u32[]{:S(2)}) copy-start(f32[1024]{0:T(1024)S(1)} %multiply_reduce_fusion.4) | copy-start | bytes 12292
  264.7 9.5 %copy-start.17 = (bf16[32,96,768]{2,1,0:T(8,128)(2,1)}, bf16[32,96,768]{2,1,0:T(8,128)(2,1)S(1)}, u32[]{:S(2)}) copy-start(bf16[32,96,768]{2,1,0:T(8,128)(2,1)S(1)} %slice.234) | copy-start | bytes 14155780
  264.7 9.5 %copy-start.6 = (bf16[1,1024,768]{1,2,0:T(8,128)(2,1)S(1)}, bf16[1,1024,768]{1,2,0:T(8,128)(2,1)}, u32[]{:S(2)}) copy-start(bf16[1,1024,768]{1,2,0:T(8,128)(2,1)} %copy.89) | copy-start | bytes 4718596
  264.7 9.5 %copy-start.53 = (f32[768]{0:T(1024)S(1)}, f32[768]{0:T(1024)}, u32[]{:S(2)}) copy-start(f32[768]{0:T(1024)} %get-tuple-element.412) | copy-start | bytes 9220
  264.7 9.5 %copy-start.54 = (f32[1024]{0:T(1024)S(1)}, f32[1024]{0:T(1024)}, u32[]{:S(2)}) copy-start(f32[1024]{0:T(1024)} %fusion.65) | copy-start | bytes 12292
  305.9 11.8 %copy-start.11 = (f32[1024,768]{0,1:T(8,128)S(1)}, f32[1024,768]{0,1:T(8,128)}, u32[]{:S(2)}) copy-start(f32[1024,768]{0,1:T(8,128)} %copy-done.10) | copy-start | bytes 9437188
  305.9 11.8 %copy-start.74 = (bf16[1024,3072]{1,0:T(8,128)(2,1)S(1)}, bf16[1024,3072]{1,0:T(8,128)(2,1)}, u32[]{:S(2)}) copy-start(bf16[1024,3072]{1,0:T(8,128)(2,1)} %get-tuple-element.437) | copy-start | bytes 18874372
  325.7 15.6 %copy-start.8 = (f32[1024,768]{0,1:T(8,128)}, f32[1024,768]{0,1:T(8,128)S(1)}, u32[]{:S(2)}) copy-start(f32[1024,768]{0,1:T(8,128)S(1)} %get-tuple-element.386) | copy-start | bytes 9437188
  325.8 15.6 %copy-start.60 = (f32[1024]{0:T(1024)}, f32[1024]{0:T(1024)S(1)}, u32[]{:S(2)}) copy-start(f32[1024]{0:T(1024)S(1)} %negate_multiply_fusion.1) | copy-start | bytes 12292
  355.0 10.2 %copy-start.7 = (bf16[2,512,12,64]{1,3,2,0:T(8,128)(2,1)S(1)}, bf16[2,512,12,64]{1,3,2,0:T(8,128)(2,1)}, u32[]{:S(2)}) copy-start(bf16[2,512,12,64]{1,3,2,0:T(8,128)(2,1)} %get-tuple-element.605) | copy-start | bytes 4718596 | tf_op jit(solution)/shard_map/while
  435.5 10.2 %copy-start.7 = (bf16[2,512,12,64]{1,3,2,0:T(8,128)(2,1)S(1)}, bf16[2,512,12,64]{1,3,2,0:T(8,128)(2,1)}, u32[]{:S(2)}) copy-start(bf16[2,512,12,64]{1,3,2,0:T(8,128)(2,1)} %get-tuple-element.605) | copy-start | bytes 4718596 | tf_op jit(solution)/shard_map/while
  536.7 11.9 %slice-start = ((s8[4718592]{0:T(1024)(128)(4,1)}), s8[524288]{0:T(1024)(128)(4,1)S(1)}, s32[]{:S(2)}) async-start(s8[4718592]{0:T(1024)(128)(4,1)} %bitcast.226), calls=%async_computation.3 | async-start | bytes 1048576
  558.3 18.0 %copy-start.9 = (f32[1024,768]{0,1:T(8,128)S(1)}, f32[1024,768]{0,1:T(8,128)}, u32[]{:S(2)}) copy-start(f32[1024,768]{0,1:T(8,128)} %copy-done.8) | copy-start | bytes 9437188
  558.3 18.0 %copy-start.61 = (f32[1024]{0:T(1024)S(1)}, f32[1024]{0:T(1024)}, u32[]{:S(2)}) copy-start(f32[1024]{0:T(1024)} %copy-done.60) | copy-start | bytes 12292
  561.4 1.3 collective-permute-start.5
  562.7 4.0 collective-permute-start.6
  566.7 4.0 collective-permute-start.7
  570.7 4.0 collective-permute-start.8
  574.7 16.6 %collective-permute-start.9 = (f32[72,128]{1,0:T(8,128)S(1)}, f32[72,128]{1,0:T(8,128)}, u32[]{:S(2)}, u32[]{:S(2)}) collective-permute-start(f32[72,128]{1,0:T(8,128)S(1)} %add.268), channel_id=1, source_target_pairs={{0,16},{1,17},{2,18},{3,19},{4,20},{5,21},{6,22},{7,23},{8,24},{9,... | collective-permute-start | bytes 110600 | tf_op jit(solution)/shard_map/ppermute | solution.py:43
  588.6 132.0 %copy-start.44 = (f32[24,768]{1,0:T(8,128)S(1)}, f32[24,768]{1,0:T(8,128)}, u32[]{:S(2)}) copy-start(f32[24,768]{1,0:T(8,128)} %param.28) | copy-start | bytes 221188
  588.6 133.6 %copy-start.19 = (f32[96,768]{1,0:T(8,128)S(1)}, f32[96,768]{1,0:T(8,128)}, u32[]{:S(2)}) copy-start(f32[96,768]{1,0:T(8,128)} %param.30) | copy-start | bytes 884740
  591.2 133.0 %copy-start.21 = (f32[24,2304]{1,0:T(8,128)S(1)}, f32[24,2304]{1,0:T(8,128)}, u32[]{:S(2)}) copy-start(f32[24,2304]{1,0:T(8,128)} %param.27) | copy-start | bytes 663556
  591.2 133.0 %copy-start.51 = (f32[24,2304]{1,0:T(8,128)S(1)}, f32[24,2304]{1,0:T(8,128)}, u32[]{:S(2)}) copy-start(f32[24,2304]{1,0:T(8,128)} %param.32) | copy-start | bytes 663556
  591.2 133.0 %copy-start.52 = (f32[24,2304]{1,0:T(8,128)S(1)}, f32[24,2304]{1,0:T(8,128)}, u32[]{:S(2)}) copy-start(f32[24,2304]{1,0:T(8,128)} %param.37) | copy-start | bytes 663556
  591.2 133.8 %copy-start.20 = (f32[24,3072]{1,0:T(8,128)S(1)}, f32[24,3072]{1,0:T(8,128)}, u32[]{:S(2)}) copy-start(f32[24,3072]{1,0:T(8,128)} %param.29) | copy-start | bytes 884740
  591.2 133.8 %copy-start.49 = (f32[24,3072]{1,0:T(8,128)S(1)}, f32[24,3072]{1,0:T(8,128)}, u32[]{:S(2)}) copy-start(f32[24,3072]{1,0:T(8,128)} %param.34) | copy-start | bytes 884740
  722.2 33.6 %copy-start.47 = (f32[24,768]{1,0:T(8,128)}, f32[24,768]{1,0:T(8,128)S(1)}, u32[]{:S(2)}) copy-start(f32[24,768]{1,0:T(8,128)S(1)} %get-tuple-element.381) | copy-start | bytes 221188
  722.2 33.6 %copy-start.48 = (f32[24,768]{1,0:T(8,128)}, f32[24,768]{1,0:T(8,128)S(1)}, u32[]{:S(2)}) copy-start(f32[24,768]{1,0:T(8,128)S(1)} %get-tuple-element.382) | copy-start | bytes 221188
  724.2 32.5 %copy-start.38 = (f32[96,768]{1,0:T(8,128)}, f32[96,768]{1,0:T(8,128)S(1)}, u32[]{:S(2)}) copy-start(f32[96,768]{1,0:T(8,128)S(1)} %get-tuple-element.377) | copy-start | bytes 884740
  724.2 32.5 %copy-start.39 = (f32[96,768]{1,0:T(8,128)}, f32[96,768]{1,0:T(8,128)S(1)}, u32[]{:S(2)}) copy-start(f32[96,768]{1,0:T(8,128)S(1)} %get-tuple-element.378) | copy-start | bytes 884740
  725.0 31.6 %copy-start.42 = (f32[24,2304]{1,0:T(8,128)}, f32[24,2304]{1,0:T(8,128)S(1)}, u32[]{:S(2)}) copy-start(f32[24,2304]{1,0:T(8,128)S(1)} %get-tuple-element.383) | copy-start | bytes 663556
  725.1 31.6 %copy-start.43 = (f32[24,2304]{1,0:T(8,128)}, f32[24,2304]{1,0:T(8,128)S(1)}, u32[]{:S(2)}) copy-start(f32[24,2304]{1,0:T(8,128)S(1)} %get-tuple-element.384) | copy-start | bytes 663556
  726.1 30.6 %copy-start.40 = (f32[24,3072]{1,0:T(8,128)}, f32[24,3072]{1,0:T(8,128)S(1)}, u32[]{:S(2)}) copy-start(f32[24,3072]{1,0:T(8,128)S(1)} %get-tuple-element.379) | copy-start | bytes 884740
  726.1 30.6 %copy-start.41 = (f32[24,3072]{1,0:T(8,128)}, f32[24,3072]{1,0:T(8,128)S(1)}, u32[]{:S(2)}) copy-start(f32[24,3072]{1,0:T(8,128)S(1)} %get-tuple-element.380) | copy-start | bytes 884740
  731.3 1.1 collective-permute-start
  732.4 3.5 collective-permute-start.1
  735.9 3.5 collective-permute-start.2
  739.5 3.5 collective-permute-start.3
  743.0 4.4 collective-permute-start.4
  747.5 9.2 %copy-start.57 = (f32[8]{0:T(128)}, f32[8]{0:T(128)S(1)}, u32[]{:S(2)}) copy-start(f32[8]{0:T(128)S(1)} %add_sqrt_fusion) | copy-start | bytes 100
  (47 other events, 168.1 us)
Sparse Core Ops, SparseCore 0:
  15.4 107.6 all-gather.1
  558.3 161.0 reduce-scatter.1

commit v2 on v0

v2 whole, which is shorter than its diff:
```python
from functools import partial

import jax
import jax.numpy as jnp
from jax import lax
from jax.experimental import pallas as pl
from jax.experimental.pallas import tpu as pltpu
from jax.sharding import PartitionSpec as P

D = 768
FF = 3072
HEADS = 12
HEAD_DIM = 64
PAIRS = HEADS // 2
WIDE = 2 * HEAD_DIM
CHUNKS = FF // D
STEP = 10
MASKED = -1e9
VMEM = 60 * 2**20
BF16 = jnp.bfloat16
F32 = jnp.float32


def dot(a, b):
    return jnp.dot(a, b, preferred_element_type=F32)


def dot_nt(a, b):
    return lax.dot_general(a, b, (((1,), (1,)), ((), ())), preferred_element_type=F32)


def dot_tn(a, b):
    return lax.dot_general(a, b, (((0,), (0,)), ((), ())), preferred_element_type=F32)


def cost(us):
    return pl.CostEstimate(flops=int(us * 5.0e7), bytes_accessed=0, transcendentals=0)


def arrange(value, matrix):
    return dot(value, matrix).astype(BF16)


def project_kernel(xa_ref, xb_ref, la_ref, lb_ref, ra_ref, rb_ref, bias_ref, out_ref):
    width = la_ref.shape[1]
    left = jnp.concatenate([la_ref[...], lb_ref[...]], axis=0)
    out_ref[:, :width] = (dot(xa_ref[...], left) + bias_ref[:, :width]).astype(BF16)
    right = jnp.concatenate([ra_ref[:, :width], rb_ref[:, :width]], axis=0)
    out_ref[:, width:] = (dot(xb_ref[...], right) + bias_ref[:, width:]).astype(BF16)


def project(x_a, x_b, left, right, bias):
    seq = x_a.shape[0]
    rows = min(512, seq)

    def fixed(shape):
        return pl.BlockSpec(shape, lambda i: (0, 0), pipeline_mode=pl.Buffered(1))

    return pl.pallas_call(
        project_kernel,
        grid=(seq // rows,),
        in_specs=[pl.BlockSpec((rows, D), lambda i: (i, 0))] * 2
        + [fixed(part.shape) for part in (*left, *right, bias)],
        out_specs=pl.BlockSpec((rows, 3 * D), lambda i: (i, 0)),
        out_shape=jax.ShapeDtypeStruct((seq, 3 * D), BF16),
        compiler_params=pltpu.CompilerParams(vmem_limit_bytes=VMEM),
        cost_estimate=cost(5),
        name="project",
    )(x_a, x_b, *left, *right, bias)


def attend_kernel(len_ref, q_ref, k_ref, v_ref, ctx_ref, ctxt_ref, lse_ref):
    seq = q_ref.shape[0]
    qt = (q_ref[...].astype(F32) * 0.125).T.astype(BF16)
    vt = v_ref[...].astype(F32).T.astype(BF16)
    k = k_ref[...]
    keep = lax.broadcasted_iota(jnp.int32, (seq, seq), 0) < len_ref[0]
    zero = jnp.zeros((HEAD_DIM, seq), BF16)
    ones = jnp.ones((16, seq), BF16)
    for h in range(2):
        rows = slice(h * HEAD_DIM, (h + 1) * HEAD_DIM)
        q = jnp.concatenate([qt[rows], zero] if h == 0 else [zero, qt[rows]], axis=0)
        scores = jnp.where(keep, dot(k, q), MASKED)
        peak = jnp.max(scores, axis=0, keepdims=True)
        expo = jnp.exp(scores - peak).astype(BF16)
        both = dot(jnp.concatenate([vt[rows], ones], axis=0), expo)
        total = both[HEAD_DIM : HEAD_DIM + 1]
        ctxt_ref[rows, :] = both[:HEAD_DIM] / total
        lse_ref[0, h : h + 1, :] = peak + jnp.log(total)
    ctx_ref[...] = ctxt_ref[...].T.astype(BF16)


def after(kernel, first, count):
    def call(*refs):
        kernel(*refs[:first], *refs[first + count :])

    return call


def untouched(values):
    return [pl.BlockSpec(memory_space=pl.ANY)] * len(values)


def attend(lengths, packed, first, count, before=(), waits=()):
    seq = packed.shape[0]
    extra = (*before, *waits)
    return pl.pallas_call(
        after(attend_kernel, 4, len(extra)),
        grid_spec=pltpu.PrefetchScalarGridSpec(
            num_scalar_prefetch=1,
            grid=(count,),
            in_specs=[
                pl.BlockSpec((seq, WIDE), lambda p, _, i=i: (0, i * PAIRS + first + p))
                for i in range(3)
            ]
            + untouched(extra),
            out_specs=[
                pl.BlockSpec((seq, WIDE), lambda p, _: (0, first + p)),
                pl.BlockSpec((WIDE, seq), lambda p, _: (first + p, 0)),
                pl.BlockSpec((1, 2, seq), lambda p, _: (first + p, 0, 0)),
            ],
        ),
        out_shape=[
            jax.ShapeDtypeStruct((seq, D), BF16),
            jax.ShapeDtypeStruct((D, seq), F32),
            jax.ShapeDtypeStruct((PAIRS, 2, seq), F32),
        ],
        input_output_aliases={4 + i: i for i in range(len(before))},
        compiler_params=pltpu.CompilerParams(vmem_limit_bytes=VMEM),
        cost_estimate=cost(4 * count),
        name="attend",
    )(lengths, packed, packed, packed, *extra)


def attend_back_kernel(
    block, len_ref, q_ref, k_ref, v_ref, do_ref, ctxt_ref, lse_ref, out_ref, sum_ref, dqt_ref
):
    seq = q_ref.shape[0]
    q = q_ref[...].astype(F32) * 0.125
    qt = q.T.astype(BF16)
    q = q.astype(BF16)
    do = do_ref[...]
    dof = do.astype(F32).T
    dot_ = dof.astype(BF16)
    prod = dof * ctxt_ref[...]
    kt = k_ref[...].astype(F32).T.astype(BF16)
    row = lax.broadcasted_iota(jnp.int32, (HEAD_DIM, seq), 0)

    def pieces(vec):
        high = vec.astype(BF16).astype(F32)
        mid = (vec - high).astype(BF16).astype(F32)
        low = vec - high - mid
        picked = jnp.where(row == 1, mid, jnp.where(row == 2, low, 0.0))
        return jnp.where(row == 0, high, picked).astype(BF16)

    q_aug, do_aug, fill = [], [], []
    for h in range(2):
        rows = slice(h * HEAD_DIM, (h + 1) * HEAD_DIM)
        lse = lse_ref[0, h : h + 1]
        delta = jnp.sum(prod[rows], axis=0, keepdims=True)
        q_parts = [qt[rows], pieces(-lse)]
        do_parts = [dot_[rows], pieces(-delta)]
        q_aug.append(jnp.concatenate(q_parts if h == 0 else q_parts[::-1], axis=0))
        do_aug.append(jnp.concatenate(do_parts if h == 0 else do_parts[::-1], axis=0))
        fill.append(MASKED - lse)
    lane = lax.broadcasted_iota(jnp.int32, (block, WIDE), 1)
    mine = (lane < HEAD_DIM, lane >= HEAD_DIM)
    one = (
        jnp.where(lane < HEAD_DIM + 3, 1.0, 0.0).astype(BF16),
        jnp.where(lane < 3, 1.0, 0.0).astype(BF16),
    )
    for j in range(seq // block):
        rows = slice(j * block, (j + 1) * block)
        keep = lax.broadcasted_iota(jnp.int32, (block, seq), 0) + j * block < len_ref[0]
        k, v = k_ref[rows, :], v_ref[rows, :]
        dv, dk = [], []
        for h in range(2):
            heads = slice(h * HEAD_DIM, (h + 1) * HEAD_DIM)
            k_aug, v_aug = jnp.where(mine[h], k, one[h]), jnp.where(mine[h], v, one[h])
            prob = jnp.exp(jnp.where(keep, dot(k_aug, q_aug[h]), fill[h]))
            dscore = (prob * dot(v_aug, do_aug[h])).astype(BF16)
            dv.append(dot(prob.astype(BF16), do))
            dk.append(dot(dscore, q))
            dq = dot(kt[heads, rows], dscore)
            if j == 0:
                dqt_ref[heads, :] = dq
            else:
                dqt_ref[heads, :] += dq
        out_ref[1, rows, :] = jnp.where(mine[0], dk[0], dk[1]).astype(BF16)
        out_ref[2, rows, :] = jnp.where(mine[0], dv[0], dv[1]).astype(BF16)
    out_ref[0] = (dqt_ref[...] * 0.125).T.astype(BF16)
    sum_ref[0, 0:1] = jnp.sum(out_ref[0].astype(F32), axis=0, keepdims=True)
    sum_ref[0, 1:2] = jnp.sum(out_ref[2].astype(F32), axis=0, keepdims=True)


def attend_back(lengths, packed, dctx, ctxt, lse, first, count, before=None, waits=()):
    seq = packed.shape[0]
    extra = tuple(waits) if before is None else (before, *waits)
    return pl.pallas_call(
        after(partial(attend_back_kernel, min(512, seq)), 7, len(extra)),
        grid_spec=pltpu.PrefetchScalarGridSpec(
            num_scalar_prefetch=1,
            grid=(count,),
            in_specs=[
                pl.BlockSpec((seq, WIDE), lambda p, _, i=i: (0, i * PAIRS + first + p))
                for i in range(3)
            ]
            + [
                pl.BlockSpec((seq, WIDE), lambda p, _: (0, first + p)),
                pl.BlockSpec((WIDE, seq), lambda p, _: (first + p, 0)),
                pl.BlockSpec((1, 2, seq), lambda p, _: (first + p, 0, 0)),
            ]
            + untouched(extra),
            out_specs=[
                pl.BlockSpec((3, seq, WIDE), lambda p, _: (0, 0, first + p)),
                pl.BlockSpec((1, 2, WIDE), lambda p, _: (p, 0, 0)),
            ],
            scratch_shapes=[pltpu.VMEM((WIDE, seq), F32)],
        ),
        out_shape=[
            jax.ShapeDtypeStruct((3, seq, D), BF16),
            jax.ShapeDtypeStruct((count, 2, WIDE), F32),
        ],
        input_output_aliases={} if before is None else {7: 0},
        compiler_params=pltpu.CompilerParams(vmem_limit_bytes=VMEM),
        cost_estimate=cost(6 * count),
        name="attend_back",
    )(lengths, packed, packed, packed, dctx, ctxt, lse, *extra)


def normal_parts(u):
    return 0.5 + 0.5 * lax.erf(u * 0.7071067811865476), jnp.exp(-0.5 * u * u)


def norm_forward(resid):
    center = resid - jnp.mean(resid, axis=-1, keepdims=True)
    inverse = lax.rsqrt(jnp.mean(center * center, axis=-1, keepdims=True) + 1e-05)
    return center * inverse, inverse


def norm_back(grad, gain, unit, inverse):
    du = grad * gain
    mean = jnp.mean(du, axis=-1, keepdims=True)
    return inverse * (du - mean - unit * jnp.mean(du * unit, axis=-1, keepdims=True))


def column_sum(value):
    return jnp.sum(value.astype(F32), axis=0, keepdims=True)


def feed_kernel(
    pieces,
    len_ref,
    place_ref,
    x_ref,
    ctx_ref,
    cot_ref,
    wo_ref,
    w1a_ref,
    w1b_ref,
    w1c_ref,
    w1d_ref,
    vec_ref,
    to_a_ref,
    to_b_ref,
    *refs,
):
    parts = refs[: len(pieces)]
    refs = refs[len(pieces) :]
    feed_step(
        pieces,
        parts,
        len_ref,
        place_ref,
        x_ref,
        ctx_ref,
        cot_ref,
        wo_ref,
        (w1a_ref, w1b_ref, w1c_ref, w1d_ref),
        vec_ref,
        to_a_ref,
        to_b_ref,
        *refs,
    )


def feed_step(
    pieces,
    parts,
    len_ref,
    place_ref,
    x_ref,
    ctx_ref,
    cot_ref,
    wo_ref,
    w1_refs,
    vec_ref,
    to_a_ref,
    to_b_ref,
    mixed_ref,
    first_ref,
    ctx_out_ref,
    act_ref,
    dbranch_ref,
    dhidden_ref,
    dres_ref,
    unit_ref,
    inverse_ref,
    sum_ref,
    slope_ref,
    w2_ref,
    sems,
):
    step = pl.program_id(0)
    rows = x_ref.shape[0]

    def copies():
        made = []
        for part, (first, count, column) in zip(parts, pieces):
            size, width = part.shape[0] // count, part.shape[1]
            for i in range(count):
                where = pl.multiple_of(place_ref[first + i] * size, size)
                target = w2_ref.at[pl.ds(where, size), pl.ds(column, width)]
                source = part.at[pl.ds(i * size, size), :]
                made.append(pltpu.make_async_copy(source, target, sems.at[len(made)]))
        return made

    def vec(i):
        return vec_ref[i : i + 1, :]

    @pl.when(step == 0)
    def _():
        for copy in copies():
            copy.start()
        sum_ref[...] = jnp.zeros_like(sum_ref)

    resid = x_ref[...].astype(F32) + (dot(ctx_ref[...], wo_ref[...]) + vec(2))
    unit1, inverse1 = norm_forward(resid)
    unit_ref[...] = unit1
    inverse_ref[...] = jnp.broadcast_to(inverse1, inverse_ref.shape)
    first = unit1 * vec(3) + vec(4)
    first_b = first.astype(BF16)
    first_ref[...] = arrange(first_b, to_a_ref[...])
    ctx_out_ref[...] = arrange(ctx_ref[...], to_b_ref[...])

    @pl.when(step == 0)
    def _():
        for copy in copies():
            copy.wait()

    branch = None
    for c in range(CHUNKS):
        cols = slice(c * D, (c + 1) * D)
        hidden = dot(first_b, w1_refs[c][...]) + vec(5 + c)
        phi, bell = normal_parts(hidden)
        active = (hidden * phi).astype(BF16)
        act_ref[:, cols] = active
        slope_ref[:, cols] = phi + hidden * bell * 0.3989422804014327
        part = dot(active, w2_ref[cols, :])
        branch = part if branch is None else branch + part
    unit2, inverse2 = norm_forward(first + (branch + vec(9)))
    place = lax.broadcasted_iota(jnp.int32, (rows, 1), 0) + step * rows
    keep = (place < len_ref[0]).astype(F32)
    mixed_ref[...] = ((unit2 * vec(10) + vec(11)) * keep).astype(BF16)
    dz = cot_ref[...].astype(F32) * keep
    dres2 = norm_back(dz, vec(10), unit2, inverse2)
    dres_ref[...] = dres2
    dbranch = dres2.astype(BF16)
    dbranch_ref[...] = dbranch
    sum_ref[9:10, :] += column_sum(dbranch)
    sum_ref[10:11, :] += column_sum(dz * unit2)
    sum_ref[11:12, :] += column_sum(dz)
    for c in range(CHUNKS):
        cols = slice(c * D, (c + 1) * D)
        dhidden = (dot_nt(dbranch, w2_ref[cols, :]) * slope_ref[:, cols]).astype(BF16)
        dhidden_ref[:, cols] = dhidden
        sum_ref[5 + c : 6 + c, :] += column_sum(dhidden)


def feed(lengths, x, ctx, cot, attn_in, vec, to_a, to_b, places, parts, pieces):
    seq = x.shape[0]
    rows = min(256, seq)

    def row(width):
        return pl.BlockSpec((rows, width), lambda i, *_: (i, 0))

    def fixed(shape, column=0):
        return pl.BlockSpec(shape, lambda i, *_: (0, column), pipeline_mode=pl.Buffered(1))

    outs = ((D, BF16), (D, BF16), (D, BF16), (FF, BF16), (D, BF16), (FF, BF16), (D, F32), (D, F32), (128, F32))
    return pl.pallas_call(
        partial(feed_kernel, pieces),
        grid_spec=pltpu.PrefetchScalarGridSpec(
            num_scalar_prefetch=2,
            grid=(seq // rows,),
            in_specs=[row(D), row(D), row(D)]
            + [fixed((D, D), c) for c in range(1 + CHUNKS)]
            + [fixed((12, D)), fixed((D, D)), fixed((D, D))]
            + untouched(parts),
            out_specs=[row(width) for width, _ in outs]
            + [pl.BlockSpec((12, D), lambda i, *_: (0, 0))],
            scratch_shapes=[
                pltpu.VMEM((rows, FF), F32),
                pltpu.VMEM((FF, D), BF16),
                pltpu.SemaphoreType.DMA((sum(count for _, count, _ in pieces),)),
            ],
        ),
        out_shape=[jax.ShapeDtypeStruct((seq, width), kind) for width, kind in outs]
        + [jax.ShapeDtypeStruct((12, D), F32)],
        compiler_params=pltpu.CompilerParams(vmem_limit_bytes=VMEM),
        cost_estimate=cost(28),
        name="feed",
    )(lengths, places, x, ctx, cot, *(attn_in,) * (1 + CHUNKS), vec, to_a, to_b, *parts)


def out_grad_kernel(blocks, where_ref, act_ref, grad_ref, out_ref, held_ref, sems):
    step, slot = pl.program_id(0), lax.rem(pl.program_id(0), 2)
    size = held_ref.shape[1] // blocks

    def copies(step, slot):
        made = []
        for i in range(blocks):
            place = pl.multiple_of(where_ref[step * blocks + i] * size, size)
            source = held_ref.at[slot, pl.ds(i * size, size), :]
            target = out_ref.at[pl.ds(place, size), :]
            made.append(pltpu.make_async_copy(source, target, sems.at[slot, i]))
        return made

    @pl.when(step >= 2)
    def _():
        for copy in copies(step - 2, slot):
            copy.wait()

    held_ref[slot] = dot_tn(act_ref[...], grad_ref[...]).astype(BF16)
    for copy in copies(step, slot):
        copy.start()

    @pl.when(step == CHUNKS - 1)
    def _():
        for copy in copies(step - 1, 1 - slot) + copies(step, slot):
            copy.wait()


def out_grad(act, grad, where):
    seq, blocks = act.shape[0], where.shape[0] // CHUNKS
    return pl.pallas_call(
        partial(out_grad_kernel, blocks),
        grid_spec=pltpu.PrefetchScalarGridSpec(
            num_scalar_prefetch=1,
            grid=(CHUNKS,),
            in_specs=[
                pl.BlockSpec((seq, D), lambda i, _: (0, i)),
                pl.BlockSpec((seq, D), lambda i, _: (0, 0), pipeline_mode=pl.Buffered(1)),
            ],
            out_specs=pl.BlockSpec(memory_space=pl.ANY),
            scratch_shapes=[
                pltpu.VMEM((2, D, D), BF16),
                pltpu.SemaphoreType.DMA((2, blocks)),
            ],
        ),
        out_shape=jax.ShapeDtypeStruct((FF, D), BF16),
        compiler_params=pltpu.CompilerParams(vmem_limit_bytes=VMEM),
        cost_estimate=cost(8),
        name="out_grad",
    )(where, act, grad)


def feed_back_kernel(
    dhidden_ref,
    dres_ref,
    unit_ref,
    inverse_ref,
    wo_ref,
    w1a_ref,
    w1b_ref,
    w1c_ref,
    w1d_ref,
    vec_ref,
    dres1_ref,
    dattend_ref,
    dctx_ref,
    sum_ref,
):
    @pl.when(pl.program_id(0) == 0)
    def _():
        sum_ref[...] = jnp.zeros_like(sum_ref)

    dfirst = dres_ref[...]
    for c, w1_ref in enumerate((w1a_ref, w1b_ref, w1c_ref, w1d_ref)):
        dfirst = dfirst + dot_nt(dhidden_ref[:, c * D : (c + 1) * D], w1_ref[...])
    unit = unit_ref[...]
    dres1 = norm_back(dfirst, vec_ref[3:4, :], unit, inverse_ref[:, 0:1])
    dres1_ref[...] = dres1
    dattend = dres1.astype(BF16)
    dattend_ref[...] = dattend
    dctx_ref[...] = dot_nt(dattend, wo_ref[...]).astype(BF16)
    sum_ref[2:3, :] += column_sum(dattend)
    sum_ref[3:4, :] += column_sum(dfirst * unit)
    sum_ref[4:5, :] += column_sum(dfirst)


def feed_back(dhidden, dres2, unit, inverse, attn_in, vec, waits=()):
    seq = dhidden.shape[0]
    rows = min(256, seq)

    def row(width):
        return pl.BlockSpec((rows, width), lambda i: (i, 0))

    def fixed(shape, column=0):
        return pl.BlockSpec(shape, lambda i: (0, column), pipeline_mode=pl.Buffered(1))

    return pl.pallas_call(
        after(feed_back_kernel, 10, len(waits)),
        grid=(seq // rows,),
        in_specs=[row(FF), row(D), row(D), row(128)]
        + [fixed((D, D), c) for c in range(1 + CHUNKS)]
        + [fixed((12, D))]
        + untouched(waits),
        out_specs=[row(D), row(D), row(D), pl.BlockSpec((8, D), lambda i: (0, 0))],
        out_shape=[
            jax.ShapeDtypeStruct((seq, D), F32),
            jax.ShapeDtypeStruct((seq, D), BF16),
            jax.ShapeDtypeStruct((seq, D), BF16),
            jax.ShapeDtypeStruct((8, D), F32),
        ],
        compiler_params=pltpu.CompilerParams(vmem_limit_bytes=VMEM),
        cost_estimate=cost(14),
        name="feed_back",
    )(dhidden, dres2, unit, inverse, *(attn_in,) * (1 + CHUNKS), vec, *waits)


def swap(value, bit, n):
    return lax.ppermute(value, "dp", [(i, i ^ (1 << bit)) for i in range(n)])


def sum_all(value, n):
    for bit in range(n.bit_length() - 1):
        value = value + swap(value, bit, n)
    return value


def own_bit(bit):
    return (lax.axis_index("dp") >> bit) & 1


def phase(*values):
    return lax.optimization_barrier(values)


class Order:
    def __init__(self, bits):
        self.bits, self.n = bits, 2 ** len(bits)

    def mask(self, place):
        return sum(((place >> k) & 1) << bit for k, bit in enumerate(self.bits))

    def matrix(self):
        rows = D // self.n
        place = jnp.arange(D, dtype=jnp.int32)
        block = self.mask(place // rows) ^ lax.axis_index("dp")
        source = block * rows + place % rows
        return (place[:, None] == source[None, :]).astype(BF16)

    def where(self):
        other = jnp.arange(self.n, dtype=jnp.int32) ^ lax.axis_index("dp")
        return sum(((other >> bit) & 1) << k for k, bit in enumerate(self.bits))

    def places(self, count):
        return self.mask(jnp.arange(count, dtype=jnp.int32)) ^ lax.axis_index("dp")


class Gather:
    def __init__(self, shard, n):
        self.value, self.n = shard, n

    def step(self, bit):
        self.value = jnp.concatenate([self.value, swap(self.value, bit, self.n)], axis=0)

    def cut(self, start, stop):
        return Gather(self.value[:, start:stop], self.n)


class Scatter:
    def __init__(self, value, n):
        self.terms, self.n = [value], n

    def step(self, bit):
        half = self.terms[0].shape[0] // 2
        away = self.total([t[half:] for t in self.terms]).astype(BF16)
        self.terms = [t[:half] for t in self.terms] + [swap(away, bit, self.n)]

    def total(self, parts=None):
        parts = self.terms if parts is None else parts
        result = parts[0].astype(F32)
        for part in parts[1:]:
            result = result + part.astype(F32)
        return result

    def join(self, other):
        self.terms = [jnp.concatenate([self.total(), other.total()], axis=1)]
        return self


def adapt(weight, grad, moment, square, decay):
    new_moment = 0.9 * moment + 0.1 * grad
    new_square = 0.999 * square + 0.001 * grad * grad
    update = new_moment / (1.0 - 0.9**STEP) / (jnp.sqrt(new_square / (1.0 - 0.999**STEP)) + 1e-06)
    return (new_moment, new_square, update + decay * weight)


def lane_sums(value):
    columns = jnp.sum(value * value, axis=0, keepdims=True)
    result = columns[:, :128]
    for start in range(128, value.shape[1], 128):
        result = result + columns[:, start : start + 128]
    return result


def adapt_kernel(first, *refs):
    before_ref, sums_ref = refs[8], refs[15]
    sums = before_ref[...]
    row = lax.broadcasted_iota(jnp.int32, sums.shape, 0)
    for i in range(2):
        weight_ref, grad_ref, moment_ref, square_ref = refs[i * 4 : i * 4 + 4]
        outs = refs[9 + i * 3 : 12 + i * 3]
        weight = weight_ref[...]
        values = adapt(weight, grad_ref[...], moment_ref[...], square_ref[...], 0.01)
        for out, value in zip(outs, values):
            out[...] = value
        sums = jnp.where(row == first + i, lane_sums(weight), sums)
        sums = jnp.where(row == 4 + first + i, lane_sums(values[2]), sums)
    sums_ref[...] = sums


def adapt_two(first, before, *operands):
    shapes = [jax.ShapeDtypeStruct(operands[i * 4].shape, F32) for i in (0, 0, 0, 1, 1, 1)]
    return pl.pallas_call(
        partial(adapt_kernel, first),
        out_shape=shapes + [jax.ShapeDtypeStruct((8, 128), F32)],
        compiler_params=pltpu.CompilerParams(vmem_limit_bytes=VMEM),
        cost_estimate=cost(2),
        name="adapt",
    )(*operands, before)


def renew_kernel(sums_ref, *refs):
    norms = jnp.sqrt(jnp.sum(sums_ref[...], axis=1, keepdims=True))
    refs[12][...] = jnp.broadcast_to(norms, (8, 128))
    for i in range(4):
        rate = 0.25 * (norms[i : i + 1] / norms[4 + i : 5 + i])
        refs[8 + i][...] = refs[i][...] - rate * refs[4 + i][...]


def renew(sums, weights, updates):
    return pl.pallas_call(
        renew_kernel,
        out_shape=[jax.ShapeDtypeStruct(weight.shape, F32) for weight in weights]
        + [jax.ShapeDtypeStruct((8, 128), F32)],
        compiler_params=pltpu.CompilerParams(vmem_limit_bytes=VMEM),
        cost_estimate=cost(2),
        name="renew",
    )(sums, *weights, *updates)


def body(
    n,
    frames,
    cotangent,
    lengths,
    w_qkv,
    w_attn,
    w_in,
    w_out,
    vectors,
    moment_qkv,
    moment_attn,
    moment_in,
    moment_out,
    moment_vec,
    square_qkv,
    square_attn,
    square_in,
    square_out,
    square_vec,
):
    rows_d, rows_f, width = w_qkv.shape[0], w_out.shape[0], vectors.shape[0]
    core, one, two, *others = range(n.bit_length() - 1)
    far = others[::-1]
    order_a, order_b = Order(far + [two, one, core]), Order(far + [one, two, core])
    x = frames[0]

    half = w_qkv.shape[1] // 2
    tail = jnp.pad(vectors.reshape(rows_d, 12), ((0, 0), (0, 116)))
    low_qkv = jnp.concatenate([w_qkv, tail], axis=1).astype(BF16)
    low_qkv, w_first, w_second, w_third = phase(low_qkv, w_attn, w_in, w_out)
    attn_in = jnp.concatenate([w_first, w_second], axis=1).astype(BF16)
    attn_in = lax.all_gather(attn_in, "dp", axis=0, tiled=True)
    qkv, out = Gather(low_qkv, n), Gather(w_third.astype(BF16), n)
    to_a, to_b = order_a.matrix(), order_b.matrix()
    x_a, x_b = arrange(x, to_a), arrange(x, to_b)
    for bit in far:
        qkv.step(bit)
        qkv.value, x_a, x_b = phase(qkv.value, x_a, x_b)
    left, right = qkv.cut(0, half), qkv.cut(half, 2 * half + 128)
    left.step(two)
    right.step(one)
    left.value, right.value, out.value = phase(left.value, right.value, out.value)
    for bit in far[:1]:
        out.step(bit)
    left.step(one)
    right.step(two)
    left.value, right.value = phase(left.value, right.value)
    left = (left.value, swap(left.value, core, n))
    right = (right.value, swap(right.value, core, n))
    left, right, out.value = phase(left, right, out.value)
    for bit in far[1:]:
        out.step(bit)
    vec_rows = jnp.concatenate([part[:, half:] for part in right], axis=0)
    vec = dot(to_b, vec_rows)[:, :12].reshape(12, D)
    bias_qkv = jnp.concatenate([vec[:1], jnp.zeros((1, D), F32), vec[1:2]], axis=1)

    packed = project(x_a, x_b, left, right, bias_qkv)
    packed, out.value = phase(packed, out.value)
    out_left, out_right = out.cut(0, D // 2), out.cut(D // 2, D)
    out_left.step(two)
    out_right.step(one)
    some = PAIRS // 2
    heads = attend(lengths, packed, 0, some)
    heads, out_left.value, out_right.value, attn_in = phase(
        heads, out_left.value, out_right.value, attn_in
    )
    out_left.step(one)
    out_right.step(two)
    heads = attend(lengths, packed, some, some, heads)
    heads, out_left.value, out_right.value = phase(heads, out_left.value, out_right.value)
    parts = [out_left.value, swap(out_left.value, core, n)]
    parts += [out_right.value, swap(out_right.value, core, n)]
    if rows_f % 16 == 0:
        places = jnp.concatenate([order_a.places(n), order_b.places(n)])
        pieces = tuple((i * n // 2, n // 2, i // 2 * (D // 2)) for i in range(4))
    else:
        sides = []
        for i, order in ((0, order_a), (2, order_b)):
            side = jnp.concatenate(parts[i : i + 2], axis=0).reshape(n, rows_f, D // 2)
            sides.append(side[jnp.argsort(order.places(n))].reshape(FF, D // 2))
        parts = [jnp.concatenate(sides, axis=1)]
        places, pieces = jnp.zeros((1,), jnp.int32), ((0, 1, 0),)
    ctx, ctxt, lse = heads

    mixed, first, ctx_b, act, dbranch, dhidden, dres2, unit, inverse, sums2 = feed(
        lengths, x, ctx, cotangent[0], attn_in, vec, to_a, to_b, places, parts, pieces
    )
    if rows_f % 16 == 0:
        grad_out = out_grad(act, dbranch, order_b.where())
    else:
        grad_out = dot_tn(act, dbranch).astype(BF16).reshape(n, rows_f, D)
        grad_out = grad_out[order_b.places(n)].reshape(FF, D)
    dhidden, grad_out = phase(dhidden, grad_out)
    sum_out = Scatter(grad_out, n)
    sum_out.step(core)
    grad_in = dot_tn(first, dhidden).astype(BF16)
    dhidden, grad_in = phase(dhidden, grad_in)
    sum_in = Scatter(grad_in, n)
    sum_in.step(core)
    dres1, dattend, dctx, sums1 = feed_back(dhidden, dres2, unit, inverse, attn_in, vec)

    sum_in.terms[-1], sum_out.terms[-1], dattend, dctx = phase(
        sum_in.terms[-1], sum_out.terms[-1], dattend, dctx
    )
    sum_in.step(one)
    sum_out.step(two)
    grad_attn = dot_tn(ctx_b, dattend).astype(BF16)
    some = 2 * PAIRS // 3
    dqkv, bias_a = attend_back(lengths, packed, dctx, ctxt, lse, 0, some, None, (grad_attn,))
    sum_in.terms[-1], sum_out.terms[-1], dqkv = phase(
        sum_in.terms[-1], sum_out.terms[-1], dqkv
    )
    sum_in.step(two)
    sum_out.step(one)
    dqkv, bias_b = attend_back(lengths, packed, dctx, ctxt, lse, some, PAIRS - some, dqkv)
    sum_in.terms[-1], sum_out.terms[-1], dqkv, bias_b = phase(
        sum_in.terms[-1], sum_out.terms[-1], dqkv, bias_b
    )
    sum_in.step(others[0])
    sum_out.step(others[0])
    late_a = Scatter(
        jnp.concatenate([dot_tn(x_a, dqkv[i]).astype(BF16) for i in range(2)], axis=1), n
    )
    late_b = Scatter(
        jnp.concatenate([dot_tn(x_b, dqkv[2]).astype(BF16), grad_attn], axis=1), n
    )
    bias_sums = jnp.concatenate([bias_a, bias_b], axis=0)
    grad_vec = jnp.concatenate(
        [
            bias_sums[:, 0].reshape(1, D),
            bias_sums[:, 1].reshape(1, D),
            sums1[2:5],
            sums2[5:],
        ]
    ).reshape(-1, 128)
    late_a.terms, late_b.terms, sum_in.terms[-1], sum_out.terms[-1] = phase(
        late_a.terms, late_b.terms, sum_in.terms[-1], sum_out.terms[-1]
    )
    for bit in others[1:]:
        sum_in.step(bit)
        sum_out.step(bit)
    share_in, share_out = sum_in.total(), sum_out.total()
    for bits in ((core, core), (one, two), (two, one)):
        late_a.step(bits[0])
        late_b.step(bits[1])
        late_a.terms[-1], late_b.terms[-1] = phase(late_a.terms[-1], late_b.terms[-1])
    late = late_a.join(late_b)
    for bit in others:
        late.step(bit)
    share_late = late.total()
    full_qkv = jnp.concatenate(
        [
            arrange(to_a, jnp.concatenate(left, axis=0)),
            arrange(to_b, jnp.concatenate([part[:, :half] for part in right], axis=0)),
        ],
        axis=1,
    )
    input_grad = dres1
    for i in range(3):
        input_grad = input_grad + dot_nt(dqkv[i], full_qkv[:, i * D : (i + 1) * D])

    next_in = adapt_two(
        2,
        jnp.zeros((8, 128), F32),
        *(w_in, share_in, moment_in, square_in),
        *(w_out, share_out, moment_out, square_out),
    )
    next_attn = adapt_two(
        0,
        next_in[6],
        *(w_qkv, share_late[:, : 3 * D], moment_qkv, square_qkv),
        *(w_attn, share_late[:, 3 * D :], moment_attn, square_attn),
    )
    sums = sum_all(jnp.concatenate([next_attn[6], grad_vec], axis=0), n)
    place = lax.axis_index("dp") * width
    share_vec = lax.dynamic_slice_in_dim(sums[8:].reshape(-1), place, width, 0)
    updates = (next_attn[2], next_attn[5], next_in[2], next_in[5])
    *new_weights, norms = renew(sums[:8], (w_qkv, w_attn, w_in, w_out), updates)
    vec_moment, vec_square, vec_update = adapt(vectors, share_vec, moment_vec, square_vec, 0.0)
    return (
        mixed[None],
        input_grad[None],
        *new_weights,
        vectors - 0.4 * vec_update,
        *(next_attn[0], next_attn[3], next_in[0], next_in[3], vec_moment),
        *(next_attn[1], next_attn[4], next_in[1], next_in[4], vec_square),
        norms[:, 0],
    )


def solution(mesh):
    clips, matrix, vector = P("dp", None, None), P("dp", None), P("dp")
    parameters = (matrix,) * 4 + (vector,)
    return jax.shard_map(
        partial(body, mesh.shape["dp"]),
        mesh=mesh,
        in_specs=(clips, clips, vector) + parameters * 3,
        out_specs=(clips, clips) + parameters * 3 + (P(),),
        check_vma=False,
    )
```

time: 1040 us -> 378 us (0.36)
  waiting for transfers between devices: 468 us -> 87.1 us
  matrix products: 286 us -> 33.9 us
  Pallas kernels: 0 us -> 139 us
  blocking collectives: 83 us -> 0 us
  other arithmetic: 109 us -> 37.2 us
  starting transfers between devices: 0.21 us -> 41.2 us
  local copies, waits for them, and re-layouts: 54.5 us -> 18.5 us
  loops' own time: 11.3 us -> 0 us
    psum x1 -> x0, waiting for transfers between devices: 417 us -> none  [body(): lax.psum((locals_all[0], locals_all[1], locals_all[2], locals_all[3], loc...]
    dot_general x26 -> x13, matrix products: 286 us -> 33.9 us  [the longest x5 16.7 us: dot_tn(): lax.dot_general(a, b, (((0,), (0,)), ((), ())), preferred_element_type=F32)]
    pallas_call x0 -> x11, Pallas kernels: none -> 139 us  [the longest x2 37.9 us: attend_back(): pl.pallas_call(after(partial(attend_back_kernel, min(512, seq)), 7, len(e...]
    ppermute x0 -> x39, waiting for transfers between devices: none -> 87.1 us  [swap(): return lax.ppermute(value, 'dp', [(i, i ^ 1 << bit) for i in range(n)])]
    all_gather x4 -> x1, waiting for transfers between devices: 50.4 us -> 0.02 us  [body(): attn_in = lax.all_gather(attn_in, 'dp', axis=0, tiled=True)]
    reduce_sum x13 -> x0, other arithmetic: 44.6 us -> none  [the longest x2 23 us: attend(): total = jnp.sum(expo, axis=-1, keepdims=True)]
    unnamed x1 -> x0, blocking collectives: 42.4 us -> none
    ppermute x0 -> x39, starting transfers between devices: none -> 41.2 us  [swap(): return lax.ppermute(value, 'dp', [(i, i ^ 1 << bit) for i in range(n)])]
  transfers between devices with their start and end apart: 5 -> 40, of which waited for: 4 -> 22; matrix products, arithmetic and copies ran while one was open for 15% -> 13% of each run, Pallas kernels for 0% -> 24%
where the time goes in v2:
time: 378 us; the launch traced here: 373 us
  Pallas kernels  139 us (37%)
  waiting for transfers between devices  87.1 us (23%)
  starting transfers between devices  41.2 us (11%)
  other arithmetic  37.2 us (10%)
  matrix products  33.9 us (9%)
  local copies, waits for them, and re-layouts  18.5 us (5%)
  between operations  15.9 us (4%)
    ppermute x39, waiting for transfers between devices, swap(): return lax.ppermute(value, 'dp', [(i, i ^ 1 << bit) for i in range(n)])  87.1 us
    ppermute x39, starting transfers between devices, swap(): return lax.ppermute(value, 'dp', [(i, i ^ 1 << bit) for i in range(n)])  41.2 us
    pallas_call x2, Pallas kernels, attend_back(): pl.pallas_call(after(partial(attend_back_kernel, min(512, seq)), 7, len(e...  37.9 us
    pallas_call x1, Pallas kernels, feed(): pl.pallas_call(partial(feed_kernel, pieces), grid_spec=pltpu.PrefetchScal...  34.4 us
    pallas_call x2, Pallas kernels, attend(): pl.pallas_call(after(attend_kernel, 4, len(extra)), grid_spec=pltpu.Prefe...  24.6 us
    convert_element_type x13, other arithmetic, step(): away = self.total([t[half:] for t in self.terms]).astype(BF16)  19.6 us
    dot_general x5, matrix products, dot_tn(): lax.dot_general(a, b, (((0,), (0,)), ((), ())), preferred_element_type=F32)  16.7 us
    pallas_call x1, Pallas kernels, feed_back(): pl.pallas_call(after(feed_back_kernel, 10, len(waits)), grid=(seq // rows...  15.3 us
  transfers between devices with their start and end apart: 40, of which 22 were waited for; matrix products, arithmetic and copies ran while one was open for 13% of the time, Pallas kernels for 24%

profile of v2, /device:TPU:0, one launch (start us, length us, event | category | flops | bytes accessed | tf_op | source)
XLA Modules:
  0.0 372.6 jit_solution(6990509857633641629)
XLA Ops:
  11.6 4.1 %collective-permute-start = (bf16[24,2432]{1,0:T(8,128)(2,1)S(1)}, bf16[24,2432]{1,0:T(8,128)(2,1)S(1)}, u32[]{:S(2)}, u32[]{:S(2)}) collective-permute-start(bf16[24,2432]{1,0:T(8,128)(2,1)S(1)} %fusion.63), channel_id=1, source_target_pairs={{0,16},{1,17},{2,18},{3,19},{4,20},{5,21},{6,22},{7,23},{8,24},{9,... | collective-permute-start | bytes 350216 | tf_op jit(solution)/shard_map/ppermute | solution.py:533
  15.7 4.2 %fusion.35.xa_ref = bf16[1024,768]{1,0:T(8,128)(2,1)} fusion(s32[768]{0:T(1024)S(1)} %get-tuple-element.230, bf16[1,1024,768]{2,1,0:T(8,128)(2,1)} %param.18), kind=kOutput, calls=%fused_computation.40 | convolution fusion | flops 1209335808 | bytes 3148800 | tf_op jit(solution)/shard_map/dot_general | solution.py:25
  19.9 2.6 fusion.34.xb_ref
  24.2 7.9 %collective-permute-done.1 = bf16[48,2432]{1,0:T(8,128)(2,1)S(1)} collective-permute-done((bf16[48,2432]{1,0:T(8,128)(2,1)S(1)}, bf16[48,2432]{1,0:T(8,128)(2,1)S(1)}, u32[]{:S(2)}, u32[]{:S(2)}) %collective-permute-start.1) | collective-permute-done | bytes 233504 | tf_op jit(solution)/shard_map/ppermute | solution.py:533
  32.1 1.8 collective-permute-start.2
  35.4 3.2 collective-permute-done.2
  38.7 2.0 collective-permute-done.3
  42.9 13.4 %collective-permute-done.4 = bf16[192,1152]{1,0:T(8,128)(2,1)S(1)} collective-permute-done((bf16[192,1152]{1,0:T(8,128)(2,1)S(1)}, bf16[192,1152]{1,0:T(8,128)(2,1)S(1)}, u32[]{:S(2)}, u32[]{:S(2)}) %collective-permute-start.4) | collective-permute-done | bytes 442400 | tf_op jit(solution)/shard_map/ppermute | solution.py:533
  57.0 1.8 collective-permute-start.8
  58.8 8.3 %collective-permute-done.8 = bf16[96,768]{1,0:T(8,128)(2,1)S(1)} collective-permute-done((bf16[96,768]{1,0:T(8,128)(2,1)S(1)}, bf16[96,768]{1,0:T(8,128)(2,1)S(1)}, u32[]{:S(2)}, u32[]{:S(2)}) %collective-permute-start.8) | collective-permute-done | bytes 147488 | tf_op jit(solution)/shard_map/ppermute | solution.py:533
  69.9 1.7 collective-permute-start.9
  72.2 8.6 %project.1.refs_1_.refs_2_.refs_3_ = bf16[1024,2304]{1,0:T(8,128)(2,1)} custom-call(bf16[1024,768]{1,0:T(8,128)(2,1)} %fusion.35.xa_ref, bf16[1024,768]{1,0:T(8,128)(2,1)} %fusion.34.xb_ref, bf16[384,1152]{1,0:T(8,128)(2,1)} %copy-done.9, bf16[384,1152]{1,0:T(8,128)(2,1)} %copy-done.19, bf16[384,1280]{1,0:T(8,128)(2,1)} %copy-done.2, ...), custom_call_target="tpu_custom_call" | custom-call | flops 250000000 | tf_op jit(solution)/shard_map/project/pallas_call | solution.py:59
  80.8 8.3 %collective-permute-done.9 = bf16[192,768]{1,0:T(8,128)(2,1)S(1)} collective-permute-done((bf16[192,768]{1,0:T(8,128)(2,1)S(1)}, bf16[192,768]{1,0:T(8,128)(2,1)S(1)}, u32[]{:S(2)}, u32[]{:S(2)}) %collective-permute-start.9) | collective-permute-done | bytes 294944 | tf_op jit(solution)/shard_map/ppermute | solution.py:533
  92.3 12.3 %attend.2 = (bf16[1024,768]{1,0:T(8,128)(2,1)}, f32[768,1024]{1,0:T(8,128)}, f32[6,2,1024]{2,1,0:T(2,128)}) custom-call(s32[1]{0:T(128)S(6)} %copy.70.refs_0_.len_ref, bf16[1024,2304]{1,0:T(8,128)(2,1)} %project.1.refs_1_.refs_2_.refs_3_, bf16[1024,2304]{1,0:T(8,128)(2,1)} %project.1.refs_1_.refs_2_.refs_3_, bf16[1024,2304]{1,0:T(8,128)(2,1)} %project.1.refs_1_.refs_2_.refs_3_), custom_call_target="tpu_custom_call" | custom-call | flops 600000000 | tf_op jit(solution)/shard_map/attend/pallas_call | solution.py:107
  106.6 12.3 %attend.3 = (bf16[1024,768]{1,0:T(8,128)(2,1)}, f32[768,1024]{1,0:T(8,128)}, f32[6,2,1024]{2,1,0:T(2,128)}) custom-call(s32[1]{0:T(128)S(6)} %copy.70.refs_0_.len_ref, bf16[1024,2304]{1,0:T(8,128)(2,1)} %project.1.refs_1_.refs_2_.refs_3_, ...), custom_call_target="tpu_custom_call", output_to_operand_aliasing={{0}: (4, {}), {1}: (5, {}), {2}: (6, {})} | custom-call | flops 600000000 | tf_op jit(solution)/shard_map/attend/pallas_call | solution.py:107
  125.4 34.4 %feed.1 = (bf16[1024,768]{1,0:T(8,128)(2,1)}, bf16[1024,768]{1,0:T(8,128)(2,1)}, bf16[1024,768]{1,0:T(8,128)(2,1)}, bf16[1024,3072]{1,0:T(8,128)(2,1)}, bf16[102...) custom-call(s32[1]{0:T(128)S(6)} %copy.70.refs_0_.len_ref, ...), custom_call_target="tpu_custom_call" | custom-call | flops 1400000000 | tf_op jit(solution)/shard_map/feed/pallas_call | solution.py:391
  159.9 10.0 %out_grad.1 = bf16[3072,768]{1,0:T(8,128)(2,1)} custom-call(s32[32]{0:T(128)} %shift-left_add_fusion.1.where_ref, bf16[1024,3072]{1,0:T(8,128)(2,1)} %get-tuple-element.158.act_ref, bf16[1024,768]{1,0:T(8,128)(2,1)} %get-tuple-element.159.grad_ref), custom_call_target="tpu_custom_call" | custom-call | flops 400000000 | tf_op jit(solution)/shard_map/out_grad/pallas_call | solution.py:446
  169.9 3.4 slice.373
  173.3 8.1 %convolution_convert_fusion = bf16[768,3072]{1,0:T(8,128)(2,1)S(1)} fusion(bf16[1024,768]{1,0:T(8,128)(2,1)S(1)} %copy-done.38, bf16[1024,3072]{1,0:T(8,128)(2,1)} %get-tuple-element.162.refs_0_), kind=kOutput, calls=%fused_computation | convolution fusion | flops 4834197504 | bytes 12582912 | tf_op jit(solution)/shard_map/dot_general | solution.py:33
  184.7 15.3 %feed_back.1 = (f32[1024,768]{1,0:T(8,128)}, bf16[1024,768]{1,0:T(8,128)(2,1)}, bf16[1024,768]{1,0:T(8,128)(2,1)}, f32[8,768]{1,0:T(8,128)}) custom-call(bf16[1024,3072]{1,0:T(8,128)(2,1)} %get-tuple-element.162.refs_0_, f32[1024,768]{1,0:T(8,128)} %get-tuple-element.163.refs_1_, f32[1024,768]{1,0:T(8,128)} %get-tuple-element.164.refs_2_, ...), custom_call_target="tpu_custom_call" | custom-call | flops 700000000 | tf_op jit(solution)/shard_map/feed_back/pallas_call | solution.py:512
  200.1 2.9 add_convert_fusion.1
  203.0 2.7 add_convert_fusion
  208.2 2.5 convolution_convert_fusion.3.refs_7_
  210.7 24.4 %attend_back.2 = (bf16[3,1024,768]{2,1,0:T(8,128)(2,1)}, f32[4,2,128]{2,1,0:T(2,128)}) custom-call(s32[1]{0:T(128)S(6)} %copy.70.refs_0_.len_ref, bf16[1024,2304]{1,0:T(8,128)(2,1)} %project.1.refs_1_.refs_2_.refs_3_, bf16[1024,2304]{1,0:T(8,128)(2,1)} %project.1.refs_1_.refs_2_.refs_3_, bf16[1024,2304]{1,0:T(8,128)(2,1)} %project.1.refs_1_.refs_2_.refs_3_, ...), custom_call_target="tpu_custom_call" | custom-call | flops 1200000000 | tf_op jit(solution)/shard_map/attend_back/pallas_call | solution.py:199
  235.1 2.5 add_convert_fusion.5
  237.6 2.3 add_convert_fusion.4
  241.4 13.5 %attend_back.3 = (bf16[3,1024,768]{2,1,0:T(8,128)(2,1)}, f32[2,2,128]{2,1,0:T(2,128)}) custom-call(s32[1]{0:T(128)S(6)} %copy.70.refs_0_.len_ref, bf16[1024,2304]{1,0:T(8,128)(2,1)} %project.1.refs_1_.refs_2_.refs_3_, bf16[1024,2304]{1,0:T(8,128)(2,1)} %project.1.refs_1_.refs_2_.refs_3_, ...), custom_call_target="tpu_custom_call", output_to_operand_aliasing={{0}: (7, {})} | custom-call | flops 600000000 | tf_op jit(solution)/shard_map/attend_back/pallas_call | solution.py:199
  255.3 3.1 fusion.31
  264.6 2.0 collective-permute-start.22
  266.8 7.7 %collective-permute-done.23 = bf16[192,768]{1,0:T(8,128)(2,1)S(1)} collective-permute-done((bf16[192,768]{1,0:T(8,128)(2,1)S(1)}, bf16[192,768]{1,0:T(8,128)(2,1)S(1)}, u32[]{:S(2)}, u32[]{:S(2)}) %collective-permute-start.23) | collective-permute-done | bytes 294944 | tf_op jit(solution)/shard_map/ppermute | solution.py:533
  274.5 4.2 %collective-permute-done.22 = bf16[48,3072]{1,0:T(8,128)(2,1)S(1)} collective-permute-done((bf16[48,3072]{1,0:T(8,128)(2,1)S(1)}, bf16[48,3072]{1,0:T(8,128)(2,1)S(1)}, u32[]{:S(2)}, u32[]{:S(2)}) %collective-permute-start.22) | collective-permute-done | bytes 294944 | tf_op jit(solution)/shard_map/ppermute | solution.py:533
  279.9 2.3 collective-permute-done.25
  282.2 1.7 collective-permute-done.24
  292.1 9.6 %collective-permute-done.27 = bf16[192,1536]{1,0:T(8,128)(2,1)} collective-permute-done((bf16[192,1536]{1,0:T(8,128)(2,1)}, bf16[192,1536]{1,0:T(8,128)(2,1)}, u32[]{:S(2)}, u32[]{:S(2)}) %collective-permute-start.27) | collective-permute-done | bytes 589856 | tf_op jit(solution)/shard_map/ppermute | solution.py:533
  309.2 2.1 collective-permute-start.33
  316.8 7.2 %collective-permute-done.32 = bf16[24,3072]{1,0:T(8,128)(2,1)S(1)} collective-permute-done((bf16[24,3072]{1,0:T(8,128)(2,1)S(1)}, bf16[24,3072]{1,0:T(8,128)(2,1)S(1)}, u32[]{:S(2)}, u32[]{:S(2)}) %collective-permute-start.32) | collective-permute-done | bytes 147488 | tf_op jit(solution)/shard_map/ppermute | solution.py:533
  323.9 1.9 convert_add_fusion.3.refs_1_
  325.8 2.4 collective-permute-done.30
  328.2 2.0 collective-permute-start.31
  330.2 1.9 convert_add_fusion.2.refs_5_
  332.7 3.0 adapt.2
  338.1 2.4 adapt.3
  341.3 1.8 convolution_convert_fusion.2
  344.2 2.1 convolution_convert_fusion.1
  348.9 2.4 collective-permute-done.36
  355.3 1.7 collective-permute-start.38
  357.0 3.1 add_bitcast_fusion
  360.8 2.6 renew.1
  (232 shorter events, 75.3 us)
Async XLA Ops:
  7.2 97.6 %all-gather.2.cloned.1.call-start = ((), (), s32[]{:S(2)}) async-start(), calls=%async_computation | async-start | bytes 6082560 | tf_op jit(solution)/shard_map/all_gather | solution.py:697
  11.6 10.9 %collective-permute-start = (bf16[24,2432]{1,0:T(8,128)(2,1)S(1)}, bf16[24,2432]{1,0:T(8,128)(2,1)S(1)}, u32[]{:S(2)}, u32[]{:S(2)}) collective-permute-start(bf16[24,2432]{1,0:T(8,128)(2,1)S(1)} %fusion.63), channel_id=1, source_target_pairs={{0,16},{1,17},{2,18},{3,19},{4,20},{5,21},{6,22},{7,23},{8,24},{9,... | collective-permute-start | bytes 350216 | tf_op jit(solution)/shard_map/ppermute | solution.py:533
  22.5 9.5 %collective-permute-start.1 = (bf16[48,2432]{1,0:T(8,128)(2,1)S(1)}, bf16[48,2432]{1,0:T(8,128)(2,1)S(1)}, u32[]{:S(2)}, u32[]{:S(2)}) collective-permute-start(bf16[48,2432]{1,0:T(8,128)(2,1)S(1)} %pad_maximum_fusion.16), channel_id=1, source_target_pairs={{0,8},{1,9},{2,10},{3,11},{4,12},{5,13},{6,14},{7,15},{8,0},{9,1},... | collective-permute-start | bytes 700424 | tf_op jit(solution)/shard_map/ppermute | solution.py:533
  32.1 6.6 %collective-permute-start.2 = (bf16[96,1152]{1,0:T(8,128)(2,1)S(1)}, bf16[96,1152]{1,0:T(8,128)(2,1)S(1)}, u32[]{:S(2)}, u32[]{:S(2)}) collective-permute-start(bf16[96,1152]{1,0:T(8,128)(2,1)S(1)} %slice.360), channel_id=1, source_target_pairs={{0,4},{1,5},{2,6},{3,7},{4,0},{5,1},{6,2},{7,3},{8,12},{9,13},{10,... | collective-permute-start | bytes 663560 | tf_op jit(solution)/shard_map/ppermute | solution.py:533
  33.9 6.9 %collective-permute-start.3 = (bf16[96,1280]{1,0:T(8,128)(2,1)S(1)}, bf16[96,1280]{1,0:T(8,128)(2,1)S(1)}, u32[]{:S(2)}, u32[]{:S(2)}) collective-permute-start(bf16[96,1280]{1,0:T(8,128)(2,1)S(1)} %slice.361), channel_id=1, source_target_pairs={{0,2},{1,3},{2,0},{3,1},{4,6},{5,7},{6,4},{7,5},{8,10},{9,11},{10,... | collective-permute-start | bytes 737288 | tf_op jit(solution)/shard_map/ppermute | solution.py:533
  40.8 15.4 %collective-permute-start.4 = (bf16[192,1152]{1,0:T(8,128)(2,1)S(1)}, bf16[192,1152]{1,0:T(8,128)(2,1)S(1)}, u32[]{:S(2)}, u32[]{:S(2)}) collective-permute-start(bf16[192,1152]{1,0:T(8,128)(2,1)S(1)} %pad_maximum_fusion.13), channel_id=1, source_target_pairs={{0,2},{1,3},{2,0},{3,1},{4,6},{5,7},{6,4},{7,5},{8,10},{9,11},{10,... | collective-permute-start | bytes 1327112 | tf_op jit(solution)/shard_map/ppermute | solution.py:533
  42.3 14.0 %collective-permute-start.5 = (bf16[192,1280]{1,0:T(8,128)(2,1)S(1)}, bf16[192,1280]{1,0:T(8,128)(2,1)S(1)}, u32[]{:S(2)}, u32[]{:S(2)}) collective-permute-start(bf16[192,1280]{1,0:T(8,128)(2,1)S(1)} %pad_maximum_fusion.11), channel_id=1, source_target_pairs={{0,4},{1,5},{2,6},{3,7},{4,0},{5,1},{6,2},{7,3},{8,12},{9,13},{10,... | collective-permute-start | bytes 1474568 | tf_op jit(solution)/shard_map/ppermute | solution.py:533
  56.4 15.8 %copy-start.2 = (bf16[384,1280]{1,0:T(8,128)(2,1)}, bf16[384,1280]{1,0:T(8,128)(2,1)S(1)}, u32[]{:S(2)}) copy-start(bf16[384,1280]{1,0:T(8,128)(2,1)S(1)} %pad_maximum_fusion.6.ra_ref) | copy-start | bytes 2949124
  56.4 10.7 %collective-permute-start.7 = (bf16[384,1280]{1,0:T(8,128)(2,1)S(1)}, bf16[384,1280]{1,0:T(8,128)(2,1)S(1)}, u32[]{:S(2)}, u32[]{:S(2)}) collective-permute-start(bf16[384,1280]{1,0:T(8,128)(2,1)S(1)} %pad_maximum_fusion.6.ra_ref), channel_id=1, source_target_pairs={{0,1},{1,0},{2,3},{3,2},{4,5},{5,4},{6,7},{7,6},{8,9},{9,8},{10,11... | collective-permute-start | bytes 2949128 | tf_op jit(solution)/shard_map/ppermute | solution.py:533
  56.5 10.6 %collective-permute-start.6 = (bf16[384,1152]{1,0:T(8,128)(2,1)S(1)}, bf16[384,1152]{1,0:T(8,128)(2,1)S(1)}, u32[]{:S(2)}, u32[]{:S(2)}) collective-permute-start(bf16[384,1152]{1,0:T(8,128)(2,1)S(1)} %pad_maximum_fusion.7.la_ref), channel_id=1, source_target_pairs={{0,1},{1,0},{2,3},{3,2},{4,5},{5,4},{6,7},{7,6},{8,9},{9,8},{10,11... | collective-permute-start | bytes 2654216 | tf_op jit(solution)/shard_map/ppermute | solution.py:533
  57.0 10.1 %collective-permute-start.8 = (bf16[96,768]{1,0:T(8,128)(2,1)S(1)}, bf16[96,768]{1,0:T(8,128)(2,1)S(1)}, u32[]{:S(2)}, u32[]{:S(2)}) collective-permute-start(bf16[96,768]{1,0:T(8,128)(2,1)S(1)} %convert_element_type.281), channel_id=1, source_target_pairs={{0,16},{1,17},{2,18},{3,19},{4,20},{5,21},{6,22},{7,23},{8,24},{9,... | collective-permute-start | bytes 442376 | tf_op jit(solution)/shard_map/ppermute | solution.py:533
  69.9 19.2 %collective-permute-start.9 = (bf16[192,768]{1,0:T(8,128)(2,1)S(1)}, bf16[192,768]{1,0:T(8,128)(2,1)S(1)}, u32[]{:S(2)}, u32[]{:S(2)}) collective-permute-start(bf16[192,768]{1,0:T(8,128)(2,1)S(1)} %pad_maximum_fusion.15), channel_id=1, source_target_pairs={{0,8},{1,9},{2,10},{3,11},{4,12},{5,13},{6,14},{7,15},{8,0},{9,1},... | collective-permute-start | bytes 884744 | tf_op jit(solution)/shard_map/ppermute | solution.py:533
  89.2 15.4 %collective-permute-start.11 = (bf16[384,384]{1,0:T(8,128)(2,1)S(1)}, bf16[384,384]{1,0:T(8,128)(2,1)S(1)}, u32[]{:S(2)}, u32[]{:S(2)}) collective-permute-start(bf16[384,384]{1,0:T(8,128)(2,1)S(1)} %get-tuple-element.223), channel_id=1, source_target_pairs={{0,2},{1,3},{2,0},{3,1},{4,6},{5,7},{6,4},{7,5},{8,10},{9,11},{10,... | collective-permute-start | bytes 884744 | tf_op jit(solution)/shard_map/ppermute | solution.py:533
  90.6 14.1 %collective-permute-start.10 = (bf16[384,384]{1,0:T(8,128)(2,1)S(1)}, bf16[384,384]{1,0:T(8,128)(2,1)S(1)}, u32[]{:S(2)}, u32[]{:S(2)}) collective-permute-start(bf16[384,384]{1,0:T(8,128)(2,1)S(1)} %get-tuple-element.224), channel_id=1, source_target_pairs={{0,4},{1,5},{2,6},{3,7},{4,0},{5,1},{6,2},{7,3},{8,12},{9,13},{10,... | collective-permute-start | bytes 884744 | tf_op jit(solution)/shard_map/ppermute | solution.py:533
  104.8 14.1 %collective-permute-start.12 = (bf16[768,384]{1,0:T(8,128)(2,1)S(1)}, bf16[768,384]{1,0:T(8,128)(2,1)S(1)}, u32[]{:S(2)}, u32[]{:S(2)}) collective-permute-start(bf16[768,384]{1,0:T(8,128)(2,1)S(1)} %pad_maximum_fusion.9), channel_id=1, source_target_pairs={{0,2},{1,3},{2,0},{3,1},{4,6},{5,7},{6,4},{7,5},{8,10},{9,11},{10,... | collective-permute-start | bytes 1769480 | tf_op jit(solution)/shard_map/ppermute | solution.py:533
  105.4 14.3 %collective-permute-start.13 = (bf16[768,384]{1,0:T(8,128)(2,1)S(1)}, bf16[768,384]{1,0:T(8,128)(2,1)S(1)}, u32[]{:S(2)}, u32[]{:S(2)}) collective-permute-start(bf16[768,384]{1,0:T(8,128)(2,1)S(1)} %pad_maximum_fusion.10), channel_id=1, source_target_pairs={{0,4},{1,5},{2,6},{3,7},{4,0},{5,1},{6,2},{7,3},{8,12},{9,13},{10,... | collective-permute-start | bytes 1769480 | tf_op jit(solution)/shard_map/ppermute | solution.py:533
  119.8 5.7 %collective-permute-start.14 = (bf16[1536,384]{1,0:T(8,128)(2,1)S(1)}, bf16[1536,384]{1,0:T(8,128)(2,1)}, u32[]{:S(2)}, u32[]{:S(2)}) collective-permute-start(bf16[1536,384]{1,0:T(8,128)(2,1)S(1)} %pad_maximum_fusion.4.refs_0_), channel_id=1, source_target_pairs={{0,1},{1,0},{2,3},{3,2},{4,5},{5,4},{6,7},{7,6},{8,9},{9,8},{10,11... | collective-permute-start | bytes 3538952 | tf_op jit(solution)/shard_map/ppermute | solution.py:533
  119.9 5.6 %collective-permute-start.15 = (bf16[1536,384]{1,0:T(8,128)(2,1)S(1)}, bf16[1536,384]{1,0:T(8,128)(2,1)}, u32[]{:S(2)}, u32[]{:S(2)}) collective-permute-start(bf16[1536,384]{1,0:T(8,128)(2,1)S(1)} %pad_maximum_fusion.5.refs_2_), channel_id=1, source_target_pairs={{0,1},{1,0},{2,3},{3,2},{4,5},{5,4},{6,7},{7,6},{8,9},{9,8},{10,11... | collective-permute-start | bytes 3538952 | tf_op jit(solution)/shard_map/ppermute | solution.py:533
  173.2 26.8 %collective-permute-start.17 = (bf16[1536,768]{1,0:T(8,128)(2,1)}, bf16[1536,768]{1,0:T(8,128)(2,1)S(1)}, u32[]{:S(2)}, u32[]{:S(2)}) collective-permute-start(bf16[1536,768]{1,0:T(8,128)(2,1)} %slice.373), channel_id=1, source_target_pairs={{0,1},{1,0},{2,3},{3,2},{4,5},{5,4},{6,7},{7,6},{8,9},{9,8},{10,11... | collective-permute-start | bytes 7077896 | tf_op jit(solution)/shard_map/ppermute | solution.py:533
  184.3 15.8 %collective-permute-start.16 = (bf16[384,3072]{1,0:T(8,128)(2,1)}, bf16[384,3072]{1,0:T(8,128)(2,1)}, u32[]{:S(2)}, u32[]{:S(2)}) collective-permute-start(bf16[384,3072]{1,0:T(8,128)(2,1)} %slice.372), channel_id=1, source_target_pairs={{0,1},{1,0},{2,3},{3,2},{4,5},{5,4},{6,7},{7,6},{8,9},{9,8},{10,11... | collective-permute-start | bytes 7077896 | tf_op jit(solution)/shard_map/ppermute | solution.py:533
  200.1 37.5 %copy-start.13 = (bf16[1536,768]{1,0:T(8,128)(2,1)}, bf16[1536,768]{1,0:T(8,128)(2,1)S(1)}, u32[]{:S(2)}) copy-start(bf16[1536,768]{1,0:T(8,128)(2,1)S(1)} %collective-permute-done.17) | copy-start | bytes 7077892
  205.7 29.4 %collective-permute-start.19 = (bf16[768,768]{1,0:T(8,128)(2,1)}, bf16[768,768]{1,0:T(8,128)(2,1)}, u32[]{:S(2)}, u32[]{:S(2)}) collective-permute-start(bf16[768,768]{1,0:T(8,128)(2,1)} %add_convert_fusion), channel_id=1, source_target_pairs={{0,4},{1,5},{2,6},{3,7},{4,0},{5,1},{6,2},{7,3},{8,12},{9,13},{10,... | collective-permute-start | bytes 3538952 | tf_op jit(solution)/shard_map/ppermute | solution.py:533
  206.9 28.1 %collective-permute-start.18 = (bf16[192,3072]{1,0:T(8,128)(2,1)S(1)}, bf16[192,3072]{1,0:T(8,128)(2,1)}, u32[]{:S(2)}, u32[]{:S(2)}) collective-permute-start(bf16[192,3072]{1,0:T(8,128)(2,1)S(1)} %add_convert_fusion.1), channel_id=1, source_target_pairs={{0,2},{1,3},{2,0},{3,1},{4,6},{5,7},{6,4},{7,5},{8,10},{9,11},{10,... | collective-permute-start | bytes 3538952 | tf_op jit(solution)/shard_map/ppermute | solution.py:533
  239.8 15.4 %copy-start.16 = (bf16[1024,768]{1,0:T(8,128)(2,1)S(1)}, bf16[1024,768]{1,0:T(8,128)(2,1)}, u32[]{:S(2)}) copy-start(bf16[1024,768]{1,0:T(8,128)(2,1)} %fusion.34.xb_ref) | copy-start | bytes 4718596
  239.8 15.1 %collective-permute-start.21 = (bf16[384,768]{1,0:T(8,128)(2,1)}, bf16[384,768]{1,0:T(8,128)(2,1)S(1)}, u32[]{:S(2)}, u32[]{:S(2)}) collective-permute-start(bf16[384,768]{1,0:T(8,128)(2,1)} %add_convert_fusion.4), channel_id=1, source_target_pairs={{0,2},{1,3},{2,0},{3,1},{4,6},{5,7},{6,4},{7,5},{8,10},{9,11},{10,... | collective-permute-start | bytes 1769480 | tf_op jit(solution)/shard_map/ppermute | solution.py:533
  240.7 14.6 %collective-permute-start.20 = (bf16[96,3072]{1,0:T(8,128)(2,1)}, bf16[96,3072]{1,0:T(8,128)(2,1)S(1)}, u32[]{:S(2)}, u32[]{:S(2)}) collective-permute-start(bf16[96,3072]{1,0:T(8,128)(2,1)} %add_convert_fusion.5), channel_id=1, source_target_pairs={{0,4},{1,5},{2,6},{3,7},{4,0},{5,1},{6,2},{7,3},{8,12},{9,13},{10,... | collective-permute-start | bytes 1769480 | tf_op jit(solution)/shard_map/ppermute | solution.py:533
  264.5 10.0 %collective-permute-start.23 = (bf16[192,768]{1,0:T(8,128)(2,1)S(1)}, bf16[192,768]{1,0:T(8,128)(2,1)S(1)}, u32[]{:S(2)}, u32[]{:S(2)}) collective-permute-start(bf16[192,768]{1,0:T(8,128)(2,1)S(1)} %add_convert_fusion.8), channel_id=1, source_target_pairs={{0,8},{1,9},{2,10},{3,11},{4,12},{5,13},{6,14},{7,15},{8,0},{9,1},... | collective-permute-start | bytes 884744 | tf_op jit(solution)/shard_map/ppermute | solution.py:533
  264.6 14.1 %collective-permute-start.22 = (bf16[48,3072]{1,0:T(8,128)(2,1)S(1)}, bf16[48,3072]{1,0:T(8,128)(2,1)S(1)}, u32[]{:S(2)}, u32[]{:S(2)}) collective-permute-start(bf16[48,3072]{1,0:T(8,128)(2,1)S(1)} %add_convert_fusion.9), channel_id=1, source_target_pairs={{0,8},{1,9},{2,10},{3,11},{4,12},{5,13},{6,14},{7,15},{8,0},{9,1},... | collective-permute-start | bytes 884744 | tf_op jit(solution)/shard_map/ppermute | solution.py:533
  266.8 17.2 %copy-start.1 = (bf16[768,1536]{1,0:T(8,128)(2,1)}, bf16[768,1536]{1,0:T(8,128)(2,1)S(1)}, u32[]{:S(2)}) copy-start(bf16[768,1536]{1,0:T(8,128)(2,1)S(1)} %pad_maximum_fusion) | copy-start | bytes 7077892
  279.4 2.8 collective-permute-start.25
  279.4 4.5 %collective-permute-start.24 = (bf16[384,1536]{1,0:T(8,128)(2,1)S(1)}, bf16[384,1536]{1,0:T(8,128)(2,1)S(1)}, u32[]{:S(2)}, u32[]{:S(2)}) collective-permute-start(bf16[384,1536]{1,0:T(8,128)(2,1)S(1)} %slice.400), channel_id=1, source_target_pairs={{0,1},{1,0},{2,3},{3,2},{4,5},{5,4},{6,7},{7,6},{8,9},{9,8},{10,11... | collective-permute-start | bytes 3538952 | tf_op jit(solution)/shard_map/ppermute | solution.py:533
  283.9 18.7 %copy-start.17 = (bf16[384,1536]{1,0:T(8,128)(2,1)}, bf16[384,1536]{1,0:T(8,128)(2,1)S(1)}, u32[]{:S(2)}) copy-start(bf16[384,1536]{1,0:T(8,128)(2,1)S(1)} %collective-permute-done.24) | copy-start | bytes 3538948
  286.0 15.7 %collective-permute-start.27 = (bf16[192,1536]{1,0:T(8,128)(2,1)}, bf16[192,1536]{1,0:T(8,128)(2,1)}, u32[]{:S(2)}, u32[]{:S(2)}) collective-permute-start(bf16[192,1536]{1,0:T(8,128)(2,1)} %add_convert_fusion.2), channel_id=1, source_target_pairs={{0,4},{1,5},{2,6},{3,7},{4,0},{5,1},{6,2},{7,3},{8,12},{9,13},{10,... | collective-permute-start | bytes 1769480 | tf_op jit(solution)/shard_map/ppermute | solution.py:533
  287.2 15.4 %collective-permute-start.26 = (bf16[192,1536]{1,0:T(8,128)(2,1)}, bf16[192,1536]{1,0:T(8,128)(2,1)}, u32[]{:S(2)}, u32[]{:S(2)}) collective-permute-start(bf16[192,1536]{1,0:T(8,128)(2,1)} %add_convert_fusion.3), channel_id=1, source_target_pairs={{0,2},{1,3},{2,0},{3,1},{4,6},{5,7},{6,4},{7,5},{8,10},{9,11},{10,... | collective-permute-start | bytes 1769480 | tf_op jit(solution)/shard_map/ppermute | solution.py:533
  292.1 14.7 %copy-start.28 = (bf16[48,3072]{1,0:T(8,128)(2,1)S(1)}, bf16[48,3072]{1,0:T(8,128)(2,1)}, u32[]{:S(2)}) copy-start(bf16[48,3072]{1,0:T(8,128)(2,1)} %copy-done.27) | copy-start | bytes 884740
  292.1 15.9 %copy-start.22 = (bf16[384,768]{1,0:T(8,128)(2,1)S(1)}, bf16[384,768]{1,0:T(8,128)(2,1)}, u32[]{:S(2)}) copy-start(bf16[384,768]{1,0:T(8,128)(2,1)} %copy-done.21) | copy-start | bytes 1769476
  292.1 15.9 %copy-start.26 = (bf16[192,768]{1,0:T(8,128)(2,1)S(1)}, bf16[192,768]{1,0:T(8,128)(2,1)}, u32[]{:S(2)}) copy-start(bf16[192,768]{1,0:T(8,128)(2,1)} %copy-done.25) | copy-start | bytes 884740
  305.0 8.0 %collective-permute-start.29 = (bf16[96,1536]{1,0:T(8,128)(2,1)S(1)}, bf16[96,1536]{1,0:T(8,128)(2,1)S(1)}, u32[]{:S(2)}, u32[]{:S(2)}) collective-permute-start(bf16[96,1536]{1,0:T(8,128)(2,1)S(1)} %add_convert_fusion.6), channel_id=1, source_target_pairs={{0,2},{1,3},{2,0},{3,1},{4,6},{5,7},{6,4},{7,5},{8,10},{9,11},{10,... | collective-permute-start | bytes 884744 | tf_op jit(solution)/shard_map/ppermute | solution.py:533
  306.3 7.6 %collective-permute-start.28 = (bf16[96,1536]{1,0:T(8,128)(2,1)S(1)}, bf16[96,1536]{1,0:T(8,128)(2,1)S(1)}, u32[]{:S(2)}, u32[]{:S(2)}) collective-permute-start(bf16[96,1536]{1,0:T(8,128)(2,1)S(1)} %add_convert_fusion.7), channel_id=1, source_target_pairs={{0,4},{1,5},{2,6},{3,7},{4,0},{5,1},{6,2},{7,3},{8,12},{9,13},{10,... | collective-permute-start | bytes 884744 | tf_op jit(solution)/shard_map/ppermute | solution.py:533
  309.2 21.0 %collective-permute-start.33 = (bf16[96,768]{1,0:T(8,128)(2,1)S(1)}, bf16[96,768]{1,0:T(8,128)(2,1)S(1)}, u32[]{:S(2)}, u32[]{:S(2)}) collective-permute-start(bf16[96,768]{1,0:T(8,128)(2,1)S(1)} %add_convert_fusion.10), channel_id=1, source_target_pairs={{0,16},{1,17},{2,18},{3,19},{4,20},{5,21},{6,22},{7,23},{8,24},{9,... | collective-permute-start | bytes 442376 | tf_op jit(solution)/shard_map/ppermute | solution.py:533
  311.3 12.7 %collective-permute-start.32 = (bf16[24,3072]{1,0:T(8,128)(2,1)S(1)}, bf16[24,3072]{1,0:T(8,128)(2,1)S(1)}, u32[]{:S(2)}, u32[]{:S(2)}) collective-permute-start(bf16[24,3072]{1,0:T(8,128)(2,1)S(1)} %add_convert_fusion.11), channel_id=1, source_target_pairs={{0,16},{1,17},{2,18},{3,19},{4,20},{5,21},{6,22},{7,23},{8,24},{9,... | collective-permute-start | bytes 442376 | tf_op jit(solution)/shard_map/ppermute | solution.py:533
  316.4 11.8 %collective-permute-start.30 = (bf16[48,3072]{1,0:T(8,128)(2,1)S(1)}, bf16[48,3072]{1,0:T(8,128)(2,1)S(1)}, u32[]{:S(2)}, u32[]{:S(2)}) collective-permute-start(bf16[48,3072]{1,0:T(8,128)(2,1)S(1)} %fusion.53), channel_id=1, source_target_pairs={{0,8},{1,9},{2,10},{3,11},{4,12},{5,13},{6,14},{7,15},{8,0},{9,1},... | collective-permute-start | bytes 884744 | tf_op jit(solution)/shard_map/ppermute | solution.py:533
  328.2 8.5 %collective-permute-start.31 = (bf16[24,3072]{1,0:T(8,128)(2,1)S(1)}, bf16[24,3072]{1,0:T(8,128)(2,1)S(1)}, u32[]{:S(2)}, u32[]{:S(2)}) collective-permute-start(bf16[24,3072]{1,0:T(8,128)(2,1)S(1)} %fusion.58), channel_id=1, source_target_pairs={{0,16},{1,17},{2,18},{3,19},{4,20},{5,21},{6,22},{7,23},{8,24},{9,... | collective-permute-start | bytes 442376 | tf_op jit(solution)/shard_map/ppermute | solution.py:533
  341.2 2.0 collective-permute-start.34
  343.2 4.1 %collective-permute-start.35 = (f32[80,128]{1,0:T(8,128)S(1)}, f32[80,128]{1,0:T(8,128)S(1)}, u32[]{:S(2)}, u32[]{:S(2)}) collective-permute-start(f32[80,128]{1,0:T(8,128)S(1)} %add.378), channel_id=1, source_target_pairs={{0,2},{1,3},{2,0},{3,1},{4,6},{5,7},{6,4},{7,5},{8,10},{9,11},{10,... | collective-permute-start | bytes 122888 | tf_op jit(solution)/shard_map/ppermute | solution.py:533
  347.3 4.0 %collective-permute-start.36 = (f32[80,128]{1,0:T(8,128)S(1)}, f32[80,128]{1,0:T(8,128)S(1)}, u32[]{:S(2)}, u32[]{:S(2)}) collective-permute-start(f32[80,128]{1,0:T(8,128)S(1)} %add.379), channel_id=1, source_target_pairs={{0,4},{1,5},{2,6},{3,7},{4,0},{5,1},{6,2},{7,3},{8,12},{9,13},{10,... | collective-permute-start | bytes 122888 | tf_op jit(solution)/shard_map/ppermute | solution.py:533
  351.3 4.0 %collective-permute-start.37 = (f32[80,128]{1,0:T(8,128)S(1)}, f32[80,128]{1,0:T(8,128)S(1)}, u32[]{:S(2)}, u32[]{:S(2)}) collective-permute-start(f32[80,128]{1,0:T(8,128)S(1)} %add.380), channel_id=1, source_target_pairs={{0,8},{1,9},{2,10},{3,11},{4,12},{5,13},{6,14},{7,15},{8,0},{9,1},... | collective-permute-start | bytes 122888 | tf_op jit(solution)/shard_map/ppermute | solution.py:533
  355.3 4.9 %collective-permute-start.38 = (f32[80,128]{1,0:T(8,128)S(1)}, f32[80,128]{1,0:T(8,128)S(1)}, u32[]{:S(2)}, u32[]{:S(2)}) collective-permute-start(f32[80,128]{1,0:T(8,128)S(1)} %add.381), channel_id=1, source_target_pairs={{0,16},{1,17},{2,18},{3,19},{4,20},{5,21},{6,22},{7,23},{8,24},{9,... | collective-permute-start | bytes 122888 | tf_op jit(solution)/shard_map/ppermute | solution.py:533
  (35 other events, 179.9 us)
Sparse Core Ops, SparseCore 0:
  11.7 78.5 all-gather.1

commit v3 on v2

--- a/solution.py
+++ b/solution.py
@@ -248,285 +248,251 @@
     return jnp.sum(value.astype(F32), axis=0, keepdims=True)
 
 
-def feed_kernel(
-    pieces,
-    len_ref,
-    place_ref,
-    x_ref,
-    ctx_ref,
-    cot_ref,
-    wo_ref,
-    w1a_ref,
-    w1b_ref,
-    w1c_ref,
-    w1d_ref,
-    vec_ref,
-    to_a_ref,
-    to_b_ref,
-    *refs,
-):
-    parts = refs[: len(pieces)]
-    refs = refs[len(pieces) :]
-    feed_step(
-        pieces,
-        parts,
-        len_ref,
-        place_ref,
-        x_ref,
-        ctx_ref,
-        cot_ref,
-        wo_ref,
-        (w1a_ref, w1b_ref, w1c_ref, w1d_ref),
-        vec_ref,
-        to_a_ref,
-        to_b_ref,
-        *refs,
-    )
-
-
-def feed_step(
-    pieces,
-    parts,
-    len_ref,
-    place_ref,
-    x_ref,
-    ctx_ref,
-    cot_ref,
-    wo_ref,
-    w1_refs,
-    vec_ref,
-    to_a_ref,
-    to_b_ref,
-    mixed_ref,
-    first_ref,
-    ctx_out_ref,
-    act_ref,
-    dbranch_ref,
-    dhidden_ref,
-    dres_ref,
-    unit_ref,
-    inverse_ref,
-    sum_ref,
-    slope_ref,
-    w2_ref,
-    sems,
-):
+def waited(copies):
+    for copy in copies:
+        copy.wait()
+
+
+def feed_kernel(pieces, steps, *refs):
+    len_ref, place_ref, where_ref, x_ref, ctx_ref, cot_ref, vec_ref, to_a_ref, to_b_ref = refs[:9]
+    attn_in_ref, parts, refs = refs[9], refs[10 : 10 + len(pieces)], refs[10 + len(pieces) :]
+    mixed_ref, dres1_ref, dctx_ref, sum_ref, *grads = refs[:10]
+    out_grads, in_grads, attn_grads = grads[:2], grads[2:4], grads[4:6]
+    w_ref, w2_ref, act_ref, dhid_ref, first_ref, ctxb_ref, dbr_ref, dres_ref = refs[10:18]
+    unit_ref, inverse_ref, slope_ref, held_ref, in_sems, part_sems, out_sems = refs[18:]
     step = pl.program_id(0)
-    rows = x_ref.shape[0]
-
-    def copies():
+    size = x_ref.shape[0]
+    blocks = where_ref.shape[0] // CHUNKS
+    first_grad, second_grad = steps, steps + CHUNKS
+    back, last = steps + 2 * CHUNKS, 2 * steps + 2 * CHUNKS
+
+    def vec(i):
+        return vec_ref[i : i + 1, :]
+
+    def weight(c):
+        cols = slice(c * D, (c + 1) * D)
+        return w_ref.at[:, cols]
+
+    def load(c):
+        cols = slice(c * D, (c + 1) * D)
+        return pltpu.make_async_copy(attn_in_ref.at[:, cols], weight(c), in_sems.at[c])
+
+    def part_copies():
         made = []
         for part, (first, count, column) in zip(parts, pieces):
-            size, width = part.shape[0] // count, part.shape[1]
+            rows, width = part.shape[0] // count, part.shape[1]
             for i in range(count):
-                where = pl.multiple_of(place_ref[first + i] * size, size)
-                target = w2_ref.at[pl.ds(where, size), pl.ds(column, width)]
-                source = part.at[pl.ds(i * size, size), :]
-                made.append(pltpu.make_async_copy(source, target, sems.at[len(made)]))
+                where = pl.multiple_of(place_ref[first + i] * rows, rows)
+                target = w2_ref.at[pl.ds(where, rows), pl.ds(column, width)]
+                source = part.at[pl.ds(i * rows, rows), :]
+                made.append(pltpu.make_async_copy(source, target, part_sems.at[len(made)]))
         return made
-
-    def vec(i):
-        return vec_ref[i : i + 1, :]
 
     @pl.when(step == 0)
     def _():
-        for copy in copies():
+        for c in range(1 + CHUNKS):
+            load(c).start()
+        for copy in part_copies():
             copy.start()
         sum_ref[...] = jnp.zeros_like(sum_ref)
 
-    resid = x_ref[...].astype(F32) + (dot(ctx_ref[...], wo_ref[...]) + vec(2))
-    unit1, inverse1 = norm_forward(resid)
-    unit_ref[...] = unit1
-    inverse_ref[...] = jnp.broadcast_to(inverse1, inverse_ref.shape)
-    first = unit1 * vec(3) + vec(4)
-    first_b = first.astype(BF16)
-    first_ref[...] = arrange(first_b, to_a_ref[...])
-    ctx_out_ref[...] = arrange(ctx_ref[...], to_b_ref[...])
-
-    @pl.when(step == 0)
+    @pl.when(step < steps)
     def _():
-        for copy in copies():
-            copy.wait()
-
-    branch = None
-    for c in range(CHUNKS):
-        cols = slice(c * D, (c + 1) * D)
-        hidden = dot(first_b, w1_refs[c][...]) + vec(5 + c)
-        phi, bell = normal_parts(hidden)
-        active = (hidden * phi).astype(BF16)
-        act_ref[:, cols] = active
-        slope_ref[:, cols] = phi + hidden * bell * 0.3989422804014327
-        part = dot(active, w2_ref[cols, :])
-        branch = part if branch is None else branch + part
-    unit2, inverse2 = norm_forward(first + (branch + vec(9)))
-    place = lax.broadcasted_iota(jnp.int32, (rows, 1), 0) + step * rows
-    keep = (place < len_ref[0]).astype(F32)
-    mixed_ref[...] = ((unit2 * vec(10) + vec(11)) * keep).astype(BF16)
-    dz = cot_ref[...].astype(F32) * keep
-    dres2 = norm_back(dz, vec(10), unit2, inverse2)
-    dres_ref[...] = dres2
-    dbranch = dres2.astype(BF16)
-    dbranch_ref[...] = dbranch
-    sum_ref[9:10, :] += column_sum(dbranch)
-    sum_ref[10:11, :] += column_sum(dz * unit2)
-    sum_ref[11:12, :] += column_sum(dz)
-    for c in range(CHUNKS):
-        cols = slice(c * D, (c + 1) * D)
-        dhidden = (dot_nt(dbranch, w2_ref[cols, :]) * slope_ref[:, cols]).astype(BF16)
-        dhidden_ref[:, cols] = dhidden
-        sum_ref[5 + c : 6 + c, :] += column_sum(dhidden)
-
-
-def feed(lengths, x, ctx, cot, attn_in, vec, to_a, to_b, places, parts, pieces):
+        rows = pl.ds(pl.multiple_of(step * size, size), size)
+
+        def arrived(c):
+            @pl.when(step == 0)
+            def _():
+                load(c).wait()
+
+        arrived(0)
+        resid = x_ref[...].astype(F32) + (dot(ctx_ref[...], weight(0)[...]) + vec(2))
+        unit1, inverse1 = norm_forward(resid)
+        unit_ref[rows, :] = unit1
+        inverse_ref[rows, :] = jnp.broadcast_to(inverse1, (size, 128))
+        first = unit1 * vec(3) + vec(4)
+        first_b = first.astype(BF16)
+        first_ref[rows, :] = arrange(first_b, to_a_ref[...])
+        ctxb_ref[rows, :] = arrange(ctx_ref[...], to_b_ref[...])
+        for c in range(CHUNKS):
+            arrived(1 + c)
+        @pl.when(step == 0)
+        def _():
+            waited(part_copies())
+
+        branch = None
+        for c in range(CHUNKS):
+            cols = slice(c * D, (c + 1) * D)
+            hidden = dot(first_b, weight(1 + c)[...]) + vec(5 + c)
+            phi, bell = normal_parts(hidden)
+            active = (hidden * phi).astype(BF16)
+            act_ref[rows, cols] = active
+            slope_ref[:, cols] = phi + hidden * bell * 0.3989422804014327
+            part = dot(active, w2_ref[cols, :])
+            branch = part if branch is None else branch + part
+        unit2, inverse2 = norm_forward(first + (branch + vec(9)))
+        place = lax.broadcasted_iota(jnp.int32, (size, 1), 0) + step * size
+        keep = (place < len_ref[0]).astype(F32)
+        mixed_ref[...] = ((unit2 * vec(10) + vec(11)) * keep).astype(BF16)
+        dz = cot_ref[...].astype(F32) * keep
+        dres2 = norm_back(dz, vec(10), unit2, inverse2)
+        dres_ref[rows, :] = dres2
+        dbranch = dres2.astype(BF16)
+        dbr_ref[rows, :] = dbranch
+        sum_ref[9:10, :] += column_sum(dbranch)
+        sum_ref[10:11, :] += column_sum(dz * unit2)
+        sum_ref[11:12, :] += column_sum(dz)
+        for c in range(CHUNKS):
+            cols = slice(c * D, (c + 1) * D)
+            dhidden = (dot_nt(dbranch, w2_ref[cols, :]) * slope_ref[:, cols]).astype(BF16)
+            dhid_ref[rows, cols] = dhidden
+            sum_ref[5 + c : 6 + c, :] += column_sum(dhidden)
+
+    def out_copies(step, go):
+        chunk = step - first_grad
+        slot = lax.rem(chunk, 2)
+        rows = D // blocks
+        for i in range(blocks):
+            place = where_ref[chunk * blocks + i]
+            source = held_ref.at[slot, pl.ds(i * rows, rows), :]
+            for half in range(2):
+                where = pl.multiple_of((place - half * 2 * blocks) * rows, rows)
+
+                @pl.when((place >= 2 * blocks) == (half == 1))
+                def _(half=half, where=where, source=source, i=i):
+                    target = out_grads[half].at[pl.ds(where, rows), :]
+                    go(pltpu.make_async_copy(source, target, out_sems.at[slot, i]))
+
+    def in_copies(step, grads, column):
+        slot = lax.rem(step - first_grad, 2)
+        made = []
+        for half in range(2):
+            source = held_ref.at[slot, pl.ds(half * D // 2, D // 2), :]
+            target = grads[half].at[:, pl.ds(column, D)]
+            made.append(pltpu.make_async_copy(source, target, out_sems.at[slot, half]))
+        return made
+
+    def in_column(step):
+        return pl.multiple_of((step - second_grad) * D, D)
+
+    def start(copy):
+        copy.start()
+
+    def wait(copy):
+        copy.wait()
+
+    @pl.when((step >= first_grad) & (step < second_grad))
+    def _():
+        @pl.when(step >= first_grad + 2)
+        def _():
+            out_copies(step - 2, wait)
+
+        cols = pl.ds(pl.multiple_of((step - first_grad) * D, D), D)
+        grad = dot_tn(act_ref[:, cols], dbr_ref[...]).astype(BF16)
+        held_ref[lax.rem(step - first_grad, 2)] = grad
+        out_copies(step, start)
+
+    @pl.when((step >= second_grad) & (step < back))
+    def _():
+        @pl.when(step < second_grad + 2)
+        def _():
+            out_copies(step - 2, wait)
+
+        @pl.when(step >= second_grad + 2)
+        def _():
+            waited(in_copies(step - 2, in_grads, in_column(step - 2)))
+
+        cols = pl.ds(in_column(step), D)
+        grad = dot_tn(first_ref[...], dhid_ref[:, cols]).astype(BF16)
+        held_ref[lax.rem(step - first_grad, 2)] = grad
+        for copy in in_copies(step, in_grads, in_column(step)):
+            copy.start()
+
+    @pl.when((step >= back) & (step < last))
+    def _():
+        rows = pl.ds(pl.multiple_of((step - back) * size, size), size)
+        dfirst = dres_ref[rows, :]
+        for c in range(CHUNKS):
+            dfirst = dfirst + dot_nt(dhid_ref[rows, c * D : (c + 1) * D], weight(1 + c)[...])
+        unit = unit_ref[rows, :]
+        dres1 = norm_back(dfirst, vec(3), unit, inverse_ref[rows, 0:1])
+        dres1_ref[...] = dres1
+        dattend = dres1.astype(BF16)
+        dbr_ref[rows, :] = dattend
+        dctx_ref[...] = dot_nt(dattend, weight(0)[...]).astype(BF16)
+        sum_ref[2:3, :] += column_sum(dattend)
+        sum_ref[3:4, :] += column_sum(dfirst * unit)
+        sum_ref[4:5, :] += column_sum(dfirst)
+
+    @pl.when(step == last)
+    def _():
+        waited(in_copies(back - 2, in_grads, in_column(back - 2)))
+        waited(in_copies(back - 1, in_grads, in_column(back - 1)))
+        held_ref[0] = dot_tn(ctxb_ref[...], dbr_ref[...]).astype(BF16)
+        copies = in_copies(first_grad, attn_grads, 0)
+        for copy in copies:
+            copy.start()
+        waited(copies)
+
+
+def feed(lengths, x, ctx, cot, attn_in, vec, to_a, to_b, places, parts, pieces, where):
     seq = x.shape[0]
-    rows = min(256, seq)
-
-    def row(width):
-        return pl.BlockSpec((rows, width), lambda i, *_: (i, 0))
-
-    def fixed(shape, column=0):
-        return pl.BlockSpec(shape, lambda i, *_: (0, column), pipeline_mode=pl.Buffered(1))
-
-    outs = ((D, BF16), (D, BF16), (D, BF16), (FF, BF16), (D, BF16), (FF, BF16), (D, F32), (D, F32), (128, F32))
+    size = min(256, seq)
+    steps = seq // size
+    back = steps + 2 * CHUNKS
+    anywhere = pl.BlockSpec(memory_space=pl.ANY)
+
+    def early(width):
+        return pl.BlockSpec((size, width), lambda i, *_: (jnp.minimum(i, steps - 1), 0))
+
+    def late(width):
+        return pl.BlockSpec((size, width), lambda i, *_: (jnp.clip(i - back, 0, steps - 1), 0))
+
+    def fixed(shape):
+        return pl.BlockSpec(shape, lambda i, *_: (0, 0), pipeline_mode=pl.Buffered(1))
+
+    shape = jax.ShapeDtypeStruct
     return pl.pallas_call(
-        partial(feed_kernel, pieces),
+        partial(feed_kernel, pieces, steps),
         grid_spec=pltpu.PrefetchScalarGridSpec(
-            num_scalar_prefetch=2,
-            grid=(seq // rows,),
-            in_specs=[row(D), row(D), row(D)]
-            + [fixed((D, D), c) for c in range(1 + CHUNKS)]
+            num_scalar_prefetch=3,
+            grid=(2 * steps + 2 * CHUNKS + 1,),
+            in_specs=[early(D)] * 3
             + [fixed((12, D)), fixed((D, D)), fixed((D, D))]
-            + untouched(parts),
-            out_specs=[row(width) for width, _ in outs]
-            + [pl.BlockSpec((12, D), lambda i, *_: (0, 0))],
+            + [anywhere] * (1 + len(parts)),
+            out_specs=[early(D), late(D), late(D), pl.BlockSpec((12, D), lambda i, *_: (0, 0))]
+            + [anywhere] * 6,
             scratch_shapes=[
-                pltpu.VMEM((rows, FF), F32),
+                pltpu.VMEM((D, D + FF), BF16),
                 pltpu.VMEM((FF, D), BF16),
+                pltpu.VMEM((seq, FF), BF16),
+                pltpu.VMEM((seq, FF), BF16),
+                pltpu.VMEM((seq, D), BF16),
+                pltpu.VMEM((seq, D), BF16),
+                pltpu.VMEM((seq, D), BF16),
+                pltpu.VMEM((seq, D), F32),
+                pltpu.VMEM((seq, D), F32),
+                pltpu.VMEM((seq, 128), F32),
+                pltpu.VMEM((size, FF), F32),
+                pltpu.VMEM((2, D, D), BF16),
+                pltpu.SemaphoreType.DMA((1 + CHUNKS,)),
                 pltpu.SemaphoreType.DMA((sum(count for _, count, _ in pieces),)),
+                pltpu.SemaphoreType.DMA((2, max(2, where.shape[0] // CHUNKS))),
             ],
         ),
-        out_shape=[jax.ShapeDtypeStruct((seq, width), kind) for width, kind in outs]
-        + [jax.ShapeDtypeStruct((12, D), F32)],
+        out_shape=[
+            shape((seq, D), BF16),
+            shape((seq, D), F32),
+            shape((seq, D), BF16),
+            shape((12, D), F32),
+        ]
+        + [shape((FF // 2, D), BF16)] * 2
+        + [shape((D // 2, FF), BF16)] * 2
+        + [shape((D // 2, D), BF16)] * 2,
         compiler_params=pltpu.CompilerParams(vmem_limit_bytes=VMEM),
-        cost_estimate=cost(28),
+        cost_estimate=cost(50),
         name="feed",
-    )(lengths, places, x, ctx, cot, *(attn_in,) * (1 + CHUNKS), vec, to_a, to_b, *parts)
-
-
-def out_grad_kernel(blocks, where_ref, act_ref, grad_ref, out_ref, held_ref, sems):
-    step, slot = pl.program_id(0), lax.rem(pl.program_id(0), 2)
-    size = held_ref.shape[1] // blocks
-
-    def copies(step, slot):
-        made = []
-        for i in range(blocks):
-            place = pl.multiple_of(where_ref[step * blocks + i] * size, size)
-            source = held_ref.at[slot, pl.ds(i * size, size), :]
-            target = out_ref.at[pl.ds(place, size), :]
-            made.append(pltpu.make_async_copy(source, target, sems.at[slot, i]))
-        return made
-
-    @pl.when(step >= 2)
-    def _():
-        for copy in copies(step - 2, slot):
-            copy.wait()
-
-    held_ref[slot] = dot_tn(act_ref[...], grad_ref[...]).astype(BF16)
-    for copy in copies(step, slot):
-        copy.start()
-
-    @pl.when(step == CHUNKS - 1)
-    def _():
-        for copy in copies(step - 1, 1 - slot) + copies(step, slot):
-            copy.wait()
-
-
-def out_grad(act, grad, where):
-    seq, blocks = act.shape[0], where.shape[0] // CHUNKS
-    return pl.pallas_call(
-        partial(out_grad_kernel, blocks),
-        grid_spec=pltpu.PrefetchScalarGridSpec(
-            num_scalar_prefetch=1,
-            grid=(CHUNKS,),
-            in_specs=[
-                pl.BlockSpec((seq, D), lambda i, _: (0, i)),
-                pl.BlockSpec((seq, D), lambda i, _: (0, 0), pipeline_mode=pl.Buffered(1)),
-            ],
-            out_specs=pl.BlockSpec(memory_space=pl.ANY),
-            scratch_shapes=[
-                pltpu.VMEM((2, D, D), BF16),
-                pltpu.SemaphoreType.DMA((2, blocks)),
-            ],
-        ),
-        out_shape=jax.ShapeDtypeStruct((FF, D), BF16),
-        compiler_params=pltpu.CompilerParams(vmem_limit_bytes=VMEM),
-        cost_estimate=cost(8),
-        name="out_grad",
-    )(where, act, grad)
-
-
-def feed_back_kernel(
-    dhidden_ref,
-    dres_ref,
-    unit_ref,
-    inverse_ref,
-    wo_ref,
-    w1a_ref,
-    w1b_ref,
-    w1c_ref,
-    w1d_ref,
-    vec_ref,
-    dres1_ref,
-    dattend_ref,
-    dctx_ref,
-    sum_ref,
-):
-    @pl.when(pl.program_id(0) == 0)
-    def _():
-        sum_ref[...] = jnp.zeros_like(sum_ref)
-
-    dfirst = dres_ref[...]
-    for c, w1_ref in enumerate((w1a_ref, w1b_ref, w1c_ref, w1d_ref)):
-        dfirst = dfirst + dot_nt(dhidden_ref[:, c * D : (c + 1) * D], w1_ref[...])
-    unit = unit_ref[...]
-    dres1 = norm_back(dfirst, vec_ref[3:4, :], unit, inverse_ref[:, 0:1])
-    dres1_ref[...] = dres1
-    dattend = dres1.astype(BF16)
-    dattend_ref[...] = dattend
-    dctx_ref[...] = dot_nt(dattend, wo_ref[...]).astype(BF16)
-    sum_ref[2:3, :] += column_sum(dattend)
-    sum_ref[3:4, :] += column_sum(dfirst * unit)
-    sum_ref[4:5, :] += column_sum(dfirst)
-
-
-def feed_back(dhidden, dres2, unit, inverse, attn_in, vec, waits=()):
-    seq = dhidden.shape[0]
-    rows = min(256, seq)
-
-    def row(width):
-        return pl.BlockSpec((rows, width), lambda i: (i, 0))
-
-    def fixed(shape, column=0):
-        return pl.BlockSpec(shape, lambda i: (0, column), pipeline_mode=pl.Buffered(1))
-
-    return pl.pallas_call(
-        after(feed_back_kernel, 10, len(waits)),
-        grid=(seq // rows,),
-        in_specs=[row(FF), row(D), row(D), row(128)]
-        + [fixed((D, D), c) for c in range(1 + CHUNKS)]
-        + [fixed((12, D))]
-        + untouched(waits),
-        out_specs=[row(D), row(D), row(D), pl.BlockSpec((8, D), lambda i: (0, 0))],
-        out_shape=[
-            jax.ShapeDtypeStruct((seq, D), F32),
-            jax.ShapeDtypeStruct((seq, D), BF16),
-            jax.ShapeDtypeStruct((seq, D), BF16),
-            jax.ShapeDtypeStruct((8, D), F32),
-        ],
-        compiler_params=pltpu.CompilerParams(vmem_limit_bytes=VMEM),
-        cost_estimate=cost(14),
-        name="feed_back",
-    )(dhidden, dres2, unit, inverse, *(attn_in,) * (1 + CHUNKS), vec, *waits)
+    )(lengths, places, where, x, ctx, cot, vec, to_a, to_b, attn_in, *parts)
 
 
 def swap(value, bit, n):
@@ -581,8 +547,8 @@
 
 
 class Scatter:
-    def __init__(self, value, n):
-        self.terms, self.n = [value], n
+    def __init__(self, kept, away, bit, n):
+        self.terms, self.n = [kept, swap(away, bit, n)], n
 
     def step(self, bit):
         half = self.terms[0].shape[0] // 2
@@ -700,30 +666,24 @@
     x_a, x_b = arrange(x, to_a), arrange(x, to_b)
     for bit in far:
         qkv.step(bit)
-        qkv.value, x_a, x_b = phase(qkv.value, x_a, x_b)
+        qkv.value, out.value, x_a, x_b = phase(qkv.value, out.value, x_a, x_b)
+        out.step(bit)
     left, right = qkv.cut(0, half), qkv.cut(half, 2 * half + 128)
-    left.step(two)
-    right.step(one)
-    left.value, right.value, out.value = phase(left.value, right.value, out.value)
-    for bit in far[:1]:
-        out.step(bit)
-    left.step(one)
-    right.step(two)
-    left.value, right.value = phase(left.value, right.value)
+    for bits in ((two, one), (one, two)):
+        left.step(bits[0])
+        right.step(bits[1])
+        left.value, right.value, out.value = phase(left.value, right.value, out.value)
     left = (left.value, swap(left.value, core, n))
     right = (right.value, swap(right.value, core, n))
     left, right, out.value = phase(left, right, out.value)
-    for bit in far[1:]:
-        out.step(bit)
     vec_rows = jnp.concatenate([part[:, half:] for part in right], axis=0)
     vec = dot(to_b, vec_rows)[:, :12].reshape(12, D)
     bias_qkv = jnp.concatenate([vec[:1], jnp.zeros((1, D), F32), vec[1:2]], axis=1)
 
-    packed = project(x_a, x_b, left, right, bias_qkv)
-    packed, out.value = phase(packed, out.value)
     out_left, out_right = out.cut(0, D // 2), out.cut(D // 2, D)
     out_left.step(two)
     out_right.step(one)
+    packed = project(x_a, x_b, left, right, bias_qkv)
     some = PAIRS // 2
     heads = attend(lengths, packed, 0, some)
     heads, out_left.value, out_right.value, attn_in = phase(
@@ -747,72 +707,69 @@
         places, pieces = jnp.zeros((1,), jnp.int32), ((0, 1, 0),)
     ctx, ctxt, lse = heads
 
-    mixed, first, ctx_b, act, dbranch, dhidden, dres2, unit, inverse, sums2 = feed(
-        lengths, x, ctx, cotangent[0], attn_in, vec, to_a, to_b, places, parts, pieces
-    )
-    if rows_f % 16 == 0:
-        grad_out = out_grad(act, dbranch, order_b.where())
-    else:
-        grad_out = dot_tn(act, dbranch).astype(BF16).reshape(n, rows_f, D)
-        grad_out = grad_out[order_b.places(n)].reshape(FF, D)
-    dhidden, grad_out = phase(dhidden, grad_out)
-    sum_out = Scatter(grad_out, n)
-    sum_out.step(core)
-    grad_in = dot_tn(first, dhidden).astype(BF16)
-    dhidden, grad_in = phase(dhidden, grad_in)
-    sum_in = Scatter(grad_in, n)
-    sum_in.step(core)
-    dres1, dattend, dctx, sums1 = feed_back(dhidden, dres2, unit, inverse, attn_in, vec)
-
-    sum_in.terms[-1], sum_out.terms[-1], dattend, dctx = phase(
-        sum_in.terms[-1], sum_out.terms[-1], dattend, dctx
-    )
-    sum_in.step(one)
-    sum_out.step(two)
-    grad_attn = dot_tn(ctx_b, dattend).astype(BF16)
-    some = 2 * PAIRS // 3
-    dqkv, bias_a = attend_back(lengths, packed, dctx, ctxt, lse, 0, some, None, (grad_attn,))
-    sum_in.terms[-1], sum_out.terms[-1], dqkv = phase(
-        sum_in.terms[-1], sum_out.terms[-1], dqkv
-    )
-    sum_in.step(two)
-    sum_out.step(one)
-    dqkv, bias_b = attend_back(lengths, packed, dctx, ctxt, lse, some, PAIRS - some, dqkv)
-    sum_in.terms[-1], sum_out.terms[-1], dqkv, bias_b = phase(
-        sum_in.terms[-1], sum_out.terms[-1], dqkv, bias_b
-    )
+    aligned = rows_f % 16 == 0
+    where = order_b.where() if aligned else jnp.arange(CHUNKS, dtype=jnp.int32)
+    mixed, dres1, dctx, sums, *grads = feed(
+        lengths, x, ctx, cotangent[0], attn_in, vec, to_a, to_b, places, parts, pieces, where
+    )
+    if not aligned:
+        grad = jnp.concatenate(grads[:2], axis=0).reshape(n, rows_f, D)
+        grads[:2] = jnp.split(grad[order_b.places(n)].reshape(FF, D), 2)
+    sum_out = Scatter(*grads[:2], core, n)
+    sum_in = Scatter(*grads[2:4], core, n)
+
+    dqkv, biases = None, []
+    for first, count, bits in ((0, 1, (one, two)), (1, 4, (two, one)), (5, 1, None)):
+        dqkv, bias = attend_back(lengths, packed, dctx, ctxt, lse, first, count, dqkv)
+        biases.append(bias)
+        if bits is not None:
+            sum_in.terms[-1], sum_out.terms[-1], dqkv = phase(
+                sum_in.terms[-1], sum_out.terms[-1], dqkv
+            )
+            sum_in.step(bits[0])
+            sum_out.step(bits[1])
+    dqkv, sum_in.terms[-1], sum_out.terms[-1] = phase(
+        dqkv, sum_in.terms[-1], sum_out.terms[-1]
+    )
+
+    def late_grads(side):
+        cols = slice(side * D // 2, (side + 1) * D // 2)
+        queries, keys = [dot_tn(x_a[:, cols], dqkv[i]).astype(BF16) for i in range(2)]
+        values = dot_tn(x_b[:, cols], dqkv[2]).astype(BF16)
+        return (
+            jnp.concatenate([queries, keys], axis=1),
+            jnp.concatenate([values, grads[4 + side]], axis=1),
+        )
+
+    away_a, away_b = late_grads(1)
+    away_a, away_b, dqkv = phase(away_a, away_b, dqkv)
+    kept_a, kept_b = late_grads(0)
+    late_a, late_b = Scatter(kept_a, away_a, core, n), Scatter(kept_b, away_b, core, n)
     sum_in.step(others[0])
     sum_out.step(others[0])
-    late_a = Scatter(
-        jnp.concatenate([dot_tn(x_a, dqkv[i]).astype(BF16) for i in range(2)], axis=1), n
-    )
-    late_b = Scatter(
-        jnp.concatenate([dot_tn(x_b, dqkv[2]).astype(BF16), grad_attn], axis=1), n
-    )
-    bias_sums = jnp.concatenate([bias_a, bias_b], axis=0)
-    grad_vec = jnp.concatenate(
-        [
-            bias_sums[:, 0].reshape(1, D),
-            bias_sums[:, 1].reshape(1, D),
-            sums1[2:5],
-            sums2[5:],
-        ]
-    ).reshape(-1, 128)
     late_a.terms, late_b.terms, sum_in.terms[-1], sum_out.terms[-1] = phase(
         late_a.terms, late_b.terms, sum_in.terms[-1], sum_out.terms[-1]
     )
+    late_a.step(one)
+    late_b.step(two)
     for bit in others[1:]:
         sum_in.step(bit)
         sum_out.step(bit)
+    late_a.terms[-1], late_b.terms[-1], sum_in.terms[-1], sum_out.terms[-1] = phase(
+        late_a.terms[-1], late_b.terms[-1], sum_in.terms[-1], sum_out.terms[-1]
+    )
+    late_a.step(two)
+    late_b.step(one)
+    late_a.terms[-1], late_b.terms[-1] = phase(late_a.terms[-1], late_b.terms[-1])
     share_in, share_out = sum_in.total(), sum_out.total()
-    for bits in ((core, core), (one, two), (two, one)):
-        late_a.step(bits[0])
-        late_b.step(bits[1])
-        late_a.terms[-1], late_b.terms[-1] = phase(late_a.terms[-1], late_b.terms[-1])
     late = late_a.join(late_b)
     for bit in others:
         late.step(bit)
     share_late = late.total()
+    bias_sums = jnp.concatenate(biases, axis=0)
+    grad_vec = jnp.concatenate(
+        [bias_sums[:, 0].reshape(1, D), bias_sums[:, 1].reshape(1, D), sums[2:]]
+    ).reshape(-1, 128)
     full_qkv = jnp.concatenate(
         [
             arrange(to_a, jnp.concatenate(left, axis=0)),
@@ -836,11 +793,11 @@
         *(w_qkv, share_late[:, : 3 * D], moment_qkv, square_qkv),
         *(w_attn, share_late[:, 3 * D :], moment_attn, square_attn),
     )
-    sums = sum_all(jnp.concatenate([next_attn[6], grad_vec], axis=0), n)
+    reduced = sum_all(jnp.concatenate([next_attn[6], grad_vec], axis=0), n)
     place = lax.axis_index("dp") * width
-    share_vec = lax.dynamic_slice_in_dim(sums[8:].reshape(-1), place, width, 0)
+    share_vec = lax.dynamic_slice_in_dim(reduced[8:].reshape(-1), place, width, 0)
     updates = (next_attn[2], next_attn[5], next_in[2], next_in[5])
-    *new_weights, norms = renew(sums[:8], (w_qkv, w_attn, w_in, w_out), updates)
+    *new_weights, norms = renew(reduced[:8], (w_qkv, w_attn, w_in, w_out), updates)
     vec_moment, vec_square, vec_update = adapt(vectors, share_vec, moment_vec, square_vec, 0.0)
     return (
         mixed[None],

time: 378 us -> 349 us (0.923)
  waiting for transfers between devices: 87.1 us -> 74.8 us
  matrix products: 33.9 us -> 23.3 us
  local copies, waits for them, and re-layouts: 18.5 us -> 12.8 us
  starting transfers between devices: 41.2 us -> 35.7 us
  Pallas kernels: 139 us -> 143 us
    ppermute x39, waiting for transfers between devices: 87.1 us -> 73.7 us  [swap(): return lax.ppermute(value, 'dp', [(i, i ^ 1 << bit) for i in range(n)])]
    dot_general x5 -> x6, matrix products: 16.7 us -> 8.18 us  [dot_tn(): lax.dot_general(a, b, (((0,), (0,)), ((), ())), preferred_element_type=F32)]
    slice x7 -> x2, local copies, waits for them, and re-layouts: 7.28 us -> 0.59 us  [the longest x1 0.58 us: body(): reduced[:8]]
    ppermute x39, starting transfers between devices: 41.2 us -> 35.6 us  [swap(): return lax.ppermute(value, 'dp', [(i, i ^ 1 << bit) for i in range(n)])]
    pallas_call x2 -> x3, Pallas kernels: 37.9 us -> 40.4 us  [attend_back(): pl.pallas_call(after(partial(attend_back_kernel, min(512, seq)), 7, len(e...]
    pallas_call x3 -> x1, Pallas kernels: 59.7 us -> 61.3 us  [feed(): pl.pallas_call(partial(feed_kernel, pieces, steps), grid_spec=pltpu.Prefe...]
  transfers between devices with their start and end apart: 40 -> 40, of which waited for: 22 -> 28; matrix products, arithmetic and copies ran while one was open for 13% -> 12% of each run, Pallas kernels for 24% -> 22%
where the time goes in v3:
time: 349 us; the launch traced here: 343 us
  Pallas kernels  143 us (41%)
  waiting for transfers between devices  74.8 us (21%)
  other arithmetic  38.2 us (11%)
  starting transfers between devices  35.7 us (10%)
  matrix products  23.3 us (7%)
  between operations  15.9 us (5%)
  local copies, waits for them, and re-layouts  12.8 us (4%)
    ppermute x39, waiting for transfers between devices, swap(): return lax.ppermute(value, 'dp', [(i, i ^ 1 << bit) for i in range(n)])  73.7 us
    pallas_call x1, Pallas kernels, feed(): pl.pallas_call(partial(feed_kernel, pieces, steps), grid_spec=pltpu.Prefe...  61.3 us
    pallas_call x3, Pallas kernels, attend_back(): pl.pallas_call(after(partial(attend_back_kernel, min(512, seq)), 7, len(e...  40.4 us
    ppermute x39, starting transfers between devices, swap(): return lax.ppermute(value, 'dp', [(i, i ^ 1 << bit) for i in range(n)])  35.6 us
    pallas_call x2, Pallas kernels, attend(): pl.pallas_call(after(attend_kernel, 4, len(extra)), grid_spec=pltpu.Prefe...  24.6 us
    convert_element_type x13, other arithmetic, step(): away = self.total([t[half:] for t in self.terms]).astype(BF16)  17.2 us
    dot_general x5, matrix products, dot(): return jnp.dot(a, b, preferred_element_type=F32)  10.8 us
    pallas_call x1, Pallas kernels, project(): pl.pallas_call(project_kernel, grid=(seq // rows,), in_specs=[pl.BlockSpe...  8.57 us
  transfers between devices with their start and end apart: 40, of which 28 were waited for; matrix products, arithmetic and copies ran while one was open for 12% of the time, Pallas kernels for 22%

profile of v3, /device:TPU:0, one launch (start us, length us, event | category | flops | bytes accessed | tf_op | source)
XLA Modules:
  0.0 343.4 jit_solution(2897972461921432809)
XLA Ops:
  11.7 4.1 %collective-permute-start = (bf16[24,2432]{1,0:T(8,128)(2,1)S(1)}, bf16[24,2432]{1,0:T(8,128)(2,1)S(1)}, u32[]{:S(2)}, u32[]{:S(2)}) collective-permute-start(bf16[24,2432]{1,0:T(8,128)(2,1)S(1)} %fusion.85), channel_id=1, source_target_pairs={{0,16},{1,17},{2,18},{3,19},{4,20},{5,21},{6,22},{7,23},{8,24},{9,... | collective-permute-start | bytes 350216 | tf_op jit(solution)/shard_map/ppermute | solution.py:499
  15.8 2.6 fusion.35.xa_ref
  18.4 2.6 fusion.34.xb_ref
  21.8 3.9 %collective-permute-start.1 = (bf16[48,2432]{1,0:T(8,128)(2,1)S(1)}, bf16[48,2432]{1,0:T(8,128)(2,1)S(1)}, u32[]{:S(2)}, u32[]{:S(2)}) collective-permute-start(bf16[48,2432]{1,0:T(8,128)(2,1)S(1)} %pad_maximum_fusion.18), channel_id=1, source_target_pairs={{0,8},{1,9},{2,10},{3,11},{4,12},{5,13},{6,14},{7,15},{8,0},{9,1},... | collective-permute-start | bytes 700424 | tf_op jit(solution)/shard_map/ppermute | solution.py:499
  25.7 7.7 %collective-permute-done.2 = bf16[96,768]{1,0:T(8,128)(2,1)S(1)} collective-permute-done((bf16[96,768]{1,0:T(8,128)(2,1)S(1)}, bf16[96,768]{1,0:T(8,128)(2,1)S(1)}, u32[]{:S(2)}, u32[]{:S(2)}) %collective-permute-start.2) | collective-permute-done | bytes 147488 | tf_op jit(solution)/shard_map/ppermute | solution.py:499
  33.4 2.8 collective-permute-done.1
  36.3 1.6 collective-permute-start.3
  39.5 3.9 %collective-permute-done.3 = bf16[96,1152]{1,0:T(8,128)(2,1)S(1)} collective-permute-done((bf16[96,1152]{1,0:T(8,128)(2,1)S(1)}, bf16[96,1152]{1,0:T(8,128)(2,1)S(1)}, u32[]{:S(2)}, u32[]{:S(2)}) %collective-permute-start.3) | collective-permute-done | bytes 221216 | tf_op jit(solution)/shard_map/ppermute | solution.py:499
  43.4 1.8 collective-permute-done.4
  45.2 4.8 %collective-permute-done.5 = bf16[192,768]{1,0:T(8,128)(2,1)S(1)} collective-permute-done((bf16[192,768]{1,0:T(8,128)(2,1)S(1)}, bf16[192,768]{1,0:T(8,128)(2,1)S(1)}, u32[]{:S(2)}, u32[]{:S(2)}) %collective-permute-start.5) | collective-permute-done | bytes 294944 | tf_op jit(solution)/shard_map/ppermute | solution.py:499
  50.9 10.2 %collective-permute-done.6 = bf16[192,1152]{1,0:T(8,128)(2,1)S(1)} collective-permute-done((bf16[192,1152]{1,0:T(8,128)(2,1)S(1)}, bf16[192,1152]{1,0:T(8,128)(2,1)S(1)}, u32[]{:S(2)}, u32[]{:S(2)}) %collective-permute-start.6) | collective-permute-done | bytes 442400 | tf_op jit(solution)/shard_map/ppermute | solution.py:499
  62.5 2.6 collective-permute-done.8.lb_ref
  71.1 8.6 %project.1.refs_1_.refs_2_.refs_3_ = bf16[1024,2304]{1,0:T(8,128)(2,1)} custom-call(bf16[1024,768]{1,0:T(8,128)(2,1)} %fusion.35.xa_ref, bf16[1024,768]{1,0:T(8,128)(2,1)} %fusion.34.xb_ref, bf16[384,1152]{1,0:T(8,128)(2,1)} %copy-done.6, bf16[384,1152]{1,0:T(8,128)(2,1)} %copy-done.19, bf16[384,1280]{1,0:T(8,128)(2,1)} %copy-done.1, ...), custom_call_target="tpu_custom_call" | custom-call | flops 250000000 | tf_op jit(solution)/shard_map/project/pallas_call | solution.py:59
  79.7 12.3 %attend.2 = (bf16[1024,768]{1,0:T(8,128)(2,1)}, f32[768,1024]{1,0:T(8,128)}, f32[6,2,1024]{2,1,0:T(2,128)}) custom-call(s32[1]{0:T(128)S(6)} %copy.61.refs_0_, bf16[1024,2304]{1,0:T(8,128)(2,1)} %project.1.refs_1_.refs_2_.refs_3_, bf16[1024,2304]{1,0:T(8,128)(2,1)} %project.1.refs_1_.refs_2_.refs_3_, bf16[1024,2304]{1,0:T(8,128)(2,1)} %project.1.refs_1_.refs_2_.refs_3_), custom_call_target="tpu_custom_call" | custom-call | flops 600000000 | tf_op jit(solution)/shard_map/attend/pallas_call | solution.py:107
  95.9 12.3 %attend.3 = (bf16[1024,768]{1,0:T(8,128)(2,1)}, f32[768,1024]{1,0:T(8,128)}, f32[6,2,1024]{2,1,0:T(2,128)}) custom-call(s32[1]{0:T(128)S(6)} %copy.61.refs_0_, bf16[1024,2304]{1,0:T(8,128)(2,1)} %project.1.refs_1_.refs_2_.refs_3_, bf16[1024,2304]{1,0:T(8,128)(2,1)} %project.1.refs_1_.refs_2_.refs_3_, ...), custom_call_target="tpu_custom_call", output_to_operand_aliasing={{0}: (4, {}), {1}: (5, {}), {2}: (6, {})} | custom-call | flops 600000000 | tf_op jit(solution)/shard_map/attend/pallas_call | solution.py:107
  115.3 61.3 %feed.1 = (bf16[1024,768]{1,0:T(8,128)(2,1)}, f32[1024,768]{1,0:T(8,128)}, bf16[1024,768]{1,0:T(8,128)(2,1)}, f32[12,768]{1,0:T(8,128)}, bf16[1536,768]{1,0:T(8,...) custom-call(s32[1]{0:T(128)S(6)} %copy.61.refs_0_, ...), custom_call_target="tpu_custom_call" | custom-call | flops 2500000000 | tf_op jit(solution)/shard_map/feed/pallas_call | solution.py:455
  177.2 8.0 %attend_back.3 = (bf16[3,1024,768]{2,1,0:T(8,128)(2,1)}, f32[1,2,128]{2,1,0:T(2,128)}) custom-call(s32[1]{0:T(128)S(6)} %copy.61.refs_0_, bf16[1024,2304]{1,0:T(8,128)(2,1)} %project.1.refs_1_.refs_2_.refs_3_, bf16[1024,2304]{1,0:T(8,128)(2,1)} %project.1.refs_1_.refs_2_.refs_3_, bf16[1024,2304]{1,0:T(8,128)(2,1)} %project.1.refs_1_.refs_2_.refs_3_, ...), custom_call_target="tpu_custom_call" | custom-call | flops 300000000 | tf_op jit(solution)/shard_map/attend_back/pallas_call | solution.py:199
  185.2 1.7 add_convert_fusion
  186.9 1.6 collective-permute-start.19
  188.6 2.8 add_convert_fusion.1
  192.2 24.6 %attend_back.4 = (bf16[3,1024,768]{2,1,0:T(8,128)(2,1)}, f32[4,2,128]{2,1,0:T(2,128)}) custom-call(s32[1]{0:T(128)S(6)} %copy.61.refs_0_, bf16[1024,2304]{1,0:T(8,128)(2,1)} %project.1.refs_1_.refs_2_.refs_3_, bf16[1024,2304]{1,0:T(8,128)(2,1)} %project.1.refs_1_.refs_2_.refs_3_, ...), custom_call_target="tpu_custom_call", output_to_operand_aliasing={{0}: (7, {})} | custom-call | flops 1200000000 | tf_op jit(solution)/shard_map/attend_back/pallas_call | solution.py:199
  216.8 2.6 collective-permute-done.18
  219.4 2.5 add_convert_fusion.5
  221.8 2.4 add_convert_fusion.4
  227.4 3.1 convolution_convert_fusion.1
  230.5 7.8 %attend_back.5 = (bf16[3,1024,768]{2,1,0:T(8,128)(2,1)}, f32[1,2,128]{2,1,0:T(2,128)}) custom-call(s32[1]{0:T(128)S(6)} %copy.61.refs_0_, bf16[1024,2304]{1,0:T(8,128)(2,1)} %project.1.refs_1_.refs_2_.refs_3_, bf16[1024,2304]{1,0:T(8,128)(2,1)} %project.1.refs_1_.refs_2_.refs_3_, ...), custom_call_target="tpu_custom_call", output_to_operand_aliasing={{0}: (7, {})} | custom-call | flops 300000000 | tf_op jit(solution)/shard_map/attend_back/pallas_call | solution.py:199
  239.2 2.6 fusion.48
  242.3 2.1 fusion.45
  247.9 1.9 collective-permute-start.25
  254.4 3.4 collective-permute-done.25
  257.9 3.2 collective-permute-done.24
  261.0 1.9 add_convert_fusion.10
  263.0 3.0 collective-permute-start.29
  270.1 2.4 collective-permute-done.29
  272.5 4.5 %collective-permute-done.28 = bf16[24,3072]{1,0:T(8,128)(2,1)S(1)} collective-permute-done((bf16[24,3072]{1,0:T(8,128)(2,1)S(1)}, bf16[24,3072]{1,0:T(8,128)(2,1)S(1)}, u32[]{:S(2)}, u32[]{:S(2)}) %collective-permute-start.28) | collective-permute-done | bytes 147488 | tf_op jit(solution)/shard_map/ppermute | solution.py:499
  284.6 3.9 %collective-permute-done.31 = bf16[96,1536]{1,0:T(8,128)(2,1)} collective-permute-done((bf16[96,1536]{1,0:T(8,128)(2,1)}, bf16[96,1536]{1,0:T(8,128)(2,1)}, u32[]{:S(2)}, u32[]{:S(2)}) %collective-permute-start.31) | collective-permute-done | bytes 294944 | tf_op jit(solution)/shard_map/ppermute | solution.py:499
  293.0 1.9 convert_add_fusion.3.refs_1_
  295.0 4.9 %collective-permute-done.32 = bf16[48,3072]{1,0:T(8,128)(2,1)S(1)} collective-permute-done((bf16[48,3072]{1,0:T(8,128)(2,1)S(1)}, bf16[48,3072]{1,0:T(8,128)(2,1)S(1)}, u32[]{:S(2)}, u32[]{:S(2)}) %collective-permute-start.32) | collective-permute-done | bytes 294944 | tf_op jit(solution)/shard_map/ppermute | solution.py:499
  300.4 1.9 convert_add_fusion.2.refs_5_
  302.9 3.0 adapt.2
  306.0 1.6 collective-permute-done.33
  309.0 2.4 adapt.3
  312.2 1.8 convolution_convert_fusion
  314.0 1.6 collective-permute-start.35
  319.5 2.6 collective-permute-done.36
  323.6 2.5 collective-permute-done.37
  327.0 2.5 add_bitcast_fusion
  331.6 2.6 renew.1
  (237 shorter events, 69.3 us)
Async XLA Ops:
  7.2 86.1 %all-gather.2.cloned.1.call-start = ((), (), s32[]{:S(2)}) async-start(), calls=%async_computation | async-start | bytes 6082560 | tf_op jit(solution)/shard_map/all_gather | solution.py:663
  11.7 9.8 %collective-permute-start = (bf16[24,2432]{1,0:T(8,128)(2,1)S(1)}, bf16[24,2432]{1,0:T(8,128)(2,1)S(1)}, u32[]{:S(2)}, u32[]{:S(2)}) collective-permute-start(bf16[24,2432]{1,0:T(8,128)(2,1)S(1)} %fusion.85), channel_id=1, source_target_pairs={{0,16},{1,17},{2,18},{3,19},{4,20},{5,21},{6,22},{7,23},{8,24},{9,... | collective-permute-start | bytes 350216 | tf_op jit(solution)/shard_map/ppermute | solution.py:499
  15.8 97.0 %copy-start.34 = (s32[768]{0:T(1024)}, s32[768]{0:T(1024)S(1)}, u32[]{:S(2)}) copy-start(s32[768]{0:T(1024)S(1)} %get-tuple-element.225) | copy-start | bytes 9220
  21.5 11.9 %collective-permute-start.2 = (bf16[96,768]{1,0:T(8,128)(2,1)S(1)}, bf16[96,768]{1,0:T(8,128)(2,1)S(1)}, u32[]{:S(2)}, u32[]{:S(2)}) collective-permute-start(bf16[96,768]{1,0:T(8,128)(2,1)S(1)} %convert_element_type.272), channel_id=1, source_target_pairs={{0,16},{1,17},{2,18},{3,19},{4,20},{5,21},{6,22},{7,23},{8,24},{9,... | collective-permute-start | bytes 442376 | tf_op jit(solution)/shard_map/ppermute | solution.py:499
  21.8 14.4 %collective-permute-start.1 = (bf16[48,2432]{1,0:T(8,128)(2,1)S(1)}, bf16[48,2432]{1,0:T(8,128)(2,1)S(1)}, u32[]{:S(2)}, u32[]{:S(2)}) collective-permute-start(bf16[48,2432]{1,0:T(8,128)(2,1)S(1)} %pad_maximum_fusion.18), channel_id=1, source_target_pairs={{0,8},{1,9},{2,10},{3,11},{4,12},{5,13},{6,14},{7,15},{8,0},{9,1},... | collective-permute-start | bytes 700424 | tf_op jit(solution)/shard_map/ppermute | solution.py:499
  36.3 7.1 %collective-permute-start.3 = (bf16[96,1152]{1,0:T(8,128)(2,1)S(1)}, bf16[96,1152]{1,0:T(8,128)(2,1)S(1)}, u32[]{:S(2)}, u32[]{:S(2)}) collective-permute-start(bf16[96,1152]{1,0:T(8,128)(2,1)S(1)} %slice.356), channel_id=1, source_target_pairs={{0,4},{1,5},{2,6},{3,7},{4,0},{5,1},{6,2},{7,3},{8,12},{9,13},{10,... | collective-permute-start | bytes 663560 | tf_op jit(solution)/shard_map/ppermute | solution.py:499
  37.9 7.2 %collective-permute-start.4 = (bf16[96,1280]{1,0:T(8,128)(2,1)S(1)}, bf16[96,1280]{1,0:T(8,128)(2,1)S(1)}, u32[]{:S(2)}, u32[]{:S(2)}) collective-permute-start(bf16[96,1280]{1,0:T(8,128)(2,1)S(1)} %slice.357), channel_id=1, source_target_pairs={{0,2},{1,3},{2,0},{3,1},{4,6},{5,7},{6,4},{7,5},{8,10},{9,11},{10,... | collective-permute-start | bytes 737288 | tf_op jit(solution)/shard_map/ppermute | solution.py:499
  39.5 10.5 %collective-permute-start.5 = (bf16[192,768]{1,0:T(8,128)(2,1)S(1)}, bf16[192,768]{1,0:T(8,128)(2,1)S(1)}, u32[]{:S(2)}, u32[]{:S(2)}) collective-permute-start(bf16[192,768]{1,0:T(8,128)(2,1)S(1)} %pad_maximum_fusion.17), channel_id=1, source_target_pairs={{0,8},{1,9},{2,10},{3,11},{4,12},{5,13},{6,14},{7,15},{8,0},{9,1},... | collective-permute-start | bytes 884744 | tf_op jit(solution)/shard_map/ppermute | solution.py:499
  50.9 10.2 %collective-permute-start.6 = (bf16[192,1152]{1,0:T(8,128)(2,1)S(1)}, bf16[192,1152]{1,0:T(8,128)(2,1)S(1)}, u32[]{:S(2)}, u32[]{:S(2)}) collective-permute-start(bf16[192,1152]{1,0:T(8,128)(2,1)S(1)} %pad_maximum_fusion.15), channel_id=1, source_target_pairs={{0,2},{1,3},{2,0},{3,1},{4,6},{5,7},{6,4},{7,5},{8,10},{9,11},{10,... | collective-permute-start | bytes 1327112 | tf_op jit(solution)/shard_map/ppermute | solution.py:499
  50.9 10.3 %collective-permute-start.7 = (bf16[192,1280]{1,0:T(8,128)(2,1)S(1)}, bf16[192,1280]{1,0:T(8,128)(2,1)S(1)}, u32[]{:S(2)}, u32[]{:S(2)}) collective-permute-start(bf16[192,1280]{1,0:T(8,128)(2,1)S(1)} %pad_maximum_fusion.13), channel_id=1, source_target_pairs={{0,4},{1,5},{2,6},{3,7},{4,0},{5,1},{6,2},{7,3},{8,12},{9,13},{10,... | collective-permute-start | bytes 1474568 | tf_op jit(solution)/shard_map/ppermute | solution.py:499
  61.2 9.9 %copy-start.1 = (bf16[384,1280]{1,0:T(8,128)(2,1)}, bf16[384,1280]{1,0:T(8,128)(2,1)S(1)}, u32[]{:S(2)}) copy-start(bf16[384,1280]{1,0:T(8,128)(2,1)S(1)} %pad_maximum_fusion.8.ra_ref) | copy-start | bytes 2949124
  61.2 3.9 %collective-permute-start.9 = (bf16[384,1280]{1,0:T(8,128)(2,1)S(1)}, bf16[384,1280]{1,0:T(8,128)(2,1)S(1)}, u32[]{:S(2)}, u32[]{:S(2)}) collective-permute-start(bf16[384,1280]{1,0:T(8,128)(2,1)S(1)} %pad_maximum_fusion.8.ra_ref), channel_id=1, source_target_pairs={{0,1},{1,0},{2,3},{3,2},{4,5},{5,4},{6,7},{7,6},{8,9},{9,8},{10,11... | collective-permute-start | bytes 2949128 | tf_op jit(solution)/shard_map/ppermute | solution.py:499
  61.3 3.8 %collective-permute-start.8 = (bf16[384,1152]{1,0:T(8,128)(2,1)S(1)}, bf16[384,1152]{1,0:T(8,128)(2,1)S(1)}, u32[]{:S(2)}, u32[]{:S(2)}) collective-permute-start(bf16[384,1152]{1,0:T(8,128)(2,1)S(1)} %pad_maximum_fusion.9.la_ref), channel_id=1, source_target_pairs={{0,1},{1,0},{2,3},{3,2},{4,5},{5,4},{6,7},{7,6},{8,9},{9,8},{10,11... | collective-permute-start | bytes 2654216 | tf_op jit(solution)/shard_map/ppermute | solution.py:499
  68.4 23.6 %collective-permute-start.11 = (bf16[384,384]{1,0:T(8,128)(2,1)S(1)}, bf16[384,384]{1,0:T(8,128)(2,1)S(1)}, u32[]{:S(2)}, u32[]{:S(2)}) collective-permute-start(bf16[384,384]{1,0:T(8,128)(2,1)S(1)} %get-tuple-element.219), channel_id=1, source_target_pairs={{0,2},{1,3},{2,0},{3,1},{4,6},{5,7},{6,4},{7,5},{8,10},{9,11},{10,... | collective-permute-start | bytes 884744 | tf_op jit(solution)/shard_map/ppermute | solution.py:499
  69.0 23.0 %collective-permute-start.10 = (bf16[384,384]{1,0:T(8,128)(2,1)S(1)}, bf16[384,384]{1,0:T(8,128)(2,1)S(1)}, u32[]{:S(2)}, u32[]{:S(2)}) collective-permute-start(bf16[384,384]{1,0:T(8,128)(2,1)S(1)} %get-tuple-element.220), channel_id=1, source_target_pairs={{0,4},{1,5},{2,6},{3,7},{4,0},{5,1},{6,2},{7,3},{8,12},{9,13},{10,... | collective-permute-start | bytes 884744 | tf_op jit(solution)/shard_map/ppermute | solution.py:499
  93.3 15.5 %collective-permute-start.12 = (bf16[768,384]{1,0:T(8,128)(2,1)S(1)}, bf16[768,384]{1,0:T(8,128)(2,1)S(1)}, u32[]{:S(2)}, u32[]{:S(2)}) collective-permute-start(bf16[768,384]{1,0:T(8,128)(2,1)S(1)} %pad_maximum_fusion.11), channel_id=1, source_target_pairs={{0,2},{1,3},{2,0},{3,1},{4,6},{5,7},{6,4},{7,5},{8,10},{9,11},{10,... | collective-permute-start | bytes 1769480 | tf_op jit(solution)/shard_map/ppermute | solution.py:499
  94.3 15.2 %collective-permute-start.13 = (bf16[768,384]{1,0:T(8,128)(2,1)S(1)}, bf16[768,384]{1,0:T(8,128)(2,1)S(1)}, u32[]{:S(2)}, u32[]{:S(2)}) collective-permute-start(bf16[768,384]{1,0:T(8,128)(2,1)S(1)} %pad_maximum_fusion.12), channel_id=1, source_target_pairs={{0,4},{1,5},{2,6},{3,7},{4,0},{5,1},{6,2},{7,3},{8,12},{9,13},{10,... | collective-permute-start | bytes 1769480 | tf_op jit(solution)/shard_map/ppermute | solution.py:499
  109.7 5.7 %collective-permute-start.14 = (bf16[1536,384]{1,0:T(8,128)(2,1)S(1)}, bf16[1536,384]{1,0:T(8,128)(2,1)}, u32[]{:S(2)}, u32[]{:S(2)}) collective-permute-start(bf16[1536,384]{1,0:T(8,128)(2,1)S(1)} %pad_maximum_fusion.2.refs_10_), channel_id=1, source_target_pairs={{0,1},{1,0},{2,3},{3,2},{4,5},{5,4},{6,7},{7,6},{8,9},{9,8},{10,11... | collective-permute-start | bytes 3538952 | tf_op jit(solution)/shard_map/ppermute | solution.py:499
  109.7 5.6 %collective-permute-start.15 = (bf16[1536,384]{1,0:T(8,128)(2,1)S(1)}, bf16[1536,384]{1,0:T(8,128)(2,1)}, u32[]{:S(2)}, u32[]{:S(2)}) collective-permute-start(bf16[1536,384]{1,0:T(8,128)(2,1)S(1)} %pad_maximum_fusion.3.refs_12_), channel_id=1, source_target_pairs={{0,1},{1,0},{2,3},{3,2},{4,5},{5,4},{6,7},{7,6},{8,9},{9,8},{10,11... | collective-permute-start | bytes 3538952 | tf_op jit(solution)/shard_map/ppermute | solution.py:499
  176.6 8.6 %collective-permute-start.16 = (bf16[384,3072]{1,0:T(8,128)(2,1)}, bf16[384,3072]{1,0:T(8,128)(2,1)}, u32[]{:S(2)}, u32[]{:S(2)}) collective-permute-start(bf16[384,3072]{1,0:T(8,128)(2,1)} %get-tuple-element.161), channel_id=1, source_target_pairs={{0,1},{1,0},{2,3},{3,2},{4,5},{5,4},{6,7},{7,6},{8,9},{9,8},{10,11... | collective-permute-start | bytes 7077896 | tf_op jit(solution)/shard_map/ppermute | solution.py:499
  176.8 8.4 %collective-permute-start.17 = (bf16[1536,768]{1,0:T(8,128)(2,1)}, bf16[1536,768]{1,0:T(8,128)(2,1)}, u32[]{:S(2)}, u32[]{:S(2)}) collective-permute-start(bf16[1536,768]{1,0:T(8,128)(2,1)} %get-tuple-element.162), channel_id=1, source_target_pairs={{0,1},{1,0},{2,3},{3,2},{4,5},{5,4},{6,7},{7,6},{8,9},{9,8},{10,11... | collective-permute-start | bytes 7077896 | tf_op jit(solution)/shard_map/ppermute | solution.py:499
  186.9 29.9 %collective-permute-start.19 = (bf16[768,768]{1,0:T(8,128)(2,1)S(1)}, bf16[768,768]{1,0:T(8,128)(2,1)}, u32[]{:S(2)}, u32[]{:S(2)}) collective-permute-start(bf16[768,768]{1,0:T(8,128)(2,1)S(1)} %add_convert_fusion), channel_id=1, source_target_pairs={{0,4},{1,5},{2,6},{3,7},{4,0},{5,1},{6,2},{7,3},{8,12},{9,13},{10,... | collective-permute-start | bytes 3538952 | tf_op jit(solution)/shard_map/ppermute | solution.py:499
  191.4 28.0 %collective-permute-start.18 = (bf16[192,3072]{1,0:T(8,128)(2,1)}, bf16[192,3072]{1,0:T(8,128)(2,1)}, u32[]{:S(2)}, u32[]{:S(2)}) collective-permute-start(bf16[192,3072]{1,0:T(8,128)(2,1)} %add_convert_fusion.1), channel_id=1, source_target_pairs={{0,2},{1,3},{2,0},{3,1},{4,6},{5,7},{6,4},{7,5},{8,10},{9,11},{10,... | collective-permute-start | bytes 3538952 | tf_op jit(solution)/shard_map/ppermute | solution.py:499
  224.2 14.5 %collective-permute-start.21 = (bf16[384,768]{1,0:T(8,128)(2,1)}, bf16[384,768]{1,0:T(8,128)(2,1)}, u32[]{:S(2)}, u32[]{:S(2)}) collective-permute-start(bf16[384,768]{1,0:T(8,128)(2,1)} %add_convert_fusion.4), channel_id=1, source_target_pairs={{0,2},{1,3},{2,0},{3,1},{4,6},{5,7},{6,4},{7,5},{8,10},{9,11},{10,... | collective-permute-start | bytes 1769480 | tf_op jit(solution)/shard_map/ppermute | solution.py:499
  225.0 14.2 %collective-permute-start.20 = (bf16[96,3072]{1,0:T(8,128)(2,1)}, bf16[96,3072]{1,0:T(8,128)(2,1)}, u32[]{:S(2)}, u32[]{:S(2)}) collective-permute-start(bf16[96,3072]{1,0:T(8,128)(2,1)} %add_convert_fusion.5), channel_id=1, source_target_pairs={{0,4},{1,5},{2,6},{3,7},{4,0},{5,1},{6,2},{7,3},{8,12},{9,13},{10,... | collective-permute-start | bytes 1769480 | tf_op jit(solution)/shard_map/ppermute | solution.py:499
  247.9 9.9 %collective-permute-start.25 = (bf16[192,768]{1,0:T(8,128)(2,1)S(1)}, bf16[192,768]{1,0:T(8,128)(2,1)S(1)}, u32[]{:S(2)}, u32[]{:S(2)}) collective-permute-start(bf16[192,768]{1,0:T(8,128)(2,1)S(1)} %add_convert_fusion.8), channel_id=1, source_target_pairs={{0,8},{1,9},{2,10},{3,11},{4,12},{5,13},{6,14},{7,15},{8,0},{9,1},... | collective-permute-start | bytes 884744 | tf_op jit(solution)/shard_map/ppermute | solution.py:499
  249.8 11.2 %collective-permute-start.24 = (bf16[48,3072]{1,0:T(8,128)(2,1)S(1)}, bf16[48,3072]{1,0:T(8,128)(2,1)S(1)}, u32[]{:S(2)}, u32[]{:S(2)}) collective-permute-start(bf16[48,3072]{1,0:T(8,128)(2,1)S(1)} %add_convert_fusion.9), channel_id=1, source_target_pairs={{0,8},{1,9},{2,10},{3,11},{4,12},{5,13},{6,14},{7,15},{8,0},{9,1},... | collective-permute-start | bytes 884744 | tf_op jit(solution)/shard_map/ppermute | solution.py:499
  250.2 10.8 %collective-permute-start.22 = (bf16[384,1536]{1,0:T(8,128)(2,1)S(1)}, bf16[384,1536]{1,0:T(8,128)(2,1)S(1)}, u32[]{:S(2)}, u32[]{:S(2)}) collective-permute-start(bf16[384,1536]{1,0:T(8,128)(2,1)S(1)} %pad_maximum_fusion.4), channel_id=1, source_target_pairs={{0,1},{1,0},{2,3},{3,2},{4,5},{5,4},{6,7},{7,6},{8,9},{9,8},{10,11... | collective-permute-start | bytes 3538952 | tf_op jit(solution)/shard_map/ppermute | solution.py:499
  250.3 10.7 %collective-permute-start.23 = (bf16[384,1536]{1,0:T(8,128)(2,1)S(1)}, bf16[384,1536]{1,0:T(8,128)(2,1)S(1)}, u32[]{:S(2)}, u32[]{:S(2)}) collective-permute-start(bf16[384,1536]{1,0:T(8,128)(2,1)S(1)} %pad_maximum_fusion.5), channel_id=1, source_target_pairs={{0,1},{1,0},{2,3},{3,2},{4,5},{5,4},{6,7},{7,6},{8,9},{9,8},{10,11... | collective-permute-start | bytes 3538952 | tf_op jit(solution)/shard_map/ppermute | solution.py:499
  257.9 9.7 %copy-start.23 = (bf16[192,768]{1,0:T(8,128)(2,1)}, bf16[192,768]{1,0:T(8,128)(2,1)S(1)}, u32[]{:S(2)}) copy-start(bf16[192,768]{1,0:T(8,128)(2,1)S(1)} %collective-permute-done.25) | copy-start | bytes 884740
  261.0 18.8 %copy-start.16 = (bf16[384,1536]{1,0:T(8,128)(2,1)}, bf16[384,1536]{1,0:T(8,128)(2,1)S(1)}, u32[]{:S(2)}) copy-start(bf16[384,1536]{1,0:T(8,128)(2,1)S(1)} %collective-permute-done.22) | copy-start | bytes 3538948
  261.0 19.6 %copy-start.17 = (bf16[384,1536]{1,0:T(8,128)(2,1)}, bf16[384,1536]{1,0:T(8,128)(2,1)S(1)}, u32[]{:S(2)}) copy-start(bf16[384,1536]{1,0:T(8,128)(2,1)S(1)} %collective-permute-done.23) | copy-start | bytes 3538948
  263.0 9.5 %collective-permute-start.29 = (bf16[96,768]{1,0:T(8,128)(2,1)S(1)}, bf16[96,768]{1,0:T(8,128)(2,1)S(1)}, u32[]{:S(2)}, u32[]{:S(2)}) collective-permute-start(bf16[96,768]{1,0:T(8,128)(2,1)S(1)} %add_convert_fusion.10), channel_id=1, source_target_pairs={{0,16},{1,17},{2,18},{3,19},{4,20},{5,21},{6,22},{7,23},{8,24},{9,... | collective-permute-start | bytes 442376 | tf_op jit(solution)/shard_map/ppermute | solution.py:499
  266.1 12.1 %collective-permute-start.27 = (bf16[192,1536]{1,0:T(8,128)(2,1)S(1)}, bf16[192,1536]{1,0:T(8,128)(2,1)S(1)}, u32[]{:S(2)}, u32[]{:S(2)}) collective-permute-start(bf16[192,1536]{1,0:T(8,128)(2,1)S(1)} %add_convert_fusion.2), channel_id=1, source_target_pairs={{0,4},{1,5},{2,6},{3,7},{4,0},{5,1},{6,2},{7,3},{8,12},{9,13},{10,... | collective-permute-start | bytes 1769480 | tf_op jit(solution)/shard_map/ppermute | solution.py:499
  267.5 12.3 %collective-permute-start.26 = (bf16[192,1536]{1,0:T(8,128)(2,1)S(1)}, bf16[192,1536]{1,0:T(8,128)(2,1)S(1)}, u32[]{:S(2)}, u32[]{:S(2)}) collective-permute-start(bf16[192,1536]{1,0:T(8,128)(2,1)S(1)} %add_convert_fusion.3), channel_id=1, source_target_pairs={{0,2},{1,3},{2,0},{3,1},{4,6},{5,7},{6,4},{7,5},{8,10},{9,11},{10,... | collective-permute-start | bytes 1769480 | tf_op jit(solution)/shard_map/ppermute | solution.py:499
  269.3 7.7 %collective-permute-start.28 = (bf16[24,3072]{1,0:T(8,128)(2,1)S(1)}, bf16[24,3072]{1,0:T(8,128)(2,1)S(1)}, u32[]{:S(2)}, u32[]{:S(2)}) collective-permute-start(bf16[24,3072]{1,0:T(8,128)(2,1)S(1)} %add_convert_fusion.11), channel_id=1, source_target_pairs={{0,16},{1,17},{2,18},{3,19},{4,20},{5,21},{6,22},{7,23},{8,24},{9,... | collective-permute-start | bytes 442376 | tf_op jit(solution)/shard_map/ppermute | solution.py:499
  272.5 9.0 %copy-start.28 = (bf16[96,768]{1,0:T(8,128)(2,1)}, bf16[96,768]{1,0:T(8,128)(2,1)S(1)}, u32[]{:S(2)}) copy-start(bf16[96,768]{1,0:T(8,128)(2,1)S(1)} %collective-permute-done.29) | copy-start | bytes 442372
  281.5 7.0 %collective-permute-start.31 = (bf16[96,1536]{1,0:T(8,128)(2,1)}, bf16[96,1536]{1,0:T(8,128)(2,1)}, u32[]{:S(2)}, u32[]{:S(2)}) collective-permute-start(bf16[96,1536]{1,0:T(8,128)(2,1)} %add_convert_fusion.6), channel_id=1, source_target_pairs={{0,2},{1,3},{2,0},{3,1},{4,6},{5,7},{6,4},{7,5},{8,10},{9,11},{10,... | collective-permute-start | bytes 884744 | tf_op jit(solution)/shard_map/ppermute | solution.py:499
  282.0 7.0 %collective-permute-start.30 = (bf16[96,1536]{1,0:T(8,128)(2,1)}, bf16[96,1536]{1,0:T(8,128)(2,1)}, u32[]{:S(2)}, u32[]{:S(2)}) collective-permute-start(bf16[96,1536]{1,0:T(8,128)(2,1)} %add_convert_fusion.7), channel_id=1, source_target_pairs={{0,4},{1,5},{2,6},{3,7},{4,0},{5,1},{6,2},{7,3},{8,12},{9,13},{10,... | collective-permute-start | bytes 884744 | tf_op jit(solution)/shard_map/ppermute | solution.py:499
  291.5 8.9 %copy-start.24 = (bf16[192,768]{1,0:T(8,128)(2,1)S(1)}, bf16[192,768]{1,0:T(8,128)(2,1)}, u32[]{:S(2)}) copy-start(bf16[192,768]{1,0:T(8,128)(2,1)} %copy-done.23) | copy-start | bytes 884740
  291.5 8.9 %copy-start.29 = (bf16[96,768]{1,0:T(8,128)(2,1)S(1)}, bf16[96,768]{1,0:T(8,128)(2,1)}, u32[]{:S(2)}) copy-start(bf16[96,768]{1,0:T(8,128)(2,1)} %copy-done.28) | copy-start | bytes 442372
  291.5 8.4 %collective-permute-start.32 = (bf16[48,3072]{1,0:T(8,128)(2,1)S(1)}, bf16[48,3072]{1,0:T(8,128)(2,1)S(1)}, u32[]{:S(2)}, u32[]{:S(2)}) collective-permute-start(bf16[48,3072]{1,0:T(8,128)(2,1)S(1)} %fusion.75), channel_id=1, source_target_pairs={{0,8},{1,9},{2,10},{3,11},{4,12},{5,13},{6,14},{7,15},{8,0},{9,1},... | collective-permute-start | bytes 884744 | tf_op jit(solution)/shard_map/ppermute | solution.py:499
  299.9 7.7 %collective-permute-start.33 = (bf16[24,3072]{1,0:T(8,128)(2,1)S(1)}, bf16[24,3072]{1,0:T(8,128)(2,1)S(1)}, u32[]{:S(2)}, u32[]{:S(2)}) collective-permute-start(bf16[24,3072]{1,0:T(8,128)(2,1)S(1)} %fusion.80), channel_id=1, source_target_pairs={{0,16},{1,17},{2,18},{3,19},{4,20},{5,21},{6,22},{7,23},{8,24},{9,... | collective-permute-start | bytes 442376 | tf_op jit(solution)/shard_map/ppermute | solution.py:499
  312.1 1.9 collective-permute-start.34
  314.0 4.1 %collective-permute-start.35 = (f32[80,128]{1,0:T(8,128)S(1)}, f32[80,128]{1,0:T(8,128)S(1)}, u32[]{:S(2)}, u32[]{:S(2)}) collective-permute-start(f32[80,128]{1,0:T(8,128)S(1)} %add.378), channel_id=1, source_target_pairs={{0,2},{1,3},{2,0},{3,1},{4,6},{5,7},{6,4},{7,5},{8,10},{9,11},{10,... | collective-permute-start | bytes 122888 | tf_op jit(solution)/shard_map/ppermute | solution.py:499
  318.1 4.0 %collective-permute-start.36 = (f32[80,128]{1,0:T(8,128)S(1)}, f32[80,128]{1,0:T(8,128)S(1)}, u32[]{:S(2)}, u32[]{:S(2)}) collective-permute-start(f32[80,128]{1,0:T(8,128)S(1)} %add.379), channel_id=1, source_target_pairs={{0,4},{1,5},{2,6},{3,7},{4,0},{5,1},{6,2},{7,3},{8,12},{9,13},{10,... | collective-permute-start | bytes 122888 | tf_op jit(solution)/shard_map/ppermute | solution.py:499
  322.1 4.0 %collective-permute-start.37 = (f32[80,128]{1,0:T(8,128)S(1)}, f32[80,128]{1,0:T(8,128)S(1)}, u32[]{:S(2)}, u32[]{:S(2)}) collective-permute-start(f32[80,128]{1,0:T(8,128)S(1)} %add.380), channel_id=1, source_target_pairs={{0,8},{1,9},{2,10},{3,11},{4,12},{5,13},{6,14},{7,15},{8,0},{9,1},... | collective-permute-start | bytes 122888 | tf_op jit(solution)/shard_map/ppermute | solution.py:499
  326.1 4.9 %collective-permute-start.38 = (f32[80,128]{1,0:T(8,128)S(1)}, f32[80,128]{1,0:T(8,128)S(1)}, u32[]{:S(2)}, u32[]{:S(2)}) collective-permute-start(f32[80,128]{1,0:T(8,128)S(1)} %add.381), channel_id=1, source_target_pairs={{0,16},{1,17},{2,18},{3,19},{4,20},{5,21},{6,22},{7,23},{8,24},{9,... | collective-permute-start | bytes 122888 | tf_op jit(solution)/shard_map/ppermute | solution.py:499
  (38 other events, 160.2 us)
Sparse Core Ops, SparseCore 0:
  11.8 81.3 all-gather.1

commit v4 on v3

--- a/solution.py
+++ b/solution.py
@@ -17,6 +17,7 @@
 STEP = 10
 MASKED = -1e9
 VMEM = 60 * 2**20
+ROOM = 24 * 2**20
 BF16 = jnp.bfloat16
 F32 = jnp.float32
 
@@ -63,7 +64,7 @@
         + [fixed(part.shape) for part in (*left, *right, bias)],
         out_specs=pl.BlockSpec((rows, 3 * D), lambda i: (i, 0)),
         out_shape=jax.ShapeDtypeStruct((seq, 3 * D), BF16),
-        compiler_params=pltpu.CompilerParams(vmem_limit_bytes=VMEM),
+        compiler_params=pltpu.CompilerParams(vmem_limit_bytes=ROOM),
         cost_estimate=cost(5),
         name="project",
     )(x_a, x_b, *left, *right, bias)
@@ -126,7 +127,7 @@
             jax.ShapeDtypeStruct((PAIRS, 2, seq), F32),
         ],
         input_output_aliases={4 + i: i for i in range(len(before))},
-        compiler_params=pltpu.CompilerParams(vmem_limit_bytes=VMEM),
+        compiler_params=pltpu.CompilerParams(vmem_limit_bytes=ROOM),
         cost_estimate=cost(4 * count),
         name="attend",
     )(lengths, packed, packed, packed, *extra)
@@ -222,7 +223,7 @@
             jax.ShapeDtypeStruct((count, 2, WIDE), F32),
         ],
         input_output_aliases={} if before is None else {7: 0},
-        compiler_params=pltpu.CompilerParams(vmem_limit_bytes=VMEM),
+        compiler_params=pltpu.CompilerParams(vmem_limit_bytes=ROOM),
         cost_estimate=cost(6 * count),
         name="attend_back",
     )(lengths, packed, packed, packed, dctx, ctxt, lse, *extra)
@@ -253,9 +254,10 @@
         copy.wait()
 
 
-def feed_kernel(pieces, steps, *refs):
+def feed_kernel(in_pieces, out_pieces, steps, *refs):
     len_ref, place_ref, where_ref, x_ref, ctx_ref, cot_ref, vec_ref, to_a_ref, to_b_ref = refs[:9]
-    attn_in_ref, parts, refs = refs[9], refs[10 : 10 + len(pieces)], refs[10 + len(pieces) :]
+    in_parts, refs = refs[9 : 9 + len(in_pieces)], refs[9 + len(in_pieces) :]
+    out_parts, refs = refs[: len(out_pieces)], refs[len(out_pieces) :]
     mixed_ref, dres1_ref, dctx_ref, sum_ref, *grads = refs[:10]
     out_grads, in_grads, attn_grads = grads[:2], grads[2:4], grads[4:6]
     w_ref, w2_ref, act_ref, dhid_ref, first_ref, ctxb_ref, dbr_ref, dres_ref = refs[10:18]
@@ -270,29 +272,30 @@
         return vec_ref[i : i + 1, :]
 
     def weight(c):
-        cols = slice(c * D, (c + 1) * D)
-        return w_ref.at[:, cols]
-
-    def load(c):
-        cols = slice(c * D, (c + 1) * D)
-        return pltpu.make_async_copy(attn_in_ref.at[:, cols], weight(c), in_sems.at[c])
-
-    def part_copies():
-        made = []
+        return w_ref.at[:, c * D : (c + 1) * D]
+
+    def part_copies(whole_ref, parts, pieces, sems):
+        made, total = [], 0
         for part, (first, count, column) in zip(parts, pieces):
             rows, width = part.shape[0] // count, part.shape[1]
+            columns = pl.ds(pl.multiple_of(place_ref[column] * 128, 128), width)
             for i in range(count):
                 where = pl.multiple_of(place_ref[first + i] * rows, rows)
-                target = w2_ref.at[pl.ds(where, rows), pl.ds(column, width)]
+                target = whole_ref.at[pl.ds(where, rows), columns]
                 source = part.at[pl.ds(i * rows, rows), :]
-                made.append(pltpu.make_async_copy(source, target, part_sems.at[len(made)]))
+                made.append(pltpu.make_async_copy(source, target, sems.at[total]))
+                total += 1
         return made
+
+    def in_weights():
+        return part_copies(w_ref, in_parts, in_pieces, in_sems)
+
+    def out_weights():
+        return part_copies(w2_ref, out_parts, out_pieces, part_sems)
 
     @pl.when(step == 0)
     def _():
-        for c in range(1 + CHUNKS):
-            load(c).start()
-        for copy in part_copies():
+        for copy in in_weights() + out_weights():
             copy.start()
         sum_ref[...] = jnp.zeros_like(sum_ref)
 
@@ -300,12 +303,10 @@
     def _():
         rows = pl.ds(pl.multiple_of(step * size, size), size)
 
-        def arrived(c):
-            @pl.when(step == 0)
-            def _():
-                load(c).wait()
-
-        arrived(0)
+        @pl.when(step == 0)
+        def _():
+            waited(in_weights())
+
         resid = x_ref[...].astype(F32) + (dot(ctx_ref[...], weight(0)[...]) + vec(2))
         unit1, inverse1 = norm_forward(resid)
         unit_ref[rows, :] = unit1
@@ -314,11 +315,10 @@
         first_b = first.astype(BF16)
         first_ref[rows, :] = arrange(first_b, to_a_ref[...])
         ctxb_ref[rows, :] = arrange(ctx_ref[...], to_b_ref[...])
-        for c in range(CHUNKS):
-            arrived(1 + c)
+
         @pl.when(step == 0)
         def _():
-            waited(part_copies())
+            waited(out_weights())
 
         branch = None
         for c in range(CHUNKS):
@@ -435,7 +435,8 @@
         waited(copies)
 
 
-def feed(lengths, x, ctx, cot, attn_in, vec, to_a, to_b, places, parts, pieces, where):
+def feed(lengths, x, ctx, cot, vec, to_a, to_b, places, where, in_side, out_side):
+    (in_parts, in_pieces), (out_parts, out_pieces) = in_side, out_side
     seq = x.shape[0]
     size = min(256, seq)
     steps = seq // size
@@ -453,13 +454,14 @@
 
     shape = jax.ShapeDtypeStruct
     return pl.pallas_call(
-        partial(feed_kernel, pieces, steps),
+        partial(feed_kernel, in_pieces, out_pieces, steps),
         grid_spec=pltpu.PrefetchScalarGridSpec(
             num_scalar_prefetch=3,
             grid=(2 * steps + 2 * CHUNKS + 1,),
             in_specs=[early(D)] * 3
             + [fixed((12, D)), fixed((D, D)), fixed((D, D))]
-            + [anywhere] * (1 + len(parts)),
+            + untouched(in_parts)
+            + untouched(out_parts),
             out_specs=[early(D), late(D), late(D), pl.BlockSpec((12, D), lambda i, *_: (0, 0))]
             + [anywhere] * 6,
             scratch_shapes=[
@@ -475,8 +477,8 @@
                 pltpu.VMEM((seq, 128), F32),
                 pltpu.VMEM((size, FF), F32),
                 pltpu.VMEM((2, D, D), BF16),
-                pltpu.SemaphoreType.DMA((1 + CHUNKS,)),
-                pltpu.SemaphoreType.DMA((sum(count for _, count, _ in pieces),)),
+                pltpu.SemaphoreType.DMA((sum(count for _, count, _ in in_pieces),)),
+                pltpu.SemaphoreType.DMA((sum(count for _, count, _ in out_pieces),)),
                 pltpu.SemaphoreType.DMA((2, max(2, where.shape[0] // CHUNKS))),
             ],
         ),
@@ -492,7 +494,7 @@
         compiler_params=pltpu.CompilerParams(vmem_limit_bytes=VMEM),
         cost_estimate=cost(50),
         name="feed",
-    )(lengths, places, where, x, ctx, cot, vec, to_a, to_b, attn_in, *parts)
+    )(lengths, places, where, x, ctx, cot, vec, to_a, to_b, *in_parts, *out_parts)
 
 
 def swap(value, bit, n):
@@ -547,13 +549,18 @@
 
 
 class Scatter:
-    def __init__(self, kept, away, bit, n):
-        self.terms, self.n = [kept, swap(away, bit, n)], n
+    def __init__(self, kept, got, n):
+        self.terms, self.n = [kept, got], n
+
+    def away(self):
+        half = self.terms[0].shape[0] // 2
+        return self.total([t[half:] for t in self.terms]).astype(BF16)
+
+    def send(self, away, bit):
+        self.terms = [t[: away.shape[0]] for t in self.terms] + [swap(away, bit, self.n)]
 
     def step(self, bit):
-        half = self.terms[0].shape[0] // 2
-        away = self.total([t[half:] for t in self.terms]).astype(BF16)
-        self.terms = [t[:half] for t in self.terms] + [swap(away, bit, self.n)]
+        self.send(self.away(), bit)
 
     def total(self, parts=None):
         parts = self.terms if parts is None else parts
@@ -655,68 +662,114 @@
     order_a, order_b = Order(far + [two, one, core]), Order(far + [one, two, core])
     x = frames[0]
 
+    aligned = rows_d % 8 == 0
     half = w_qkv.shape[1] // 2
     tail = jnp.pad(vectors.reshape(rows_d, 12), ((0, 0), (0, 116)))
     low_qkv = jnp.concatenate([w_qkv, tail], axis=1).astype(BF16)
-    low_qkv, w_first, w_second, w_third = phase(low_qkv, w_attn, w_in, w_out)
-    attn_in = jnp.concatenate([w_first, w_second], axis=1).astype(BF16)
-    attn_in = lax.all_gather(attn_in, "dp", axis=0, tiled=True)
-    qkv, out = Gather(low_qkv, n), Gather(w_third.astype(BF16), n)
-    to_a, to_b = order_a.matrix(), order_b.matrix()
+    low_qkv, *masters = phase(low_qkv, w_attn, w_in, w_out)
+    low_in = jnp.concatenate(masters[:2], axis=1).astype(BF16)
+    qkv, out = Gather(low_qkv, n), Gather(masters[2].astype(BF16), n)
+    to_a, to_b = phase(order_a.matrix(), order_b.matrix())
     x_a, x_b = arrange(x, to_a), arrange(x, to_b)
-    for bit in far:
+    inner = Gather(low_in, n)
+    if aligned:
+        side = low_in.shape[1] // 2
+        mine = own_bit(core)
+        kept = lax.dynamic_slice_in_dim(low_in, mine * side, side, 1)
+        got = swap(lax.dynamic_slice_in_dim(low_in, (1 - mine) * side, side, 1), core, n)
+        pair = [jnp.where(mine == 0, kept, got), jnp.where(mine == 0, got, kept)]
+        inner.value = jnp.concatenate(pair, axis=0)
+    else:
+        attn_in = lax.all_gather(low_in, "dp", axis=0, tiled=True)
+    qkv.step(far[0])
+    qkv.value, inner.value, x_a, x_b = phase(qkv.value, inner.value, x_a, x_b)
+    for bit in far[1:]:
         qkv.step(bit)
-        qkv.value, out.value, x_a, x_b = phase(qkv.value, out.value, x_a, x_b)
-        out.step(bit)
+        (qkv.value,) = phase(qkv.value)
     left, right = qkv.cut(0, half), qkv.cut(half, 2 * half + 128)
-    for bits in ((two, one), (one, two)):
+    for bits, more in (((two, one), far[:1]), ((one, two), far[1:])):
         left.step(bits[0])
         right.step(bits[1])
-        left.value, right.value, out.value = phase(left.value, right.value, out.value)
+        for bit in more if aligned else ():
+            inner.step(bit)
+        left.value, right.value, inner.value = phase(left.value, right.value, inner.value)
     left = (left.value, swap(left.value, core, n))
     right = (right.value, swap(right.value, core, n))
-    left, right, out.value = phase(left, right, out.value)
+    cut = 1024 if aligned else low_in.shape[1]
+    in_left, in_right = inner.cut(0, cut), inner.cut(cut, inner.value.shape[1])
+
+    def in_step(bit_left, bit_right):
+        if aligned:
+            in_left.step(bit_left)
+            in_right.step(bit_right)
+
+    left, right, in_left.value, in_right.value, out.value = phase(
+        left, right, in_left.value, in_right.value, out.value
+    )
+    in_step(two, one)
+    out.step(far[0])
     vec_rows = jnp.concatenate([part[:, half:] for part in right], axis=0)
     vec = dot(to_b, vec_rows)[:, :12].reshape(12, D)
     bias_qkv = jnp.concatenate([vec[:1], jnp.zeros((1, D), F32), vec[1:2]], axis=1)
 
+    packed = project(x_a, x_b, left, right, bias_qkv)
+    packed, vec, in_left.value, in_right.value, out.value = phase(
+        packed, vec, in_left.value, in_right.value, out.value
+    )
+    in_step(one, two)
+    for bit in far[1:]:
+        out.step(bit)
+    some = PAIRS // 3
+    heads = attend(lengths, packed, 0, some)
+    heads, out.value = phase(heads, out.value)
     out_left, out_right = out.cut(0, D // 2), out.cut(D // 2, D)
     out_left.step(two)
     out_right.step(one)
-    packed = project(x_a, x_b, left, right, bias_qkv)
-    some = PAIRS // 2
-    heads = attend(lengths, packed, 0, some)
-    heads, out_left.value, out_right.value, attn_in = phase(
-        heads, out_left.value, out_right.value, attn_in
+    heads = attend(lengths, packed, some, some, heads)
+    heads, out_left.value, out_right.value, in_left.value, in_right.value = phase(
+        heads, out_left.value, out_right.value, in_left.value, in_right.value
     )
     out_left.step(one)
     out_right.step(two)
-    heads = attend(lengths, packed, some, some, heads)
-    heads, out_left.value, out_right.value = phase(heads, out_left.value, out_right.value)
-    parts = [out_left.value, swap(out_left.value, core, n)]
-    parts += [out_right.value, swap(out_right.value, core, n)]
-    if rows_f % 16 == 0:
-        places = jnp.concatenate([order_a.places(n), order_b.places(n)])
-        pieces = tuple((i * n // 2, n // 2, i // 2 * (D // 2)) for i in range(4))
+    in_parts = [in_left.value, in_right.value]
+    if aligned:
+        in_parts += [swap(part, core, n) for part in in_parts]
+    heads = attend(lengths, packed, 2 * some, some, heads)
+    heads, out_left.value, out_right.value, in_parts = phase(
+        heads, out_left.value, out_right.value, in_parts
+    )
+    out_parts = [out_left.value, out_right.value]
+    out_parts += [swap(part, core, n) for part in out_parts]
+    if aligned:
+        chips_a, chips_b = [order.places(n // 2) // 2 for order in (order_a, order_b)]
+        blocks_a, blocks_b = order_a.places(n), order_b.places(n)
+        first = jnp.stack([mine, 1 - mine]) * (side // 128)
+        corners = jnp.stack([first, first + cut // 128], axis=1).reshape(4)
+        columns = jnp.array([0, D // 256], jnp.int32)
+        places = jnp.concatenate([chips_a, chips_b, blocks_a, blocks_b, corners, columns])
+        base = 3 * n
+        in_pieces = tuple((i % 2 * n // 2, n // 2, base + i) for i in range(4))
+        out_pieces = tuple((n + i % 2 * n + i // 2 * n // 2, n // 2, base + 4 + i % 2) for i in range(4))
     else:
         sides = []
-        for i, order in ((0, order_a), (2, order_b)):
-            side = jnp.concatenate(parts[i : i + 2], axis=0).reshape(n, rows_f, D // 2)
-            sides.append(side[jnp.argsort(order.places(n))].reshape(FF, D // 2))
-        parts = [jnp.concatenate(sides, axis=1)]
-        places, pieces = jnp.zeros((1,), jnp.int32), ((0, 1, 0),)
+        for i, order in enumerate((order_a, order_b)):
+            value = jnp.concatenate(out_parts[i::2], axis=0).reshape(n, rows_f, D // 2)
+            sides.append(value[jnp.argsort(order.places(n))].reshape(FF, D // 2))
+        in_parts, out_parts = [attn_in], [jnp.concatenate(sides, axis=1)]
+        places = jnp.zeros((2,), jnp.int32)
+        in_pieces = out_pieces = ((0, 1, 1),)
     ctx, ctxt, lse = heads
 
-    aligned = rows_f % 16 == 0
     where = order_b.where() if aligned else jnp.arange(CHUNKS, dtype=jnp.int32)
     mixed, dres1, dctx, sums, *grads = feed(
-        lengths, x, ctx, cotangent[0], attn_in, vec, to_a, to_b, places, parts, pieces, where
+        *(lengths, x, ctx, cotangent[0], vec, to_a, to_b, places, where),
+        *((in_parts, in_pieces), (out_parts, out_pieces)),
     )
     if not aligned:
         grad = jnp.concatenate(grads[:2], axis=0).reshape(n, rows_f, D)
         grads[:2] = jnp.split(grad[order_b.places(n)].reshape(FF, D), 2)
-    sum_out = Scatter(*grads[:2], core, n)
-    sum_in = Scatter(*grads[2:4], core, n)
+    sum_out = Scatter(grads[0], swap(grads[1], core, n), n)
+    sum_in = Scatter(grads[2], swap(grads[3], core, n), n)
 
     dqkv, biases = None, []
     for first, count, bits in ((0, 1, (one, two)), (1, 4, (two, one)), (5, 1, None)):
@@ -728,8 +781,15 @@
             )
             sum_in.step(bits[0])
             sum_out.step(bits[1])
-    dqkv, sum_in.terms[-1], sum_out.terms[-1] = phase(
-        dqkv, sum_in.terms[-1], sum_out.terms[-1]
+    full_qkv = jnp.concatenate(
+        [
+            arrange(to_a, jnp.concatenate(left, axis=0)),
+            arrange(to_b, jnp.concatenate([part[:, :half] for part in right], axis=0)),
+        ],
+        axis=1,
+    )
+    dqkv, full_qkv, sum_in.terms[-1], sum_out.terms[-1] = phase(
+        dqkv, full_qkv, sum_in.terms[-1], sum_out.terms[-1]
     )
 
     def late_grads(side):
@@ -742,41 +802,43 @@
         )
 
     away_a, away_b = late_grads(1)
-    away_a, away_b, dqkv = phase(away_a, away_b, dqkv)
+    away_a, away_b, dqkv, away_in, away_out = phase(
+        away_a, away_b, dqkv, sum_in.away(), sum_out.away()
+    )
+    got_a, got_b = swap(away_a, core, n), swap(away_b, core, n)
+    sum_in.send(away_in, others[0])
+    sum_out.send(away_out, others[0])
     kept_a, kept_b = late_grads(0)
-    late_a, late_b = Scatter(kept_a, away_a, core, n), Scatter(kept_b, away_b, core, n)
-    sum_in.step(others[0])
-    sum_out.step(others[0])
-    late_a.terms, late_b.terms, sum_in.terms[-1], sum_out.terms[-1] = phase(
-        late_a.terms, late_b.terms, sum_in.terms[-1], sum_out.terms[-1]
-    )
+    got_a, got_b, kept_a, kept_b = phase(got_a, got_b, kept_a, kept_b)
+    late_a, late_b = Scatter(kept_a, got_a, n), Scatter(kept_b, got_b, n)
     late_a.step(one)
     late_b.step(two)
-    for bit in others[1:]:
+    late_a.terms[-1], late_b.terms[-1], sum_in.terms[-1], sum_out.terms[-1] = phase(
+        late_a.terms[-1], late_b.terms[-1], sum_in.terms[-1], sum_out.terms[-1]
+    )
+    away_a, away_b, *aways = phase(
+        late_a.away(), late_b.away(), *((sum_in.away(), sum_out.away()) if others[1:] else ())
+    )
+    late_a.send(away_a, two)
+    late_b.send(away_b, one)
+    for bit in others[1:2]:
+        sum_in.send(aways[0], bit)
+        sum_out.send(aways[1], bit)
+    for bit in others[2:]:
         sum_in.step(bit)
         sum_out.step(bit)
-    late_a.terms[-1], late_b.terms[-1], sum_in.terms[-1], sum_out.terms[-1] = phase(
-        late_a.terms[-1], late_b.terms[-1], sum_in.terms[-1], sum_out.terms[-1]
-    )
-    late_a.step(two)
-    late_b.step(one)
     late_a.terms[-1], late_b.terms[-1] = phase(late_a.terms[-1], late_b.terms[-1])
+    late = late_a.join(late_b)
+    late.step(others[0])
     share_in, share_out = sum_in.total(), sum_out.total()
-    late = late_a.join(late_b)
-    for bit in others:
+    late.terms[-1], share_in, share_out = phase(late.terms[-1], share_in, share_out)
+    for bit in others[1:]:
         late.step(bit)
     share_late = late.total()
     bias_sums = jnp.concatenate(biases, axis=0)
     grad_vec = jnp.concatenate(
         [bias_sums[:, 0].reshape(1, D), bias_sums[:, 1].reshape(1, D), sums[2:]]
     ).reshape(-1, 128)
-    full_qkv = jnp.concatenate(
-        [
-            arrange(to_a, jnp.concatenate(left, axis=0)),
-            arrange(to_b, jnp.concatenate([part[:, :half] for part in right], axis=0)),
-        ],
-        axis=1,
-    )
     input_grad = dres1
     for i in range(3):
         input_grad = input_grad + dot_nt(dqkv[i], full_qkv[:, i * D : (i + 1) * D])

time: 349 us -> 333 us (0.954)
  other arithmetic: 38.2 us -> 22.1 us
  between operations: 15.9 us -> 2.73 us
  Pallas kernels: 143 us -> 133 us
  local copies, waits for them, and re-layouts: 12.8 us -> 22.3 us
  waiting for transfers between devices: 74.8 us -> 83.5 us
  starting transfers between devices: 35.7 us -> 42.8 us
    convert_element_type x14, other arithmetic: 17.2 us -> 4.46 us  [the longest x13 3.79 us: away(): return self.total([t[half:] for t in self.terms]).astype(BF16)]
    unnamed x91 -> x89, local copies, waits for them, and re-layouts: 3.7 us -> 14.4 us
    ppermute x39 -> x48, waiting for transfers between devices: 73.7 us -> 83.5 us  [swap(): return lax.ppermute(value, 'dp', [(i, i ^ 1 << bit) for i in range(n)])]
    ppermute x39 -> x48, starting transfers between devices: 35.6 us -> 42.8 us  [swap(): return lax.ppermute(value, 'dp', [(i, i ^ 1 << bit) for i in range(n)])]
    pallas_call x3, Pallas kernels: 40.4 us -> 34.7 us  [attend_back(): pl.pallas_call(after(partial(attend_back_kernel, min(512, seq)), 7, len(e...]
    concatenate x12 -> x18, other arithmetic: 1.49 us -> 6.97 us  [step(): jnp.concatenate([self.value, swap(self.value, bit, self.n)], axis=0)]
    add x5, other arithmetic: 6.36 us -> 1.96 us  [total(): result = result + part.astype(F32)]
    pallas_call x1, Pallas kernels: 8.57 us -> 4.63 us  [project(): pl.pallas_call(project_kernel, grid=(seq // rows,), in_specs=[pl.BlockSpe...]
  transfers between devices with their start and end apart: 40 -> 48, of which waited for: 28 -> 28; matrix products, arithmetic and copies ran while one was open for 12% -> 12% of each run, Pallas kernels for 22% -> 20%
where the time goes in v4:
time: 333 us; the launch traced here: 328 us
  Pallas kernels  133 us (40%)
  waiting for transfers between devices  83.5 us (25%)
  starting transfers between devices  42.8 us (13%)
  local copies, waits for them, and re-layouts  22.3 us (7%)
  other arithmetic  22.1 us (7%)
  matrix products  22.1 us (7%)
    ppermute x48, waiting for transfers between devices, swap(): return lax.ppermute(value, 'dp', [(i, i ^ 1 << bit) for i in range(n)])  83.5 us
    pallas_call x1, Pallas kernels, feed(): pl.pallas_call(partial(feed_kernel, in_pieces, out_pieces, steps), grid_s...  63.6 us
    ppermute x48, starting transfers between devices, swap(): return lax.ppermute(value, 'dp', [(i, i ^ 1 << bit) for i in range(n)])  42.8 us
    pallas_call x3, Pallas kernels, attend_back(): pl.pallas_call(after(partial(attend_back_kernel, min(512, seq)), 7, len(e...  34.7 us
    pallas_call x3, Pallas kernels, attend(): pl.pallas_call(after(attend_kernel, 4, len(extra)), grid_spec=pltpu.Prefe...  21.6 us
    unnamed x89, local copies, waits for them, and re-layouts  14.4 us
    dot_general x5, matrix products, dot(): return jnp.dot(a, b, preferred_element_type=F32)  9.08 us
    dot_general x3, matrix products, dot_nt(): lax.dot_general(a, b, (((1,), (1,)), ((), ())), preferred_element_type=F32)  8.08 us
  transfers between devices with their start and end apart: 48, of which 28 were waited for; matrix products, arithmetic and copies ran while one was open for 12% of the time, Pallas kernels for 20%

profile of v4, /device:TPU:0, one launch (start us, length us, event | category | flops | bytes accessed | tf_op | source)
XLA Modules:
  0.0 328.0 jit_solution(6823405546194613188)
XLA Ops:
  2.4 4.1 %collective-permute-start = (bf16[24,2432]{1,0:T(8,128)(2,1)S(1)}, bf16[24,2432]{1,0:T(8,128)(2,1)S(1)}, u32[]{:S(2)}, u32[]{:S(2)}) collective-permute-start(bf16[24,2432]{1,0:T(8,128)(2,1)S(1)} %fusion.78), channel_id=1, source_target_pairs={{0,16},{1,17},{2,18},{3,19},{4,20},{5,21},{6,22},{7,23},{8,24},{9,... | collective-permute-start | bytes 350216 | tf_op jit(solution)/shard_map/ppermute | solution.py:501
  9.6 2.5 fusion.29.xa_ref
  12.1 2.6 fusion.30.xb_ref
  14.8 1.6 collective-permute-start.2
  16.8 8.6 %collective-permute-done.2 = bf16[48,2432]{1,0:T(8,128)(2,1)S(1)} collective-permute-done((bf16[48,2432]{1,0:T(8,128)(2,1)S(1)}, bf16[48,2432]{1,0:T(8,128)(2,1)S(1)}, u32[]{:S(2)}, u32[]{:S(2)}) %collective-permute-start.2) | collective-permute-done | bytes 233504 | tf_op jit(solution)/shard_map/ppermute | solution.py:501
  25.5 1.7 collective-permute-start.3
  28.8 3.8 %collective-permute-done.3 = bf16[96,1152]{1,0:T(8,128)(2,1)S(1)} collective-permute-done((bf16[96,1152]{1,0:T(8,128)(2,1)S(1)}, bf16[96,1152]{1,0:T(8,128)(2,1)S(1)}, u32[]{:S(2)}, u32[]{:S(2)}) %collective-permute-start.3) | collective-permute-done | bytes 221216 | tf_op jit(solution)/shard_map/ppermute | solution.py:501
  32.7 1.9 collective-permute-done.4
  34.7 1.6 collective-permute-start.6
  36.7 6.9 %collective-permute-done.8 = bf16[96,1920]{1,0:T(8,128)(2,1)S(1)} collective-permute-done((bf16[96,1920]{1,0:T(8,128)(2,1)S(1)}, bf16[96,1920]{1,0:T(8,128)(2,1)S(1)}, u32[]{:S(2)}, u32[]{:S(2)}) %collective-permute-start.8) | collective-permute-done | bytes 368672 | tf_op jit(solution)/shard_map/ppermute | solution.py:501
  43.7 1.6 collective-permute-done.6
  45.4 2.2 collective-permute-done.7
  52.6 2.9 collective-permute-start.13
  62.7 4.6 %project.1.refs_1_.refs_2_.refs_3_ = bf16[1024,2304]{1,0:T(8,128)(2,1)S(1)} custom-call(bf16[1024,768]{1,0:T(8,128)(2,1)S(1)} %copy-done.11, bf16[1024,768]{1,0:T(8,128)(2,1)S(1)} %copy-done.13, bf16[384,1152]{1,0:T(8,128)(2,1)S(1)} %pad_maximum_fusion.10.la_ref, bf16[384,1152]{1,0:T(8,128)(2,1)S(1)} %copy-done.16, ...), custom_call_target="tpu_custom_call" | custom-call | flops 250000000 | tf_op jit(solution)/shard_map/project/pallas_call | solution.py:60
  68.5 1.6 pad_maximum_fusion.13
  72.4 1.6 collective-permute-start.18
  75.5 7.2 %attend.3 = (bf16[1024,768]{1,0:T(8,128)(2,1)S(1)}, f32[768,1024]{1,0:T(8,128)S(1)}, f32[6,2,1024]{2,1,0:T(2,128)S(1)}) custom-call(s32[1]{0:T(128)S(6)} %copy.68.refs_0_, bf16[1024,2304]{1,0:T(8,128)(2,1)S(1)} %project.1.refs_1_.refs_2_.refs_3_, bf16[1024,2304]{1,0:T(8,128)(2,1)S(1)} %project.1.refs_1_.refs_2_.refs_3_, ...), custom_call_target="tpu_custom_call" | custom-call | flops 400000000 | tf_op jit(solution)/shard_map/attend/pallas_call | solution.py:108
  83.9 7.2 %attend.4 = (bf16[1024,768]{1,0:T(8,128)(2,1)S(1)}, f32[768,1024]{1,0:T(8,128)S(1)}, f32[6,2,1024]{2,1,0:T(2,128)S(1)}) custom-call(s32[1]{0:T(128)S(6)} %copy.68.refs_0_, bf16[1024,2304]{1,0:T(8,128)(2,1)S(1)} %project.1.refs_1_.refs_2_.refs_3_, ...), custom_call_target="tpu_custom_call", output_to_operand_aliasing={{0}: (4, {}), {1}: (5, {}), {2}: (6, {})} | custom-call | flops 400000000 | tf_op jit(solution)/shard_map/attend/pallas_call | solution.py:108
  91.2 7.3 %collective-permute-done.16 = bf16[384,384]{1,0:T(8,128)(2,1)S(1)} collective-permute-done((bf16[384,384]{1,0:T(8,128)(2,1)S(1)}, bf16[384,384]{1,0:T(8,128)(2,1)S(1)}, u32[]{:S(2)}, u32[]{:S(2)}) %collective-permute-start.16) | collective-permute-done | bytes 294944 | tf_op jit(solution)/shard_map/ppermute | solution.py:501
  101.9 7.2 %attend.5 = (bf16[1024,768]{1,0:T(8,128)(2,1)S(1)}, f32[768,1024]{1,0:T(8,128)S(1)}, f32[6,2,1024]{2,1,0:T(2,128)S(1)}) custom-call(s32[1]{0:T(128)S(6)} %copy.68.refs_0_, bf16[1024,2304]{1,0:T(8,128)(2,1)S(1)} %project.1.refs_1_.refs_2_.refs_3_, ...), custom_call_target="tpu_custom_call", output_to_operand_aliasing={{0}: (4, {}), {1}: (5, {}), {2}: (6, {})} | custom-call | flops 400000000 | tf_op jit(solution)/shard_map/attend/pallas_call | solution.py:108
  109.2 6.5 %collective-permute-done.19 = bf16[768,384]{1,0:T(8,128)(2,1)S(1)} collective-permute-done((bf16[768,384]{1,0:T(8,128)(2,1)S(1)}, bf16[768,384]{1,0:T(8,128)(2,1)S(1)}, u32[]{:S(2)}, u32[]{:S(2)}) %collective-permute-start.19) | collective-permute-done | bytes 589856 | tf_op jit(solution)/shard_map/ppermute | solution.py:501
  122.8 1.7 collective-permute-done.24.refs_16_
  124.5 63.6 %feed.1 = (bf16[1024,768]{1,0:T(8,128)(2,1)}, f32[1024,768]{1,0:T(8,128)}, bf16[1024,768]{1,0:T(8,128)(2,1)}, f32[12,768]{1,0:T(8,128)}, bf16[1536,768]{1,0:T(8,...) custom-call(s32[1]{0:T(128)S(6)} %copy.68.refs_0_, ...), custom_call_target="tpu_custom_call" | custom-call | flops 2500000000 | tf_op jit(solution)/shard_map/feed/pallas_call | solution.py:456
  188.7 2.3 copy-done.1
  192.4 5.6 %attend_back.3 = (bf16[3,1024,768]{2,1,0:T(8,128)(2,1)S(1)}, f32[1,2,128]{2,1,0:T(2,128)S(1)}) custom-call(s32[1]{0:T(128)S(6)} %copy.68.refs_0_, bf16[1024,2304]{1,0:T(8,128)(2,1)S(1)} %copy-done.1, bf16[1024,2304]{1,0:T(8,128)(2,1)S(1)} %copy-done.1, bf16[1024,2304]{1,0:T(8,128)(2,1)S(1)} %copy-done.1, bf16[1024,768]{1,0:T(8,128)(2,1)S(1)} %copy-done.3, ...), custom_call_target="tpu_custom_call" | custom-call | flops 300000000 | tf_op jit(solution)/shard_map/attend_back/pallas_call | solution.py:200
  202.1 1.7 convolution_convert_fusion.1
  203.8 23.4 %attend_back.4 = (bf16[3,1024,768]{2,1,0:T(8,128)(2,1)S(1)}, f32[4,2,128]{2,1,0:T(2,128)S(1)}) custom-call(s32[1]{0:T(128)S(6)} %copy.68.refs_0_, bf16[1024,2304]{1,0:T(8,128)(2,1)S(1)} %copy-done.1, bf16[1024,2304]{1,0:T(8,128)(2,1)S(1)} %copy-done.1, bf16[1024,2304]{1,0:T(8,128)(2,1)S(1)} %copy-done.1, ...), custom_call_target="tpu_custom_call", output_to_operand_aliasing={{0}: (7, {})} | custom-call | flops 1200000000 | tf_op jit(solution)/shard_map/attend_back/pallas_call | solution.py:200
  232.3 1.7 convolution_convert_fusion
  234.0 2.1 pad_maximum_fusion
  236.1 5.7 %attend_back.5 = (bf16[3,1024,768]{2,1,0:T(8,128)(2,1)S(1)}, f32[1,2,128]{2,1,0:T(2,128)S(1)}) custom-call(s32[1]{0:T(128)S(6)} %copy.68.refs_0_, bf16[1024,2304]{1,0:T(8,128)(2,1)S(1)} %bitcast.65, bf16[1024,2304]{1,0:T(8,128)(2,1)S(1)} %bitcast.65, bf16[1024,2304]{1,0:T(8,128)(2,1)S(1)} %bitcast.65, ...), custom_call_target="tpu_custom_call", output_to_operand_aliasing={{0}: (7, {})} | custom-call | flops 300000000 | tf_op jit(solution)/shard_map/attend_back/pallas_call | solution.py:200
  241.7 3.4 %collective-permute-done.30 = bf16[384,768]{1,0:T(8,128)(2,1)S(1)} collective-permute-done((bf16[384,768]{1,0:T(8,128)(2,1)}, bf16[384,768]{1,0:T(8,128)(2,1)S(1)}, u32[]{:S(2)}, u32[]{:S(2)}) %collective-permute-start.30) | collective-permute-done | bytes 589856 | tf_op jit(solution)/shard_map/ppermute | solution.py:501
  256.5 1.7 collective-permute-start.35
  258.5 7.9 %collective-permute-done.35 = bf16[48,3072]{1,0:T(8,128)(2,1)S(1)} collective-permute-done((bf16[48,3072]{1,0:T(8,128)(2,1)S(1)}, bf16[48,3072]{1,0:T(8,128)(2,1)S(1)}, u32[]{:S(2)}, u32[]{:S(2)}) %collective-permute-start.35) | collective-permute-done | bytes 294944 | tf_op jit(solution)/shard_map/ppermute | solution.py:501
  266.4 4.9 %collective-permute-done.36 = bf16[192,768]{1,0:T(8,128)(2,1)S(1)} collective-permute-done((bf16[192,768]{1,0:T(8,128)(2,1)S(1)}, bf16[192,768]{1,0:T(8,128)(2,1)S(1)}, u32[]{:S(2)}, u32[]{:S(2)}) %collective-permute-start.36) | collective-permute-done | bytes 294944 | tf_op jit(solution)/shard_map/ppermute | solution.py:501
  271.7 1.8 collective-permute-start.37
  276.4 1.5 collective-permute-start.41
  281.2 1.7 collective-permute-start.39
  282.9 4.5 %collective-permute-done.40 = bf16[24,3072]{1,0:T(8,128)(2,1)S(1)} collective-permute-done((bf16[24,3072]{1,0:T(8,128)(2,1)S(1)}, bf16[24,3072]{1,0:T(8,128)(2,1)S(1)}, u32[]{:S(2)}, u32[]{:S(2)}) %collective-permute-start.40) | collective-permute-done | bytes 147488 | tf_op jit(solution)/shard_map/ppermute | solution.py:501
  290.2 2.6 collective-permute-done.39
  293.5 3.0 adapt.2
  296.5 2.9 collective-permute-done.42
  300.8 2.4 adapt.3
  305.1 1.7 collective-permute-start.44
  306.8 2.3 collective-permute-done.44
  309.9 3.5 %fusion.14 = f32[1024,768]{1,0:T(8,128)S(1)} fusion(bf16[3,1024,768]{2,1,0:T(8,128)(2,1)} %copy-done.2, bf16[768,2304]{1,0:T(8,128)(2,1)} %pad_maximum_fusion), kind=kOutput, calls=%fused_computation.25 | convolution fusion | flops 1207959552 | bytes 5898240 | tf_op jit(solution)/shard_map/dot_general | solution.py:30
  315.0 2.5 collective-permute-done.46
  318.3 3.1 add_bitcast_fusion
  323.0 2.6 renew.1
  (266 shorter events, 78.0 us)
Async XLA Ops:
  2.4 12.3 %collective-permute-start = (bf16[24,2432]{1,0:T(8,128)(2,1)S(1)}, bf16[24,2432]{1,0:T(8,128)(2,1)S(1)}, u32[]{:S(2)}, u32[]{:S(2)}) collective-permute-start(bf16[24,2432]{1,0:T(8,128)(2,1)S(1)} %fusion.78), channel_id=1, source_target_pairs={{0,16},{1,17},{2,18},{3,19},{4,20},{5,21},{6,22},{7,23},{8,24},{9,... | collective-permute-start | bytes 350216 | tf_op jit(solution)/shard_map/ppermute | solution.py:501
  8.6 6.1 %collective-permute-start.1 = (bf16[24,1920]{1,0:T(8,128)(2,1)S(1)}, bf16[24,1920]{1,0:T(8,128)(2,1)S(1)}, u32[]{:S(2)}, u32[]{:S(2)}) collective-permute-start(bf16[24,1920]{1,0:T(8,128)(2,1)S(1)} %fusion.79), channel_id=1, source_target_pairs={{0,1},{1,0},{2,3},{3,2},{4,5},{5,4},{6,7},{7,6},{8,9},{9,8},{10,11... | collective-permute-start | bytes 276488 | tf_op jit(solution)/shard_map/ppermute | solution.py:501
  14.8 10.6 %collective-permute-start.2 = (bf16[48,2432]{1,0:T(8,128)(2,1)S(1)}, bf16[48,2432]{1,0:T(8,128)(2,1)S(1)}, u32[]{:S(2)}, u32[]{:S(2)}) collective-permute-start(bf16[48,2432]{1,0:T(8,128)(2,1)S(1)} %pad_maximum_fusion.23), channel_id=1, source_target_pairs={{0,8},{1,9},{2,10},{3,11},{4,12},{5,13},{6,14},{7,15},{8,0},{9,1},... | collective-permute-start | bytes 700424 | tf_op jit(solution)/shard_map/ppermute | solution.py:501
  16.4 12.3 %collective-permute-start.5 = (bf16[48,1920]{1,0:T(8,128)(2,1)S(1)}, bf16[48,1920]{1,0:T(8,128)(2,1)S(1)}, u32[]{:S(2)}, u32[]{:S(2)}) collective-permute-start(bf16[48,1920]{1,0:T(8,128)(2,1)S(1)} %pad_maximum_fusion.24), channel_id=1, source_target_pairs={{0,16},{1,17},{2,18},{3,19},{4,20},{5,21},{6,22},{7,23},{8,24},{9,... | collective-permute-start | bytes 552968 | tf_op jit(solution)/shard_map/ppermute | solution.py:501
  25.5 7.1 %collective-permute-start.3 = (bf16[96,1152]{1,0:T(8,128)(2,1)S(1)}, bf16[96,1152]{1,0:T(8,128)(2,1)S(1)}, u32[]{:S(2)}, u32[]{:S(2)}) collective-permute-start(bf16[96,1152]{1,0:T(8,128)(2,1)S(1)} %slice.457), channel_id=1, source_target_pairs={{0,4},{1,5},{2,6},{3,7},{4,0},{5,1},{6,2},{7,3},{8,12},{9,13},{10,... | collective-permute-start | bytes 663560 | tf_op jit(solution)/shard_map/ppermute | solution.py:501
  27.3 7.3 %collective-permute-start.4 = (bf16[96,1280]{1,0:T(8,128)(2,1)S(1)}, bf16[96,1280]{1,0:T(8,128)(2,1)S(1)}, u32[]{:S(2)}, u32[]{:S(2)}) collective-permute-start(bf16[96,1280]{1,0:T(8,128)(2,1)S(1)} %slice.458), channel_id=1, source_target_pairs={{0,2},{1,3},{2,0},{3,1},{4,6},{5,7},{6,4},{7,5},{8,10},{9,11},{10,... | collective-permute-start | bytes 737288 | tf_op jit(solution)/shard_map/ppermute | solution.py:501
  34.6 9.1 %collective-permute-start.8 = (bf16[96,1920]{1,0:T(8,128)(2,1)S(1)}, bf16[96,1920]{1,0:T(8,128)(2,1)S(1)}, u32[]{:S(2)}, u32[]{:S(2)}) collective-permute-start(bf16[96,1920]{1,0:T(8,128)(2,1)S(1)} %pad_maximum_fusion.20), channel_id=1, source_target_pairs={{0,8},{1,9},{2,10},{3,11},{4,12},{5,13},{6,14},{7,15},{8,0},{9,1},... | collective-permute-start | bytes 1105928 | tf_op jit(solution)/shard_map/ppermute | solution.py:501
  34.7 10.7 %collective-permute-start.6 = (bf16[192,1152]{1,0:T(8,128)(2,1)S(1)}, bf16[192,1152]{1,0:T(8,128)(2,1)S(1)}, u32[]{:S(2)}, u32[]{:S(2)}) collective-permute-start(bf16[192,1152]{1,0:T(8,128)(2,1)S(1)} %pad_maximum_fusion.19), channel_id=1, source_target_pairs={{0,2},{1,3},{2,0},{3,1},{4,6},{5,7},{6,4},{7,5},{8,10},{9,11},{10,... | collective-permute-start | bytes 1327112 | tf_op jit(solution)/shard_map/ppermute | solution.py:501
  36.2 11.4 %collective-permute-start.7 = (bf16[192,1280]{1,0:T(8,128)(2,1)S(1)}, bf16[192,1280]{1,0:T(8,128)(2,1)S(1)}, u32[]{:S(2)}, u32[]{:S(2)}) collective-permute-start(bf16[192,1280]{1,0:T(8,128)(2,1)S(1)} %pad_maximum_fusion.17), channel_id=1, source_target_pairs={{0,4},{1,5},{2,6},{3,7},{4,0},{5,1},{6,2},{7,3},{8,12},{9,13},{10,... | collective-permute-start | bytes 1474568 | tf_op jit(solution)/shard_map/ppermute | solution.py:501
  47.7 4.8 %collective-permute-start.10 = (bf16[384,1280]{1,0:T(8,128)(2,1)S(1)}, bf16[384,1280]{1,0:T(8,128)(2,1)S(1)}, u32[]{:S(2)}, u32[]{:S(2)}) collective-permute-start(bf16[384,1280]{1,0:T(8,128)(2,1)S(1)} %pad_maximum_fusion.9.ra_ref), channel_id=1, source_target_pairs={{0,1},{1,0},{2,3},{3,2},{4,5},{5,4},{6,7},{7,6},{8,9},{9,8},{10,11... | collective-permute-start | bytes 2949128 | tf_op jit(solution)/shard_map/ppermute | solution.py:501
  47.8 3.8 %collective-permute-start.9 = (bf16[384,1152]{1,0:T(8,128)(2,1)S(1)}, bf16[384,1152]{1,0:T(8,128)(2,1)S(1)}, u32[]{:S(2)}, u32[]{:S(2)}) collective-permute-start(bf16[384,1152]{1,0:T(8,128)(2,1)S(1)} %pad_maximum_fusion.10.la_ref), channel_id=1, source_target_pairs={{0,1},{1,0},{2,3},{3,2},{4,5},{5,4},{6,7},{7,6},{8,9},{9,8},{10,11... | collective-permute-start | bytes 2654216 | tf_op jit(solution)/shard_map/ppermute | solution.py:501
  52.6 14.8 %collective-permute-start.13 = (bf16[96,768]{1,0:T(8,128)(2,1)}, bf16[96,768]{1,0:T(8,128)(2,1)S(1)}, u32[]{:S(2)}, u32[]{:S(2)}) collective-permute-start(bf16[96,768]{1,0:T(8,128)(2,1)} %convert_element_type.278), channel_id=1, source_target_pairs={{0,16},{1,17},{2,18},{3,19},{4,20},{5,21},{6,22},{7,23},{8,24},{9,... | collective-permute-start | bytes 442376 | tf_op jit(solution)/shard_map/ppermute | solution.py:501
  56.5 12.0 %collective-permute-start.12 = (bf16[192,896]{1,0:T(8,128)(2,1)}, bf16[192,896]{1,0:T(8,128)(2,1)}, u32[]{:S(2)}, u32[]{:S(2)}) collective-permute-start(bf16[192,896]{1,0:T(8,128)(2,1)} %slice.365), channel_id=1, source_target_pairs={{0,2},{1,3},{2,0},{3,1},{4,6},{5,7},{6,4},{7,5},{8,10},{9,11},{10,... | collective-permute-start | bytes 1032200 | tf_op jit(solution)/shard_map/ppermute | solution.py:501
  57.1 13.0 %collective-permute-start.11 = (bf16[192,1024]{1,0:T(8,128)(2,1)}, bf16[192,1024]{1,0:T(8,128)(2,1)}, u32[]{:S(2)}, u32[]{:S(2)}) collective-permute-start(bf16[192,1024]{1,0:T(8,128)(2,1)} %slice.364), channel_id=1, source_target_pairs={{0,4},{1,5},{2,6},{3,7},{4,0},{5,1},{6,2},{7,3},{8,12},{9,13},{10,... | collective-permute-start | bytes 1179656 | tf_op jit(solution)/shard_map/ppermute | solution.py:501
  71.3 11.4 %collective-permute-start.14 = (bf16[192,768]{1,0:T(8,128)(2,1)S(1)}, bf16[192,768]{1,0:T(8,128)(2,1)S(1)}, u32[]{:S(2)}, u32[]{:S(2)}) collective-permute-start(bf16[192,768]{1,0:T(8,128)(2,1)S(1)} %pad_maximum_fusion.22), channel_id=1, source_target_pairs={{0,8},{1,9},{2,10},{3,11},{4,12},{5,13},{6,14},{7,15},{8,0},{9,1},... | collective-permute-start | bytes 884744 | tf_op jit(solution)/shard_map/ppermute | solution.py:501
  72.4 26.2 %collective-permute-start.18 = (bf16[384,896]{1,0:T(8,128)(2,1)S(1)}, bf16[384,896]{1,0:T(8,128)(2,1)S(1)}, u32[]{:S(2)}, u32[]{:S(2)}) collective-permute-start(bf16[384,896]{1,0:T(8,128)(2,1)S(1)} %pad_maximum_fusion.13), channel_id=1, source_target_pairs={{0,4},{1,5},{2,6},{3,7},{4,0},{5,1},{6,2},{7,3},{8,12},{9,13},{10,... | collective-permute-start | bytes 2064392 | tf_op jit(solution)/shard_map/ppermute | solution.py:501
  74.0 24.8 %collective-permute-start.17 = (bf16[384,1024]{1,0:T(8,128)(2,1)S(1)}, bf16[384,1024]{1,0:T(8,128)(2,1)S(1)}, u32[]{:S(2)}, u32[]{:S(2)}) collective-permute-start(bf16[384,1024]{1,0:T(8,128)(2,1)S(1)} %pad_maximum_fusion.11), channel_id=1, source_target_pairs={{0,2},{1,3},{2,0},{3,1},{4,6},{5,7},{6,4},{7,5},{8,10},{9,11},{10,... | collective-permute-start | bytes 2359304 | tf_op jit(solution)/shard_map/ppermute | solution.py:501
  82.8 15.7 %collective-permute-start.16 = (bf16[384,384]{1,0:T(8,128)(2,1)S(1)}, bf16[384,384]{1,0:T(8,128)(2,1)S(1)}, u32[]{:S(2)}, u32[]{:S(2)}) collective-permute-start(bf16[384,384]{1,0:T(8,128)(2,1)S(1)} %get-tuple-element.269), channel_id=1, source_target_pairs={{0,2},{1,3},{2,0},{3,1},{4,6},{5,7},{6,4},{7,5},{8,10},{9,11},{10,... | collective-permute-start | bytes 884744 | tf_op jit(solution)/shard_map/ppermute | solution.py:501
  83.4 15.1 %collective-permute-start.15 = (bf16[384,384]{1,0:T(8,128)(2,1)S(1)}, bf16[384,384]{1,0:T(8,128)(2,1)S(1)}, u32[]{:S(2)}, u32[]{:S(2)}) collective-permute-start(bf16[384,384]{1,0:T(8,128)(2,1)S(1)} %get-tuple-element.270), channel_id=1, source_target_pairs={{0,4},{1,5},{2,6},{3,7},{4,0},{5,1},{6,2},{7,3},{8,12},{9,13},{10,... | collective-permute-start | bytes 884744 | tf_op jit(solution)/shard_map/ppermute | solution.py:501
  98.9 19.1 %collective-permute-start.21 = (bf16[768,1024]{1,0:T(8,128)(2,1)S(1)}, bf16[768,1024]{1,0:T(8,128)(2,1)S(1)}, u32[]{:S(2)}, u32[]{:S(2)}) collective-permute-start(bf16[768,1024]{1,0:T(8,128)(2,1)S(1)} %pad_maximum_fusion.1.refs_9_), channel_id=1, source_target_pairs={{0,1},{1,0},{2,3},{3,2},{4,5},{5,4},{6,7},{7,6},{8,9},{9,8},{10,11... | collective-permute-start | bytes 4718600 | tf_op jit(solution)/shard_map/ppermute | solution.py:501
  99.9 18.1 %collective-permute-start.22 = (bf16[768,896]{1,0:T(8,128)(2,1)S(1)}, bf16[768,896]{1,0:T(8,128)(2,1)S(1)}, u32[]{:S(2)}, u32[]{:S(2)}) collective-permute-start(bf16[768,896]{1,0:T(8,128)(2,1)S(1)} %pad_maximum_fusion.2.refs_10_), channel_id=1, source_target_pairs={{0,1},{1,0},{2,3},{3,2},{4,5},{5,4},{6,7},{7,6},{8,9},{9,8},{10,11... | collective-permute-start | bytes 4128776 | tf_op jit(solution)/shard_map/ppermute | solution.py:501
  99.9 15.7 %collective-permute-start.19 = (bf16[768,384]{1,0:T(8,128)(2,1)S(1)}, bf16[768,384]{1,0:T(8,128)(2,1)S(1)}, u32[]{:S(2)}, u32[]{:S(2)}) collective-permute-start(bf16[768,384]{1,0:T(8,128)(2,1)S(1)} %pad_maximum_fusion.15), channel_id=1, source_target_pairs={{0,2},{1,3},{2,0},{3,1},{4,6},{5,7},{6,4},{7,5},{8,10},{9,11},{10,... | collective-permute-start | bytes 1769480 | tf_op jit(solution)/shard_map/ppermute | solution.py:501
  101.4 15.5 %collective-permute-start.20 = (bf16[768,384]{1,0:T(8,128)(2,1)S(1)}, bf16[768,384]{1,0:T(8,128)(2,1)S(1)}, u32[]{:S(2)}, u32[]{:S(2)}) collective-permute-start(bf16[768,384]{1,0:T(8,128)(2,1)S(1)} %pad_maximum_fusion.16), channel_id=1, source_target_pairs={{0,4},{1,5},{2,6},{3,7},{4,0},{5,1},{6,2},{7,3},{8,12},{9,13},{10,... | collective-permute-start | bytes 1769480 | tf_op jit(solution)/shard_map/ppermute | solution.py:501
  119.7 3.2 collective-permute-start.23
  119.7 4.9 %collective-permute-start.24 = (bf16[1536,384]{1,0:T(8,128)(2,1)}, bf16[1536,384]{1,0:T(8,128)(2,1)}, u32[]{:S(2)}, u32[]{:S(2)}) collective-permute-start(bf16[1536,384]{1,0:T(8,128)(2,1)} %pad_maximum_fusion.4.refs_14_), channel_id=1, source_target_pairs={{0,1},{1,0},{2,3},{3,2},{4,5},{5,4},{6,7},{7,6},{8,9},{9,8},{10,11... | collective-permute-start | bytes 3538952 | tf_op jit(solution)/shard_map/ppermute | solution.py:501
  188.1 10.0 %collective-permute-start.25 = (bf16[384,3072]{1,0:T(8,128)(2,1)}, bf16[384,3072]{1,0:T(8,128)(2,1)S(1)}, u32[]{:S(2)}, u32[]{:S(2)}) collective-permute-start(bf16[384,3072]{1,0:T(8,128)(2,1)} %get-tuple-element.203), channel_id=1, source_target_pairs={{0,1},{1,0},{2,3},{3,2},{4,5},{5,4},{6,7},{7,6},{8,9},{9,8},{10,11... | collective-permute-start | bytes 7077896 | tf_op jit(solution)/shard_map/ppermute | solution.py:501
  188.3 9.8 %collective-permute-start.26 = (bf16[1536,768]{1,0:T(8,128)(2,1)}, bf16[1536,768]{1,0:T(8,128)(2,1)S(1)}, u32[]{:S(2)}, u32[]{:S(2)}) collective-permute-start(bf16[1536,768]{1,0:T(8,128)(2,1)} %get-tuple-element.204), channel_id=1, source_target_pairs={{0,1},{1,0},{2,3},{3,2},{4,5},{5,4},{6,7},{7,6},{8,9},{9,8},{10,11... | collective-permute-start | bytes 7077896 | tf_op jit(solution)/shard_map/ppermute | solution.py:501
  198.4 28.8 %collective-permute-start.28 = (bf16[768,768]{1,0:T(8,128)(2,1)S(1)}, bf16[768,768]{1,0:T(8,128)(2,1)S(1)}, u32[]{:S(2)}, u32[]{:S(2)}) collective-permute-start(bf16[768,768]{1,0:T(8,128)(2,1)S(1)} %add_convert_fusion), channel_id=1, source_target_pairs={{0,4},{1,5},{2,6},{3,7},{4,0},{5,1},{6,2},{7,3},{8,12},{9,13},{10,... | collective-permute-start | bytes 3538952 | tf_op jit(solution)/shard_map/ppermute | solution.py:501
  200.2 28.1 %collective-permute-start.27 = (bf16[192,3072]{1,0:T(8,128)(2,1)S(1)}, bf16[192,3072]{1,0:T(8,128)(2,1)S(1)}, u32[]{:S(2)}, u32[]{:S(2)}) collective-permute-start(bf16[192,3072]{1,0:T(8,128)(2,1)S(1)} %add_convert_fusion.1), channel_id=1, source_target_pairs={{0,2},{1,3},{2,0},{3,1},{4,6},{5,7},{6,4},{7,5},{8,10},{9,11},{10,... | collective-permute-start | bytes 3538952 | tf_op jit(solution)/shard_map/ppermute | solution.py:501
  230.4 14.7 %collective-permute-start.30 = (bf16[384,768]{1,0:T(8,128)(2,1)}, bf16[384,768]{1,0:T(8,128)(2,1)S(1)}, u32[]{:S(2)}, u32[]{:S(2)}) collective-permute-start(bf16[384,768]{1,0:T(8,128)(2,1)} %add_convert_fusion.4), channel_id=1, source_target_pairs={{0,2},{1,3},{2,0},{3,1},{4,6},{5,7},{6,4},{7,5},{8,10},{9,11},{10,... | collective-permute-start | bytes 1769480 | tf_op jit(solution)/shard_map/ppermute | solution.py:501
  231.8 14.5 %collective-permute-start.29 = (bf16[96,3072]{1,0:T(8,128)(2,1)}, bf16[96,3072]{1,0:T(8,128)(2,1)S(1)}, u32[]{:S(2)}, u32[]{:S(2)}) collective-permute-start(bf16[96,3072]{1,0:T(8,128)(2,1)} %add_convert_fusion.5), channel_id=1, source_target_pairs={{0,4},{1,5},{2,6},{3,7},{4,0},{5,1},{6,2},{7,3},{8,12},{9,13},{10,... | collective-permute-start | bytes 1769480 | tf_op jit(solution)/shard_map/ppermute | solution.py:501
  250.5 3.5 %collective-permute-start.31 = (bf16[384,1536]{1,0:T(8,128)(2,1)S(1)}, bf16[384,1536]{1,0:T(8,128)(2,1)S(1)}, u32[]{:S(2)}, u32[]{:S(2)}) collective-permute-start(bf16[384,1536]{1,0:T(8,128)(2,1)S(1)} %pad_maximum_fusion.5), channel_id=1, source_target_pairs={{0,1},{1,0},{2,3},{3,2},{4,5},{5,4},{6,7},{7,6},{8,9},{9,8},{10,11... | collective-permute-start | bytes 3538952 | tf_op jit(solution)/shard_map/ppermute | solution.py:501
  250.6 4.5 %collective-permute-start.32 = (bf16[384,1536]{1,0:T(8,128)(2,1)S(1)}, bf16[384,1536]{1,0:T(8,128)(2,1)S(1)}, u32[]{:S(2)}, u32[]{:S(2)}) collective-permute-start(bf16[384,1536]{1,0:T(8,128)(2,1)S(1)} %pad_maximum_fusion.6), channel_id=1, source_target_pairs={{0,1},{1,0},{2,3},{3,2},{4,5},{5,4},{6,7},{7,6},{8,9},{9,8},{10,11... | collective-permute-start | bytes 3538952 | tf_op jit(solution)/shard_map/ppermute | solution.py:501
  255.3 16.0 %collective-permute-start.34 = (bf16[192,1536]{1,0:T(8,128)(2,1)S(1)}, bf16[192,1536]{1,0:T(8,128)(2,1)S(1)}, u32[]{:S(2)}, u32[]{:S(2)}) collective-permute-start(bf16[192,1536]{1,0:T(8,128)(2,1)S(1)} %add_convert_fusion.2), channel_id=1, source_target_pairs={{0,4},{1,5},{2,6},{3,7},{4,0},{5,1},{6,2},{7,3},{8,12},{9,13},{10,... | collective-permute-start | bytes 1769480 | tf_op jit(solution)/shard_map/ppermute | solution.py:501
  255.8 15.5 %collective-permute-start.33 = (bf16[192,1536]{1,0:T(8,128)(2,1)S(1)}, bf16[192,1536]{1,0:T(8,128)(2,1)S(1)}, u32[]{:S(2)}, u32[]{:S(2)}) collective-permute-start(bf16[192,1536]{1,0:T(8,128)(2,1)S(1)} %add_convert_fusion.3), channel_id=1, source_target_pairs={{0,2},{1,3},{2,0},{3,1},{4,6},{5,7},{6,4},{7,5},{8,10},{9,11},{10,... | collective-permute-start | bytes 1769480 | tf_op jit(solution)/shard_map/ppermute | solution.py:501
  256.5 9.9 %collective-permute-start.35 = (bf16[48,3072]{1,0:T(8,128)(2,1)S(1)}, bf16[48,3072]{1,0:T(8,128)(2,1)S(1)}, u32[]{:S(2)}, u32[]{:S(2)}) collective-permute-start(bf16[48,3072]{1,0:T(8,128)(2,1)S(1)} %add_convert_fusion.9), channel_id=1, source_target_pairs={{0,8},{1,9},{2,10},{3,11},{4,12},{5,13},{6,14},{7,15},{8,0},{9,1},... | collective-permute-start | bytes 884744 | tf_op jit(solution)/shard_map/ppermute | solution.py:501
  258.2 13.1 %collective-permute-start.36 = (bf16[192,768]{1,0:T(8,128)(2,1)S(1)}, bf16[192,768]{1,0:T(8,128)(2,1)S(1)}, u32[]{:S(2)}, u32[]{:S(2)}) collective-permute-start(bf16[192,768]{1,0:T(8,128)(2,1)S(1)} %add_convert_fusion.8), channel_id=1, source_target_pairs={{0,8},{1,9},{2,10},{3,11},{4,12},{5,13},{6,14},{7,15},{8,0},{9,1},... | collective-permute-start | bytes 884744 | tf_op jit(solution)/shard_map/ppermute | solution.py:501
  271.7 7.7 %collective-permute-start.37 = (bf16[96,1536]{1,0:T(8,128)(2,1)S(1)}, bf16[96,1536]{1,0:T(8,128)(2,1)S(1)}, u32[]{:S(2)}, u32[]{:S(2)}) collective-permute-start(bf16[96,1536]{1,0:T(8,128)(2,1)S(1)} %add_convert_fusion.7), channel_id=1, source_target_pairs={{0,4},{1,5},{2,6},{3,7},{4,0},{5,1},{6,2},{7,3},{8,12},{9,13},{10,... | collective-permute-start | bytes 884744 | tf_op jit(solution)/shard_map/ppermute | solution.py:501
  273.5 7.3 %collective-permute-start.38 = (bf16[96,1536]{1,0:T(8,128)(2,1)S(1)}, bf16[96,1536]{1,0:T(8,128)(2,1)S(1)}, u32[]{:S(2)}, u32[]{:S(2)}) collective-permute-start(bf16[96,1536]{1,0:T(8,128)(2,1)S(1)} %add_convert_fusion.6), channel_id=1, source_target_pairs={{0,2},{1,3},{2,0},{3,1},{4,6},{5,7},{6,4},{7,5},{8,10},{9,11},{10,... | collective-permute-start | bytes 884744 | tf_op jit(solution)/shard_map/ppermute | solution.py:501
  274.9 12.5 %collective-permute-start.40 = (bf16[24,3072]{1,0:T(8,128)(2,1)S(1)}, bf16[24,3072]{1,0:T(8,128)(2,1)S(1)}, u32[]{:S(2)}, u32[]{:S(2)}) collective-permute-start(bf16[24,3072]{1,0:T(8,128)(2,1)S(1)} %add_convert_fusion.11), channel_id=1, source_target_pairs={{0,16},{1,17},{2,18},{3,19},{4,20},{5,21},{6,22},{7,23},{8,24},{9,... | collective-permute-start | bytes 442376 | tf_op jit(solution)/shard_map/ppermute | solution.py:501
  276.4 12.9 %collective-permute-start.41 = (bf16[96,768]{1,0:T(8,128)(2,1)S(1)}, bf16[96,768]{1,0:T(8,128)(2,1)S(1)}, u32[]{:S(2)}, u32[]{:S(2)}) collective-permute-start(bf16[96,768]{1,0:T(8,128)(2,1)S(1)} %add_convert_fusion.10), channel_id=1, source_target_pairs={{0,16},{1,17},{2,18},{3,19},{4,20},{5,21},{6,22},{7,23},{8,24},{9,... | collective-permute-start | bytes 442376 | tf_op jit(solution)/shard_map/ppermute | solution.py:501
  281.2 11.6 %collective-permute-start.39 = (bf16[48,3072]{1,0:T(8,128)(2,1)S(1)}, bf16[48,3072]{1,0:T(8,128)(2,1)S(1)}, u32[]{:S(2)}, u32[]{:S(2)}) collective-permute-start(bf16[48,3072]{1,0:T(8,128)(2,1)S(1)} %fusion.67), channel_id=1, source_target_pairs={{0,8},{1,9},{2,10},{3,11},{4,12},{5,13},{6,14},{7,15},{8,0},{9,1},... | collective-permute-start | bytes 884744 | tf_op jit(solution)/shard_map/ppermute | solution.py:501
  292.7 6.7 %collective-permute-start.42 = (bf16[24,3072]{1,0:T(8,128)(2,1)S(1)}, bf16[24,3072]{1,0:T(8,128)(2,1)S(1)}, u32[]{:S(2)}, u32[]{:S(2)}) collective-permute-start(bf16[24,3072]{1,0:T(8,128)(2,1)S(1)} %fusion.72), channel_id=1, source_target_pairs={{0,16},{1,17},{2,18},{3,19},{4,20},{5,21},{6,22},{7,23},{8,24},{9,... | collective-permute-start | bytes 442376 | tf_op jit(solution)/shard_map/ppermute | solution.py:501
  303.9 1.2 collective-permute-start.43
  305.1 4.0 %collective-permute-start.44 = (f32[80,128]{1,0:T(8,128)S(1)}, f32[80,128]{1,0:T(8,128)S(1)}, u32[]{:S(2)}, u32[]{:S(2)}) collective-permute-start(f32[80,128]{1,0:T(8,128)S(1)} %add.430), channel_id=1, source_target_pairs={{0,2},{1,3},{2,0},{3,1},{4,6},{5,7},{6,4},{7,5},{8,10},{9,11},{10,... | collective-permute-start | bytes 122888 | tf_op jit(solution)/shard_map/ppermute | solution.py:501
  309.1 4.3 %collective-permute-start.45 = (f32[80,128]{1,0:T(8,128)S(1)}, f32[80,128]{1,0:T(8,128)S(1)}, u32[]{:S(2)}, u32[]{:S(2)}) collective-permute-start(f32[80,128]{1,0:T(8,128)S(1)} %add.431), channel_id=1, source_target_pairs={{0,4},{1,5},{2,6},{3,7},{4,0},{5,1},{6,2},{7,3},{8,12},{9,13},{10,... | collective-permute-start | bytes 122888 | tf_op jit(solution)/shard_map/ppermute | solution.py:501
  313.4 4.1 %collective-permute-start.46 = (f32[80,128]{1,0:T(8,128)S(1)}, f32[80,128]{1,0:T(8,128)S(1)}, u32[]{:S(2)}, u32[]{:S(2)}) collective-permute-start(f32[80,128]{1,0:T(8,128)S(1)} %add.432), channel_id=1, source_target_pairs={{0,8},{1,9},{2,10},{3,11},{4,12},{5,13},{6,14},{7,15},{8,0},{9,1},... | collective-permute-start | bytes 122888 | tf_op jit(solution)/shard_map/ppermute | solution.py:501
  317.5 4.9 %collective-permute-start.47 = (f32[80,128]{1,0:T(8,128)S(1)}, f32[80,128]{1,0:T(8,128)S(1)}, u32[]{:S(2)}, u32[]{:S(2)}) collective-permute-start(f32[80,128]{1,0:T(8,128)S(1)} %add.433), channel_id=1, source_target_pairs={{0,16},{1,17},{2,18},{3,19},{4,20},{5,21},{6,22},{7,23},{8,24},{9,... | collective-permute-start | bytes 122888 | tf_op jit(solution)/shard_map/ppermute | solution.py:501
  (44 other events, 217.7 us)

commit v5 on v4

--- a/solution.py
+++ b/solution.py
@@ -18,6 +18,8 @@
 MASKED = -1e9
 VMEM = 60 * 2**20
 ROOM = 24 * 2**20
+
+
 BF16 = jnp.bfloat16
 F32 = jnp.float32
 
@@ -42,17 +44,34 @@
     return dot(value, matrix).astype(BF16)
 
 
-def project_kernel(xa_ref, xb_ref, la_ref, lb_ref, ra_ref, rb_ref, bias_ref, out_ref):
+def project_kernel(*refs):
+    xa_ref, xb_ref, la_ref, lb_ref, ra_ref, rb_ref, source_ref, lane_ref, out_ref, bias_ref = refs
     width = la_ref.shape[1]
+
+    @pl.when(pl.program_id(0) == 0)
+    def _():
+        tail = jnp.concatenate([ra_ref[:, width:], rb_ref[:, width:]], axis=0)
+        start = source_ref[...] * 12
+        entry = lax.broadcasted_iota(jnp.int32, (D, D), 1)
+        lane = lax.broadcasted_iota(jnp.int32, (128, D), 0)
+        bias_ref[...] = jnp.zeros_like(bias_ref)
+        for i in range(2):
+            offset = entry + i * D - start
+            picked = dot_tn(tail, jnp.where((offset >= 0) & (offset < 12), 1.0, 0.0).astype(BF16))
+            picked = jnp.where(lane == lane_ref[i : i + 1, :], picked, 0.0)
+            bias_ref[:, 2 * i * D : (2 * i + 1) * D] = jnp.sum(picked, axis=0, keepdims=True)
+
     left = jnp.concatenate([la_ref[...], lb_ref[...]], axis=0)
     out_ref[:, :width] = (dot(xa_ref[...], left) + bias_ref[:, :width]).astype(BF16)
     right = jnp.concatenate([ra_ref[:, :width], rb_ref[:, :width]], axis=0)
     out_ref[:, width:] = (dot(xb_ref[...], right) + bias_ref[:, width:]).astype(BF16)
 
 
-def project(x_a, x_b, left, right, bias):
+def project(x_a, x_b, left, right, source):
     seq = x_a.shape[0]
     rows = min(512, seq)
+    lanes = (jnp.arange(2 * D, dtype=jnp.int32) % 12).reshape(2, D)
+    operands = (*left, *right, source.reshape(D, 1), lanes)
 
     def fixed(shape):
         return pl.BlockSpec(shape, lambda i: (0, 0), pipeline_mode=pl.Buffered(1))
@@ -61,13 +80,14 @@
         project_kernel,
         grid=(seq // rows,),
         in_specs=[pl.BlockSpec((rows, D), lambda i: (i, 0))] * 2
-        + [fixed(part.shape) for part in (*left, *right, bias)],
+        + [fixed(part.shape) for part in operands],
         out_specs=pl.BlockSpec((rows, 3 * D), lambda i: (i, 0)),
         out_shape=jax.ShapeDtypeStruct((seq, 3 * D), BF16),
+        scratch_shapes=[pltpu.VMEM((1, 3 * D), F32)],
         compiler_params=pltpu.CompilerParams(vmem_limit_bytes=ROOM),
         cost_estimate=cost(5),
         name="project",
-    )(x_a, x_b, *left, *right, bias)
+    )(x_a, x_b, *operands)
 
 
 def attend_kernel(len_ref, q_ref, k_ref, v_ref, ctx_ref, ctxt_ref, lse_ref):
@@ -287,6 +307,8 @@
                 total += 1
         return made
 
+    early = sum(count for _, count, _ in in_pieces[: max(1, len(in_pieces) // 2)])
+
     def in_weights():
         return part_copies(w_ref, in_parts, in_pieces, in_sems)
 
@@ -305,7 +327,7 @@
 
         @pl.when(step == 0)
         def _():
-            waited(in_weights())
+            waited(in_weights()[:early])
 
         resid = x_ref[...].astype(F32) + (dot(ctx_ref[...], weight(0)[...]) + vec(2))
         unit1, inverse1 = norm_forward(resid)
@@ -318,7 +340,7 @@
 
         @pl.when(step == 0)
         def _():
-            waited(out_weights())
+            waited(in_weights()[early:] + out_weights())
 
         branch = None
         for c in range(CHUNKS):
@@ -497,13 +519,18 @@
     )(lengths, places, where, x, ctx, cot, vec, to_a, to_b, *in_parts, *out_parts)
 
 
-def swap(value, bit, n):
-    return lax.ppermute(value, "dp", [(i, i ^ (1 << bit)) for i in range(n)])
-
-
-def sum_all(value, n):
-    for bit in range(n.bit_length() - 1):
-        value = value + swap(value, bit, n)
+def swap(value, bits, n):
+    mask = sum(1 << bit for bit in bits)
+    return lax.ppermute(value, "dp", [(i, i ^ mask) for i in range(n)])
+
+
+def subsets(bits):
+    return [[bit for k, bit in enumerate(bits) if p >> k & 1] for p in range(1, 2 ** len(bits))]
+
+
+def sum_all(value, groups, n):
+    for bits in groups:
+        value = sum([swap(value, some, n) for some in subsets(bits)], value)
     return value
 
 
@@ -522,12 +549,15 @@
     def mask(self, place):
         return sum(((place >> k) & 1) << bit for k, bit in enumerate(self.bits))
 
-    def matrix(self):
+    def source(self):
         rows = D // self.n
         place = jnp.arange(D, dtype=jnp.int32)
         block = self.mask(place // rows) ^ lax.axis_index("dp")
-        source = block * rows + place % rows
-        return (place[:, None] == source[None, :]).astype(BF16)
+        return block * rows + place % rows
+
+    def matrix(self):
+        place = jnp.arange(D, dtype=jnp.int32)
+        return (place[:, None] == self.source()[None, :]).astype(BF16)
 
     def where(self):
         other = jnp.arange(self.n, dtype=jnp.int32) ^ lax.axis_index("dp")
@@ -541,8 +571,9 @@
     def __init__(self, shard, n):
         self.value, self.n = shard, n
 
-    def step(self, bit):
-        self.value = jnp.concatenate([self.value, swap(self.value, bit, self.n)], axis=0)
+    def step(self, bits):
+        got = [swap(self.value, some, self.n) for some in subsets(bits)]
+        self.value = jnp.concatenate([self.value, *got], axis=0)
 
     def cut(self, start, stop):
         return Gather(self.value[:, start:stop], self.n)
@@ -552,22 +583,33 @@
     def __init__(self, kept, got, n):
         self.terms, self.n = [kept, got], n
 
-    def away(self):
-        half = self.terms[0].shape[0] // 2
-        return self.total([t[half:] for t in self.terms]).astype(BF16)
-
-    def send(self, away, bit):
-        self.terms = [t[: away.shape[0]] for t in self.terms] + [swap(away, bit, self.n)]
-
-    def step(self, bit):
-        self.send(self.away(), bit)
-
-    def total(self, parts=None):
+    def away(self, bits):
+        size = self.terms[0].shape[0] >> len(bits)
+        parts = range(1, 2 ** len(bits))
+        return [self.total([t[p * size : (p + 1) * size] for t in self.terms], BF16) for p in parts]
+
+    def send(self, away, bits):
+        got = [swap(part, some, self.n) for part, some in zip(away, subsets(bits))]
+        self.terms = [t[: away[0].shape[0]] for t in self.terms] + got
+        self.recent = len(got)
+
+    def step(self, bits):
+        self.send(self.away(bits), bits)
+
+    @property
+    def got(self):
+        return self.terms[-self.recent :]
+
+    @got.setter
+    def got(self, values):
+        self.terms[-self.recent :] = values
+
+    def total(self, parts=None, kind=F32):
         parts = self.terms if parts is None else parts
         result = parts[0].astype(F32)
         for part in parts[1:]:
             result = result + part.astype(F32)
-        return result
+        return result.astype(kind)
 
     def join(self, other):
         self.terms = [jnp.concatenate([self.total(), other.total()], axis=1)]
@@ -659,6 +701,7 @@
     rows_d, rows_f, width = w_qkv.shape[0], w_out.shape[0], vectors.shape[0]
     core, one, two, *others = range(n.bit_length() - 1)
     far = others[::-1]
+    groups = [far[i : i + 2] for i in range(0, len(far), 2)]
     order_a, order_b = Order(far + [two, one, core]), Order(far + [one, two, core])
     x = frames[0]
 
@@ -676,83 +719,102 @@
         side = low_in.shape[1] // 2
         mine = own_bit(core)
         kept = lax.dynamic_slice_in_dim(low_in, mine * side, side, 1)
-        got = swap(lax.dynamic_slice_in_dim(low_in, (1 - mine) * side, side, 1), core, n)
+        got = swap(lax.dynamic_slice_in_dim(low_in, (1 - mine) * side, side, 1), [core], n)
         pair = [jnp.where(mine == 0, kept, got), jnp.where(mine == 0, got, kept)]
         inner.value = jnp.concatenate(pair, axis=0)
     else:
         attn_in = lax.all_gather(low_in, "dp", axis=0, tiled=True)
-    qkv.step(far[0])
-    qkv.value, inner.value, x_a, x_b = phase(qkv.value, inner.value, x_a, x_b)
-    for bit in far[1:]:
-        qkv.step(bit)
-        (qkv.value,) = phase(qkv.value)
+    for bits in groups:
+        qkv.step(bits)
+        qkv.value, inner.value = phase(qkv.value, inner.value)
     left, right = qkv.cut(0, half), qkv.cut(half, 2 * half + 128)
-    for bits, more in (((two, one), far[:1]), ((one, two), far[1:])):
-        left.step(bits[0])
-        right.step(bits[1])
-        for bit in more if aligned else ():
-            inner.step(bit)
-        left.value, right.value, inner.value = phase(left.value, right.value, inner.value)
-    left = (left.value, swap(left.value, core, n))
-    right = (right.value, swap(right.value, core, n))
+    out_left, out_right = out.cut(0, D // 2), out.cut(D // 2, D)
+    if aligned:
+        left.value = jnp.concatenate([left.value, out_left.value], axis=1)
+        right.value = jnp.concatenate([right.value, out_right.value], axis=1)
+    else:
+        out_left.step([two])
+        out_right.step([one])
+    left.step([two])
+    right.step([one])
+    for bit in far[:1] if aligned else ():
+        inner.step([bit])
+    left.value, right.value, inner.value, x_a, x_b = phase(
+        left.value, right.value, inner.value, x_a, x_b
+    )
+    if aligned:
+        out_left, left = left.cut(half, half + D // 2), left.cut(0, half)
+        out_right, right = right.cut(half + 128, half + 128 + D // 2), right.cut(0, half + 128)
+    out = Gather(jnp.concatenate([out_left.value, out_right.value], axis=1), n)
+    left.step([one])
+    right.step([two])
+    for bit in far[1:] if aligned else ():
+        inner.step([bit])
+    left.value, right.value, inner.value, out.value = phase(
+        left.value, right.value, inner.value, out.value
+    )
+    left = (left.value, swap(left.value, [core], n))
+    right = (right.value, swap(right.value, [core], n))
     cut = 1024 if aligned else low_in.shape[1]
     in_left, in_right = inner.cut(0, cut), inner.cut(cut, inner.value.shape[1])
 
-    def in_step(bit_left, bit_right):
+    def in_step(bits_left, bits_right):
         if aligned:
-            in_left.step(bit_left)
-            in_right.step(bit_right)
+            in_left.step(bits_left)
+            in_right.step(bits_right)
 
     left, right, in_left.value, in_right.value, out.value = phase(
         left, right, in_left.value, in_right.value, out.value
     )
-    in_step(two, one)
-    out.step(far[0])
+    in_step([two], [one])
+    out.step(far[:1])
     vec_rows = jnp.concatenate([part[:, half:] for part in right], axis=0)
     vec = dot(to_b, vec_rows)[:, :12].reshape(12, D)
-    bias_qkv = jnp.concatenate([vec[:1], jnp.zeros((1, D), F32), vec[1:2]], axis=1)
-
-    packed = project(x_a, x_b, left, right, bias_qkv)
-    packed, vec, in_left.value, in_right.value, out.value = phase(
-        packed, vec, in_left.value, in_right.value, out.value
-    )
-    in_step(one, two)
+
+    packed = project(x_a, x_b, left, right, order_b.source())
+    some = PAIRS // 6
+    heads = attend(lengths, packed, 0, some)
+    heads, in_left.value, in_right.value, out.value = phase(
+        heads, in_left.value, in_right.value, out.value
+    )
+    in_step([one], [two])
     for bit in far[1:]:
-        out.step(bit)
-    some = PAIRS // 3
-    heads = attend(lengths, packed, 0, some)
-    heads, out.value = phase(heads, out.value)
+        out.step([bit])
+    heads = attend(lengths, packed, some, 3 * some, heads)
+    heads, out.value, in_left.value, in_right.value = phase(
+        heads, out.value, in_left.value, in_right.value
+    )
     out_left, out_right = out.cut(0, D // 2), out.cut(D // 2, D)
-    out_left.step(two)
-    out_right.step(one)
-    heads = attend(lengths, packed, some, some, heads)
-    heads, out_left.value, out_right.value, in_left.value, in_right.value = phase(
-        heads, out_left.value, out_right.value, in_left.value, in_right.value
-    )
-    out_left.step(one)
-    out_right.step(two)
+    out_left.step([one])
+    out_right.step([two])
     in_parts = [in_left.value, in_right.value]
     if aligned:
-        in_parts += [swap(part, core, n) for part in in_parts]
-    heads = attend(lengths, packed, 2 * some, some, heads)
-    heads, out_left.value, out_right.value, in_parts = phase(
-        heads, out_left.value, out_right.value, in_parts
+        in_parts = [in_parts[0], swap(in_parts[0], [core], n)] + [
+            in_parts[1],
+            swap(in_parts[1], [core], n),
+        ]
+    heads = attend(lengths, packed, 4 * some, 2 * some, heads)
+    heads, vec, out_left.value, out_right.value, in_parts = phase(
+        heads, vec, out_left.value, out_right.value, in_parts
     )
     out_parts = [out_left.value, out_right.value]
-    out_parts += [swap(part, core, n) for part in out_parts]
+    out_parts += [swap(part, [core], n) for part in out_parts]
+    out_a, out_b = Order([two, *far, one, core]), Order([one, *far, two, core])
     if aligned:
         chips_a, chips_b = [order.places(n // 2) // 2 for order in (order_a, order_b)]
-        blocks_a, blocks_b = order_a.places(n), order_b.places(n)
+        blocks_a, blocks_b = out_a.places(n), out_b.places(n)
         first = jnp.stack([mine, 1 - mine]) * (side // 128)
-        corners = jnp.stack([first, first + cut // 128], axis=1).reshape(4)
+        corners = jnp.concatenate([first, first + cut // 128])
         columns = jnp.array([0, D // 256], jnp.int32)
         places = jnp.concatenate([chips_a, chips_b, blocks_a, blocks_b, corners, columns])
         base = 3 * n
-        in_pieces = tuple((i % 2 * n // 2, n // 2, base + i) for i in range(4))
-        out_pieces = tuple((n + i % 2 * n + i // 2 * n // 2, n // 2, base + 4 + i % 2) for i in range(4))
+        in_pieces = tuple((i // 2 * (n // 2), n // 2, base + i) for i in range(4))
+        out_pieces = tuple(
+            (n + i % 2 * n + i // 2 * (n // 2), n // 2, base + 4 + i % 2) for i in range(4)
+        )
     else:
         sides = []
-        for i, order in enumerate((order_a, order_b)):
+        for i, order in enumerate((out_a, out_b)):
             value = jnp.concatenate(out_parts[i::2], axis=0).reshape(n, rows_f, D // 2)
             sides.append(value[jnp.argsort(order.places(n))].reshape(FF, D // 2))
         in_parts, out_parts = [attn_in], [jnp.concatenate(sides, axis=1)]
@@ -768,19 +830,18 @@
     if not aligned:
         grad = jnp.concatenate(grads[:2], axis=0).reshape(n, rows_f, D)
         grads[:2] = jnp.split(grad[order_b.places(n)].reshape(FF, D), 2)
-    sum_out = Scatter(grads[0], swap(grads[1], core, n), n)
-    sum_in = Scatter(grads[2], swap(grads[3], core, n), n)
-
+    sum_out = Scatter(grads[0], swap(grads[1], [core], n), n)
+    sum_in = Scatter(grads[2], swap(grads[3], [core], n), n)
+
+    sum_in.recent = sum_out.recent = 1
     dqkv, biases = None, []
     for first, count, bits in ((0, 1, (one, two)), (1, 4, (two, one)), (5, 1, None)):
         dqkv, bias = attend_back(lengths, packed, dctx, ctxt, lse, first, count, dqkv)
         biases.append(bias)
         if bits is not None:
-            sum_in.terms[-1], sum_out.terms[-1], dqkv = phase(
-                sum_in.terms[-1], sum_out.terms[-1], dqkv
-            )
-            sum_in.step(bits[0])
-            sum_out.step(bits[1])
+            sum_in.got, sum_out.got, dqkv = phase(sum_in.got, sum_out.got, dqkv)
+            sum_in.step([bits[0]])
+            sum_out.step([bits[1]])
     full_qkv = jnp.concatenate(
         [
             arrange(to_a, jnp.concatenate(left, axis=0)),
@@ -788,8 +849,8 @@
         ],
         axis=1,
     )
-    dqkv, full_qkv, sum_in.terms[-1], sum_out.terms[-1] = phase(
-        dqkv, full_qkv, sum_in.terms[-1], sum_out.terms[-1]
+    dqkv, full_qkv, sum_in.got, sum_out.got = phase(
+        dqkv, full_qkv, sum_in.got, sum_out.got
     )
 
     def late_grads(side):
@@ -803,37 +864,39 @@
 
     away_a, away_b = late_grads(1)
     away_a, away_b, dqkv, away_in, away_out = phase(
-        away_a, away_b, dqkv, sum_in.away(), sum_out.away()
-    )
-    got_a, got_b = swap(away_a, core, n), swap(away_b, core, n)
-    sum_in.send(away_in, others[0])
-    sum_out.send(away_out, others[0])
+        away_a, away_b, dqkv, sum_in.away(others[:1]), sum_out.away(others[:1])
+    )
+    got_a, got_b = swap(away_a, [core], n), swap(away_b, [core], n)
+    sum_in.send(away_in, others[:1])
+    sum_out.send(away_out, others[:1])
     kept_a, kept_b = late_grads(0)
     got_a, got_b, kept_a, kept_b = phase(got_a, got_b, kept_a, kept_b)
     late_a, late_b = Scatter(kept_a, got_a, n), Scatter(kept_b, got_b, n)
-    late_a.step(one)
-    late_b.step(two)
-    late_a.terms[-1], late_b.terms[-1], sum_in.terms[-1], sum_out.terms[-1] = phase(
-        late_a.terms[-1], late_b.terms[-1], sum_in.terms[-1], sum_out.terms[-1]
+    late_a.step([one])
+    late_b.step([two])
+    late_a.got, late_b.got, sum_in.got, sum_out.got = phase(
+        late_a.got, late_b.got, sum_in.got, sum_out.got
     )
     away_a, away_b, *aways = phase(
-        late_a.away(), late_b.away(), *((sum_in.away(), sum_out.away()) if others[1:] else ())
-    )
-    late_a.send(away_a, two)
-    late_b.send(away_b, one)
+        late_a.away([two]),
+        late_b.away([one]),
+        *((sum_in.away(others[1:2]), sum_out.away(others[1:2])) if others[1:] else ()),
+    )
+    late_a.send(away_a, [two])
+    late_b.send(away_b, [one])
     for bit in others[1:2]:
-        sum_in.send(aways[0], bit)
-        sum_out.send(aways[1], bit)
+        sum_in.send(aways[0], [bit])
+        sum_out.send(aways[1], [bit])
     for bit in others[2:]:
-        sum_in.step(bit)
-        sum_out.step(bit)
-    late_a.terms[-1], late_b.terms[-1] = phase(late_a.terms[-1], late_b.terms[-1])
+        sum_in.step([bit])
+        sum_out.step([bit])
+    late_a.got, late_b.got = phase(late_a.got, late_b.got)
     late = late_a.join(late_b)
-    late.step(others[0])
+    late.step(others[:1])
     share_in, share_out = sum_in.total(), sum_out.total()
-    late.terms[-1], share_in, share_out = phase(late.terms[-1], share_in, share_out)
+    late.got, share_in, share_out = phase(late.got, share_in, share_out)
     for bit in others[1:]:
-        late.step(bit)
+        late.step([bit])
     share_late = late.total()
     bias_sums = jnp.concatenate(biases, axis=0)
     grad_vec = jnp.concatenate(
@@ -855,7 +918,7 @@
         *(w_qkv, share_late[:, : 3 * D], moment_qkv, square_qkv),
         *(w_attn, share_late[:, 3 * D :], moment_attn, square_attn),
     )
-    reduced = sum_all(jnp.concatenate([next_attn[6], grad_vec], axis=0), n)
+    reduced = sum_all(jnp.concatenate([next_attn[6], grad_vec], axis=0), [[bit] for bit in range(n.bit_length() - 1)], n)
     place = lax.axis_index("dp") * width
     share_vec = lax.dynamic_slice_in_dim(reduced[8:].reshape(-1), place, width, 0)
     updates = (next_attn[2], next_attn[5], next_in[2], next_in[5])

time: 333 us -> 323 us (0.970)
  waiting for transfers between devices: 83.5 us -> 75.3 us
  other arithmetic: 22.1 us -> 26.6 us
    ppermute x48 -> x47, waiting for transfers between devices: 83.5 us -> 75.3 us  [swap(): return lax.ppermute(value, 'dp', [(i, i ^ mask) for i in range(n)])]
    unnamed x89 -> x91, local copies, waits for them, and re-layouts: 14.4 us -> 11.2 us
    dot_general x5 -> x4, matrix products: 9.08 us -> 6.21 us  [dot(): return jnp.dot(a, b, preferred_element_type=F32)]
    concatenate x19 -> x18, other arithmetic: 6.98 us -> 9.58 us  [the longest x15 9.51 us: step(): self.value = jnp.concatenate([self.value, *got], axis=0)]
    ppermute x48 -> x47, starting transfers between devices: 42.8 us -> 41.6 us  [swap(): return lax.ppermute(value, 'dp', [(i, i ^ mask) for i in range(n)])]
  transfers between devices with their start and end apart: 48 -> 47, of which waited for: 28 -> 30; matrix products, arithmetic and copies ran while one was open for 12% -> 13% of each run, Pallas kernels for 20% -> 21%
where the time goes in v5:
time: 323 us; the launch traced here: 318 us
  Pallas kernels  132 us (41%)
  waiting for transfers between devices  75.3 us (23%)
  starting transfers between devices  41.6 us (13%)
  other arithmetic  26.6 us (8%)
  matrix products  20.3 us (6%)
  local copies, waits for them, and re-layouts  19 us (6%)
    ppermute x47, waiting for transfers between devices, swap(): return lax.ppermute(value, 'dp', [(i, i ^ mask) for i in range(n)])  75.3 us
    pallas_call x1, Pallas kernels, feed(): pl.pallas_call(partial(feed_kernel, in_pieces, out_pieces, steps), grid_s...  62.2 us
    ppermute x47, starting transfers between devices, swap(): return lax.ppermute(value, 'dp', [(i, i ^ mask) for i in range(n)])  41.6 us
    pallas_call x3, Pallas kernels, attend_back(): pl.pallas_call(after(partial(attend_back_kernel, min(512, seq)), 7, len(e...  34.7 us
    pallas_call x3, Pallas kernels, attend(): pl.pallas_call(after(attend_kernel, 4, len(extra)), grid_spec=pltpu.Prefe...  21.5 us
    unnamed x91, local copies, waits for them, and re-layouts  11.2 us
    concatenate x15, other arithmetic, step(): self.value = jnp.concatenate([self.value, *got], axis=0)  9.51 us
    dot_general x3, matrix products, dot_nt(): lax.dot_general(a, b, (((1,), (1,)), ((), ())), preferred_element_type=F32)  7.96 us
  transfers between devices with their start and end apart: 47, of which 30 were waited for; matrix products, arithmetic and copies ran while one was open for 13% of the time, Pallas kernels for 21%

profile of v5, /device:TPU:0, one launch (start us, length us, event | category | flops | bytes accessed | tf_op | source)
XLA Modules:
  0.0 318.0 jit_solution(16617327476063397470)
XLA Ops:
  3.1 5.0 %collective-permute-start.2 = (bf16[24,2432]{1,0:T(8,128)(2,1)}, bf16[24,2432]{1,0:T(8,128)(2,1)}, u32[]{:S(2)}, u32[]{:S(2)}) collective-permute-start(bf16[24,2432]{1,0:T(8,128)(2,1)} %fusion.84), channel_id=1, source_target_pairs={{0,24},{1,25},{2,26},{3,27},{4,28},{5,29},{6,30},{7,31},{8,16},{9,... | collective-permute-start | bytes 350216 | tf_op jit(solution)/shard_map/ppermute | solution.py:524
  16.7 1.7 collective-permute-done
  20.6 1.6 collective-permute-start.4
  22.2 1.6 collective-permute-start.5
  23.8 6.3 %collective-permute-done.6 = bf16[48,1920]{1,0:T(8,128)(2,1)S(1)} collective-permute-done((bf16[48,1920]{1,0:T(8,128)(2,1)S(1)}, bf16[48,1920]{1,0:T(8,128)(2,1)S(1)}, u32[]{:S(2)}, u32[]{:S(2)}) %collective-permute-start.6) | collective-permute-done | bytes 184352 | tf_op jit(solution)/shard_map/ppermute | solution.py:524
  31.4 2.1 collective-permute-start.9
  35.8 5.2 %collective-permute-done.9 = bf16[96,1920]{1,0:T(8,128)(2,1)S(1)} collective-permute-done((bf16[96,1920]{1,0:T(8,128)(2,1)S(1)}, bf16[96,1920]{1,0:T(8,128)(2,1)S(1)}, u32[]{:S(2)}, u32[]{:S(2)}) %collective-permute-start.9) | collective-permute-done | bytes 368672 | tf_op jit(solution)/shard_map/ppermute | solution.py:524
  41.1 3.1 collective-permute-done.7
  44.2 2.3 collective-permute-done.8
  47.3 3.2 %collective-permute-done.10.refs_3_ = bf16[384,1152]{1,0:T(8,128)(2,1)S(1)} collective-permute-done((bf16[384,1152]{1,0:T(8,128)(2,1)S(1)}, bf16[384,1152]{1,0:T(8,128)(2,1)S(1)}, u32[]{:S(2)}, u32[]{:S(2)}) %collective-permute-start.10) | collective-permute-done | bytes 884768 | tf_op jit(solution)/shard_map/ppermute | solution.py:524
  50.5 1.7 collective-permute-start.14
  53.9 1.6 collective-permute-start.12
  55.6 6.0 %project.1.refs_1_.refs_2_.refs_3_ = bf16[1024,2304]{1,0:T(8,128)(2,1)S(1)} custom-call(bf16[1024,768]{1,0:T(8,128)(2,1)S(1)} %fusion.29.refs_0_, bf16[1024,768]{1,0:T(8,128)(2,1)S(1)} %fusion.30.refs_1_, bf16[384,1152]{1,0:T(8,128)(2,1)S(1)} %pad_maximum_fusion.11.refs_2_, bf16[384,1152]{1,0:T(8,128)(2,1)S(1)} %collective-permute-done.10.refs_3_, ...), custom_call_target="tpu_custom_call" | custom-call | flops 250000000 | tf_op jit(solution)/shard_map/project/pallas_call | solution.py:79
  61.6 3.5 %attend.3 = (bf16[1024,768]{1,0:T(8,128)(2,1)S(1)}, f32[768,1024]{1,0:T(8,128)S(1)}, f32[6,2,1024]{2,1,0:T(2,128)S(1)}) custom-call(s32[1]{0:T(128)S(6)} %copy.67.refs_0_, bf16[1024,2304]{1,0:T(8,128)(2,1)S(1)} %project.1.refs_1_.refs_2_.refs_3_, bf16[1024,2304]{1,0:T(8,128)(2,1)S(1)} %project.1.refs_1_.refs_2_.refs_3_, ...), custom_call_target="tpu_custom_call" | custom-call | flops 200000000 | tf_op jit(solution)/shard_map/attend/pallas_call | solution.py:128
  68.0 10.8 %attend.4 = (bf16[1024,768]{1,0:T(8,128)(2,1)S(1)}, f32[768,1024]{1,0:T(8,128)S(1)}, f32[6,2,1024]{2,1,0:T(2,128)S(1)}) custom-call(s32[1]{0:T(128)S(6)} %copy.67.refs_0_, bf16[1024,2304]{1,0:T(8,128)(2,1)S(1)} %project.1.refs_1_.refs_2_.refs_3_, ...), custom_call_target="tpu_custom_call", output_to_operand_aliasing={{0}: (4, {}), {1}: (5, {}), {2}: (6, {})} | custom-call | flops 600000000 | tf_op jit(solution)/shard_map/attend/pallas_call | solution.py:128
  78.8 3.3 %collective-permute-done.15 = bf16[384,768]{1,0:T(8,128)(2,1)S(1)} collective-permute-done((bf16[384,768]{1,0:T(8,128)(2,1)S(1)}, bf16[384,768]{1,0:T(8,128)(2,1)S(1)}, u32[]{:S(2)}, u32[]{:S(2)}) %collective-permute-start.15) | collective-permute-done | bytes 589856 | tf_op jit(solution)/shard_map/ppermute | solution.py:524
  82.2 2.1 collective-permute-done.17
  92.8 1.8 reshape.214.refs_6_
  94.7 2.3 copy-done.1
  98.4 7.2 %attend.5 = (bf16[1024,768]{1,0:T(8,128)(2,1)S(1)}, f32[768,1024]{1,0:T(8,128)S(1)}, f32[6,2,1024]{2,1,0:T(2,128)S(1)}) custom-call(s32[1]{0:T(128)S(6)} %copy.67.refs_0_, bf16[1024,2304]{1,0:T(8,128)(2,1)S(1)} %copy-done.1, bf16[1024,2304]{1,0:T(8,128)(2,1)S(1)} %copy-done.1, ...), custom_call_target="tpu_custom_call", output_to_operand_aliasing={{0}: (4, {}), {1}: (5, {}), {2}: (6, {})} | custom-call | flops 400000000 | tf_op jit(solution)/shard_map/attend/pallas_call | solution.py:128
  105.7 2.9 pad_maximum_fusion.5.refs_14_
  108.6 2.4 pad_maximum_fusion.4.refs_13_
  114.3 1.7 collective-permute-done.23.refs_16_
  116.0 62.2 %feed.1 = (bf16[1024,768]{1,0:T(8,128)(2,1)}, f32[1024,768]{1,0:T(8,128)}, bf16[1024,768]{1,0:T(8,128)(2,1)}, f32[12,768]{1,0:T(8,128)}, bf16[1536,768]{1,0:T(8,...) custom-call(s32[1]{0:T(128)S(6)} %copy.67.refs_0_, ...), custom_call_target="tpu_custom_call" | custom-call | flops 2500000000 | tf_op jit(solution)/shard_map/feed/pallas_call | solution.py:478
  178.8 2.3 copy-done.2
  182.5 5.6 %attend_back.3 = (bf16[3,1024,768]{2,1,0:T(8,128)(2,1)S(1)}, f32[1,2,128]{2,1,0:T(2,128)S(1)}) custom-call(s32[1]{0:T(128)S(6)} %copy.67.refs_0_, bf16[1024,2304]{1,0:T(8,128)(2,1)S(1)} %copy-done.2, bf16[1024,2304]{1,0:T(8,128)(2,1)S(1)} %copy-done.2, bf16[1024,2304]{1,0:T(8,128)(2,1)S(1)} %copy-done.2, bf16[1024,768]{1,0:T(8,128)(2,1)S(1)} %copy-done.4, ...), custom_call_target="tpu_custom_call" | custom-call | flops 300000000 | tf_op jit(solution)/shard_map/attend_back/pallas_call | solution.py:220
  192.1 1.7 convolution_convert_fusion.1
  193.9 23.4 %attend_back.4 = (bf16[3,1024,768]{2,1,0:T(8,128)(2,1)S(1)}, f32[4,2,128]{2,1,0:T(2,128)S(1)}) custom-call(s32[1]{0:T(128)S(6)} %copy.67.refs_0_, bf16[1024,2304]{1,0:T(8,128)(2,1)S(1)} %copy-done.2, bf16[1024,2304]{1,0:T(8,128)(2,1)S(1)} %copy-done.2, bf16[1024,2304]{1,0:T(8,128)(2,1)S(1)} %copy-done.2, ...), custom_call_target="tpu_custom_call", output_to_operand_aliasing={{0}: (7, {})} | custom-call | flops 1200000000 | tf_op jit(solution)/shard_map/attend_back/pallas_call | solution.py:220
  222.5 1.7 convolution_convert_fusion
  224.2 2.1 pad_maximum_fusion
  226.3 5.7 %attend_back.5 = (bf16[3,1024,768]{2,1,0:T(8,128)(2,1)S(1)}, f32[1,2,128]{2,1,0:T(2,128)S(1)}) custom-call(s32[1]{0:T(128)S(6)} %copy.67.refs_0_, bf16[1024,2304]{1,0:T(8,128)(2,1)S(1)} %bitcast.65, bf16[1024,2304]{1,0:T(8,128)(2,1)S(1)} %bitcast.65, bf16[1024,2304]{1,0:T(8,128)(2,1)S(1)} %bitcast.65, ...), custom_call_target="tpu_custom_call", output_to_operand_aliasing={{0}: (7, {})} | custom-call | flops 300000000 | tf_op jit(solution)/shard_map/attend_back/pallas_call | solution.py:220
  231.9 3.3 %collective-permute-done.29 = bf16[384,768]{1,0:T(8,128)(2,1)S(1)} collective-permute-done((bf16[384,768]{1,0:T(8,128)(2,1)}, bf16[384,768]{1,0:T(8,128)(2,1)S(1)}, u32[]{:S(2)}, u32[]{:S(2)}) %collective-permute-start.29) | collective-permute-done | bytes 589856 | tf_op jit(solution)/shard_map/ppermute | solution.py:524
  246.6 1.7 collective-permute-start.34
  248.6 7.9 %collective-permute-done.34 = bf16[48,3072]{1,0:T(8,128)(2,1)S(1)} collective-permute-done((bf16[48,3072]{1,0:T(8,128)(2,1)S(1)}, bf16[48,3072]{1,0:T(8,128)(2,1)S(1)}, u32[]{:S(2)}, u32[]{:S(2)}) %collective-permute-start.34) | collective-permute-done | bytes 294944 | tf_op jit(solution)/shard_map/ppermute | solution.py:524
  256.5 4.9 %collective-permute-done.35 = bf16[192,768]{1,0:T(8,128)(2,1)S(1)} collective-permute-done((bf16[192,768]{1,0:T(8,128)(2,1)S(1)}, bf16[192,768]{1,0:T(8,128)(2,1)S(1)}, u32[]{:S(2)}, u32[]{:S(2)}) %collective-permute-start.35) | collective-permute-done | bytes 294944 | tf_op jit(solution)/shard_map/ppermute | solution.py:524
  261.8 1.8 collective-permute-start.36
  266.0 2.1 collective-permute-start.40
  271.3 1.8 collective-permute-start.38
  273.0 4.6 %collective-permute-done.39 = bf16[24,3072]{1,0:T(8,128)(2,1)S(1)} collective-permute-done((bf16[24,3072]{1,0:T(8,128)(2,1)S(1)}, bf16[24,3072]{1,0:T(8,128)(2,1)S(1)}, u32[]{:S(2)}, u32[]{:S(2)}) %collective-permute-start.39) | collective-permute-done | bytes 147488 | tf_op jit(solution)/shard_map/ppermute | solution.py:524
  280.3 2.5 collective-permute-done.38
  283.6 3.0 adapt.2
  286.7 3.0 collective-permute-done.41
  291.1 2.4 adapt.3
  296.9 2.5 collective-permute-done.43
  299.9 3.4 %fusion.14 = f32[1024,768]{1,0:T(8,128)S(1)} fusion(bf16[3,1024,768]{2,1,0:T(8,128)(2,1)} %copy-done.3, bf16[768,2304]{1,0:T(8,128)(2,1)} %pad_maximum_fusion), kind=kOutput, calls=%fused_computation.25 | convolution fusion | flops 1207959552 | bytes 5898240 | tf_op jit(solution)/shard_map/dot_general | solution.py:32
  305.1 2.4 collective-permute-done.45
  308.1 3.1 add_bitcast_fusion
  313.1 2.6 renew.1
  (261 shorter events, 78.0 us)
Async XLA Ops:
  3.1 13.5 %collective-permute-start.2 = (bf16[24,2432]{1,0:T(8,128)(2,1)}, bf16[24,2432]{1,0:T(8,128)(2,1)}, u32[]{:S(2)}, u32[]{:S(2)}) collective-permute-start(bf16[24,2432]{1,0:T(8,128)(2,1)} %fusion.84), channel_id=1, source_target_pairs={{0,24},{1,25},{2,26},{3,27},{4,28},{5,29},{6,30},{7,31},{8,16},{9,... | collective-permute-start | bytes 350216 | tf_op jit(solution)/shard_map/ppermute | solution.py:524
  8.2 8.5 %collective-permute-start.1 = (bf16[24,2432]{1,0:T(8,128)(2,1)}, bf16[24,2432]{1,0:T(8,128)(2,1)}, u32[]{:S(2)}, u32[]{:S(2)}) collective-permute-start(bf16[24,2432]{1,0:T(8,128)(2,1)} %fusion.84), channel_id=1, source_target_pairs={{0,8},{1,9},{2,10},{3,11},{4,12},{5,13},{6,14},{7,15},{8,0},{9,1},... | collective-permute-start | bytes 350216 | tf_op jit(solution)/shard_map/ppermute | solution.py:524
  8.2 10.2 %collective-permute-start = (bf16[24,2432]{1,0:T(8,128)(2,1)}, bf16[24,2432]{1,0:T(8,128)(2,1)}, u32[]{:S(2)}, u32[]{:S(2)}) collective-permute-start(bf16[24,2432]{1,0:T(8,128)(2,1)} %fusion.84), channel_id=1, source_target_pairs={{0,16},{1,17},{2,18},{3,19},{4,20},{5,21},{6,22},{7,23},{8,24},{9,... | collective-permute-start | bytes 350216 | tf_op jit(solution)/shard_map/ppermute | solution.py:524
  11.3 4.2 %collective-permute-start.3 = (bf16[24,1920]{1,0:T(8,128)(2,1)}, bf16[24,1920]{1,0:T(8,128)(2,1)}, u32[]{:S(2)}, u32[]{:S(2)}) collective-permute-start(bf16[24,1920]{1,0:T(8,128)(2,1)} %fusion.85), channel_id=1, source_target_pairs={{0,1},{1,0},{2,3},{3,2},{4,5},{5,4},{6,7},{7,6},{8,9},{9,8},{10,11... | collective-permute-start | bytes 276488 | tf_op jit(solution)/shard_map/ppermute | solution.py:524
  19.5 10.6 %collective-permute-start.6 = (bf16[48,1920]{1,0:T(8,128)(2,1)S(1)}, bf16[48,1920]{1,0:T(8,128)(2,1)S(1)}, u32[]{:S(2)}, u32[]{:S(2)}) collective-permute-start(bf16[48,1920]{1,0:T(8,128)(2,1)S(1)} %pad_maximum_fusion.26), channel_id=1, source_target_pairs={{0,16},{1,17},{2,18},{3,19},{4,20},{5,21},{6,22},{7,23},{8,24},{9,... | collective-permute-start | bytes 552968 | tf_op jit(solution)/shard_map/ppermute | solution.py:524
  20.6 9.5 %collective-permute-start.4 = (bf16[96,1536]{1,0:T(8,128)(2,1)S(1)}, bf16[96,1536]{1,0:T(8,128)(2,1)S(1)}, u32[]{:S(2)}, u32[]{:S(2)}) collective-permute-start(bf16[96,1536]{1,0:T(8,128)(2,1)S(1)} %pad_maximum_fusion.22), channel_id=1, source_target_pairs={{0,4},{1,5},{2,6},{3,7},{4,0},{5,1},{6,2},{7,3},{8,12},{9,13},{10,... | collective-permute-start | bytes 884744 | tf_op jit(solution)/shard_map/ppermute | solution.py:524
  22.2 9.1 %collective-permute-start.5 = (bf16[96,1664]{1,0:T(8,128)(2,1)S(1)}, bf16[96,1664]{1,0:T(8,128)(2,1)S(1)}, u32[]{:S(2)}, u32[]{:S(2)}) collective-permute-start(bf16[96,1664]{1,0:T(8,128)(2,1)S(1)} %pad_maximum_fusion.20), channel_id=1, source_target_pairs={{0,2},{1,3},{2,0},{3,1},{4,6},{5,7},{6,4},{7,5},{8,10},{9,11},{10,... | collective-permute-start | bytes 958472 | tf_op jit(solution)/shard_map/ppermute | solution.py:524
  31.4 9.6 %collective-permute-start.9 = (bf16[96,1920]{1,0:T(8,128)(2,1)S(1)}, bf16[96,1920]{1,0:T(8,128)(2,1)S(1)}, u32[]{:S(2)}, u32[]{:S(2)}) collective-permute-start(bf16[96,1920]{1,0:T(8,128)(2,1)S(1)} %pad_maximum_fusion.19), channel_id=1, source_target_pairs={{0,8},{1,9},{2,10},{3,11},{4,12},{5,13},{6,14},{7,15},{8,0},{9,1},... | collective-permute-start | bytes 1105928 | tf_op jit(solution)/shard_map/ppermute | solution.py:524
  33.5 10.6 %collective-permute-start.7 = (bf16[192,1152]{1,0:T(8,128)(2,1)S(1)}, bf16[192,1152]{1,0:T(8,128)(2,1)S(1)}, u32[]{:S(2)}, u32[]{:S(2)}) collective-permute-start(bf16[192,1152]{1,0:T(8,128)(2,1)S(1)} %slice.370), channel_id=1, source_target_pairs={{0,2},{1,3},{2,0},{3,1},{4,6},{5,7},{6,4},{7,5},{8,10},{9,11},{10,... | collective-permute-start | bytes 1327112 | tf_op jit(solution)/shard_map/ppermute | solution.py:524
  35.2 11.4 %collective-permute-start.8 = (bf16[192,1280]{1,0:T(8,128)(2,1)S(1)}, bf16[192,1280]{1,0:T(8,128)(2,1)S(1)}, u32[]{:S(2)}, u32[]{:S(2)}) collective-permute-start(bf16[192,1280]{1,0:T(8,128)(2,1)S(1)} %slice.371), channel_id=1, source_target_pairs={{0,4},{1,5},{2,6},{3,7},{4,0},{5,1},{6,2},{7,3},{8,12},{9,13},{10,... | collective-permute-start | bytes 1474568 | tf_op jit(solution)/shard_map/ppermute | solution.py:524
  46.6 44.9 %copy-start.9 = (bf16[384,1280]{1,0:T(8,128)(2,1)}, bf16[384,1280]{1,0:T(8,128)(2,1)S(1)}, u32[]{:S(2)}) copy-start(bf16[384,1280]{1,0:T(8,128)(2,1)S(1)} %pad_maximum_fusion.10.refs_4_) | copy-start | bytes 2949124
  46.6 3.9 %collective-permute-start.11 = (bf16[384,1280]{1,0:T(8,128)(2,1)S(1)}, bf16[384,1280]{1,0:T(8,128)(2,1)S(1)}, u32[]{:S(2)}, u32[]{:S(2)}) collective-permute-start(bf16[384,1280]{1,0:T(8,128)(2,1)S(1)} %pad_maximum_fusion.10.refs_4_), channel_id=1, source_target_pairs={{0,1},{1,0},{2,3},{3,2},{4,5},{5,4},{6,7},{7,6},{8,9},{9,8},{10,11... | collective-permute-start | bytes 2949128 | tf_op jit(solution)/shard_map/ppermute | solution.py:524
  46.7 3.8 %collective-permute-start.10 = (bf16[384,1152]{1,0:T(8,128)(2,1)S(1)}, bf16[384,1152]{1,0:T(8,128)(2,1)S(1)}, u32[]{:S(2)}, u32[]{:S(2)}) collective-permute-start(bf16[384,1152]{1,0:T(8,128)(2,1)S(1)} %pad_maximum_fusion.11.refs_2_), channel_id=1, source_target_pairs={{0,1},{1,0},{2,3},{3,2},{4,5},{5,4},{6,7},{7,6},{8,9},{9,8},{10,11... | collective-permute-start | bytes 2654216 | tf_op jit(solution)/shard_map/ppermute | solution.py:524
  50.5 16.0 %collective-permute-start.14 = (bf16[192,768]{1,0:T(8,128)(2,1)S(1)}, bf16[192,768]{1,0:T(8,128)(2,1)S(1)}, u32[]{:S(2)}, u32[]{:S(2)}) collective-permute-start(bf16[192,768]{1,0:T(8,128)(2,1)S(1)} %pad_maximum_fusion.23), channel_id=1, source_target_pairs={{0,16},{1,17},{2,18},{3,19},{4,20},{5,21},{6,22},{7,23},{8,24},{9,... | collective-permute-start | bytes 884744 | tf_op jit(solution)/shard_map/ppermute | solution.py:524
  52.9 13.7 %collective-permute-start.13 = (bf16[192,896]{1,0:T(8,128)(2,1)S(1)}, bf16[192,896]{1,0:T(8,128)(2,1)S(1)}, u32[]{:S(2)}, u32[]{:S(2)}) collective-permute-start(bf16[192,896]{1,0:T(8,128)(2,1)S(1)} %slice.375), channel_id=1, source_target_pairs={{0,2},{1,3},{2,0},{3,1},{4,6},{5,7},{6,4},{7,5},{8,10},{9,11},{10,... | collective-permute-start | bytes 1032200 | tf_op jit(solution)/shard_map/ppermute | solution.py:524
  53.9 12.8 %collective-permute-start.12 = (bf16[192,1024]{1,0:T(8,128)(2,1)S(1)}, bf16[192,1024]{1,0:T(8,128)(2,1)S(1)}, u32[]{:S(2)}, u32[]{:S(2)}) collective-permute-start(bf16[192,1024]{1,0:T(8,128)(2,1)S(1)} %slice.374), channel_id=1, source_target_pairs={{0,4},{1,5},{2,6},{3,7},{4,0},{5,1},{6,2},{7,3},{8,12},{9,13},{10,... | collective-permute-start | bytes 1179656 | tf_op jit(solution)/shard_map/ppermute | solution.py:524
  66.7 15.3 %collective-permute-start.15 = (bf16[384,768]{1,0:T(8,128)(2,1)S(1)}, bf16[384,768]{1,0:T(8,128)(2,1)S(1)}, u32[]{:S(2)}, u32[]{:S(2)}) collective-permute-start(bf16[384,768]{1,0:T(8,128)(2,1)S(1)} %pad_maximum_fusion.17), channel_id=1, source_target_pairs={{0,8},{1,9},{2,10},{3,11},{4,12},{5,13},{6,14},{7,15},{8,0},{9,1},... | collective-permute-start | bytes 1769480 | tf_op jit(solution)/shard_map/ppermute | solution.py:524
  66.8 17.4 %collective-permute-start.17 = (bf16[384,896]{1,0:T(8,128)(2,1)S(1)}, bf16[384,896]{1,0:T(8,128)(2,1)S(1)}, u32[]{:S(2)}, u32[]{:S(2)}) collective-permute-start(bf16[384,896]{1,0:T(8,128)(2,1)S(1)} %pad_maximum_fusion.14), channel_id=1, source_target_pairs={{0,4},{1,5},{2,6},{3,7},{4,0},{5,1},{6,2},{7,3},{8,12},{9,13},{10,... | collective-permute-start | bytes 2064392 | tf_op jit(solution)/shard_map/ppermute | solution.py:524
  67.4 19.2 %collective-permute-start.16 = (bf16[384,1024]{1,0:T(8,128)(2,1)S(1)}, bf16[384,1024]{1,0:T(8,128)(2,1)S(1)}, u32[]{:S(2)}, u32[]{:S(2)}) collective-permute-start(bf16[384,1024]{1,0:T(8,128)(2,1)S(1)} %pad_maximum_fusion.12), channel_id=1, source_target_pairs={{0,2},{1,3},{2,0},{3,1},{4,6},{5,7},{6,4},{7,5},{8,10},{9,11},{10,... | collective-permute-start | bytes 2359304 | tf_op jit(solution)/shard_map/ppermute | solution.py:524
  87.9 23.1 %collective-permute-start.20 = (bf16[768,1024]{1,0:T(8,128)(2,1)}, bf16[768,1024]{1,0:T(8,128)(2,1)}, u32[]{:S(2)}, u32[]{:S(2)}) collective-permute-start(bf16[768,1024]{1,0:T(8,128)(2,1)} %pad_maximum_fusion.1.refs_9_), channel_id=1, source_target_pairs={{0,1},{1,0},{2,3},{3,2},{4,5},{5,4},{6,7},{7,6},{8,9},{9,8},{10,11... | collective-permute-start | bytes 4718600 | tf_op jit(solution)/shard_map/ppermute | solution.py:524
  87.9 23.1 %collective-permute-start.21 = (bf16[768,896]{1,0:T(8,128)(2,1)}, bf16[768,896]{1,0:T(8,128)(2,1)}, u32[]{:S(2)}, u32[]{:S(2)}) collective-permute-start(bf16[768,896]{1,0:T(8,128)(2,1)} %pad_maximum_fusion.2.refs_11_), channel_id=1, source_target_pairs={{0,1},{1,0},{2,3},{3,2},{4,5},{5,4},{6,7},{7,6},{8,9},{9,8},{10,11... | collective-permute-start | bytes 4128776 | tf_op jit(solution)/shard_map/ppermute | solution.py:524
  89.5 16.1 %collective-permute-start.19 = (bf16[768,384]{1,0:T(8,128)(2,1)}, bf16[768,384]{1,0:T(8,128)(2,1)}, u32[]{:S(2)}, u32[]{:S(2)}) collective-permute-start(bf16[768,384]{1,0:T(8,128)(2,1)} %get-tuple-element.267), channel_id=1, source_target_pairs={{0,4},{1,5},{2,6},{3,7},{4,0},{5,1},{6,2},{7,3},{8,12},{9,13},{10,... | collective-permute-start | bytes 1769480 | tf_op jit(solution)/shard_map/ppermute | solution.py:524
  91.0 17.6 %collective-permute-start.18 = (bf16[768,384]{1,0:T(8,128)(2,1)}, bf16[768,384]{1,0:T(8,128)(2,1)}, u32[]{:S(2)}, u32[]{:S(2)}) collective-permute-start(bf16[768,384]{1,0:T(8,128)(2,1)} %get-tuple-element.268), channel_id=1, source_target_pairs={{0,2},{1,3},{2,0},{3,1},{4,6},{5,7},{6,4},{7,5},{8,10},{9,11},{10,... | collective-permute-start | bytes 1769480 | tf_op jit(solution)/shard_map/ppermute | solution.py:524
  111.0 3.3 %collective-permute-start.22 = (bf16[1536,384]{1,0:T(8,128)(2,1)}, bf16[1536,384]{1,0:T(8,128)(2,1)}, u32[]{:S(2)}, u32[]{:S(2)}) collective-permute-start(bf16[1536,384]{1,0:T(8,128)(2,1)} %pad_maximum_fusion.4.refs_13_), channel_id=1, source_target_pairs={{0,1},{1,0},{2,3},{3,2},{4,5},{5,4},{6,7},{7,6},{8,9},{9,8},{10,11... | collective-permute-start | bytes 3538952 | tf_op jit(solution)/shard_map/ppermute | solution.py:524
  111.1 4.9 %collective-permute-start.23 = (bf16[1536,384]{1,0:T(8,128)(2,1)}, bf16[1536,384]{1,0:T(8,128)(2,1)}, u32[]{:S(2)}, u32[]{:S(2)}) collective-permute-start(bf16[1536,384]{1,0:T(8,128)(2,1)} %pad_maximum_fusion.5.refs_14_), channel_id=1, source_target_pairs={{0,1},{1,0},{2,3},{3,2},{4,5},{5,4},{6,7},{7,6},{8,9},{9,8},{10,11... | collective-permute-start | bytes 3538952 | tf_op jit(solution)/shard_map/ppermute | solution.py:524
  178.2 10.0 %collective-permute-start.24 = (bf16[384,3072]{1,0:T(8,128)(2,1)}, bf16[384,3072]{1,0:T(8,128)(2,1)S(1)}, u32[]{:S(2)}, u32[]{:S(2)}) collective-permute-start(bf16[384,3072]{1,0:T(8,128)(2,1)} %get-tuple-element.199), channel_id=1, source_target_pairs={{0,1},{1,0},{2,3},{3,2},{4,5},{5,4},{6,7},{7,6},{8,9},{9,8},{10,11... | collective-permute-start | bytes 7077896 | tf_op jit(solution)/shard_map/ppermute | solution.py:524
  178.4 9.8 %collective-permute-start.25 = (bf16[1536,768]{1,0:T(8,128)(2,1)}, bf16[1536,768]{1,0:T(8,128)(2,1)S(1)}, u32[]{:S(2)}, u32[]{:S(2)}) collective-permute-start(bf16[1536,768]{1,0:T(8,128)(2,1)} %get-tuple-element.200), channel_id=1, source_target_pairs={{0,1},{1,0},{2,3},{3,2},{4,5},{5,4},{6,7},{7,6},{8,9},{9,8},{10,11... | collective-permute-start | bytes 7077896 | tf_op jit(solution)/shard_map/ppermute | solution.py:524
  188.5 28.8 %collective-permute-start.27 = (bf16[768,768]{1,0:T(8,128)(2,1)S(1)}, bf16[768,768]{1,0:T(8,128)(2,1)S(1)}, u32[]{:S(2)}, u32[]{:S(2)}) collective-permute-start(bf16[768,768]{1,0:T(8,128)(2,1)S(1)} %add_convert_fusion), channel_id=1, source_target_pairs={{0,4},{1,5},{2,6},{3,7},{4,0},{5,1},{6,2},{7,3},{8,12},{9,13},{10,... | collective-permute-start | bytes 3538952 | tf_op jit(solution)/shard_map/ppermute | solution.py:524
  190.3 28.1 %collective-permute-start.26 = (bf16[192,3072]{1,0:T(8,128)(2,1)S(1)}, bf16[192,3072]{1,0:T(8,128)(2,1)S(1)}, u32[]{:S(2)}, u32[]{:S(2)}) collective-permute-start(bf16[192,3072]{1,0:T(8,128)(2,1)S(1)} %add_convert_fusion.1), channel_id=1, source_target_pairs={{0,2},{1,3},{2,0},{3,1},{4,6},{5,7},{6,4},{7,5},{8,10},{9,11},{10,... | collective-permute-start | bytes 3538952 | tf_op jit(solution)/shard_map/ppermute | solution.py:524
  220.4 14.7 %collective-permute-start.29 = (bf16[384,768]{1,0:T(8,128)(2,1)}, bf16[384,768]{1,0:T(8,128)(2,1)S(1)}, u32[]{:S(2)}, u32[]{:S(2)}) collective-permute-start(bf16[384,768]{1,0:T(8,128)(2,1)} %add_convert_fusion.4), channel_id=1, source_target_pairs={{0,2},{1,3},{2,0},{3,1},{4,6},{5,7},{6,4},{7,5},{8,10},{9,11},{10,... | collective-permute-start | bytes 1769480 | tf_op jit(solution)/shard_map/ppermute | solution.py:524
  221.9 14.5 %collective-permute-start.28 = (bf16[96,3072]{1,0:T(8,128)(2,1)}, bf16[96,3072]{1,0:T(8,128)(2,1)S(1)}, u32[]{:S(2)}, u32[]{:S(2)}) collective-permute-start(bf16[96,3072]{1,0:T(8,128)(2,1)} %add_convert_fusion.5), channel_id=1, source_target_pairs={{0,4},{1,5},{2,6},{3,7},{4,0},{5,1},{6,2},{7,3},{8,12},{9,13},{10,... | collective-permute-start | bytes 1769480 | tf_op jit(solution)/shard_map/ppermute | solution.py:524
  240.7 3.5 %collective-permute-start.30 = (bf16[384,1536]{1,0:T(8,128)(2,1)S(1)}, bf16[384,1536]{1,0:T(8,128)(2,1)S(1)}, u32[]{:S(2)}, u32[]{:S(2)}) collective-permute-start(bf16[384,1536]{1,0:T(8,128)(2,1)S(1)} %pad_maximum_fusion.6), channel_id=1, source_target_pairs={{0,1},{1,0},{2,3},{3,2},{4,5},{5,4},{6,7},{7,6},{8,9},{9,8},{10,11... | collective-permute-start | bytes 3538952 | tf_op jit(solution)/shard_map/ppermute | solution.py:524
  240.8 4.5 %collective-permute-start.31 = (bf16[384,1536]{1,0:T(8,128)(2,1)S(1)}, bf16[384,1536]{1,0:T(8,128)(2,1)S(1)}, u32[]{:S(2)}, u32[]{:S(2)}) collective-permute-start(bf16[384,1536]{1,0:T(8,128)(2,1)S(1)} %pad_maximum_fusion.7), channel_id=1, source_target_pairs={{0,1},{1,0},{2,3},{3,2},{4,5},{5,4},{6,7},{7,6},{8,9},{9,8},{10,11... | collective-permute-start | bytes 3538952 | tf_op jit(solution)/shard_map/ppermute | solution.py:524
  245.5 15.9 %collective-permute-start.33 = (bf16[192,1536]{1,0:T(8,128)(2,1)S(1)}, bf16[192,1536]{1,0:T(8,128)(2,1)S(1)}, u32[]{:S(2)}, u32[]{:S(2)}) collective-permute-start(bf16[192,1536]{1,0:T(8,128)(2,1)S(1)} %add_convert_fusion.2), channel_id=1, source_target_pairs={{0,4},{1,5},{2,6},{3,7},{4,0},{5,1},{6,2},{7,3},{8,12},{9,13},{10,... | collective-permute-start | bytes 1769480 | tf_op jit(solution)/shard_map/ppermute | solution.py:524
  246.0 15.4 %collective-permute-start.32 = (bf16[192,1536]{1,0:T(8,128)(2,1)S(1)}, bf16[192,1536]{1,0:T(8,128)(2,1)S(1)}, u32[]{:S(2)}, u32[]{:S(2)}) collective-permute-start(bf16[192,1536]{1,0:T(8,128)(2,1)S(1)} %add_convert_fusion.3), channel_id=1, source_target_pairs={{0,2},{1,3},{2,0},{3,1},{4,6},{5,7},{6,4},{7,5},{8,10},{9,11},{10,... | collective-permute-start | bytes 1769480 | tf_op jit(solution)/shard_map/ppermute | solution.py:524
  246.6 9.9 %collective-permute-start.34 = (bf16[48,3072]{1,0:T(8,128)(2,1)S(1)}, bf16[48,3072]{1,0:T(8,128)(2,1)S(1)}, u32[]{:S(2)}, u32[]{:S(2)}) collective-permute-start(bf16[48,3072]{1,0:T(8,128)(2,1)S(1)} %add_convert_fusion.9), channel_id=1, source_target_pairs={{0,8},{1,9},{2,10},{3,11},{4,12},{5,13},{6,14},{7,15},{8,0},{9,1},... | collective-permute-start | bytes 884744 | tf_op jit(solution)/shard_map/ppermute | solution.py:524
  248.2 13.1 %collective-permute-start.35 = (bf16[192,768]{1,0:T(8,128)(2,1)S(1)}, bf16[192,768]{1,0:T(8,128)(2,1)S(1)}, u32[]{:S(2)}, u32[]{:S(2)}) collective-permute-start(bf16[192,768]{1,0:T(8,128)(2,1)S(1)} %add_convert_fusion.8), channel_id=1, source_target_pairs={{0,8},{1,9},{2,10},{3,11},{4,12},{5,13},{6,14},{7,15},{8,0},{9,1},... | collective-permute-start | bytes 884744 | tf_op jit(solution)/shard_map/ppermute | solution.py:524
  261.8 7.8 %collective-permute-start.36 = (bf16[96,1536]{1,0:T(8,128)(2,1)S(1)}, bf16[96,1536]{1,0:T(8,128)(2,1)S(1)}, u32[]{:S(2)}, u32[]{:S(2)}) collective-permute-start(bf16[96,1536]{1,0:T(8,128)(2,1)S(1)} %add_convert_fusion.7), channel_id=1, source_target_pairs={{0,4},{1,5},{2,6},{3,7},{4,0},{5,1},{6,2},{7,3},{8,12},{9,13},{10,... | collective-permute-start | bytes 884744 | tf_op jit(solution)/shard_map/ppermute | solution.py:524
  263.6 7.3 %collective-permute-start.37 = (bf16[96,1536]{1,0:T(8,128)(2,1)S(1)}, bf16[96,1536]{1,0:T(8,128)(2,1)S(1)}, u32[]{:S(2)}, u32[]{:S(2)}) collective-permute-start(bf16[96,1536]{1,0:T(8,128)(2,1)S(1)} %add_convert_fusion.6), channel_id=1, source_target_pairs={{0,2},{1,3},{2,0},{3,1},{4,6},{5,7},{6,4},{7,5},{8,10},{9,11},{10,... | collective-permute-start | bytes 884744 | tf_op jit(solution)/shard_map/ppermute | solution.py:524
  265.1 12.5 %collective-permute-start.39 = (bf16[24,3072]{1,0:T(8,128)(2,1)S(1)}, bf16[24,3072]{1,0:T(8,128)(2,1)S(1)}, u32[]{:S(2)}, u32[]{:S(2)}) collective-permute-start(bf16[24,3072]{1,0:T(8,128)(2,1)S(1)} %add_convert_fusion.11), channel_id=1, source_target_pairs={{0,16},{1,17},{2,18},{3,19},{4,20},{5,21},{6,22},{7,23},{8,24},{9,... | collective-permute-start | bytes 442376 | tf_op jit(solution)/shard_map/ppermute | solution.py:524
  266.0 13.5 %collective-permute-start.40 = (bf16[96,768]{1,0:T(8,128)(2,1)S(1)}, bf16[96,768]{1,0:T(8,128)(2,1)S(1)}, u32[]{:S(2)}, u32[]{:S(2)}) collective-permute-start(bf16[96,768]{1,0:T(8,128)(2,1)S(1)} %add_convert_fusion.10), channel_id=1, source_target_pairs={{0,16},{1,17},{2,18},{3,19},{4,20},{5,21},{6,22},{7,23},{8,24},{9,... | collective-permute-start | bytes 442376 | tf_op jit(solution)/shard_map/ppermute | solution.py:524
  271.3 11.6 %collective-permute-start.38 = (bf16[48,3072]{1,0:T(8,128)(2,1)S(1)}, bf16[48,3072]{1,0:T(8,128)(2,1)S(1)}, u32[]{:S(2)}, u32[]{:S(2)}) collective-permute-start(bf16[48,3072]{1,0:T(8,128)(2,1)S(1)} %fusion.71), channel_id=1, source_target_pairs={{0,8},{1,9},{2,10},{3,11},{4,12},{5,13},{6,14},{7,15},{8,0},{9,1},... | collective-permute-start | bytes 884744 | tf_op jit(solution)/shard_map/ppermute | solution.py:524
  282.9 6.8 %collective-permute-start.41 = (bf16[24,3072]{1,0:T(8,128)(2,1)S(1)}, bf16[24,3072]{1,0:T(8,128)(2,1)S(1)}, u32[]{:S(2)}, u32[]{:S(2)}) collective-permute-start(bf16[24,3072]{1,0:T(8,128)(2,1)S(1)} %fusion.80), channel_id=1, source_target_pairs={{0,16},{1,17},{2,18},{3,19},{4,20},{5,21},{6,22},{7,23},{8,24},{9,... | collective-permute-start | bytes 442376 | tf_op jit(solution)/shard_map/ppermute | solution.py:524
  294.2 1.2 collective-permute-start.42
  295.4 4.0 %collective-permute-start.43 = (f32[80,128]{1,0:T(8,128)S(1)}, f32[80,128]{1,0:T(8,128)S(1)}, u32[]{:S(2)}, u32[]{:S(2)}) collective-permute-start(f32[80,128]{1,0:T(8,128)S(1)} %add.507), channel_id=1, source_target_pairs={{0,2},{1,3},{2,0},{3,1},{4,6},{5,7},{6,4},{7,5},{8,10},{9,11},{10,... | collective-permute-start | bytes 122888 | tf_op jit(solution)/shard_map/ppermute | solution.py:524
  299.4 4.1 %collective-permute-start.44 = (f32[80,128]{1,0:T(8,128)S(1)}, f32[80,128]{1,0:T(8,128)S(1)}, u32[]{:S(2)}, u32[]{:S(2)}) collective-permute-start(f32[80,128]{1,0:T(8,128)S(1)} %add.508), channel_id=1, source_target_pairs={{0,4},{1,5},{2,6},{3,7},{4,0},{5,1},{6,2},{7,3},{8,12},{9,13},{10,... | collective-permute-start | bytes 122888 | tf_op jit(solution)/shard_map/ppermute | solution.py:524
  303.5 4.0 %collective-permute-start.45 = (f32[80,128]{1,0:T(8,128)S(1)}, f32[80,128]{1,0:T(8,128)S(1)}, u32[]{:S(2)}, u32[]{:S(2)}) collective-permute-start(f32[80,128]{1,0:T(8,128)S(1)} %add.509), channel_id=1, source_target_pairs={{0,8},{1,9},{2,10},{3,11},{4,12},{5,13},{6,14},{7,15},{8,0},{9,1},... | collective-permute-start | bytes 122888 | tf_op jit(solution)/shard_map/ppermute | solution.py:524
  307.6 4.9 %collective-permute-start.46 = (f32[80,128]{1,0:T(8,128)S(1)}, f32[80,128]{1,0:T(8,128)S(1)}, u32[]{:S(2)}, u32[]{:S(2)}) collective-permute-start(f32[80,128]{1,0:T(8,128)S(1)} %add.510), channel_id=1, source_target_pairs={{0,16},{1,17},{2,18},{3,19},{4,20},{5,21},{6,22},{7,23},{8,24},{9,... | collective-permute-start | bytes 122888 | tf_op jit(solution)/shard_map/ppermute | solution.py:524
  (44 other events, 295.8 us)

commit v6 on v5

--- a/solution.py
+++ b/solution.py
@@ -16,7 +16,7 @@
 CHUNKS = FF // D
 STEP = 10
 MASKED = -1e9
-VMEM = 60 * 2**20
+VMEM = 56 * 2**20
 ROOM = 24 * 2**20
 
 
@@ -631,36 +631,39 @@
     return result
 
 
-def adapt_kernel(first, *refs):
+def adapt_kernel(first, columns, *refs):
     before_ref, sums_ref = refs[8], refs[15]
-    sums = before_ref[...]
+    sums = before_ref[:8, :]
     row = lax.broadcasted_iota(jnp.int32, sums.shape, 0)
     for i in range(2):
         weight_ref, grad_ref, moment_ref, square_ref = refs[i * 4 : i * 4 + 4]
         outs = refs[9 + i * 3 : 12 + i * 3]
         weight = weight_ref[...]
-        values = adapt(weight, grad_ref[...], moment_ref[...], square_ref[...], 0.01)
+        grad = grad_ref[:, columns[i] : columns[i] + weight.shape[1]]
+        values = adapt(weight, grad, moment_ref[...], square_ref[...], 0.01)
         for out, value in zip(outs, values):
             out[...] = value
         sums = jnp.where(row == first + i, lane_sums(weight), sums)
         sums = jnp.where(row == 4 + first + i, lane_sums(values[2]), sums)
-    sums_ref[...] = sums
-
-
-def adapt_two(first, before, *operands):
+    sums_ref[:8, :] = sums
+    if sums_ref.shape[0] > 8:
+        sums_ref[8:, :] = before_ref[8:, :]
+
+
+def adapt_two(first, columns, before, *operands):
     shapes = [jax.ShapeDtypeStruct(operands[i * 4].shape, F32) for i in (0, 0, 0, 1, 1, 1)]
     return pl.pallas_call(
-        partial(adapt_kernel, first),
-        out_shape=shapes + [jax.ShapeDtypeStruct((8, 128), F32)],
-        compiler_params=pltpu.CompilerParams(vmem_limit_bytes=VMEM),
+        partial(adapt_kernel, first, columns),
+        out_shape=shapes + [jax.ShapeDtypeStruct(before.shape, F32)],
+        compiler_params=pltpu.CompilerParams(vmem_limit_bytes=ROOM),
         cost_estimate=cost(2),
         name="adapt",
     )(*operands, before)
 
 
 def renew_kernel(sums_ref, *refs):
-    norms = jnp.sqrt(jnp.sum(sums_ref[...], axis=1, keepdims=True))
-    refs[12][...] = jnp.broadcast_to(norms, (8, 128))
+    norms = jnp.sqrt(jnp.sum(sums_ref[:8, :], axis=1, keepdims=True))
+    refs[12][...] = jnp.broadcast_to(norms, (8, 128)).T[:1, :]
     for i in range(4):
         rate = 0.25 * (norms[i : i + 1] / norms[4 + i : 5 + i])
         refs[8 + i][...] = refs[i][...] - rate * refs[4 + i][...]
@@ -670,8 +673,8 @@
     return pl.pallas_call(
         renew_kernel,
         out_shape=[jax.ShapeDtypeStruct(weight.shape, F32) for weight in weights]
-        + [jax.ShapeDtypeStruct((8, 128), F32)],
-        compiler_params=pltpu.CompilerParams(vmem_limit_bytes=VMEM),
+        + [jax.ShapeDtypeStruct((1, 8), F32)],
+        compiler_params=pltpu.CompilerParams(vmem_limit_bytes=ROOM),
         cost_estimate=cost(2),
         name="renew",
     )(sums, *weights, *updates)
@@ -908,21 +911,23 @@
 
     next_in = adapt_two(
         2,
-        jnp.zeros((8, 128), F32),
+        (0, 0),
+        jnp.concatenate([jnp.zeros((8, 128), F32), grad_vec], axis=0),
         *(w_in, share_in, moment_in, square_in),
         *(w_out, share_out, moment_out, square_out),
     )
     next_attn = adapt_two(
         0,
+        (0, 3 * D),
         next_in[6],
-        *(w_qkv, share_late[:, : 3 * D], moment_qkv, square_qkv),
-        *(w_attn, share_late[:, 3 * D :], moment_attn, square_attn),
-    )
-    reduced = sum_all(jnp.concatenate([next_attn[6], grad_vec], axis=0), [[bit] for bit in range(n.bit_length() - 1)], n)
+        *(w_qkv, share_late, moment_qkv, square_qkv),
+        *(w_attn, share_late, moment_attn, square_attn),
+    )
+    reduced = sum_all(next_attn[6], [[bit] for bit in range(n.bit_length() - 1)], n)
     place = lax.axis_index("dp") * width
     share_vec = lax.dynamic_slice_in_dim(reduced[8:].reshape(-1), place, width, 0)
     updates = (next_attn[2], next_attn[5], next_in[2], next_in[5])
-    *new_weights, norms = renew(reduced[:8], (w_qkv, w_attn, w_in, w_out), updates)
+    *new_weights, norms = renew(reduced, (w_qkv, w_attn, w_in, w_out), updates)
     vec_moment, vec_square, vec_update = adapt(vectors, share_vec, moment_vec, square_vec, 0.0)
     return (
         mixed[None],
@@ -931,7 +936,7 @@
         vectors - 0.4 * vec_update,
         *(next_attn[0], next_attn[3], next_in[0], next_in[3], vec_moment),
         *(next_attn[1], next_attn[4], next_in[1], next_in[4], vec_square),
-        norms[:, 0],
+        norms.reshape(8),
     )
 
 

time: 323 us -> 319 us (0.988)
  waiting for transfers between devices: 75.3 us -> 80.7 us
  local copies, waits for them, and re-layouts: 19 us -> 13.7 us
  Pallas kernels: 132 us -> 128 us
    ppermute x47, waiting for transfers between devices: 75.3 us -> 80.7 us  [swap(): return lax.ppermute(value, 'dp', [(i, i ^ mask) for i in range(n)])]
    unnamed x91 -> x120, local copies, waits for them, and re-layouts: 11.2 us -> 8.98 us
  transfers between devices with their start and end apart: 47 -> 47, of which waited for: 30 -> 31; matrix products, arithmetic and copies ran while one was open for 13% -> 12% of each run, Pallas kernels for 21% -> 20%
where the time goes in v6:
time: 319 us; the launch traced here: 314 us
  Pallas kernels  128 us (40%)
  waiting for transfers between devices  80.7 us (25%)
  starting transfers between devices  41.4 us (13%)
  other arithmetic  26.6 us (8%)
  matrix products  20.2 us (6%)
  local copies, waits for them, and re-layouts  13.7 us (4%)
    ppermute x47, waiting for transfers between devices, swap(): return lax.ppermute(value, 'dp', [(i, i ^ mask) for i in range(n)])  80.7 us
    pallas_call x1, Pallas kernels, feed(): pl.pallas_call(partial(feed_kernel, in_pieces, out_pieces, steps), grid_s...  62.4 us
    ppermute x47, starting transfers between devices, swap(): return lax.ppermute(value, 'dp', [(i, i ^ mask) for i in range(n)])  41.4 us
    pallas_call x3, Pallas kernels, attend_back(): pl.pallas_call(after(partial(attend_back_kernel, min(512, seq)), 7, len(e...  34.7 us
    pallas_call x3, Pallas kernels, attend(): pl.pallas_call(after(attend_kernel, 4, len(extra)), grid_spec=pltpu.Prefe...  21.5 us
    concatenate x15, other arithmetic, step(): self.value = jnp.concatenate([self.value, *got], axis=0)  9.51 us
    unnamed x120, local copies, waits for them, and re-layouts  8.98 us
    dot_general x3, matrix products, dot_nt(): lax.dot_general(a, b, (((1,), (1,)), ((), ())), preferred_element_type=F32)  7.86 us
  transfers between devices with their start and end apart: 47, of which 31 were waited for; matrix products, arithmetic and copies ran while one was open for 12% of the time, Pallas kernels for 20%

profile of v6, /device:TPU:0, one launch (start us, length us, event | category | flops | bytes accessed | tf_op | source)
XLA Modules:
  0.0 313.6 jit_solution(4942619198258388860)
XLA Ops:
  3.1 5.0 %collective-permute-start.2 = (bf16[24,2432]{1,0:T(8,128)(2,1)}, bf16[24,2432]{1,0:T(8,128)(2,1)}, u32[]{:S(2)}, u32[]{:S(2)}) collective-permute-start(bf16[24,2432]{1,0:T(8,128)(2,1)} %fusion.84), channel_id=1, source_target_pairs={{0,24},{1,25},{2,26},{3,27},{4,28},{5,29},{6,30},{7,31},{8,16},{9,... | collective-permute-start | bytes 350216 | tf_op jit(solution)/shard_map/ppermute | solution.py:524
  19.5 2.0 collective-permute-start.6
  21.5 1.6 collective-permute-start.4
  23.2 1.6 collective-permute-start.5
  24.7 6.4 %collective-permute-done.6 = bf16[48,1920]{1,0:T(8,128)(2,1)S(1)} collective-permute-done((bf16[48,1920]{1,0:T(8,128)(2,1)S(1)}, bf16[48,1920]{1,0:T(8,128)(2,1)S(1)}, u32[]{:S(2)}, u32[]{:S(2)}) %collective-permute-start.6) | collective-permute-done | bytes 184352 | tf_op jit(solution)/shard_map/ppermute | solution.py:524
  32.7 2.1 collective-permute-start.9
  34.9 1.6 collective-permute-start.7
  37.1 5.7 %collective-permute-done.9 = bf16[96,1920]{1,0:T(8,128)(2,1)S(1)} collective-permute-done((bf16[96,1920]{1,0:T(8,128)(2,1)S(1)}, bf16[96,1920]{1,0:T(8,128)(2,1)S(1)}, u32[]{:S(2)}, u32[]{:S(2)}) %collective-permute-start.9) | collective-permute-done | bytes 368672 | tf_op jit(solution)/shard_map/ppermute | solution.py:524
  42.8 3.1 collective-permute-done.7
  46.0 2.3 collective-permute-done.8
  49.1 3.2 %collective-permute-done.10.refs_3_ = bf16[384,1152]{1,0:T(8,128)(2,1)S(1)} collective-permute-done((bf16[384,1152]{1,0:T(8,128)(2,1)S(1)}, bf16[384,1152]{1,0:T(8,128)(2,1)S(1)}, u32[]{:S(2)}, u32[]{:S(2)}) %collective-permute-start.10) | collective-permute-done | bytes 884768 | tf_op jit(solution)/shard_map/ppermute | solution.py:524
  55.3 1.6 collective-permute-start.12
  56.9 6.0 %project.1.refs_1_.refs_2_.refs_3_ = bf16[1024,2304]{1,0:T(8,128)(2,1)S(1)} custom-call(bf16[1024,768]{1,0:T(8,128)(2,1)S(1)} %fusion.29.refs_0_, bf16[1024,768]{1,0:T(8,128)(2,1)S(1)} %fusion.30.refs_1_, bf16[384,1152]{1,0:T(8,128)(2,1)S(1)} %pad_maximum_fusion.11.refs_2_, bf16[384,1152]{1,0:T(8,128)(2,1)S(1)} %collective-permute-done.10.refs_3_, ...), custom_call_target="tpu_custom_call" | custom-call | flops 250000000 | tf_op jit(solution)/shard_map/project/pallas_call | solution.py:79
  62.9 3.5 %attend.3 = (bf16[1024,768]{1,0:T(8,128)(2,1)S(1)}, f32[768,1024]{1,0:T(8,128)S(1)}, f32[6,2,1024]{2,1,0:T(2,128)S(1)}) custom-call(s32[1]{0:T(128)S(6)} %copy.66.refs_0_, bf16[1024,2304]{1,0:T(8,128)(2,1)S(1)} %project.1.refs_1_.refs_2_.refs_3_, bf16[1024,2304]{1,0:T(8,128)(2,1)S(1)} %project.1.refs_1_.refs_2_.refs_3_, ...), custom_call_target="tpu_custom_call" | custom-call | flops 200000000 | tf_op jit(solution)/shard_map/attend/pallas_call | solution.py:128
  66.4 1.9 collective-permute-done.14
  69.7 10.8 %attend.4 = (bf16[1024,768]{1,0:T(8,128)(2,1)S(1)}, f32[768,1024]{1,0:T(8,128)S(1)}, f32[6,2,1024]{2,1,0:T(2,128)S(1)}) custom-call(s32[1]{0:T(128)S(6)} %copy.66.refs_0_, bf16[1024,2304]{1,0:T(8,128)(2,1)S(1)} %project.1.refs_1_.refs_2_.refs_3_, ...), custom_call_target="tpu_custom_call", output_to_operand_aliasing={{0}: (4, {}), {1}: (5, {}), {2}: (6, {})} | custom-call | flops 600000000 | tf_op jit(solution)/shard_map/attend/pallas_call | solution.py:128
  80.5 3.3 %collective-permute-done.15 = bf16[384,768]{1,0:T(8,128)(2,1)S(1)} collective-permute-done((bf16[384,768]{1,0:T(8,128)(2,1)S(1)}, bf16[384,768]{1,0:T(8,128)(2,1)S(1)}, u32[]{:S(2)}, u32[]{:S(2)}) %collective-permute-start.15) | collective-permute-done | bytes 589856 | tf_op jit(solution)/shard_map/ppermute | solution.py:524
  83.9 2.1 collective-permute-done.17
  94.7 1.8 reshape.217.refs_6_
  96.5 2.3 copy-done.1
  100.3 7.2 %attend.5 = (bf16[1024,768]{1,0:T(8,128)(2,1)S(1)}, f32[768,1024]{1,0:T(8,128)S(1)}, f32[6,2,1024]{2,1,0:T(2,128)S(1)}) custom-call(s32[1]{0:T(128)S(6)} %copy.66.refs_0_, bf16[1024,2304]{1,0:T(8,128)(2,1)S(1)} %copy-done.1, bf16[1024,2304]{1,0:T(8,128)(2,1)S(1)} %copy-done.1, ...), custom_call_target="tpu_custom_call", output_to_operand_aliasing={{0}: (4, {}), {1}: (5, {}), {2}: (6, {})} | custom-call | flops 400000000 | tf_op jit(solution)/shard_map/attend/pallas_call | solution.py:128
  107.5 3.0 pad_maximum_fusion.5.refs_14_
  110.5 2.4 pad_maximum_fusion.4.refs_13_
  116.1 1.7 collective-permute-done.23.refs_16_
  117.8 62.4 %feed.1 = (bf16[1024,768]{1,0:T(8,128)(2,1)}, f32[1024,768]{1,0:T(8,128)}, bf16[1024,768]{1,0:T(8,128)(2,1)}, f32[12,768]{1,0:T(8,128)}, bf16[1536,768]{1,0:T(8,...) custom-call(s32[1]{0:T(128)S(6)} %copy.66.refs_0_, ...), custom_call_target="tpu_custom_call" | custom-call | flops 2500000000 | tf_op jit(solution)/shard_map/feed/pallas_call | solution.py:478
  182.2 5.6 %attend_back.3 = (bf16[3,1024,768]{2,1,0:T(8,128)(2,1)S(1)}, f32[1,2,128]{2,1,0:T(2,128)S(1)}) custom-call(s32[1]{0:T(128)S(6)} %copy.66.refs_0_, bf16[1024,2304]{1,0:T(8,128)(2,1)S(1)} %bitcast.66, bf16[1024,2304]{1,0:T(8,128)(2,1)S(1)} %bitcast.66, bf16[1024,2304]{1,0:T(8,128)(2,1)S(1)} %bitcast.66, bf16[1024,768]{1,0:T(8,128)(2,1)S(1)} %copy-done.3, ...), custom_call_target="tpu_custom_call" | custom-call | flops 300000000 | tf_op jit(solution)/shard_map/attend_back/pallas_call | solution.py:220
  190.5 1.5 collective-permute-start.26
  192.3 1.7 convolution_convert_fusion.1
  194.0 23.4 %attend_back.4 = (bf16[3,1024,768]{2,1,0:T(8,128)(2,1)S(1)}, f32[4,2,128]{2,1,0:T(2,128)S(1)}) custom-call(s32[1]{0:T(128)S(6)} %copy.66.refs_0_, bf16[1024,2304]{1,0:T(8,128)(2,1)S(1)} %bitcast.66, bf16[1024,2304]{1,0:T(8,128)(2,1)S(1)} %bitcast.66, bf16[1024,2304]{1,0:T(8,128)(2,1)S(1)} %bitcast.66, ...), custom_call_target="tpu_custom_call", output_to_operand_aliasing={{0}: (7, {})} | custom-call | flops 1200000000 | tf_op jit(solution)/shard_map/attend_back/pallas_call | solution.py:220
  222.7 1.7 convolution_convert_fusion
  224.4 2.1 pad_maximum_fusion
  226.4 5.6 %attend_back.5 = (bf16[3,1024,768]{2,1,0:T(8,128)(2,1)S(1)}, f32[1,2,128]{2,1,0:T(2,128)S(1)}) custom-call(s32[1]{0:T(128)S(6)} %copy.66.refs_0_, bf16[1024,2304]{1,0:T(8,128)(2,1)S(1)} %bitcast.66, bf16[1024,2304]{1,0:T(8,128)(2,1)S(1)} %bitcast.66, bf16[1024,2304]{1,0:T(8,128)(2,1)S(1)} %bitcast.66, ...), custom_call_target="tpu_custom_call", output_to_operand_aliasing={{0}: (7, {})} | custom-call | flops 300000000 | tf_op jit(solution)/shard_map/attend_back/pallas_call | solution.py:220
  232.1 3.3 %collective-permute-done.29 = bf16[384,768]{1,0:T(8,128)(2,1)S(1)} collective-permute-done((bf16[384,768]{1,0:T(8,128)(2,1)}, bf16[384,768]{1,0:T(8,128)(2,1)S(1)}, u32[]{:S(2)}, u32[]{:S(2)}) %collective-permute-start.29) | collective-permute-done | bytes 589856 | tf_op jit(solution)/shard_map/ppermute | solution.py:524
  246.8 1.7 collective-permute-start.34
  248.8 7.9 %collective-permute-done.34 = bf16[48,3072]{1,0:T(8,128)(2,1)S(1)} collective-permute-done((bf16[48,3072]{1,0:T(8,128)(2,1)S(1)}, bf16[48,3072]{1,0:T(8,128)(2,1)S(1)}, u32[]{:S(2)}, u32[]{:S(2)}) %collective-permute-start.34) | collective-permute-done | bytes 294944 | tf_op jit(solution)/shard_map/ppermute | solution.py:524
  256.7 4.9 %collective-permute-done.35 = bf16[192,768]{1,0:T(8,128)(2,1)S(1)} collective-permute-done((bf16[192,768]{1,0:T(8,128)(2,1)S(1)}, bf16[192,768]{1,0:T(8,128)(2,1)S(1)}, u32[]{:S(2)}, u32[]{:S(2)}) %collective-permute-start.35) | collective-permute-done | bytes 294944 | tf_op jit(solution)/shard_map/ppermute | solution.py:524
  262.0 1.8 collective-permute-start.36
  265.8 2.5 collective-permute-start.40
  271.5 1.7 collective-permute-start.38
  273.3 4.6 %collective-permute-done.39 = bf16[24,3072]{1,0:T(8,128)(2,1)S(1)} collective-permute-done((bf16[24,3072]{1,0:T(8,128)(2,1)S(1)}, bf16[24,3072]{1,0:T(8,128)(2,1)S(1)}, u32[]{:S(2)}, u32[]{:S(2)}) %collective-permute-start.39) | collective-permute-done | bytes 147488 | tf_op jit(solution)/shard_map/ppermute | solution.py:524
  278.0 1.7 collective-permute-done.40
  279.8 3.3 %collective-permute-done.38 = bf16[48,3072]{1,0:T(8,128)(2,1)S(1)} collective-permute-done((bf16[48,3072]{1,0:T(8,128)(2,1)S(1)}, bf16[48,3072]{1,0:T(8,128)(2,1)S(1)}, u32[]{:S(2)}, u32[]{:S(2)}) %collective-permute-start.38) | collective-permute-done | bytes 294944 | tf_op jit(solution)/shard_map/ppermute | solution.py:524
  285.4 5.7 %collective-permute-done.41 = bf16[24,3072]{1,0:T(8,128)(2,1)} collective-permute-done((bf16[24,3072]{1,0:T(8,128)(2,1)}, bf16[24,3072]{1,0:T(8,128)(2,1)}, u32[]{:S(2)}, u32[]{:S(2)}) %collective-permute-start.41) | collective-permute-done | bytes 147488 | tf_op jit(solution)/shard_map/ppermute | solution.py:524
  295.7 2.7 collective-permute-done.43
  298.6 3.3 %fusion.14 = f32[1024,768]{1,0:T(8,128)S(1)} fusion(bf16[3,1024,768]{2,1,0:T(8,128)(2,1)} %copy-done.2, bf16[768,2304]{1,0:T(8,128)(2,1)} %pad_maximum_fusion), kind=kOutput, calls=%fused_computation.25 | convolution fusion | flops 1207959552 | bytes 5898240 | tf_op jit(solution)/shard_map/dot_general | solution.py:32
  304.1 2.4 collective-permute-done.45
  306.7 3.1 add_bitcast_fusion
  309.9 1.5 collective-permute-done.46
  (285 shorter events, 72.1 us)
Async XLA Ops:
  3.1 14.8 %collective-permute-start.2 = (bf16[24,2432]{1,0:T(8,128)(2,1)}, bf16[24,2432]{1,0:T(8,128)(2,1)}, u32[]{:S(2)}, u32[]{:S(2)}) collective-permute-start(bf16[24,2432]{1,0:T(8,128)(2,1)} %fusion.84), channel_id=1, source_target_pairs={{0,24},{1,25},{2,26},{3,27},{4,28},{5,29},{6,30},{7,31},{8,16},{9,... | collective-permute-start | bytes 350216 | tf_op jit(solution)/shard_map/ppermute | solution.py:524
  8.2 9.7 %collective-permute-start.1 = (bf16[24,2432]{1,0:T(8,128)(2,1)}, bf16[24,2432]{1,0:T(8,128)(2,1)}, u32[]{:S(2)}, u32[]{:S(2)}) collective-permute-start(bf16[24,2432]{1,0:T(8,128)(2,1)} %fusion.84), channel_id=1, source_target_pairs={{0,8},{1,9},{2,10},{3,11},{4,12},{5,13},{6,14},{7,15},{8,0},{9,1},... | collective-permute-start | bytes 350216 | tf_op jit(solution)/shard_map/ppermute | solution.py:524
  8.2 10.2 %collective-permute-start = (bf16[24,2432]{1,0:T(8,128)(2,1)}, bf16[24,2432]{1,0:T(8,128)(2,1)}, u32[]{:S(2)}, u32[]{:S(2)}) collective-permute-start(bf16[24,2432]{1,0:T(8,128)(2,1)} %fusion.84), channel_id=1, source_target_pairs={{0,16},{1,17},{2,18},{3,19},{4,20},{5,21},{6,22},{7,23},{8,24},{9,... | collective-permute-start | bytes 350216 | tf_op jit(solution)/shard_map/ppermute | solution.py:524
  11.3 5.6 %collective-permute-start.3 = (bf16[24,1920]{1,0:T(8,128)(2,1)}, bf16[24,1920]{1,0:T(8,128)(2,1)}, u32[]{:S(2)}, u32[]{:S(2)}) collective-permute-start(bf16[24,1920]{1,0:T(8,128)(2,1)} %fusion.85), channel_id=1, source_target_pairs={{0,1},{1,0},{2,3},{3,2},{4,5},{5,4},{6,7},{7,6},{8,9},{9,8},{10,11... | collective-permute-start | bytes 276488 | tf_op jit(solution)/shard_map/ppermute | solution.py:524
  19.5 11.7 %collective-permute-start.6 = (bf16[48,1920]{1,0:T(8,128)(2,1)S(1)}, bf16[48,1920]{1,0:T(8,128)(2,1)S(1)}, u32[]{:S(2)}, u32[]{:S(2)}) collective-permute-start(bf16[48,1920]{1,0:T(8,128)(2,1)S(1)} %pad_maximum_fusion.26), channel_id=1, source_target_pairs={{0,16},{1,17},{2,18},{3,19},{4,20},{5,21},{6,22},{7,23},{8,24},{9,... | collective-permute-start | bytes 552968 | tf_op jit(solution)/shard_map/ppermute | solution.py:524
  21.5 9.6 %collective-permute-start.4 = (bf16[96,1536]{1,0:T(8,128)(2,1)S(1)}, bf16[96,1536]{1,0:T(8,128)(2,1)S(1)}, u32[]{:S(2)}, u32[]{:S(2)}) collective-permute-start(bf16[96,1536]{1,0:T(8,128)(2,1)S(1)} %pad_maximum_fusion.22), channel_id=1, source_target_pairs={{0,4},{1,5},{2,6},{3,7},{4,0},{5,1},{6,2},{7,3},{8,12},{9,13},{10,... | collective-permute-start | bytes 884744 | tf_op jit(solution)/shard_map/ppermute | solution.py:524
  23.2 9.5 %collective-permute-start.5 = (bf16[96,1664]{1,0:T(8,128)(2,1)S(1)}, bf16[96,1664]{1,0:T(8,128)(2,1)S(1)}, u32[]{:S(2)}, u32[]{:S(2)}) collective-permute-start(bf16[96,1664]{1,0:T(8,128)(2,1)S(1)} %pad_maximum_fusion.20), channel_id=1, source_target_pairs={{0,2},{1,3},{2,0},{3,1},{4,6},{5,7},{6,4},{7,5},{8,10},{9,11},{10,... | collective-permute-start | bytes 958472 | tf_op jit(solution)/shard_map/ppermute | solution.py:524
  32.7 10.0 %collective-permute-start.9 = (bf16[96,1920]{1,0:T(8,128)(2,1)S(1)}, bf16[96,1920]{1,0:T(8,128)(2,1)S(1)}, u32[]{:S(2)}, u32[]{:S(2)}) collective-permute-start(bf16[96,1920]{1,0:T(8,128)(2,1)S(1)} %pad_maximum_fusion.19), channel_id=1, source_target_pairs={{0,8},{1,9},{2,10},{3,11},{4,12},{5,13},{6,14},{7,15},{8,0},{9,1},... | collective-permute-start | bytes 1105928 | tf_op jit(solution)/shard_map/ppermute | solution.py:524
  34.9 11.0 %collective-permute-start.7 = (bf16[192,1152]{1,0:T(8,128)(2,1)S(1)}, bf16[192,1152]{1,0:T(8,128)(2,1)S(1)}, u32[]{:S(2)}, u32[]{:S(2)}) collective-permute-start(bf16[192,1152]{1,0:T(8,128)(2,1)S(1)} %slice.358), channel_id=1, source_target_pairs={{0,2},{1,3},{2,0},{3,1},{4,6},{5,7},{6,4},{7,5},{8,10},{9,11},{10,... | collective-permute-start | bytes 1327112 | tf_op jit(solution)/shard_map/ppermute | solution.py:524
  36.5 11.8 %collective-permute-start.8 = (bf16[192,1280]{1,0:T(8,128)(2,1)S(1)}, bf16[192,1280]{1,0:T(8,128)(2,1)S(1)}, u32[]{:S(2)}, u32[]{:S(2)}) collective-permute-start(bf16[192,1280]{1,0:T(8,128)(2,1)S(1)} %slice.359), channel_id=1, source_target_pairs={{0,4},{1,5},{2,6},{3,7},{4,0},{5,1},{6,2},{7,3},{8,12},{9,13},{10,... | collective-permute-start | bytes 1474568 | tf_op jit(solution)/shard_map/ppermute | solution.py:524
  48.4 3.9 %collective-permute-start.11 = (bf16[384,1280]{1,0:T(8,128)(2,1)S(1)}, bf16[384,1280]{1,0:T(8,128)(2,1)S(1)}, u32[]{:S(2)}, u32[]{:S(2)}) collective-permute-start(bf16[384,1280]{1,0:T(8,128)(2,1)S(1)} %pad_maximum_fusion.10.refs_4_), channel_id=1, source_target_pairs={{0,1},{1,0},{2,3},{3,2},{4,5},{5,4},{6,7},{7,6},{8,9},{9,8},{10,11... | collective-permute-start | bytes 2949128 | tf_op jit(solution)/shard_map/ppermute | solution.py:524
  48.5 3.8 %collective-permute-start.10 = (bf16[384,1152]{1,0:T(8,128)(2,1)S(1)}, bf16[384,1152]{1,0:T(8,128)(2,1)S(1)}, u32[]{:S(2)}, u32[]{:S(2)}) collective-permute-start(bf16[384,1152]{1,0:T(8,128)(2,1)S(1)} %pad_maximum_fusion.11.refs_2_), channel_id=1, source_target_pairs={{0,1},{1,0},{2,3},{3,2},{4,5},{5,4},{6,7},{7,6},{8,9},{9,8},{10,11... | collective-permute-start | bytes 2654216 | tf_op jit(solution)/shard_map/ppermute | solution.py:524
  52.3 16.0 %collective-permute-start.14 = (bf16[192,768]{1,0:T(8,128)(2,1)S(1)}, bf16[192,768]{1,0:T(8,128)(2,1)S(1)}, u32[]{:S(2)}, u32[]{:S(2)}) collective-permute-start(bf16[192,768]{1,0:T(8,128)(2,1)S(1)} %pad_maximum_fusion.23), channel_id=1, source_target_pairs={{0,16},{1,17},{2,18},{3,19},{4,20},{5,21},{6,22},{7,23},{8,24},{9,... | collective-permute-start | bytes 884744 | tf_op jit(solution)/shard_map/ppermute | solution.py:524
  54.3 14.1 %collective-permute-start.13 = (bf16[192,896]{1,0:T(8,128)(2,1)S(1)}, bf16[192,896]{1,0:T(8,128)(2,1)S(1)}, u32[]{:S(2)}, u32[]{:S(2)}) collective-permute-start(bf16[192,896]{1,0:T(8,128)(2,1)S(1)} %slice.363), channel_id=1, source_target_pairs={{0,2},{1,3},{2,0},{3,1},{4,6},{5,7},{6,4},{7,5},{8,10},{9,11},{10,... | collective-permute-start | bytes 1032200 | tf_op jit(solution)/shard_map/ppermute | solution.py:524
  55.3 13.2 %collective-permute-start.12 = (bf16[192,1024]{1,0:T(8,128)(2,1)S(1)}, bf16[192,1024]{1,0:T(8,128)(2,1)S(1)}, u32[]{:S(2)}, u32[]{:S(2)}) collective-permute-start(bf16[192,1024]{1,0:T(8,128)(2,1)S(1)} %slice.362), channel_id=1, source_target_pairs={{0,4},{1,5},{2,6},{3,7},{4,0},{5,1},{6,2},{7,3},{8,12},{9,13},{10,... | collective-permute-start | bytes 1179656 | tf_op jit(solution)/shard_map/ppermute | solution.py:524
  68.5 15.3 %collective-permute-start.15 = (bf16[384,768]{1,0:T(8,128)(2,1)S(1)}, bf16[384,768]{1,0:T(8,128)(2,1)S(1)}, u32[]{:S(2)}, u32[]{:S(2)}) collective-permute-start(bf16[384,768]{1,0:T(8,128)(2,1)S(1)} %pad_maximum_fusion.17), channel_id=1, source_target_pairs={{0,8},{1,9},{2,10},{3,11},{4,12},{5,13},{6,14},{7,15},{8,0},{9,1},... | collective-permute-start | bytes 1769480 | tf_op jit(solution)/shard_map/ppermute | solution.py:524
  68.6 17.4 %collective-permute-start.17 = (bf16[384,896]{1,0:T(8,128)(2,1)S(1)}, bf16[384,896]{1,0:T(8,128)(2,1)S(1)}, u32[]{:S(2)}, u32[]{:S(2)}) collective-permute-start(bf16[384,896]{1,0:T(8,128)(2,1)S(1)} %pad_maximum_fusion.14), channel_id=1, source_target_pairs={{0,4},{1,5},{2,6},{3,7},{4,0},{5,1},{6,2},{7,3},{8,12},{9,13},{10,... | collective-permute-start | bytes 2064392 | tf_op jit(solution)/shard_map/ppermute | solution.py:524
  69.2 19.2 %collective-permute-start.16 = (bf16[384,1024]{1,0:T(8,128)(2,1)S(1)}, bf16[384,1024]{1,0:T(8,128)(2,1)S(1)}, u32[]{:S(2)}, u32[]{:S(2)}) collective-permute-start(bf16[384,1024]{1,0:T(8,128)(2,1)S(1)} %pad_maximum_fusion.12), channel_id=1, source_target_pairs={{0,2},{1,3},{2,0},{3,1},{4,6},{5,7},{6,4},{7,5},{8,10},{9,11},{10,... | collective-permute-start | bytes 2359304 | tf_op jit(solution)/shard_map/ppermute | solution.py:524
  89.7 23.2 %collective-permute-start.20 = (bf16[768,1024]{1,0:T(8,128)(2,1)}, bf16[768,1024]{1,0:T(8,128)(2,1)}, u32[]{:S(2)}, u32[]{:S(2)}) collective-permute-start(bf16[768,1024]{1,0:T(8,128)(2,1)} %pad_maximum_fusion.1.refs_9_), channel_id=1, source_target_pairs={{0,1},{1,0},{2,3},{3,2},{4,5},{5,4},{6,7},{7,6},{8,9},{9,8},{10,11... | collective-permute-start | bytes 4718600 | tf_op jit(solution)/shard_map/ppermute | solution.py:524
  89.7 23.2 %collective-permute-start.21 = (bf16[768,896]{1,0:T(8,128)(2,1)}, bf16[768,896]{1,0:T(8,128)(2,1)}, u32[]{:S(2)}, u32[]{:S(2)}) collective-permute-start(bf16[768,896]{1,0:T(8,128)(2,1)} %pad_maximum_fusion.2.refs_11_), channel_id=1, source_target_pairs={{0,1},{1,0},{2,3},{3,2},{4,5},{5,4},{6,7},{7,6},{8,9},{9,8},{10,11... | collective-permute-start | bytes 4128776 | tf_op jit(solution)/shard_map/ppermute | solution.py:524
  91.3 16.2 %collective-permute-start.19 = (bf16[768,384]{1,0:T(8,128)(2,1)}, bf16[768,384]{1,0:T(8,128)(2,1)}, u32[]{:S(2)}, u32[]{:S(2)}) collective-permute-start(bf16[768,384]{1,0:T(8,128)(2,1)} %get-tuple-element.267), channel_id=1, source_target_pairs={{0,4},{1,5},{2,6},{3,7},{4,0},{5,1},{6,2},{7,3},{8,12},{9,13},{10,... | collective-permute-start | bytes 1769480 | tf_op jit(solution)/shard_map/ppermute | solution.py:524
  92.9 17.6 %collective-permute-start.18 = (bf16[768,384]{1,0:T(8,128)(2,1)}, bf16[768,384]{1,0:T(8,128)(2,1)}, u32[]{:S(2)}, u32[]{:S(2)}) collective-permute-start(bf16[768,384]{1,0:T(8,128)(2,1)} %get-tuple-element.268), channel_id=1, source_target_pairs={{0,2},{1,3},{2,0},{3,1},{4,6},{5,7},{6,4},{7,5},{8,10},{9,11},{10,... | collective-permute-start | bytes 1769480 | tf_op jit(solution)/shard_map/ppermute | solution.py:524
  112.9 3.3 %collective-permute-start.22 = (bf16[1536,384]{1,0:T(8,128)(2,1)}, bf16[1536,384]{1,0:T(8,128)(2,1)}, u32[]{:S(2)}, u32[]{:S(2)}) collective-permute-start(bf16[1536,384]{1,0:T(8,128)(2,1)} %pad_maximum_fusion.4.refs_13_), channel_id=1, source_target_pairs={{0,1},{1,0},{2,3},{3,2},{4,5},{5,4},{6,7},{7,6},{8,9},{9,8},{10,11... | collective-permute-start | bytes 3538952 | tf_op jit(solution)/shard_map/ppermute | solution.py:524
  112.9 4.9 %collective-permute-start.23 = (bf16[1536,384]{1,0:T(8,128)(2,1)}, bf16[1536,384]{1,0:T(8,128)(2,1)}, u32[]{:S(2)}, u32[]{:S(2)}) collective-permute-start(bf16[1536,384]{1,0:T(8,128)(2,1)} %pad_maximum_fusion.5.refs_14_), channel_id=1, source_target_pairs={{0,1},{1,0},{2,3},{3,2},{4,5},{5,4},{6,7},{7,6},{8,9},{9,8},{10,11... | collective-permute-start | bytes 3538952 | tf_op jit(solution)/shard_map/ppermute | solution.py:524
  117.8 63.0 %slice-start.1 = ((s8[4718592]{0:T(1024)(128)(4,1)}), s8[524288]{0:T(1024)(128)(4,1)S(1)}, s32[]{:S(2)}) async-start(s8[4718592]{0:T(1024)(128)(4,1)} %bitcast.65), calls=%async_computation.1 | async-start | bytes 1048576
  180.2 7.6 %collective-permute-start.24 = (bf16[384,3072]{1,0:T(8,128)(2,1)}, bf16[384,3072]{1,0:T(8,128)(2,1)S(1)}, u32[]{:S(2)}, u32[]{:S(2)}) collective-permute-start(bf16[384,3072]{1,0:T(8,128)(2,1)} %get-tuple-element.199), channel_id=1, source_target_pairs={{0,1},{1,0},{2,3},{3,2},{4,5},{5,4},{6,7},{7,6},{8,9},{9,8},{10,11... | collective-permute-start | bytes 7077896 | tf_op jit(solution)/shard_map/ppermute | solution.py:524
  180.4 8.0 %collective-permute-start.25 = (bf16[1536,768]{1,0:T(8,128)(2,1)}, bf16[1536,768]{1,0:T(8,128)(2,1)S(1)}, u32[]{:S(2)}, u32[]{:S(2)}) collective-permute-start(bf16[1536,768]{1,0:T(8,128)(2,1)} %get-tuple-element.200), channel_id=1, source_target_pairs={{0,1},{1,0},{2,3},{3,2},{4,5},{5,4},{6,7},{7,6},{8,9},{9,8},{10,11... | collective-permute-start | bytes 7077896 | tf_op jit(solution)/shard_map/ppermute | solution.py:524
  188.7 28.8 %collective-permute-start.27 = (bf16[768,768]{1,0:T(8,128)(2,1)S(1)}, bf16[768,768]{1,0:T(8,128)(2,1)S(1)}, u32[]{:S(2)}, u32[]{:S(2)}) collective-permute-start(bf16[768,768]{1,0:T(8,128)(2,1)S(1)} %add_convert_fusion), channel_id=1, source_target_pairs={{0,4},{1,5},{2,6},{3,7},{4,0},{5,1},{6,2},{7,3},{8,12},{9,13},{10,... | collective-permute-start | bytes 3538952 | tf_op jit(solution)/shard_map/ppermute | solution.py:524
  190.5 28.1 %collective-permute-start.26 = (bf16[192,3072]{1,0:T(8,128)(2,1)S(1)}, bf16[192,3072]{1,0:T(8,128)(2,1)S(1)}, u32[]{:S(2)}, u32[]{:S(2)}) collective-permute-start(bf16[192,3072]{1,0:T(8,128)(2,1)S(1)} %add_convert_fusion.1), channel_id=1, source_target_pairs={{0,2},{1,3},{2,0},{3,1},{4,6},{5,7},{6,4},{7,5},{8,10},{9,11},{10,... | collective-permute-start | bytes 3538952 | tf_op jit(solution)/shard_map/ppermute | solution.py:524
  220.6 14.8 %collective-permute-start.29 = (bf16[384,768]{1,0:T(8,128)(2,1)}, bf16[384,768]{1,0:T(8,128)(2,1)S(1)}, u32[]{:S(2)}, u32[]{:S(2)}) collective-permute-start(bf16[384,768]{1,0:T(8,128)(2,1)} %add_convert_fusion.4), channel_id=1, source_target_pairs={{0,2},{1,3},{2,0},{3,1},{4,6},{5,7},{6,4},{7,5},{8,10},{9,11},{10,... | collective-permute-start | bytes 1769480 | tf_op jit(solution)/shard_map/ppermute | solution.py:524
  222.1 14.5 %collective-permute-start.28 = (bf16[96,3072]{1,0:T(8,128)(2,1)}, bf16[96,3072]{1,0:T(8,128)(2,1)S(1)}, u32[]{:S(2)}, u32[]{:S(2)}) collective-permute-start(bf16[96,3072]{1,0:T(8,128)(2,1)} %add_convert_fusion.5), channel_id=1, source_target_pairs={{0,4},{1,5},{2,6},{3,7},{4,0},{5,1},{6,2},{7,3},{8,12},{9,13},{10,... | collective-permute-start | bytes 1769480 | tf_op jit(solution)/shard_map/ppermute | solution.py:524
  240.9 3.5 %collective-permute-start.30 = (bf16[384,1536]{1,0:T(8,128)(2,1)S(1)}, bf16[384,1536]{1,0:T(8,128)(2,1)S(1)}, u32[]{:S(2)}, u32[]{:S(2)}) collective-permute-start(bf16[384,1536]{1,0:T(8,128)(2,1)S(1)} %pad_maximum_fusion.6), channel_id=1, source_target_pairs={{0,1},{1,0},{2,3},{3,2},{4,5},{5,4},{6,7},{7,6},{8,9},{9,8},{10,11... | collective-permute-start | bytes 3538952 | tf_op jit(solution)/shard_map/ppermute | solution.py:524
  241.0 4.5 %collective-permute-start.31 = (bf16[384,1536]{1,0:T(8,128)(2,1)S(1)}, bf16[384,1536]{1,0:T(8,128)(2,1)S(1)}, u32[]{:S(2)}, u32[]{:S(2)}) collective-permute-start(bf16[384,1536]{1,0:T(8,128)(2,1)S(1)} %pad_maximum_fusion.7), channel_id=1, source_target_pairs={{0,1},{1,0},{2,3},{3,2},{4,5},{5,4},{6,7},{7,6},{8,9},{9,8},{10,11... | collective-permute-start | bytes 3538952 | tf_op jit(solution)/shard_map/ppermute | solution.py:524
  245.7 15.9 %collective-permute-start.33 = (bf16[192,1536]{1,0:T(8,128)(2,1)S(1)}, bf16[192,1536]{1,0:T(8,128)(2,1)S(1)}, u32[]{:S(2)}, u32[]{:S(2)}) collective-permute-start(bf16[192,1536]{1,0:T(8,128)(2,1)S(1)} %add_convert_fusion.2), channel_id=1, source_target_pairs={{0,4},{1,5},{2,6},{3,7},{4,0},{5,1},{6,2},{7,3},{8,12},{9,13},{10,... | collective-permute-start | bytes 1769480 | tf_op jit(solution)/shard_map/ppermute | solution.py:524
  246.1 15.4 %collective-permute-start.32 = (bf16[192,1536]{1,0:T(8,128)(2,1)S(1)}, bf16[192,1536]{1,0:T(8,128)(2,1)S(1)}, u32[]{:S(2)}, u32[]{:S(2)}) collective-permute-start(bf16[192,1536]{1,0:T(8,128)(2,1)S(1)} %add_convert_fusion.3), channel_id=1, source_target_pairs={{0,2},{1,3},{2,0},{3,1},{4,6},{5,7},{6,4},{7,5},{8,10},{9,11},{10,... | collective-permute-start | bytes 1769480 | tf_op jit(solution)/shard_map/ppermute | solution.py:524
  246.8 9.9 %collective-permute-start.34 = (bf16[48,3072]{1,0:T(8,128)(2,1)S(1)}, bf16[48,3072]{1,0:T(8,128)(2,1)S(1)}, u32[]{:S(2)}, u32[]{:S(2)}) collective-permute-start(bf16[48,3072]{1,0:T(8,128)(2,1)S(1)} %add_convert_fusion.9), channel_id=1, source_target_pairs={{0,8},{1,9},{2,10},{3,11},{4,12},{5,13},{6,14},{7,15},{8,0},{9,1},... | collective-permute-start | bytes 884744 | tf_op jit(solution)/shard_map/ppermute | solution.py:524
  248.4 13.1 %collective-permute-start.35 = (bf16[192,768]{1,0:T(8,128)(2,1)S(1)}, bf16[192,768]{1,0:T(8,128)(2,1)S(1)}, u32[]{:S(2)}, u32[]{:S(2)}) collective-permute-start(bf16[192,768]{1,0:T(8,128)(2,1)S(1)} %add_convert_fusion.8), channel_id=1, source_target_pairs={{0,8},{1,9},{2,10},{3,11},{4,12},{5,13},{6,14},{7,15},{8,0},{9,1},... | collective-permute-start | bytes 884744 | tf_op jit(solution)/shard_map/ppermute | solution.py:524
  262.0 7.8 %collective-permute-start.36 = (bf16[96,1536]{1,0:T(8,128)(2,1)S(1)}, bf16[96,1536]{1,0:T(8,128)(2,1)S(1)}, u32[]{:S(2)}, u32[]{:S(2)}) collective-permute-start(bf16[96,1536]{1,0:T(8,128)(2,1)S(1)} %add_convert_fusion.7), channel_id=1, source_target_pairs={{0,4},{1,5},{2,6},{3,7},{4,0},{5,1},{6,2},{7,3},{8,12},{9,13},{10,... | collective-permute-start | bytes 884744 | tf_op jit(solution)/shard_map/ppermute | solution.py:524
  263.8 7.3 %collective-permute-start.37 = (bf16[96,1536]{1,0:T(8,128)(2,1)S(1)}, bf16[96,1536]{1,0:T(8,128)(2,1)S(1)}, u32[]{:S(2)}, u32[]{:S(2)}) collective-permute-start(bf16[96,1536]{1,0:T(8,128)(2,1)S(1)} %add_convert_fusion.6), channel_id=1, source_target_pairs={{0,2},{1,3},{2,0},{3,1},{4,6},{5,7},{6,4},{7,5},{8,10},{9,11},{10,... | collective-permute-start | bytes 884744 | tf_op jit(solution)/shard_map/ppermute | solution.py:524
  265.3 12.5 %collective-permute-start.39 = (bf16[24,3072]{1,0:T(8,128)(2,1)S(1)}, bf16[24,3072]{1,0:T(8,128)(2,1)S(1)}, u32[]{:S(2)}, u32[]{:S(2)}) collective-permute-start(bf16[24,3072]{1,0:T(8,128)(2,1)S(1)} %add_convert_fusion.11), channel_id=1, source_target_pairs={{0,16},{1,17},{2,18},{3,19},{4,20},{5,21},{6,22},{7,23},{8,24},{9,... | collective-permute-start | bytes 442376 | tf_op jit(solution)/shard_map/ppermute | solution.py:524
  265.8 13.9 %collective-permute-start.40 = (bf16[96,768]{1,0:T(8,128)(2,1)S(1)}, bf16[96,768]{1,0:T(8,128)(2,1)S(1)}, u32[]{:S(2)}, u32[]{:S(2)}) collective-permute-start(bf16[96,768]{1,0:T(8,128)(2,1)S(1)} %add_convert_fusion.10), channel_id=1, source_target_pairs={{0,16},{1,17},{2,18},{3,19},{4,20},{5,21},{6,22},{7,23},{8,24},{9,... | collective-permute-start | bytes 442376 | tf_op jit(solution)/shard_map/ppermute | solution.py:524
  271.5 11.6 %collective-permute-start.38 = (bf16[48,3072]{1,0:T(8,128)(2,1)S(1)}, bf16[48,3072]{1,0:T(8,128)(2,1)S(1)}, u32[]{:S(2)}, u32[]{:S(2)}) collective-permute-start(bf16[48,3072]{1,0:T(8,128)(2,1)S(1)} %fusion.71), channel_id=1, source_target_pairs={{0,8},{1,9},{2,10},{3,11},{4,12},{5,13},{6,14},{7,15},{8,0},{9,1},... | collective-permute-start | bytes 884744 | tf_op jit(solution)/shard_map/ppermute | solution.py:524
  283.9 7.3 %collective-permute-start.41 = (bf16[24,3072]{1,0:T(8,128)(2,1)}, bf16[24,3072]{1,0:T(8,128)(2,1)}, u32[]{:S(2)}, u32[]{:S(2)}) collective-permute-start(bf16[24,3072]{1,0:T(8,128)(2,1)} %fusion.80), channel_id=1, source_target_pairs={{0,16},{1,17},{2,18},{3,19},{4,20},{5,21},{6,22},{7,23},{8,24},{9,... | collective-permute-start | bytes 442376 | tf_op jit(solution)/shard_map/ppermute | solution.py:524
  293.1 1.2 collective-permute-start.42
  294.4 4.0 %collective-permute-start.43 = (f32[80,128]{1,0:T(8,128)S(1)}, f32[80,128]{1,0:T(8,128)S(1)}, u32[]{:S(2)}, u32[]{:S(2)}) collective-permute-start(f32[80,128]{1,0:T(8,128)S(1)} %add.509), channel_id=1, source_target_pairs={{0,2},{1,3},{2,0},{3,1},{4,6},{5,7},{6,4},{7,5},{8,10},{9,11},{10,... | collective-permute-start | bytes 122888 | tf_op jit(solution)/shard_map/ppermute | solution.py:524
  298.4 4.1 %collective-permute-start.44 = (f32[80,128]{1,0:T(8,128)S(1)}, f32[80,128]{1,0:T(8,128)S(1)}, u32[]{:S(2)}, u32[]{:S(2)}) collective-permute-start(f32[80,128]{1,0:T(8,128)S(1)} %add.510), channel_id=1, source_target_pairs={{0,4},{1,5},{2,6},{3,7},{4,0},{5,1},{6,2},{7,3},{8,12},{9,13},{10,... | collective-permute-start | bytes 122888 | tf_op jit(solution)/shard_map/ppermute | solution.py:524
  302.5 4.0 %collective-permute-start.45 = (f32[80,128]{1,0:T(8,128)S(1)}, f32[80,128]{1,0:T(8,128)S(1)}, u32[]{:S(2)}, u32[]{:S(2)}) collective-permute-start(f32[80,128]{1,0:T(8,128)S(1)} %add.511), channel_id=1, source_target_pairs={{0,8},{1,9},{2,10},{3,11},{4,12},{5,13},{6,14},{7,15},{8,0},{9,1},... | collective-permute-start | bytes 122888 | tf_op jit(solution)/shard_map/ppermute | solution.py:524
  306.5 4.9 %collective-permute-start.46 = (f32[80,128]{1,0:T(8,128)S(1)}, f32[80,128]{1,0:T(8,128)S(1)}, u32[]{:S(2)}, u32[]{:S(2)}) collective-permute-start(f32[80,128]{1,0:T(8,128)S(1)} %add.512), channel_id=1, source_target_pairs={{0,16},{1,17},{2,18},{3,19},{4,20},{5,21},{6,22},{7,23},{8,24},{9,... | collective-permute-start | bytes 122888 | tf_op jit(solution)/shard_map/ppermute | solution.py:524
  (59 other events, 506.5 us)

commit v7 on v6

--- a/solution.py
+++ b/solution.py
@@ -788,8 +788,8 @@
         heads, out.value, in_left.value, in_right.value
     )
     out_left, out_right = out.cut(0, D // 2), out.cut(D // 2, D)
-    out_left.step([one])
-    out_right.step([two])
+    out_sides = [out_left.value, out_right.value]
+    out_got = [swap(out_sides[0], [one], n), swap(out_sides[1], [two], n)]
     in_parts = [in_left.value, in_right.value]
     if aligned:
         in_parts = [in_parts[0], swap(in_parts[0], [core], n)] + [
@@ -797,11 +797,10 @@
             swap(in_parts[1], [core], n),
         ]
     heads = attend(lengths, packed, 4 * some, 2 * some, heads)
-    heads, vec, out_left.value, out_right.value, in_parts = phase(
-        heads, vec, out_left.value, out_right.value, in_parts
-    )
-    out_parts = [out_left.value, out_right.value]
-    out_parts += [swap(part, [core], n) for part in out_parts]
+    heads, vec, out_got, in_parts = phase(heads, vec, out_got, in_parts)
+    out_across = [swap(value, [core], n) for value in out_sides]
+    out_ends = [swap(value, [core], n) for value in out_got]
+    out_sides = list(zip(out_sides, out_got, out_across, out_ends))
     out_a, out_b = Order([two, *far, one, core]), Order([one, *far, two, core])
     if aligned:
         chips_a, chips_b = [order.places(n // 2) // 2 for order in (order_a, order_b)]
@@ -812,13 +811,15 @@
         places = jnp.concatenate([chips_a, chips_b, blocks_a, blocks_b, corners, columns])
         base = 3 * n
         in_pieces = tuple((i // 2 * (n // 2), n // 2, base + i) for i in range(4))
+        out_parts = [part for parts in out_sides for part in parts]
+        quarter = n // 4
         out_pieces = tuple(
-            (n + i % 2 * n + i // 2 * (n // 2), n // 2, base + 4 + i % 2) for i in range(4)
+            (n + i * n + j * quarter, quarter, base + 4 + i) for i in range(2) for j in range(4)
         )
     else:
         sides = []
-        for i, order in enumerate((out_a, out_b)):
-            value = jnp.concatenate(out_parts[i::2], axis=0).reshape(n, rows_f, D // 2)
+        for parts, order in zip(out_sides, (out_a, out_b)):
+            value = jnp.concatenate(parts, axis=0).reshape(n, rows_f, D // 2)
             sides.append(value[jnp.argsort(order.places(n))].reshape(FF, D // 2))
         in_parts, out_parts = [attn_in], [jnp.concatenate(sides, axis=1)]
         places = jnp.zeros((2,), jnp.int32)

time: 319 us -> 314 us (0.984)
  other arithmetic: 26.6 us -> 21.3 us
    concatenate x15 -> x13, other arithmetic: 9.51 us -> 4.16 us  [step(): self.value = jnp.concatenate([self.value, *got], axis=0)]
    ppermute x47 -> x49, waiting for transfers between devices: 80.7 us -> 80.2 us  [swap(): return lax.ppermute(value, 'dp', [(i, i ^ mask) for i in range(n)])]
    ppermute x47 -> x49, starting transfers between devices: 41.4 us -> 41.8 us  [swap(): return lax.ppermute(value, 'dp', [(i, i ^ mask) for i in range(n)])]
  transfers between devices with their start and end apart: 47 -> 49, of which waited for: 31 -> 32; matrix products, arithmetic and copies ran while one was open for 12% -> 11% of each run, Pallas kernels for 20% -> 21%
where the time goes in v7:
time: 314 us; the launch traced here: 309 us
  Pallas kernels  128 us (41%)
  waiting for transfers between devices  80.2 us (26%)
  starting transfers between devices  41.8 us (13%)
  other arithmetic  21.3 us (7%)
  matrix products  20.2 us (6%)
  local copies, waits for them, and re-layouts  14.8 us (5%)
    ppermute x49, waiting for transfers between devices, swap(): return lax.ppermute(value, 'dp', [(i, i ^ mask) for i in range(n)])  80.2 us
    pallas_call x1, Pallas kernels, feed(): pl.pallas_call(partial(feed_kernel, in_pieces, out_pieces, steps), grid_s...  62.5 us
    ppermute x49, starting transfers between devices, swap(): return lax.ppermute(value, 'dp', [(i, i ^ mask) for i in range(n)])  41.8 us
    pallas_call x3, Pallas kernels, attend_back(): pl.pallas_call(after(partial(attend_back_kernel, min(512, seq)), 7, len(e...  34.7 us
    pallas_call x3, Pallas kernels, attend(): pl.pallas_call(after(attend_kernel, 4, len(extra)), grid_spec=pltpu.Prefe...  21.5 us
    unnamed x120, local copies, waits for them, and re-layouts  10.1 us
    dot_general x3, matrix products, dot_nt(): lax.dot_general(a, b, (((1,), (1,)), ((), ())), preferred_element_type=F32)  7.86 us
  transfers between devices with their start and end apart: 49, of which 32 were waited for; matrix products, arithmetic and copies ran while one was open for 11% of the time, Pallas kernels for 21%

profile of v7, /device:TPU:0, one launch (start us, length us, event | category | flops | bytes accessed | tf_op | source)
XLA Modules:
  0.0 309.3 jit_solution(11695928035463529643)
XLA Ops:
  3.1 5.0 %collective-permute-start.2 = (bf16[24,2432]{1,0:T(8,128)(2,1)}, bf16[24,2432]{1,0:T(8,128)(2,1)}, u32[]{:S(2)}, u32[]{:S(2)}) collective-permute-start(bf16[24,2432]{1,0:T(8,128)(2,1)} %fusion.84), channel_id=1, source_target_pairs={{0,24},{1,25},{2,26},{3,27},{4,28},{5,29},{6,30},{7,31},{8,16},{9,... | collective-permute-start | bytes 350216 | tf_op jit(solution)/shard_map/ppermute | solution.py:524
  19.5 2.0 collective-permute-start.6
  21.5 1.6 collective-permute-start.4
  23.1 1.6 collective-permute-start.5
  24.7 6.4 %collective-permute-done.6 = bf16[48,1920]{1,0:T(8,128)(2,1)S(1)} collective-permute-done((bf16[48,1920]{1,0:T(8,128)(2,1)S(1)}, bf16[48,1920]{1,0:T(8,128)(2,1)S(1)}, u32[]{:S(2)}, u32[]{:S(2)}) %collective-permute-start.6) | collective-permute-done | bytes 184352 | tf_op jit(solution)/shard_map/ppermute | solution.py:524
  32.7 2.1 collective-permute-start.9
  34.9 1.6 collective-permute-start.7
  37.1 5.7 %collective-permute-done.9 = bf16[96,1920]{1,0:T(8,128)(2,1)S(1)} collective-permute-done((bf16[96,1920]{1,0:T(8,128)(2,1)S(1)}, bf16[96,1920]{1,0:T(8,128)(2,1)S(1)}, u32[]{:S(2)}, u32[]{:S(2)}) %collective-permute-start.9) | collective-permute-done | bytes 368672 | tf_op jit(solution)/shard_map/ppermute | solution.py:524
  42.8 3.1 collective-permute-done.7
  46.0 2.3 collective-permute-done.8
  49.1 3.2 %collective-permute-done.10.refs_3_ = bf16[384,1152]{1,0:T(8,128)(2,1)S(1)} collective-permute-done((bf16[384,1152]{1,0:T(8,128)(2,1)S(1)}, bf16[384,1152]{1,0:T(8,128)(2,1)S(1)}, u32[]{:S(2)}, u32[]{:S(2)}) %collective-permute-start.10) | collective-permute-done | bytes 884768 | tf_op jit(solution)/shard_map/ppermute | solution.py:524
  55.3 1.6 collective-permute-start.12
  56.9 6.0 %project.1.refs_1_.refs_2_.refs_3_ = bf16[1024,2304]{1,0:T(8,128)(2,1)S(1)} custom-call(bf16[1024,768]{1,0:T(8,128)(2,1)S(1)} %fusion.29.refs_0_, bf16[1024,768]{1,0:T(8,128)(2,1)S(1)} %fusion.30.refs_1_, bf16[384,1152]{1,0:T(8,128)(2,1)S(1)} %pad_maximum_fusion.9.refs_2_, bf16[384,1152]{1,0:T(8,128)(2,1)S(1)} %collective-permute-done.10.refs_3_, ...), custom_call_target="tpu_custom_call" | custom-call | flops 250000000 | tf_op jit(solution)/shard_map/project/pallas_call | solution.py:79
  62.9 3.5 %attend.3 = (bf16[1024,768]{1,0:T(8,128)(2,1)S(1)}, f32[768,1024]{1,0:T(8,128)S(1)}, f32[6,2,1024]{2,1,0:T(2,128)S(1)}) custom-call(s32[1]{0:T(128)S(6)} %copy.66.refs_0_, bf16[1024,2304]{1,0:T(8,128)(2,1)S(1)} %project.1.refs_1_.refs_2_.refs_3_, bf16[1024,2304]{1,0:T(8,128)(2,1)S(1)} %project.1.refs_1_.refs_2_.refs_3_, ...), custom_call_target="tpu_custom_call" | custom-call | flops 200000000 | tf_op jit(solution)/shard_map/attend/pallas_call | solution.py:128
  66.4 1.9 collective-permute-done.14
  69.7 10.8 %attend.4 = (bf16[1024,768]{1,0:T(8,128)(2,1)S(1)}, f32[768,1024]{1,0:T(8,128)S(1)}, f32[6,2,1024]{2,1,0:T(2,128)S(1)}) custom-call(s32[1]{0:T(128)S(6)} %copy.66.refs_0_, bf16[1024,2304]{1,0:T(8,128)(2,1)S(1)} %project.1.refs_1_.refs_2_.refs_3_, ...), custom_call_target="tpu_custom_call", output_to_operand_aliasing={{0}: (4, {}), {1}: (5, {}), {2}: (6, {})} | custom-call | flops 600000000 | tf_op jit(solution)/shard_map/attend/pallas_call | solution.py:128
  80.5 3.3 %collective-permute-done.15 = bf16[384,768]{1,0:T(8,128)(2,1)S(1)} collective-permute-done((bf16[384,768]{1,0:T(8,128)(2,1)S(1)}, bf16[384,768]{1,0:T(8,128)(2,1)S(1)}, u32[]{:S(2)}, u32[]{:S(2)}) %collective-permute-start.15) | collective-permute-done | bytes 589856 | tf_op jit(solution)/shard_map/ppermute | solution.py:524
  83.9 2.1 collective-permute-done.17
  91.3 1.5 collective-permute-start.19
  94.6 1.8 reshape.217.refs_6_
  96.5 2.3 copy-done.1
  100.2 7.2 %attend.5 = (bf16[1024,768]{1,0:T(8,128)(2,1)S(1)}, f32[768,1024]{1,0:T(8,128)S(1)}, f32[6,2,1024]{2,1,0:T(2,128)S(1)}) custom-call(s32[1]{0:T(128)S(6)} %copy.66.refs_0_, bf16[1024,2304]{1,0:T(8,128)(2,1)S(1)} %copy-done.1, bf16[1024,2304]{1,0:T(8,128)(2,1)S(1)} %copy-done.1, ...), custom_call_target="tpu_custom_call", output_to_operand_aliasing={{0}: (4, {}), {1}: (5, {}), {2}: (6, {})} | custom-call | flops 400000000 | tf_op jit(solution)/shard_map/attend/pallas_call | solution.py:128
  112.8 62.5 %feed.1 = (bf16[1024,768]{1,0:T(8,128)(2,1)}, f32[1024,768]{1,0:T(8,128)}, bf16[1024,768]{1,0:T(8,128)(2,1)}, f32[12,768]{1,0:T(8,128)}, bf16[1536,768]{1,0:T(8,...) custom-call(s32[1]{0:T(128)S(6)} %copy.66.refs_0_, ...), custom_call_target="tpu_custom_call" | custom-call | flops 2500000000 | tf_op jit(solution)/shard_map/feed/pallas_call | solution.py:478
  177.3 5.6 %attend_back.3 = (bf16[3,1024,768]{2,1,0:T(8,128)(2,1)S(1)}, f32[1,2,128]{2,1,0:T(2,128)S(1)}) custom-call(s32[1]{0:T(128)S(6)} %copy.66.refs_0_, bf16[1024,2304]{1,0:T(8,128)(2,1)S(1)} %bitcast.66, bf16[1024,2304]{1,0:T(8,128)(2,1)S(1)} %bitcast.66, bf16[1024,2304]{1,0:T(8,128)(2,1)S(1)} %bitcast.66, bf16[1024,768]{1,0:T(8,128)(2,1)S(1)} %copy-done.3, ...), custom_call_target="tpu_custom_call" | custom-call | flops 300000000 | tf_op jit(solution)/shard_map/attend_back/pallas_call | solution.py:220
  185.6 1.6 collective-permute-start.28
  187.4 1.7 convolution_convert_fusion.1
  189.1 23.4 %attend_back.4 = (bf16[3,1024,768]{2,1,0:T(8,128)(2,1)S(1)}, f32[4,2,128]{2,1,0:T(2,128)S(1)}) custom-call(s32[1]{0:T(128)S(6)} %copy.66.refs_0_, bf16[1024,2304]{1,0:T(8,128)(2,1)S(1)} %bitcast.66, bf16[1024,2304]{1,0:T(8,128)(2,1)S(1)} %bitcast.66, bf16[1024,2304]{1,0:T(8,128)(2,1)S(1)} %bitcast.66, ...), custom_call_target="tpu_custom_call", output_to_operand_aliasing={{0}: (7, {})} | custom-call | flops 1200000000 | tf_op jit(solution)/shard_map/attend_back/pallas_call | solution.py:220
  216.0 1.5 collective-permute-start.31
  218.0 1.7 convolution_convert_fusion
  219.7 2.1 pad_maximum_fusion
  221.8 5.6 %attend_back.5 = (bf16[3,1024,768]{2,1,0:T(8,128)(2,1)S(1)}, f32[1,2,128]{2,1,0:T(2,128)S(1)}) custom-call(s32[1]{0:T(128)S(6)} %copy.66.refs_0_, bf16[1024,2304]{1,0:T(8,128)(2,1)S(1)} %bitcast.66, bf16[1024,2304]{1,0:T(8,128)(2,1)S(1)} %bitcast.66, bf16[1024,2304]{1,0:T(8,128)(2,1)S(1)} %bitcast.66, ...), custom_call_target="tpu_custom_call", output_to_operand_aliasing={{0}: (7, {})} | custom-call | flops 300000000 | tf_op jit(solution)/shard_map/attend_back/pallas_call | solution.py:220
  227.5 3.5 %collective-permute-done.31 = bf16[384,768]{1,0:T(8,128)(2,1)S(1)} collective-permute-done((bf16[384,768]{1,0:T(8,128)(2,1)}, bf16[384,768]{1,0:T(8,128)(2,1)S(1)}, u32[]{:S(2)}, u32[]{:S(2)}) %collective-permute-start.31) | collective-permute-done | bytes 589856 | tf_op jit(solution)/shard_map/ppermute | solution.py:524
  242.4 1.7 collective-permute-start.36
  244.4 7.9 %collective-permute-done.36 = bf16[48,3072]{1,0:T(8,128)(2,1)S(1)} collective-permute-done((bf16[48,3072]{1,0:T(8,128)(2,1)S(1)}, bf16[48,3072]{1,0:T(8,128)(2,1)S(1)}, u32[]{:S(2)}, u32[]{:S(2)}) %collective-permute-start.36) | collective-permute-done | bytes 294944 | tf_op jit(solution)/shard_map/ppermute | solution.py:524
  252.3 4.9 %collective-permute-done.37 = bf16[192,768]{1,0:T(8,128)(2,1)S(1)} collective-permute-done((bf16[192,768]{1,0:T(8,128)(2,1)S(1)}, bf16[192,768]{1,0:T(8,128)(2,1)S(1)}, u32[]{:S(2)}, u32[]{:S(2)}) %collective-permute-start.37) | collective-permute-done | bytes 294944 | tf_op jit(solution)/shard_map/ppermute | solution.py:524
  257.6 1.8 collective-permute-start.38
  261.5 2.5 collective-permute-start.42
  263.9 1.5 collective-permute-done.38
  267.1 1.7 collective-permute-start.40
  268.9 4.6 %collective-permute-done.41 = bf16[24,3072]{1,0:T(8,128)(2,1)S(1)} collective-permute-done((bf16[24,3072]{1,0:T(8,128)(2,1)S(1)}, bf16[24,3072]{1,0:T(8,128)(2,1)S(1)}, u32[]{:S(2)}, u32[]{:S(2)}) %collective-permute-start.41) | collective-permute-done | bytes 147488 | tf_op jit(solution)/shard_map/ppermute | solution.py:524
  273.6 1.7 collective-permute-done.42
  275.5 3.3 %collective-permute-done.40 = bf16[48,3072]{1,0:T(8,128)(2,1)S(1)} collective-permute-done((bf16[48,3072]{1,0:T(8,128)(2,1)S(1)}, bf16[48,3072]{1,0:T(8,128)(2,1)S(1)}, u32[]{:S(2)}, u32[]{:S(2)}) %collective-permute-start.40) | collective-permute-done | bytes 294944 | tf_op jit(solution)/shard_map/ppermute | solution.py:524
  281.1 5.8 %collective-permute-done.43 = bf16[24,3072]{1,0:T(8,128)(2,1)} collective-permute-done((bf16[24,3072]{1,0:T(8,128)(2,1)}, bf16[24,3072]{1,0:T(8,128)(2,1)}, u32[]{:S(2)}, u32[]{:S(2)}) %collective-permute-start.43) | collective-permute-done | bytes 147488 | tf_op jit(solution)/shard_map/ppermute | solution.py:524
  291.3 2.7 collective-permute-done.45
  294.3 3.3 %fusion.14 = f32[1024,768]{1,0:T(8,128)S(1)} fusion(bf16[3,1024,768]{2,1,0:T(8,128)(2,1)} %copy-done.2, bf16[768,2304]{1,0:T(8,128)(2,1)} %pad_maximum_fusion), kind=kOutput, calls=%fused_computation.25 | convolution fusion | flops 1207959552 | bytes 5898240 | tf_op jit(solution)/shard_map/dot_general | solution.py:32
  299.8 2.4 collective-permute-done.47
  302.4 3.1 %add_bitcast_fusion = f32[1,1024,768]{2,1,0:T(8,128)} fusion(f32[1024,768]{1,0:T(8,128)S(1)} %fusion.14, f32[1024,768]{1,0:T(8,128)S(1)} %copy-done.41, f32[1024,768]{1,0:T(8,128)S(1)} %fusion.18, bf16[3,1024,768]{2,1,0:T(8,128)(2,1)S(1)} %bitcast.68, bf16[768,2304]{1,0:T(8,128)(2,1)S(1)} %copy-done.38), kind=kOutput, calls=%fused_computation.3 | convolution fusion | flops 1210318848 | bytes 15335424 | tf_op jit(solution)/shard_map/dot_general | solution.py:32
  305.5 1.6 collective-permute-done.48
  (287 shorter events, 69.7 us)
Async XLA Ops:
  3.1 14.8 %collective-permute-start.2 = (bf16[24,2432]{1,0:T(8,128)(2,1)}, bf16[24,2432]{1,0:T(8,128)(2,1)}, u32[]{:S(2)}, u32[]{:S(2)}) collective-permute-start(bf16[24,2432]{1,0:T(8,128)(2,1)} %fusion.84), channel_id=1, source_target_pairs={{0,24},{1,25},{2,26},{3,27},{4,28},{5,29},{6,30},{7,31},{8,16},{9,... | collective-permute-start | bytes 350216 | tf_op jit(solution)/shard_map/ppermute | solution.py:524
  8.2 9.7 %collective-permute-start.1 = (bf16[24,2432]{1,0:T(8,128)(2,1)}, bf16[24,2432]{1,0:T(8,128)(2,1)}, u32[]{:S(2)}, u32[]{:S(2)}) collective-permute-start(bf16[24,2432]{1,0:T(8,128)(2,1)} %fusion.84), channel_id=1, source_target_pairs={{0,8},{1,9},{2,10},{3,11},{4,12},{5,13},{6,14},{7,15},{8,0},{9,1},... | collective-permute-start | bytes 350216 | tf_op jit(solution)/shard_map/ppermute | solution.py:524
  8.2 10.2 %collective-permute-start = (bf16[24,2432]{1,0:T(8,128)(2,1)}, bf16[24,2432]{1,0:T(8,128)(2,1)}, u32[]{:S(2)}, u32[]{:S(2)}) collective-permute-start(bf16[24,2432]{1,0:T(8,128)(2,1)} %fusion.84), channel_id=1, source_target_pairs={{0,16},{1,17},{2,18},{3,19},{4,20},{5,21},{6,22},{7,23},{8,24},{9,... | collective-permute-start | bytes 350216 | tf_op jit(solution)/shard_map/ppermute | solution.py:524
  11.3 5.6 %collective-permute-start.3 = (bf16[24,1920]{1,0:T(8,128)(2,1)}, bf16[24,1920]{1,0:T(8,128)(2,1)}, u32[]{:S(2)}, u32[]{:S(2)}) collective-permute-start(bf16[24,1920]{1,0:T(8,128)(2,1)} %fusion.85), channel_id=1, source_target_pairs={{0,1},{1,0},{2,3},{3,2},{4,5},{5,4},{6,7},{7,6},{8,9},{9,8},{10,11... | collective-permute-start | bytes 276488 | tf_op jit(solution)/shard_map/ppermute | solution.py:524
  19.5 11.6 %collective-permute-start.6 = (bf16[48,1920]{1,0:T(8,128)(2,1)S(1)}, bf16[48,1920]{1,0:T(8,128)(2,1)S(1)}, u32[]{:S(2)}, u32[]{:S(2)}) collective-permute-start(bf16[48,1920]{1,0:T(8,128)(2,1)S(1)} %pad_maximum_fusion.24), channel_id=1, source_target_pairs={{0,16},{1,17},{2,18},{3,19},{4,20},{5,21},{6,22},{7,23},{8,24},{9,... | collective-permute-start | bytes 552968 | tf_op jit(solution)/shard_map/ppermute | solution.py:524
  21.5 9.6 %collective-permute-start.4 = (bf16[96,1536]{1,0:T(8,128)(2,1)S(1)}, bf16[96,1536]{1,0:T(8,128)(2,1)S(1)}, u32[]{:S(2)}, u32[]{:S(2)}) collective-permute-start(bf16[96,1536]{1,0:T(8,128)(2,1)S(1)} %pad_maximum_fusion.20), channel_id=1, source_target_pairs={{0,4},{1,5},{2,6},{3,7},{4,0},{5,1},{6,2},{7,3},{8,12},{9,13},{10,... | collective-permute-start | bytes 884744 | tf_op jit(solution)/shard_map/ppermute | solution.py:524
  23.1 9.5 %collective-permute-start.5 = (bf16[96,1664]{1,0:T(8,128)(2,1)S(1)}, bf16[96,1664]{1,0:T(8,128)(2,1)S(1)}, u32[]{:S(2)}, u32[]{:S(2)}) collective-permute-start(bf16[96,1664]{1,0:T(8,128)(2,1)S(1)} %pad_maximum_fusion.18), channel_id=1, source_target_pairs={{0,2},{1,3},{2,0},{3,1},{4,6},{5,7},{6,4},{7,5},{8,10},{9,11},{10,... | collective-permute-start | bytes 958472 | tf_op jit(solution)/shard_map/ppermute | solution.py:524
  32.7 10.0 %collective-permute-start.9 = (bf16[96,1920]{1,0:T(8,128)(2,1)S(1)}, bf16[96,1920]{1,0:T(8,128)(2,1)S(1)}, u32[]{:S(2)}, u32[]{:S(2)}) collective-permute-start(bf16[96,1920]{1,0:T(8,128)(2,1)S(1)} %pad_maximum_fusion.17), channel_id=1, source_target_pairs={{0,8},{1,9},{2,10},{3,11},{4,12},{5,13},{6,14},{7,15},{8,0},{9,1},... | collective-permute-start | bytes 1105928 | tf_op jit(solution)/shard_map/ppermute | solution.py:524
  34.9 11.0 %collective-permute-start.7 = (bf16[192,1152]{1,0:T(8,128)(2,1)S(1)}, bf16[192,1152]{1,0:T(8,128)(2,1)S(1)}, u32[]{:S(2)}, u32[]{:S(2)}) collective-permute-start(bf16[192,1152]{1,0:T(8,128)(2,1)S(1)} %slice.358), channel_id=1, source_target_pairs={{0,2},{1,3},{2,0},{3,1},{4,6},{5,7},{6,4},{7,5},{8,10},{9,11},{10,... | collective-permute-start | bytes 1327112 | tf_op jit(solution)/shard_map/ppermute | solution.py:524
  36.5 11.8 %collective-permute-start.8 = (bf16[192,1280]{1,0:T(8,128)(2,1)S(1)}, bf16[192,1280]{1,0:T(8,128)(2,1)S(1)}, u32[]{:S(2)}, u32[]{:S(2)}) collective-permute-start(bf16[192,1280]{1,0:T(8,128)(2,1)S(1)} %slice.359), channel_id=1, source_target_pairs={{0,4},{1,5},{2,6},{3,7},{4,0},{5,1},{6,2},{7,3},{8,12},{9,13},{10,... | collective-permute-start | bytes 1474568 | tf_op jit(solution)/shard_map/ppermute | solution.py:524
  48.4 3.9 %collective-permute-start.11 = (bf16[384,1280]{1,0:T(8,128)(2,1)S(1)}, bf16[384,1280]{1,0:T(8,128)(2,1)S(1)}, u32[]{:S(2)}, u32[]{:S(2)}) collective-permute-start(bf16[384,1280]{1,0:T(8,128)(2,1)S(1)} %pad_maximum_fusion.8.refs_4_), channel_id=1, source_target_pairs={{0,1},{1,0},{2,3},{3,2},{4,5},{5,4},{6,7},{7,6},{8,9},{9,8},{10,11... | collective-permute-start | bytes 2949128 | tf_op jit(solution)/shard_map/ppermute | solution.py:524
  48.5 3.8 %collective-permute-start.10 = (bf16[384,1152]{1,0:T(8,128)(2,1)S(1)}, bf16[384,1152]{1,0:T(8,128)(2,1)S(1)}, u32[]{:S(2)}, u32[]{:S(2)}) collective-permute-start(bf16[384,1152]{1,0:T(8,128)(2,1)S(1)} %pad_maximum_fusion.9.refs_2_), channel_id=1, source_target_pairs={{0,1},{1,0},{2,3},{3,2},{4,5},{5,4},{6,7},{7,6},{8,9},{9,8},{10,11... | collective-permute-start | bytes 2654216 | tf_op jit(solution)/shard_map/ppermute | solution.py:524
  52.3 16.0 %collective-permute-start.14 = (bf16[192,768]{1,0:T(8,128)(2,1)S(1)}, bf16[192,768]{1,0:T(8,128)(2,1)S(1)}, u32[]{:S(2)}, u32[]{:S(2)}) collective-permute-start(bf16[192,768]{1,0:T(8,128)(2,1)S(1)} %pad_maximum_fusion.21), channel_id=1, source_target_pairs={{0,16},{1,17},{2,18},{3,19},{4,20},{5,21},{6,22},{7,23},{8,24},{9,... | collective-permute-start | bytes 884744 | tf_op jit(solution)/shard_map/ppermute | solution.py:524
  54.3 14.1 %collective-permute-start.13 = (bf16[192,896]{1,0:T(8,128)(2,1)S(1)}, bf16[192,896]{1,0:T(8,128)(2,1)S(1)}, u32[]{:S(2)}, u32[]{:S(2)}) collective-permute-start(bf16[192,896]{1,0:T(8,128)(2,1)S(1)} %slice.363), channel_id=1, source_target_pairs={{0,2},{1,3},{2,0},{3,1},{4,6},{5,7},{6,4},{7,5},{8,10},{9,11},{10,... | collective-permute-start | bytes 1032200 | tf_op jit(solution)/shard_map/ppermute | solution.py:524
  55.3 13.2 %collective-permute-start.12 = (bf16[192,1024]{1,0:T(8,128)(2,1)S(1)}, bf16[192,1024]{1,0:T(8,128)(2,1)S(1)}, u32[]{:S(2)}, u32[]{:S(2)}) collective-permute-start(bf16[192,1024]{1,0:T(8,128)(2,1)S(1)} %slice.362), channel_id=1, source_target_pairs={{0,4},{1,5},{2,6},{3,7},{4,0},{5,1},{6,2},{7,3},{8,12},{9,13},{10,... | collective-permute-start | bytes 1179656 | tf_op jit(solution)/shard_map/ppermute | solution.py:524
  68.5 15.3 %collective-permute-start.15 = (bf16[384,768]{1,0:T(8,128)(2,1)S(1)}, bf16[384,768]{1,0:T(8,128)(2,1)S(1)}, u32[]{:S(2)}, u32[]{:S(2)}) collective-permute-start(bf16[384,768]{1,0:T(8,128)(2,1)S(1)} %pad_maximum_fusion.15), channel_id=1, source_target_pairs={{0,8},{1,9},{2,10},{3,11},{4,12},{5,13},{6,14},{7,15},{8,0},{9,1},... | collective-permute-start | bytes 1769480 | tf_op jit(solution)/shard_map/ppermute | solution.py:524
  68.6 17.4 %collective-permute-start.17 = (bf16[384,896]{1,0:T(8,128)(2,1)S(1)}, bf16[384,896]{1,0:T(8,128)(2,1)S(1)}, u32[]{:S(2)}, u32[]{:S(2)}) collective-permute-start(bf16[384,896]{1,0:T(8,128)(2,1)S(1)} %pad_maximum_fusion.12), channel_id=1, source_target_pairs={{0,4},{1,5},{2,6},{3,7},{4,0},{5,1},{6,2},{7,3},{8,12},{9,13},{10,... | collective-permute-start | bytes 2064392 | tf_op jit(solution)/shard_map/ppermute | solution.py:524
  69.2 19.2 %collective-permute-start.16 = (bf16[384,1024]{1,0:T(8,128)(2,1)S(1)}, bf16[384,1024]{1,0:T(8,128)(2,1)S(1)}, u32[]{:S(2)}, u32[]{:S(2)}) collective-permute-start(bf16[384,1024]{1,0:T(8,128)(2,1)S(1)} %pad_maximum_fusion.10), channel_id=1, source_target_pairs={{0,2},{1,3},{2,0},{3,1},{4,6},{5,7},{6,4},{7,5},{8,10},{9,11},{10,... | collective-permute-start | bytes 2359304 | tf_op jit(solution)/shard_map/ppermute | solution.py:524
  89.7 19.5 %collective-permute-start.20 = (bf16[768,1024]{1,0:T(8,128)(2,1)}, bf16[768,1024]{1,0:T(8,128)(2,1)}, u32[]{:S(2)}, u32[]{:S(2)}) collective-permute-start(bf16[768,1024]{1,0:T(8,128)(2,1)} %pad_maximum_fusion.1.refs_9_), channel_id=1, source_target_pairs={{0,1},{1,0},{2,3},{3,2},{4,5},{5,4},{6,7},{7,6},{8,9},{9,8},{10,11... | collective-permute-start | bytes 4718600 | tf_op jit(solution)/shard_map/ppermute | solution.py:524
  89.7 19.5 %collective-permute-start.21 = (bf16[768,896]{1,0:T(8,128)(2,1)}, bf16[768,896]{1,0:T(8,128)(2,1)}, u32[]{:S(2)}, u32[]{:S(2)}) collective-permute-start(bf16[768,896]{1,0:T(8,128)(2,1)} %pad_maximum_fusion.2.refs_11_), channel_id=1, source_target_pairs={{0,1},{1,0},{2,3},{3,2},{4,5},{5,4},{6,7},{7,6},{8,9},{9,8},{10,11... | collective-permute-start | bytes 4128776 | tf_op jit(solution)/shard_map/ppermute | solution.py:524
  91.3 17.3 %collective-permute-start.19 = (bf16[768,384]{1,0:T(8,128)(2,1)}, bf16[768,384]{1,0:T(8,128)(2,1)}, u32[]{:S(2)}, u32[]{:S(2)}) collective-permute-start(bf16[768,384]{1,0:T(8,128)(2,1)} %get-tuple-element.267.refs_17_), channel_id=1, source_target_pairs={{0,4},{1,5},{2,6},{3,7},{4,0},{5,1},{6,2},{7,3},{8,12},{9,13},{10,... | collective-permute-start | bytes 1769480 | tf_op jit(solution)/shard_map/ppermute | solution.py:524
  92.8 16.3 %collective-permute-start.18 = (bf16[768,384]{1,0:T(8,128)(2,1)}, bf16[768,384]{1,0:T(8,128)(2,1)}, u32[]{:S(2)}, u32[]{:S(2)}) collective-permute-start(bf16[768,384]{1,0:T(8,128)(2,1)} %get-tuple-element.268.refs_13_), channel_id=1, source_target_pairs={{0,2},{1,3},{2,0},{3,1},{4,6},{5,7},{6,4},{7,5},{8,10},{9,11},{10,... | collective-permute-start | bytes 1769480 | tf_op jit(solution)/shard_map/ppermute | solution.py:524
  96.5 14.5 %collective-permute-start.24 = (bf16[768,384]{1,0:T(8,128)(2,1)}, bf16[768,384]{1,0:T(8,128)(2,1)}, u32[]{:S(2)}, u32[]{:S(2)}) collective-permute-start(bf16[768,384]{1,0:T(8,128)(2,1)} %get-tuple-element.267.refs_17_), channel_id=1, source_target_pairs={{0,1},{1,0},{2,3},{3,2},{4,5},{5,4},{6,7},{7,6},{8,9},{9,8},{10,11... | collective-permute-start | bytes 1769480 | tf_op jit(solution)/shard_map/ppermute | solution.py:524
  108.6 2.5 collective-permute-start.22
  109.2 2.8 collective-permute-start.23
  109.2 3.6 %collective-permute-start.25 = (bf16[768,384]{1,0:T(8,128)(2,1)}, bf16[768,384]{1,0:T(8,128)(2,1)}, u32[]{:S(2)}, u32[]{:S(2)}) collective-permute-start(bf16[768,384]{1,0:T(8,128)(2,1)} %collective-permute-done.19.refs_18_), channel_id=1, source_target_pairs={{0,1},{1,0},{2,3},{3,2},{4,5},{5,4},{6,7},{7,6},{8,9},{9,8},{10,11... | collective-permute-start | bytes 1769480 | tf_op jit(solution)/shard_map/ppermute | solution.py:524
  175.3 7.6 %collective-permute-start.26 = (bf16[384,3072]{1,0:T(8,128)(2,1)}, bf16[384,3072]{1,0:T(8,128)(2,1)S(1)}, u32[]{:S(2)}, u32[]{:S(2)}) collective-permute-start(bf16[384,3072]{1,0:T(8,128)(2,1)} %get-tuple-element.199), channel_id=1, source_target_pairs={{0,1},{1,0},{2,3},{3,2},{4,5},{5,4},{6,7},{7,6},{8,9},{9,8},{10,11... | collective-permute-start | bytes 7077896 | tf_op jit(solution)/shard_map/ppermute | solution.py:524
  175.7 7.7 %collective-permute-start.27 = (bf16[1536,768]{1,0:T(8,128)(2,1)}, bf16[1536,768]{1,0:T(8,128)(2,1)S(1)}, u32[]{:S(2)}, u32[]{:S(2)}) collective-permute-start(bf16[1536,768]{1,0:T(8,128)(2,1)} %get-tuple-element.200), channel_id=1, source_target_pairs={{0,1},{1,0},{2,3},{3,2},{4,5},{5,4},{6,7},{7,6},{8,9},{9,8},{10,11... | collective-permute-start | bytes 7077896 | tf_op jit(solution)/shard_map/ppermute | solution.py:524
  183.8 28.8 %collective-permute-start.29 = (bf16[768,768]{1,0:T(8,128)(2,1)S(1)}, bf16[768,768]{1,0:T(8,128)(2,1)S(1)}, u32[]{:S(2)}, u32[]{:S(2)}) collective-permute-start(bf16[768,768]{1,0:T(8,128)(2,1)S(1)} %add_convert_fusion), channel_id=1, source_target_pairs={{0,4},{1,5},{2,6},{3,7},{4,0},{5,1},{6,2},{7,3},{8,12},{9,13},{10,... | collective-permute-start | bytes 3538952 | tf_op jit(solution)/shard_map/ppermute | solution.py:524
  185.6 28.3 %collective-permute-start.28 = (bf16[192,3072]{1,0:T(8,128)(2,1)S(1)}, bf16[192,3072]{1,0:T(8,128)(2,1)S(1)}, u32[]{:S(2)}, u32[]{:S(2)}) collective-permute-start(bf16[192,3072]{1,0:T(8,128)(2,1)S(1)} %add_convert_fusion.1), channel_id=1, source_target_pairs={{0,2},{1,3},{2,0},{3,1},{4,6},{5,7},{6,4},{7,5},{8,10},{9,11},{10,... | collective-permute-start | bytes 3538952 | tf_op jit(solution)/shard_map/ppermute | solution.py:524
  216.0 15.0 %collective-permute-start.31 = (bf16[384,768]{1,0:T(8,128)(2,1)}, bf16[384,768]{1,0:T(8,128)(2,1)S(1)}, u32[]{:S(2)}, u32[]{:S(2)}) collective-permute-start(bf16[384,768]{1,0:T(8,128)(2,1)} %add_convert_fusion.4), channel_id=1, source_target_pairs={{0,2},{1,3},{2,0},{3,1},{4,6},{5,7},{6,4},{7,5},{8,10},{9,11},{10,... | collective-permute-start | bytes 1769480 | tf_op jit(solution)/shard_map/ppermute | solution.py:524
  217.5 14.7 %collective-permute-start.30 = (bf16[96,3072]{1,0:T(8,128)(2,1)}, bf16[96,3072]{1,0:T(8,128)(2,1)S(1)}, u32[]{:S(2)}, u32[]{:S(2)}) collective-permute-start(bf16[96,3072]{1,0:T(8,128)(2,1)} %add_convert_fusion.5), channel_id=1, source_target_pairs={{0,4},{1,5},{2,6},{3,7},{4,0},{5,1},{6,2},{7,3},{8,12},{9,13},{10,... | collective-permute-start | bytes 1769480 | tf_op jit(solution)/shard_map/ppermute | solution.py:524
  236.5 3.5 %collective-permute-start.32 = (bf16[384,1536]{1,0:T(8,128)(2,1)S(1)}, bf16[384,1536]{1,0:T(8,128)(2,1)S(1)}, u32[]{:S(2)}, u32[]{:S(2)}) collective-permute-start(bf16[384,1536]{1,0:T(8,128)(2,1)S(1)} %pad_maximum_fusion.4), channel_id=1, source_target_pairs={{0,1},{1,0},{2,3},{3,2},{4,5},{5,4},{6,7},{7,6},{8,9},{9,8},{10,11... | collective-permute-start | bytes 3538952 | tf_op jit(solution)/shard_map/ppermute | solution.py:524
  236.6 4.5 %collective-permute-start.33 = (bf16[384,1536]{1,0:T(8,128)(2,1)S(1)}, bf16[384,1536]{1,0:T(8,128)(2,1)S(1)}, u32[]{:S(2)}, u32[]{:S(2)}) collective-permute-start(bf16[384,1536]{1,0:T(8,128)(2,1)S(1)} %pad_maximum_fusion.5), channel_id=1, source_target_pairs={{0,1},{1,0},{2,3},{3,2},{4,5},{5,4},{6,7},{7,6},{8,9},{9,8},{10,11... | collective-permute-start | bytes 3538952 | tf_op jit(solution)/shard_map/ppermute | solution.py:524
  241.3 15.9 %collective-permute-start.35 = (bf16[192,1536]{1,0:T(8,128)(2,1)S(1)}, bf16[192,1536]{1,0:T(8,128)(2,1)S(1)}, u32[]{:S(2)}, u32[]{:S(2)}) collective-permute-start(bf16[192,1536]{1,0:T(8,128)(2,1)S(1)} %add_convert_fusion.2), channel_id=1, source_target_pairs={{0,4},{1,5},{2,6},{3,7},{4,0},{5,1},{6,2},{7,3},{8,12},{9,13},{10,... | collective-permute-start | bytes 1769480 | tf_op jit(solution)/shard_map/ppermute | solution.py:524
  241.8 15.4 %collective-permute-start.34 = (bf16[192,1536]{1,0:T(8,128)(2,1)S(1)}, bf16[192,1536]{1,0:T(8,128)(2,1)S(1)}, u32[]{:S(2)}, u32[]{:S(2)}) collective-permute-start(bf16[192,1536]{1,0:T(8,128)(2,1)S(1)} %add_convert_fusion.3), channel_id=1, source_target_pairs={{0,2},{1,3},{2,0},{3,1},{4,6},{5,7},{6,4},{7,5},{8,10},{9,11},{10,... | collective-permute-start | bytes 1769480 | tf_op jit(solution)/shard_map/ppermute | solution.py:524
  242.4 9.9 %collective-permute-start.36 = (bf16[48,3072]{1,0:T(8,128)(2,1)S(1)}, bf16[48,3072]{1,0:T(8,128)(2,1)S(1)}, u32[]{:S(2)}, u32[]{:S(2)}) collective-permute-start(bf16[48,3072]{1,0:T(8,128)(2,1)S(1)} %add_convert_fusion.9), channel_id=1, source_target_pairs={{0,8},{1,9},{2,10},{3,11},{4,12},{5,13},{6,14},{7,15},{8,0},{9,1},... | collective-permute-start | bytes 884744 | tf_op jit(solution)/shard_map/ppermute | solution.py:524
  244.0 13.2 %collective-permute-start.37 = (bf16[192,768]{1,0:T(8,128)(2,1)S(1)}, bf16[192,768]{1,0:T(8,128)(2,1)S(1)}, u32[]{:S(2)}, u32[]{:S(2)}) collective-permute-start(bf16[192,768]{1,0:T(8,128)(2,1)S(1)} %add_convert_fusion.8), channel_id=1, source_target_pairs={{0,8},{1,9},{2,10},{3,11},{4,12},{5,13},{6,14},{7,15},{8,0},{9,1},... | collective-permute-start | bytes 884744 | tf_op jit(solution)/shard_map/ppermute | solution.py:524
  257.6 7.8 %collective-permute-start.38 = (bf16[96,1536]{1,0:T(8,128)(2,1)S(1)}, bf16[96,1536]{1,0:T(8,128)(2,1)S(1)}, u32[]{:S(2)}, u32[]{:S(2)}) collective-permute-start(bf16[96,1536]{1,0:T(8,128)(2,1)S(1)} %add_convert_fusion.7), channel_id=1, source_target_pairs={{0,4},{1,5},{2,6},{3,7},{4,0},{5,1},{6,2},{7,3},{8,12},{9,13},{10,... | collective-permute-start | bytes 884744 | tf_op jit(solution)/shard_map/ppermute | solution.py:524
  259.4 7.4 %collective-permute-start.39 = (bf16[96,1536]{1,0:T(8,128)(2,1)S(1)}, bf16[96,1536]{1,0:T(8,128)(2,1)S(1)}, u32[]{:S(2)}, u32[]{:S(2)}) collective-permute-start(bf16[96,1536]{1,0:T(8,128)(2,1)S(1)} %add_convert_fusion.6), channel_id=1, source_target_pairs={{0,2},{1,3},{2,0},{3,1},{4,6},{5,7},{6,4},{7,5},{8,10},{9,11},{10,... | collective-permute-start | bytes 884744 | tf_op jit(solution)/shard_map/ppermute | solution.py:524
  261.0 12.5 %collective-permute-start.41 = (bf16[24,3072]{1,0:T(8,128)(2,1)S(1)}, bf16[24,3072]{1,0:T(8,128)(2,1)S(1)}, u32[]{:S(2)}, u32[]{:S(2)}) collective-permute-start(bf16[24,3072]{1,0:T(8,128)(2,1)S(1)} %add_convert_fusion.11), channel_id=1, source_target_pairs={{0,16},{1,17},{2,18},{3,19},{4,20},{5,21},{6,22},{7,23},{8,24},{9,... | collective-permute-start | bytes 442376 | tf_op jit(solution)/shard_map/ppermute | solution.py:524
  261.5 13.9 %collective-permute-start.42 = (bf16[96,768]{1,0:T(8,128)(2,1)S(1)}, bf16[96,768]{1,0:T(8,128)(2,1)S(1)}, u32[]{:S(2)}, u32[]{:S(2)}) collective-permute-start(bf16[96,768]{1,0:T(8,128)(2,1)S(1)} %add_convert_fusion.10), channel_id=1, source_target_pairs={{0,16},{1,17},{2,18},{3,19},{4,20},{5,21},{6,22},{7,23},{8,24},{9,... | collective-permute-start | bytes 442376 | tf_op jit(solution)/shard_map/ppermute | solution.py:524
  267.1 11.6 %collective-permute-start.40 = (bf16[48,3072]{1,0:T(8,128)(2,1)S(1)}, bf16[48,3072]{1,0:T(8,128)(2,1)S(1)}, u32[]{:S(2)}, u32[]{:S(2)}) collective-permute-start(bf16[48,3072]{1,0:T(8,128)(2,1)S(1)} %fusion.71), channel_id=1, source_target_pairs={{0,8},{1,9},{2,10},{3,11},{4,12},{5,13},{6,14},{7,15},{8,0},{9,1},... | collective-permute-start | bytes 884744 | tf_op jit(solution)/shard_map/ppermute | solution.py:524
  279.6 7.3 %collective-permute-start.43 = (bf16[24,3072]{1,0:T(8,128)(2,1)}, bf16[24,3072]{1,0:T(8,128)(2,1)}, u32[]{:S(2)}, u32[]{:S(2)}) collective-permute-start(bf16[24,3072]{1,0:T(8,128)(2,1)} %fusion.80), channel_id=1, source_target_pairs={{0,16},{1,17},{2,18},{3,19},{4,20},{5,21},{6,22},{7,23},{8,24},{9,... | collective-permute-start | bytes 442376 | tf_op jit(solution)/shard_map/ppermute | solution.py:524
  290.1 4.0 %collective-permute-start.45 = (f32[80,128]{1,0:T(8,128)S(1)}, f32[80,128]{1,0:T(8,128)S(1)}, u32[]{:S(2)}, u32[]{:S(2)}) collective-permute-start(f32[80,128]{1,0:T(8,128)S(1)} %add.509), channel_id=1, source_target_pairs={{0,2},{1,3},{2,0},{3,1},{4,6},{5,7},{6,4},{7,5},{8,10},{9,11},{10,... | collective-permute-start | bytes 122888 | tf_op jit(solution)/shard_map/ppermute | solution.py:524
  294.1 4.1 %collective-permute-start.46 = (f32[80,128]{1,0:T(8,128)S(1)}, f32[80,128]{1,0:T(8,128)S(1)}, u32[]{:S(2)}, u32[]{:S(2)}) collective-permute-start(f32[80,128]{1,0:T(8,128)S(1)} %add.510), channel_id=1, source_target_pairs={{0,4},{1,5},{2,6},{3,7},{4,0},{5,1},{6,2},{7,3},{8,12},{9,13},{10,... | collective-permute-start | bytes 122888 | tf_op jit(solution)/shard_map/ppermute | solution.py:524
  298.2 4.0 %collective-permute-start.47 = (f32[80,128]{1,0:T(8,128)S(1)}, f32[80,128]{1,0:T(8,128)S(1)}, u32[]{:S(2)}, u32[]{:S(2)}) collective-permute-start(f32[80,128]{1,0:T(8,128)S(1)} %add.511), channel_id=1, source_target_pairs={{0,8},{1,9},{2,10},{3,11},{4,12},{5,13},{6,14},{7,15},{8,0},{9,1},... | collective-permute-start | bytes 122888 | tf_op jit(solution)/shard_map/ppermute | solution.py:524
  302.2 4.9 %collective-permute-start.48 = (f32[80,128]{1,0:T(8,128)S(1)}, f32[80,128]{1,0:T(8,128)S(1)}, u32[]{:S(2)}, u32[]{:S(2)}) collective-permute-start(f32[80,128]{1,0:T(8,128)S(1)} %add.512), channel_id=1, source_target_pairs={{0,16},{1,17},{2,18},{3,19},{4,20},{5,21},{6,22},{7,23},{8,24},{9,... | collective-permute-start | bytes 122888 | tf_op jit(solution)/shard_map/ppermute | solution.py:524
  (61 other events, 568.0 us)
